TPU v7x, 32 devices: a whole 2x2x4 slice. The times are simulated.
32 devices in a mesh: blk: 8 (over y, x, core), sub: 4 (over z).
Axes of the slice: x: 2, y: 2, z: 4, core: 2. Of those that a mesh axis runs over, the one named last changes fastest.
Arguments:
- fluid_temp: float32 [256, 128, 512], P('blk', 'sub'), may hold values from -6 to 6
- velocity: float32 [3, 256, 128, 512], P(None, 'blk', 'sub'), may hold values from -6 to 6
- eddy_diff: float32 [256, 128, 512], P('blk', 'sub'), may hold values from 0.05 to 0.5
- wall_prev: float32 [32768], P(('blk', 'sub')), may hold values from -6 to 6
- row_count: int32 [32], P(('blk', 'sub')), may hold values from 256 to 1024, as said below
- owner_table: int32 [32, 128], P(('blk', 'sub')), may hold values from 0 to 4, as said below
- landing_cell: int32 [32, 1536], P(('blk', 'sub')), may hold values from 0 to 1023
- solid_temp: float32 [256, 128, 256], P('blk', 'sub'), may hold values from -6 to 6
- conductivity: float32 [256, 128, 256], P('blk', 'sub'), may hold values from 0.2 to 5
- sink: float32 [256, 128, 256], P('blk', 'sub'), may hold values from 0.2 to 2
- heat_source: float32 [256, 128, 256], P('blk', 'sub'), may hold values from -6 to 6
Outputs:
- fluid_new: float32 [256, 128, 512], P('blk', 'sub')
- solid_new: float32 [256, 128, 256], P('blk', 'sub')
- wall_new: float32 [32768], P(('blk', 'sub'))
Inputs may be any that keep to these rules, and one draw needn't show every extreme that they name: `row_count`: live rows of a fluid block; some block has all 1024 live in every draw. `owner_table`: no group points outside the grid of blocks; at least half of a block's groups are 0; at most 16 groups of a block have any one direction from 1 to 4, and some solid block receives exactly that many from every neighbour it has.
All inputs are finite; a program needn't handle non-finite values.
Results may differ from a plain program's by a relative error of at most 0.0003.
Values sent between devices are 32-bit elements; how exact they have to be, the bound alone decides.
No kernel may reach another device: no remote copies, remote signals or barrier semaphores. Data moves between devices by JAX's collectives and lax.ppermute only.
A program may use at most 128 MiB of HBM per device.

v0:
```python
import jax
import jax.numpy as jnp
from jax import lax
from jax.sharding import PartitionSpec as P

FLUID_SWEEPS = 2
SWEEPS = 8


RELAX_FACTOR = 0.8
EIG_LOW = 0.02
EIG_HIGH = 2.0


def from_behind(value, axis, steps):
    count = lax.axis_size(axis)
    initial, last = (max(0, -steps), min(count, count - steps))
    return lax.ppermute(value, axis, [(source, source + steps) for source in range(initial, last)])


def extended(block, sides, width):
    for axis, dim in sides:
        count = lax.axis_size(axis)
        forward = [(i, i + 1) for i in range(count - 1)]
        backward = [(target, source) for source, target in forward]
        low = lax.ppermute(
            lax.slice_in_dim(block, block.shape[dim] - width, None, axis=dim), axis, forward
        )
        high = lax.ppermute(lax.slice_in_dim(block, 0, width, axis=dim), axis, backward)
        block = jnp.concatenate([low, block, high], axis=dim)
    return block


def face_slice(values_in, axis_no, start):
    slicer = [slice(1, -1)] * 3
    slicer[axis_no] = slice(start, values_in.shape[axis_no] - 1 + start)
    return values_in[tuple(slicer)]


def fluid_update(temp_pad, velo_pad, alpha_pad):
    center_val = temp_pad[1:-1, 1:-1, 1:-1]
    residue = jnp.zeros_like(center_val)
    weight = jnp.zeros_like(center_val)
    for axis_no in range(3):
        lower_val = face_slice(temp_pad, axis_no, 0)
        upper_val = face_slice(temp_pad, axis_no, 1)
        face_speed = 0.5 * (
            face_slice(velo_pad[axis_no], axis_no, 0) + face_slice(velo_pad[axis_no], axis_no, 1)
        )
        face_diff = 0.5 * (face_slice(alpha_pad, axis_no, 0) + face_slice(alpha_pad, axis_no, 1))
        face_flux = (
            jnp.maximum(face_speed, 0.0) * lower_val
            + jnp.minimum(face_speed, 0.0) * upper_val
            - face_diff * (upper_val - lower_val)
        )
        count_faces = face_flux.shape[axis_no]
        residue = residue - (
            lax.slice_in_dim(face_flux, 1, count_faces, axis=axis_no)
            - lax.slice_in_dim(face_flux, 0, count_faces - 1, axis=axis_no)
        )
        face_weight = face_diff + 0.5 * jnp.abs(face_speed)
        weight = (
            weight
            + lax.slice_in_dim(face_weight, 1, count_faces, axis=axis_no)
            + lax.slice_in_dim(face_weight, 0, count_faces - 1, axis=axis_no)
        )
    return center_val + RELAX_FACTOR * residue / weight


def wall_pad(temp_rim, wall_temp, live_plane):
    wall_cell = temp_rim[1:-1, 1:-1, 0]
    ghost_val = jnp.pad(wall_cell + live_plane * 2.0 * (wall_temp - wall_cell), 1)
    return jnp.concatenate(
        [ghost_val[:, :, None], temp_rim, jnp.zeros_like(ghost_val)[:, :, None]], axis=2
    )


def edge_pad(values_in):
    return jnp.pad(values_in, ((0, 0), (0, 0), (1, 1)), mode="edge")


def flow_pad(flow_rim):
    normal_speed = flow_rim[2]
    normal_pad = jnp.concatenate(
        [-normal_speed[:, :, :1], normal_speed, normal_speed[:, :, -1:]], axis=2
    )
    velo_pad = jnp.stack([edge_pad(flow_rim[0]), edge_pad(flow_rim[1]), normal_pad])
    return (velo_pad, edge_pad(flow_rim[3]))


def conduct(state_pad, cond_pad, diag_extra, rhs_field):
    center_val = state_pad[1:-1, 1:-1]
    center_cond = cond_pad[1:-1, 1:-1]
    state_z = jnp.pad(center_val, ((0, 0), (0, 0), (1, 1)))
    cond_z = jnp.pad(center_cond, ((0, 0), (0, 0), (1, 1)))
    neighbours = [
        (state_pad[2:, 1:-1], cond_pad[2:, 1:-1]),
        (state_pad[:-2, 1:-1], cond_pad[:-2, 1:-1]),
        (state_pad[1:-1, 2:], cond_pad[1:-1, 2:]),
        (state_pad[1:-1, :-2], cond_pad[1:-1, :-2]),
        (state_z[:, :, 2:], cond_z[:, :, 2:]),
        (state_z[:, :, :-2], cond_z[:, :, :-2]),
    ]
    applied = diag_extra * center_val
    diag_sum = diag_extra
    for near_val, near_cond in neighbours:
        summed = center_cond + near_cond
        conduct_face = 2.0 * center_cond * near_cond / jnp.where(summed > 0.0, summed, 1.0)
        applied = applied + conduct_face * (center_val - near_val)
        diag_sum = diag_sum + conduct_face
    return (rhs_field - applied) / jnp.where(diag_sum > 0.0, diag_sum, 1.0)


def cheby_coefficients(count_sweeps):
    center_eig = 0.5 * (EIG_HIGH + EIG_LOW)
    half_width = 0.5 * (EIG_HIGH - EIG_LOW)
    ratio_eig = center_eig / half_width
    damping = 1.0 / ratio_eig
    coefficients = [(0.0, 1.0 / center_eig)]
    for sweep_no in range(1, count_sweeps):
        damping_new = 1.0 / (2.0 * ratio_eig - damping)
        coefficients.append((damping_new * damping, 2.0 * damping_new / half_width))
        damping = damping_new
    return coefficients


def trim_rim(values_in, width):
    if width == 0:
        return values_in
    return values_in[width:-width, width:-width]


def inside_mask(pad_now, solid_x, solid_y):
    row_pos = (
        lax.axis_index("blk") * solid_x
        + jnp.arange(solid_x + 2 * pad_now, dtype=jnp.int32)
        - pad_now
    )
    col_pos = (
        lax.axis_index("sub") * solid_y
        + jnp.arange(solid_y + 2 * pad_now, dtype=jnp.int32)
        - pad_now
    )
    row_good = (row_pos >= 0) & (row_pos < solid_x * lax.axis_size("blk"))
    col_good = (col_pos >= 0) & (col_pos < solid_y * lax.axis_size("sub"))
    return (row_good[:, None] & col_good[None, :]).astype(jnp.float32)[:, :, None]


def run_block(
    solid_now, update, wide_cond, wide_extra, wide_rhs, coefficients, depth_cut, solid_x, solid_y
):
    for counter, (decay, gain_term) in enumerate(coefficients):
        pad_now = depth_cut - counter
        scaled_res = conduct(
            solid_now,
            trim_rim(wide_cond, counter),
            trim_rim(wide_extra, counter + 1),
            trim_rim(wide_rhs, counter + 1),
        )
        scaled_res = scaled_res * inside_mask(pad_now - 1, solid_x, solid_y)
        update = decay * trim_rim(update, 1) + gain_term * scaled_res
        solid_now = trim_rim(solid_now, 1) + update
    return (solid_now, update)


def pick_groups(group_dirs, dir_code, near_groups):
    matched = group_dirs == dir_code
    group_rank = jnp.cumsum(matched.astype(jnp.int32)) - 1
    slot_ids = jnp.arange(near_groups, dtype=jnp.int32)
    return (matched[:, None] & (group_rank[:, None] == slot_ids[None, :])).astype(jnp.float32)


def move_span(payload, step_by):
    return from_behind(payload, "blk", step_by)


def move_chord(payload, step_by):
    return from_behind(payload, "sub", step_by)


def return_span(payload, step_by):
    return from_behind(payload, "blk", step_by)


def return_chord(payload, step_by):
    return from_behind(payload, "sub", step_by)


def on_device(
    fluid_temp,
    velocity,
    eddy_diff,
    wall_prev,
    row_count,
    owner_table,
    landing_cell,
    solid_temp,
    conductivity,
    sink,
    heat_source,
):
    cells_x, cells_y, cells_z = fluid_temp.shape
    row_total = cells_x * cells_y
    live_rows = (jnp.arange(row_total, dtype=jnp.int32) < row_count[0]).astype(jnp.float32)
    wall_temp = wall_prev.reshape(cells_x, cells_y)
    live_plane = live_rows.reshape(cells_x, cells_y)
    flow_stack = jnp.concatenate([velocity, eddy_diff[None]], axis=0)
    flow_rim = extended(flow_stack, (("blk", 1), ("sub", 2)), 1)
    velo_pad, alpha_pad = flow_pad(flow_rim)
    fluid_now = fluid_temp
    for sweep_no in range(FLUID_SWEEPS):
        temp_rim = extended(fluid_now, (("blk", 0), ("sub", 1)), 1)
        fluid_now = fluid_update(wall_pad(temp_rim, wall_temp, live_plane), velo_pad, alpha_pad)
    group_dirs = owner_table[0]
    group_total = group_dirs.shape[0]
    slot_cap = row_total // group_total
    near_groups = group_total // 8
    near_rows = near_groups * slot_cap
    dir_rows = jnp.repeat(group_dirs, slot_cap)
    self_mask = (dir_rows == 0).astype(jnp.float32)
    gas_temp = fluid_now[:, :, 0].reshape(-1)
    film_coeff = 2.0 * eddy_diff[:, :, 0].reshape(-1) * live_rows
    row_pair = jnp.stack([film_coeff, gas_temp]).reshape(2, group_total, slot_cap)
    selections = [pick_groups(group_dirs, dir_code, near_groups) for dir_code in (1, 2, 3, 4)]
    outbound = [
        jnp.einsum("cgk,gs->csk", row_pair, selection, precision=lax.Precision.HIGHEST).reshape(
            2, near_rows
        )
        for selection in selections
    ]
    arrived = [
        move_span(outbound[0], 1),
        move_span(outbound[1], -1),
        move_chord(outbound[2], 1),
        move_chord(outbound[3], -1),
    ]
    film_in = jnp.concatenate([film_coeff * self_mask] + [piece[0] for piece in arrived])
    gas_in = jnp.concatenate([gas_temp] + [piece[1] for piece in arrived])
    solid_x, solid_y, solid_z = solid_temp.shape
    landing = landing_cell[0]
    film_sum = jax.ops.segment_sum(film_in, landing, num_segments=solid_x * solid_y)
    film_gas = jax.ops.segment_sum(film_in * gas_in, landing, num_segments=solid_x * solid_y)
    surface_mask = (jnp.arange(solid_z, dtype=jnp.int32) == 0).astype(jnp.float32)
    diag_extra = sink + film_sum.reshape(solid_x, solid_y)[:, :, None] * surface_mask
    rhs_field = heat_source + film_gas.reshape(solid_x, solid_y)[:, :, None] * surface_mask
    coefficients = cheby_coefficients(SWEEPS)
    depth_cut = SWEEPS // 2
    packed = extended(
        jnp.stack([conductivity, diag_extra, rhs_field, solid_temp]),
        (("blk", 1), ("sub", 2)),
        depth_cut,
    )
    wide_cond = packed[0]
    wide_extra = packed[1]
    wide_rhs = packed[2]
    solid_now, update = run_block(
        packed[3],
        jnp.zeros_like(packed[3]),
        wide_cond,
        wide_extra,
        wide_rhs,
        coefficients[:depth_cut],
        depth_cut,
        solid_x,
        solid_y,
    )
    restack = extended(jnp.stack([solid_now, update]), (("blk", 1), ("sub", 2)), depth_cut)
    solid_now, update = run_block(
        restack[0],
        restack[1],
        wide_cond,
        wide_extra,
        wide_rhs,
        coefficients[depth_cut:],
        depth_cut,
        solid_x,
        solid_y,
    )
    surface = solid_now[:, :, 0].reshape(-1)
    slot_values = surface[landing]
    band_values = [
        slot_values[row_total + dir_index * near_rows : row_total + (dir_index + 1) * near_rows]
        for dir_index in range(4)
    ]
    returned_bands = [
        return_span(band_values[0], -1),
        return_span(band_values[1], 1),
        return_chord(band_values[2], -1),
        return_chord(band_values[3], 1),
    ]
    wall_sum = self_mask * slot_values[:row_total]
    for dir_index in range(4):
        spread = jnp.einsum(
            "sk,gs->gk",
            returned_bands[dir_index].reshape(near_groups, slot_cap),
            selections[dir_index],
            precision=lax.Precision.HIGHEST,
        )
        wall_sum = wall_sum + spread.reshape(row_total)
    wall_new = wall_sum * live_rows
    return (fluid_now, solid_now, wall_new)


def solution(mesh):
    return jax.shard_map(
        on_device,
        mesh=mesh,
        in_specs=(
            P("blk", "sub", None),
            P(None, "blk", "sub", None),
            P("blk", "sub", None),
            P(("blk", "sub")),
            P(("blk", "sub")),
            P(("blk", "sub"), None),
            P(("blk", "sub"), None),
            P("blk", "sub", None),
            P("blk", "sub", None),
            P("blk", "sub", None),
            P("blk", "sub", None),
        ),
        out_specs=(P("blk", "sub", None), P("blk", "sub", None), P(("blk", "sub"))),
        check_vma=False,
    )
```

profile of v0, /device:TPU:27, one launch (start us, length us, event | category | flops | bytes accessed | tf_op | source)
XLA Modules:
  0.0 294.8 jit_solution(14493114021661385094)
XLA Ops:
  44.0 7.0 %pad_maximum_fusion = f32[4,34,34,512]{3,2,1,0:T(8,128)} fusion(f32[4,34,1,512]{3,2,1,0:T(1,128)S(1)} %copy.235, f32[4,1,32,512]{3,2,1,0:T(8,128)S(1)} %collective-permute-done.1, f32[1,32,32,512]{3,2,1,0:T(8,128)S(1)} %bitcast.119, f32[3,32,32,512]{3,2,1,0:T(8,128)S(1)} %bitcast.116, f32[4,1,32,512]{3,2,1,0:T(8,128)S(1)} %collective-permute-done, ...), kind=kLoop, calls=%fused_computation.3 | loop fusion | flops 11837440 | bytes 18939904 | tf_op jit(solution)/shard_map/concatenate | solution.py:30
  50.9 7.5 %slice_bitcast_fusion.3 = (f32[34,34,512]{2,1,0:T(8,128)}, f32[34,34,512]{2,1,0:T(8,128)S(1)}, f32[34,34,512]{2,1,0:T(8,128)S(1)}, f32[34,34,512]{2,1,0:T(8,128)S(1)}) fusion(f32[4,34,34,512]{3,2,1,0:T(8,128)} %pad_maximum_fusion), kind=kLoop, calls=%fused_computation.37 | loop fusion | bytes 18939904 | tf_op jit(solution)/shard_map/squeeze | solution.py:87
  66.5 5.6 %multiply_add_fusion = f32[32,32,513]{2,1,0:T(8,128)S(1)} fusion(f32[34,34,1]{2,1,0:T(8,128)S(1)} %get-tuple-element.56, f32[34,34,512]{2,1,0:T(8,128)S(1)} %get-tuple-element.32, f32[34,34,1]{2,1,0:T(8,128)S(1)} %get-tuple-element.55, f32[34,34,1]{2,1,0:T(8,128)} %get-tuple-element.54, f32[34,34,512]{2,1,0:T(8,128)S(1)} %get-tuple-element.34, ...), kind=kLoop, calls=%fused_computation.83 | loop fusion | flops 5778432 | bytes 6854720 | tf_op jit(solution)/shard_map/add | solution.py:61
  72.2 4.7 %multiply_subtract_fusion.2 = f32[32,32,513]{2,1,0:T(8,128)S(1)} fusion(f32[34,1,512]{2,1,0:T(1,128)S(1)} %collective-permute-done.7, f32[34,32,512]{2,1,0:T(8,128)S(1)} %copy-done.15, f32[34,1,512]{2,1,0:T(1,128)} %collective-permute-done.6, f32[34,34,1]{2,1,0:T(8,128)S(1)} %copy-done.20, f32[34,34,1]{2,1,0:T(8,128)S(1)} %get-tuple-element.56, ...), kind=kLoop, calls=%fused_computation.85 | loop fusion | flops 13132800 | bytes 9226832 | tf_op jit(solution)/shard_map/sub | solution.py:52
  77.0 4.6 %multiply_add_fusion.1 = (f32[32,33,512]{2,1,0:T(8,128)S(1)}, f32[32,33,512]{2,1,0:T(8,128)}) fusion(f32[34,34,512]{2,1,0:T(8,128)S(1)} %get-tuple-element.33, f32[34,34,512]{2,1,0:T(8,128)S(1)} %get-tuple-element.34, f32[34,1,512]{2,1,0:T(1,128)S(1)} %collective-permute-done.7, f32[34,32,512]{2,1,0:T(8,128)S(1)} %copy-done.15, ...), kind=kLoop, calls=%fused_computation.84 | loop fusion | flops 9191424 | bytes 15343616 | tf_op jit(solution)/shard_map/add | solution.py:61
  81.6 6.5 %fusion.23 = (f32[32,32,512]{2,1,0:T(8,128)S(1)}, f32[32,32,512]{2,1,0:T(8,128)}) fusion(f32[32,32,512]{2,1,0:T(8,128)} %param.11, f32[32,32,513]{2,1,0:T(8,128)S(1)} %multiply_subtract_fusion.2, f32[32,33,512]{2,1,0:T(8,128)} %get-tuple-element.46, f32[33,32,512]{2,1,0:T(8,128)S(1)} %get-tuple-element.44, f32[32,32,513]{2,1,0:T(8,128)S(1)} %multiply_add_fusion, ...), kind=kLoop, calls=%fused_computation.132 | loop fusion | flops 7340032 | bytes 31457280 | tf_op jit(solution)/shard_map/add | solution.py:67
  91.7 4.5 %collective-permute-start.8 = (f32[1,32,512]{2,1,0:T(8,128)}, f32[1,32,512]{2,1,0:T(8,128)}, u32[]{:S(2)}, u32[]{:S(2)}) collective-permute-start(f32[1,32,512]{2,1,0:T(8,128)} %get-tuple-element.65), channel_id=1, source_target_pairs={{0,4},{4,8},{8,12},{12,16},{16,20},{20,24},{24,28},{1,5},{5,9},{9,... | collective-permute-start | bytes 196616 | tf_op jit(solution)/shard_map/ppermute | solution.py:26
  111.6 6.8 %multiply_subtract_fusion = f32[32,32,513]{2,1,0:T(8,128)S(1)} fusion(f32[34,1,512]{2,1,0:T(1,128)S(1)} %collective-permute-done.11, f32[1,32,512]{2,1,0:T(8,128)S(1)} %collective-permute-done.9, f32[32,32,512]{2,1,0:T(8,128)S(1)} %copy-done.1, f32[1,32,512]{2,1,0:T(8,128)} %collective-permute-done.8, f32[34,1,512]{2,1,0:T(1,128)S(1)} %collective-permute-done.10, ...), kind=kLoop, calls=%fused_computation.81 | loop fusion | flops 16284672 | bytes 9226832 | tf_op jit(solution)/shard_map/sub | solution.py:52
  122.7 4.8 %collective-permute-start.12 = (f32[2,128]{1,0:T(2,128)S(1)}, f32[2,128]{1,0:T(2,128)S(1)}, u32[]{:S(2)}, u32[]{:S(2)}) collective-permute-start(f32[2,128]{1,0:T(2,128)S(1)} %reshape.465), channel_id=1, source_target_pairs={{0,4},{4,8},{8,12},{12,16},{16,20},{20,24},{24,28},{1,5},{5,9},{9,... | collective-permute-start | bytes 3080 | tf_op jit(solution)/shard_map/ppermute | solution.py:18
  131.7 4.3 %collective-permute-start.15 = (f32[2,128]{1,0:T(2,128)S(1)}, f32[2,128]{1,0:T(2,128)S(1)}, u32[]{:S(2)}, u32[]{:S(2)}) collective-permute-start(f32[2,128]{1,0:T(2,128)S(1)} %reshape.468), channel_id=1, source_target_pairs={{1,0},{2,1},{3,2},{5,4},{6,5},{7,6},{9,8},{10,9},{11,10},{13,12},{... | collective-permute-start | bytes 3080 | tf_op jit(solution)/shard_map/ppermute | solution.py:18
  136.8 11.3 %scatter_custom_fusion = f32[1024]{0:T(1024)S(1)} fusion(s32[1536]{0:T(1024)} %reduce.1, f32[1536]{0:T(1024)S(1)} %get-tuple-element.83, f32[]{:T(128)} %constant.36.clone.1), kind=kCustom, calls=%fused_computation.462 | custom fusion | flops 1536 | bytes 4608 | tf_op jit(solution)/shard_map/scatter-add | solution.py:241
  148.1 11.5 %scatter_custom_fusion.1 = f32[1024]{0:T(1024)S(1)} fusion(s32[1536]{0:T(1024)} %reduce.1, f32[1536]{0:T(1024)S(1)} %mul.702, f32[]{:T(128)} %constant.36.clone.1), kind=kCustom, calls=%fused_computation.460 | custom fusion | flops 1536 | bytes 4608 | tf_op jit(solution)/shard_map/scatter-add | solution.py:242
  163.9 5.4 %collective-permute-start.16 = (f32[4,4,32,256]{3,2,1,0:T(8,128)S(1)}, f32[4,4,32,256]{3,2,1,0:T(8,128)S(1)}, u32[]{:S(2)}, u32[]{:S(2)}) collective-permute-start(f32[4,4,32,256]{3,2,1,0:T(8,128)S(1)} %get-tuple-element.49), channel_id=1, source_target_pairs={{0,4},{4,8},{8,12},{12,16},{16,20},{20,24},{24,28},{1,5},{5,9},{9,... | collective-permute-start | bytes 1572872 | tf_op jit(solution)/shard_map/ppermute | solution.py:26
  169.5 8.6 %collective-permute-done.17 = f32[4,4,32,256]{3,2,1,0:T(8,128)S(1)} collective-permute-done((f32[4,4,32,256]{3,2,1,0:T(8,128)S(1)}, f32[4,4,32,256]{3,2,1,0:T(8,128)S(1)}, u32[]{:S(2)}, u32[]{:S(2)}) %collective-permute-start.17) | collective-permute-done | bytes 524320 | tf_op jit(solution)/shard_map/ppermute | solution.py:29
  183.8 8.6 %collective-permute-done.19 = f32[4,40,4,256]{3,2,1,0:T(4,128)S(1)} collective-permute-done((f32[4,40,4,256]{3,2,1,0:T(4,128)S(1)}, f32[4,40,4,256]{3,2,1,0:T(4,128)S(1)}, u32[]{:S(2)}, u32[]{:S(2)}) %collective-permute-start.19) | collective-permute-done | bytes 655392 | tf_op jit(solution)/shard_map/ppermute | solution.py:29
  199.2 6.0 %slice_add_fusion.14 = (f32[38,38,256]{2,1,0:T(8,128)S(1)}, f32[38,38,256]{2,1,0:T(8,128)S(1)}) fusion(f32[40,40,256]{2,1,0:T(8,128)S(1)} %get-tuple-element.42, f32[38,38]{1,0:T(8,128)S(1)} %and_convert_fusion.2, f32[38,38,256]{2,1,0:T(8,128)S(1)} %slice.916, f32[38,38,256]{2,1,0:T(8,128)S(1)} %slice.922, f32[40,40,256]{2,1,0:T(8,128)S(1)} %get-tuple-element.40, ...), kind=kLoop, calls=%fused_computation.495 | loop fusion | flops 23658496 | bytes 23664272 | tf_op jit(solution)/shard_map/add | solution.py:162
  205.3 5.6 %slice_add_fusion.12 = (f32[36,36,256]{2,1,0:T(8,128)S(1)}, f32[36,36,256]{2,1,0:T(8,128)S(1)}) fusion(f32[38,38,256]{2,1,0:T(8,128)S(1)} %get-tuple-element.27, f32[36,36]{1,0:T(8,128)S(1)} %and_convert_fusion.1, f32[36,36,256]{2,1,0:T(8,128)S(1)} %slice.931, f32[36,36,256]{2,1,0:T(8,128)S(1)} %slice.935, f32[40,40,256]{2,1,0:T(8,128)S(1)} %get-tuple-element.40, ...), kind=kLoop, calls=%fused_computation.493 | loop fusion | flops 21897216 | bytes 22565952 | tf_op jit(solution)/shard_map/add | solution.py:162
  211.0 5.5 %slice_add_fusion.10 = (f32[34,34,256]{2,1,0:T(8,128)S(1)}, f32[34,34,256]{2,1,0:T(8,128)S(1)}) fusion(f32[36,36,256]{2,1,0:T(8,128)S(1)} %get-tuple-element.25, f32[34,34]{1,0:T(8,128)S(1)} %and_convert_fusion, f32[34,34,256]{2,1,0:T(8,128)S(1)} %slice.944, f32[34,34,256]{2,1,0:T(8,128)S(1)} %slice.948, f32[40,40,256]{2,1,0:T(8,128)S(1)} %get-tuple-element.40, ...), kind=kLoop, calls=%fused_computation.491 | loop fusion | flops 19531776 | bytes 20128272 | tf_op jit(solution)/shard_map/add | solution.py:162
  222.9 8.1 %collective-permute-start.20 = (f32[2,4,32,256]{3,2,1,0:T(8,128)S(1)}, f32[2,4,32,256]{3,2,1,0:T(8,128)S(1)}, u32[]{:S(2)}, u32[]{:S(2)}) collective-permute-start(f32[2,4,32,256]{3,2,1,0:T(8,128)S(1)} %get-tuple-element.63), channel_id=1, source_target_pairs={{0,4},{4,8},{8,12},{12,16},{16,20},{20,24},{24,28},{1,5},{5,9},{9,... | collective-permute-start | bytes 786440 | tf_op jit(solution)/shard_map/ppermute | solution.py:26
  246.6 6.2 %slice_add_fusion.13 = (f32[38,38,256]{2,1,0:T(8,128)S(1)}, f32[38,38,256]{2,1,0:T(8,128)S(1)}) fusion(f32[40,40,256]{2,1,0:T(8,128)S(1)} %get-tuple-element.52, f32[38,38]{1,0:T(8,128)S(1)} %and_convert_fusion.2, f32[38,38,256]{2,1,0:T(8,128)S(1)} %slice.971, f32[38,38,256]{2,1,0:T(8,128)S(1)} %slice.922, f32[40,40,256]{2,1,0:T(8,128)S(1)} %get-tuple-element.40, ...), kind=kLoop, calls=%fused_computation.494 | loop fusion | flops 24397824 | bytes 25142928 | tf_op jit(solution)/shard_map/add | solution.py:162
  252.9 5.6 %slice_add_fusion.11 = (f32[36,36,256]{2,1,0:T(8,128)S(1)}, f32[36,36,256]{2,1,0:T(8,128)S(1)}) fusion(f32[38,38,256]{2,1,0:T(8,128)S(1)} %get-tuple-element.19, f32[36,36]{1,0:T(8,128)S(1)} %and_convert_fusion.1, f32[36,36,256]{2,1,0:T(8,128)S(1)} %slice.978, f32[36,36,256]{2,1,0:T(8,128)S(1)} %slice.935, f32[40,40,256]{2,1,0:T(8,128)S(1)} %get-tuple-element.40, ...), kind=kLoop, calls=%fused_computation.492 | loop fusion | flops 21897216 | bytes 22565952 | tf_op jit(solution)/shard_map/add | solution.py:162
  258.6 5.6 %slice_add_fusion.9 = (f32[34,34,256]{2,1,0:T(8,128)S(1)}, f32[34,34,256]{2,1,0:T(8,128)S(1)}) fusion(f32[36,36,256]{2,1,0:T(8,128)S(1)} %get-tuple-element.17, f32[34,34]{1,0:T(8,128)S(1)} %and_convert_fusion, f32[34,34,256]{2,1,0:T(8,128)S(1)} %slice.984, f32[34,34,256]{2,1,0:T(8,128)S(1)} %slice.948, f32[40,40,256]{2,1,0:T(8,128)S(1)} %get-tuple-element.40, ...), kind=kLoop, calls=%fused_computation.490 | loop fusion | flops 19531776 | bytes 20128272 | tf_op jit(solution)/shard_map/add | solution.py:162
  268.7 5.8 %gather_fusion = f32[1536]{0:T(1024)S(1)} fusion(f32[1024]{0:T(1024)S(1)} %reshape_squeeze.8, s32[2048]{0:T(1024)S(1)} %pad_clamp_fusion), kind=kCustom, calls=%fused_computation | custom fusion | bytes 18432 | tf_op jit(solution)/shard_map/gather | solution.py:280
  279.9 7.8 %collective-permute-start.25 = (f32[128]{0:T(128)S(1)}, f32[128]{0:T(128)S(1)}, u32[]{:S(2)}, u32[]{:S(2)}) collective-permute-start(f32[128]{0:T(128)S(1)} %get-tuple-element.78), channel_id=1, source_target_pairs={{0,4},{4,8},{8,12},{12,16},{16,20},{20,24},{24,28},{1,5},{5,9},{9,... | collective-permute-start | bytes 1544 | tf_op jit(solution)/shard_map/ppermute | solution.py:18
  (264 shorter events, 133.8 us)
Async XLA Ops:
  2.1 25.7 %collective-permute-start.4 = (f32[1,32,512]{2,1,0:T(8,128)}, f32[1,32,512]{2,1,0:T(8,128)S(1)}, u32[]{:S(2)}, u32[]{:S(2)}) collective-permute-start(f32[1,32,512]{2,1,0:T(8,128)} %get-tuple-element.71), channel_id=1, source_target_pairs={{0,4},{4,8},{8,12},{12,16},{16,20},{20,24},{24,28},{1,5},{5,9},{9,... | collective-permute-start | bytes 196616 | tf_op jit(solution)/shard_map/ppermute | solution.py:26
  5.8 29.6 %collective-permute-start.5 = (f32[1,32,512]{2,1,0:T(8,128)S(1)}, f32[1,32,512]{2,1,0:T(8,128)S(1)}, u32[]{:S(2)}, u32[]{:S(2)}) collective-permute-start(f32[1,32,512]{2,1,0:T(8,128)S(1)} %get-tuple-element.70), channel_id=1, source_target_pairs={{4,0},{8,4},{12,8},{16,12},{20,16},{24,20},{28,24},{5,1},{9,5},{13... | collective-permute-start | bytes 196616 | tf_op jit(solution)/shard_map/ppermute | solution.py:29
  9.7 20.8 %collective-permute-start.1 = (f32[4,1,32,512]{3,2,1,0:T(8,128)}, f32[4,1,32,512]{3,2,1,0:T(8,128)S(1)}, u32[]{:S(2)}, u32[]{:S(2)}) collective-permute-start(f32[4,1,32,512]{3,2,1,0:T(8,128)} %get-tuple-element.38), channel_id=1, source_target_pairs={{4,0},{8,4},{12,8},{16,12},{20,16},{24,20},{28,24},{5,1},{9,5},{13... | collective-permute-start | bytes 786440 | tf_op jit(solution)/shard_map/ppermute | solution.py:29
  12.3 18.1 %collective-permute-start = (f32[4,1,32,512]{3,2,1,0:T(8,128)}, f32[4,1,32,512]{3,2,1,0:T(8,128)S(1)}, u32[]{:S(2)}, u32[]{:S(2)}) collective-permute-start(f32[4,1,32,512]{3,2,1,0:T(8,128)} %get-tuple-element.37), channel_id=1, source_target_pairs={{0,4},{4,8},{8,12},{12,16},{16,20},{20,24},{24,28},{1,5},{5,9},{9,... | collective-permute-start | bytes 786440 | tf_op jit(solution)/shard_map/ppermute | solution.py:26
  31.9 10.3 %collective-permute-start.3 = (f32[4,34,1,512]{3,0,2,1:T(4,128)S(1)}, f32[4,34,1,512]{3,0,2,1:T(4,128)S(1)}, u32[]{:S(2)}, u32[]{:S(2)}) collective-permute-start(f32[4,34,1,512]{3,0,2,1:T(4,128)S(1)} %copy.258), channel_id=1, source_target_pairs={{1,0},{2,1},{3,2},{5,4},{6,5},{7,6},{9,8},{10,9},{11,10},{13,12},{... | collective-permute-start | bytes 835592 | tf_op jit(solution)/shard_map/ppermute | solution.py:29
  34.1 9.5 %collective-permute-start.2 = (f32[4,34,1,512]{3,0,2,1:T(4,128)S(1)}, f32[4,34,1,512]{3,0,2,1:T(4,128)S(1)}, u32[]{:S(2)}, u32[]{:S(2)}) collective-permute-start(f32[4,34,1,512]{3,0,2,1:T(4,128)S(1)} %copy.257), channel_id=1, source_target_pairs={{0,1},{1,2},{2,3},{4,5},{5,6},{6,7},{8,9},{9,10},{10,11},{12,13},{... | collective-permute-start | bytes 835592 | tf_op jit(solution)/shard_map/ppermute | solution.py:26
  36.4 35.7 %collective-permute-start.7 = (f32[34,1,512]{2,1,0:T(1,128)}, f32[34,1,512]{2,1,0:T(1,128)S(1)}, u32[]{:S(2)}, u32[]{:S(2)}) collective-permute-start(f32[34,1,512]{2,1,0:T(1,128)} %get-tuple-element.62), channel_id=1, source_target_pairs={{1,0},{2,1},{3,2},{5,4},{6,5},{7,6},{9,8},{10,9},{11,10},{13,12},{... | collective-permute-start | bytes 208904 | tf_op jit(solution)/shard_map/ppermute | solution.py:29
  40.4 31.8 %collective-permute-start.6 = (f32[34,1,512]{2,1,0:T(1,128)}, f32[34,1,512]{2,1,0:T(1,128)}, u32[]{:S(2)}, u32[]{:S(2)}) collective-permute-start(f32[34,1,512]{2,1,0:T(1,128)} %get-tuple-element.61), channel_id=1, source_target_pairs={{0,1},{1,2},{2,3},{4,5},{5,6},{6,7},{8,9},{9,10},{10,11},{12,13},{... | collective-permute-start | bytes 208904 | tf_op jit(solution)/shard_map/ppermute | solution.py:26
  89.8 9.1 %collective-permute-start.9 = (f32[1,32,512]{2,1,0:T(8,128)}, f32[1,32,512]{2,1,0:T(8,128)S(1)}, u32[]{:S(2)}, u32[]{:S(2)}) collective-permute-start(f32[1,32,512]{2,1,0:T(8,128)} %get-tuple-element.66), channel_id=1, source_target_pairs={{4,0},{8,4},{12,8},{16,12},{20,16},{24,20},{28,24},{5,1},{9,5},{13... | collective-permute-start | bytes 196616 | tf_op jit(solution)/shard_map/ppermute | solution.py:29
  91.7 7.2 %collective-permute-start.8 = (f32[1,32,512]{2,1,0:T(8,128)}, f32[1,32,512]{2,1,0:T(8,128)}, u32[]{:S(2)}, u32[]{:S(2)}) collective-permute-start(f32[1,32,512]{2,1,0:T(8,128)} %get-tuple-element.65), channel_id=1, source_target_pairs={{0,4},{4,8},{8,12},{12,16},{16,20},{20,24},{24,28},{1,5},{5,9},{9,... | collective-permute-start | bytes 196616 | tf_op jit(solution)/shard_map/ppermute | solution.py:26
  100.4 8.5 %collective-permute-start.11 = (f32[34,1,512]{2,1,0:T(1,128)S(1)}, f32[34,1,512]{2,1,0:T(1,128)S(1)}, u32[]{:S(2)}, u32[]{:S(2)}) collective-permute-start(f32[34,1,512]{2,1,0:T(1,128)S(1)} %get-tuple-element.60), channel_id=1, source_target_pairs={{1,0},{2,1},{3,2},{5,4},{6,5},{7,6},{9,8},{10,9},{11,10},{13,12},{... | collective-permute-start | bytes 208904 | tf_op jit(solution)/shard_map/ppermute | solution.py:29
  122.7 13.4 %collective-permute-start.12 = (f32[2,128]{1,0:T(2,128)S(1)}, f32[2,128]{1,0:T(2,128)S(1)}, u32[]{:S(2)}, u32[]{:S(2)}) collective-permute-start(f32[2,128]{1,0:T(2,128)S(1)} %reshape.465), channel_id=1, source_target_pairs={{0,4},{4,8},{8,12},{12,16},{16,20},{20,24},{24,28},{1,5},{5,9},{9,... | collective-permute-start | bytes 3080 | tf_op jit(solution)/shard_map/ppermute | solution.py:18
  127.8 8.3 %collective-permute-start.13 = (f32[2,128]{1,0:T(2,128)S(1)}, f32[2,128]{1,0:T(2,128)S(1)}, u32[]{:S(2)}, u32[]{:S(2)}) collective-permute-start(f32[2,128]{1,0:T(2,128)S(1)} %reshape.466), channel_id=1, source_target_pairs={{4,0},{8,4},{12,8},{16,12},{20,16},{24,20},{28,24},{5,1},{9,5},{13... | collective-permute-start | bytes 3080 | tf_op jit(solution)/shard_map/ppermute | solution.py:18
  162.0 16.1 %collective-permute-start.17 = (f32[4,4,32,256]{3,2,1,0:T(8,128)S(1)}, f32[4,4,32,256]{3,2,1,0:T(8,128)S(1)}, u32[]{:S(2)}, u32[]{:S(2)}) collective-permute-start(f32[4,4,32,256]{3,2,1,0:T(8,128)S(1)} %get-tuple-element.50), channel_id=1, source_target_pairs={{4,0},{8,4},{12,8},{16,12},{20,16},{24,20},{28,24},{5,1},{9,5},{13... | collective-permute-start | bytes 1572872 | tf_op jit(solution)/shard_map/ppermute | solution.py:29
  163.9 14.1 %collective-permute-start.16 = (f32[4,4,32,256]{3,2,1,0:T(8,128)S(1)}, f32[4,4,32,256]{3,2,1,0:T(8,128)S(1)}, u32[]{:S(2)}, u32[]{:S(2)}) collective-permute-start(f32[4,4,32,256]{3,2,1,0:T(8,128)S(1)} %get-tuple-element.49), channel_id=1, source_target_pairs={{0,4},{4,8},{8,12},{12,16},{16,20},{20,24},{24,28},{1,5},{5,9},{9,... | collective-permute-start | bytes 1572872 | tf_op jit(solution)/shard_map/ppermute | solution.py:26
  178.3 14.1 %collective-permute-start.19 = (f32[4,40,4,256]{3,2,1,0:T(4,128)S(1)}, f32[4,40,4,256]{3,2,1,0:T(4,128)S(1)}, u32[]{:S(2)}, u32[]{:S(2)}) collective-permute-start(f32[4,40,4,256]{3,2,1,0:T(4,128)S(1)} %get-tuple-element.48), channel_id=1, source_target_pairs={{1,0},{2,1},{3,2},{5,4},{6,5},{7,6},{9,8},{10,9},{11,10},{13,12},{... | collective-permute-start | bytes 1966088 | tf_op jit(solution)/shard_map/ppermute | solution.py:29
  182.3 14.3 %collective-permute-start.18 = (f32[4,40,4,256]{3,2,1,0:T(4,128)S(1)}, f32[4,40,4,256]{3,2,1,0:T(4,128)S(1)}, u32[]{:S(2)}, u32[]{:S(2)}) collective-permute-start(f32[4,40,4,256]{3,2,1,0:T(4,128)S(1)} %get-tuple-element.47), channel_id=1, source_target_pairs={{0,1},{1,2},{2,3},{4,5},{5,6},{6,7},{8,9},{9,10},{10,11},{12,13},{... | collective-permute-start | bytes 1966088 | tf_op jit(solution)/shard_map/ppermute | solution.py:26
  220.9 12.2 %collective-permute-start.21 = (f32[2,4,32,256]{3,2,1,0:T(8,128)S(1)}, f32[2,4,32,256]{3,2,1,0:T(8,128)S(1)}, u32[]{:S(2)}, u32[]{:S(2)}) collective-permute-start(f32[2,4,32,256]{3,2,1,0:T(8,128)S(1)} %get-tuple-element.64), channel_id=1, source_target_pairs={{4,0},{8,4},{12,8},{16,12},{20,16},{24,20},{28,24},{5,1},{9,5},{13... | collective-permute-start | bytes 786440 | tf_op jit(solution)/shard_map/ppermute | solution.py:29
  222.9 11.4 %collective-permute-start.20 = (f32[2,4,32,256]{3,2,1,0:T(8,128)S(1)}, f32[2,4,32,256]{3,2,1,0:T(8,128)S(1)}, u32[]{:S(2)}, u32[]{:S(2)}) collective-permute-start(f32[2,4,32,256]{3,2,1,0:T(8,128)S(1)} %get-tuple-element.63), channel_id=1, source_target_pairs={{0,4},{4,8},{8,12},{12,16},{16,20},{20,24},{24,28},{1,5},{5,9},{9,... | collective-permute-start | bytes 786440 | tf_op jit(solution)/shard_map/ppermute | solution.py:26
  234.4 7.4 %collective-permute-start.23 = (f32[2,40,4,256]{3,2,1,0:T(4,128)S(1)}, f32[2,40,4,256]{3,2,1,0:T(4,128)S(1)}, u32[]{:S(2)}, u32[]{:S(2)}) collective-permute-start(f32[2,40,4,256]{3,2,1,0:T(4,128)S(1)} %get-tuple-element.58), channel_id=1, source_target_pairs={{1,0},{2,1},{3,2},{5,4},{6,5},{7,6},{9,8},{10,9},{11,10},{13,12},{... | collective-permute-start | bytes 983048 | tf_op jit(solution)/shard_map/ppermute | solution.py:29
  237.8 7.8 %collective-permute-start.22 = (f32[2,40,4,256]{3,2,1,0:T(4,128)S(1)}, f32[2,40,4,256]{3,2,1,0:T(4,128)S(1)}, u32[]{:S(2)}, u32[]{:S(2)}) collective-permute-start(f32[2,40,4,256]{3,2,1,0:T(4,128)S(1)} %get-tuple-element.57), channel_id=1, source_target_pairs={{0,1},{1,2},{2,3},{4,5},{5,6},{6,7},{8,9},{9,10},{10,11},{12,13},{... | collective-permute-start | bytes 983048 | tf_op jit(solution)/shard_map/ppermute | solution.py:26
  274.6 15.0 %collective-permute-start.27 = (f32[128]{0:T(128)S(1)}, f32[128]{0:T(128)S(1)}, u32[]{:S(2)}, u32[]{:S(2)}) collective-permute-start(f32[128]{0:T(128)S(1)} %get-tuple-element.79), channel_id=1, source_target_pairs={{0,1},{1,2},{2,3},{4,5},{5,6},{6,7},{8,9},{9,10},{10,11},{12,13},{... | collective-permute-start | bytes 1544 | tf_op jit(solution)/shard_map/ppermute | solution.py:18
  275.9 14.1 %collective-permute-start.26 = (f32[128]{0:T(128)S(1)}, f32[128]{0:T(128)S(1)}, u32[]{:S(2)}, u32[]{:S(2)}) collective-permute-start(f32[128]{0:T(128)S(1)} %get-tuple-element.77), channel_id=1, source_target_pairs={{1,0},{2,1},{3,2},{5,4},{6,5},{7,6},{9,8},{10,9},{11,10},{13,12},{... | collective-permute-start | bytes 1544 | tf_op jit(solution)/shard_map/ppermute | solution.py:18
  279.9 10.4 %collective-permute-start.25 = (f32[128]{0:T(128)S(1)}, f32[128]{0:T(128)S(1)}, u32[]{:S(2)}, u32[]{:S(2)}) collective-permute-start(f32[128]{0:T(128)S(1)} %get-tuple-element.78), channel_id=1, source_target_pairs={{0,4},{4,8},{8,12},{12,16},{16,20},{20,24},{24,28},{1,5},{5,9},{9,... | collective-permute-start | bytes 1544 | tf_op jit(solution)/shard_map/ppermute | solution.py:18
  (50 other events, 456.7 us)
where the time goes:
time: 299 us; the launch traced here: 295 us
  other arithmetic  132 us (44%)
  starting transfers between devices  86.9 us (29%)
  local copies, waits for them, and re-layouts  36.3 us (12%)
  waiting for transfers between devices  35.1 us (12%)
    add x7, other arithmetic, run_block(): solid_now = trim_rim(solid_now, 1) + update  38.6 us
    ppermute x10, starting transfers between devices, extended(): lax.ppermute(lax.slice_in_dim(block, block.shape[dim] - width, None, axis...  32.9 us
    ppermute x8, starting transfers between devices, from_behind(): lax.ppermute(value, axis, [(source, source + steps) for source in range(i...  27.3 us
    ppermute x10, starting transfers between devices, extended(): lax.ppermute(lax.slice_in_dim(block, 0, width, axis=dim), axis, backward)  26.6 us
    ppermute x10, waiting for transfers between devices, extended(): lax.ppermute(lax.slice_in_dim(block, 0, width, axis=dim), axis, backward)  21.7 us
    sub x4, other arithmetic, fluid_update(): jnp.maximum(face_speed, 0.0) * lower_val  18.4 us
    add x3, other arithmetic, fluid_update(): face_weight = face_diff + 0.5 * jnp.abs(face_speed)  14.2 us
    scatter-add x1, other arithmetic, on_device(): jax.ops.segment_sum(film_in * gas_in, landing, num_segments=solid_x * sol...  11.5 us
  transfers between devices with their start and end apart: 28, of which 10 were waited for; matrix products, arithmetic and copies ran while one was open for 18% of the time, Pallas kernels for 0%

commit v1 on v0

v1 whole, which is shorter than its diff:
```python
import functools

import jax
import jax.numpy as jnp
from jax import lax
from jax.experimental import pallas as pl
from jax.experimental.pallas import tpu as pltpu
from jax.sharding import PartitionSpec as P

FLUID_SWEEPS = 2
SWEEPS = 8
RELAX_FACTOR = 0.8
EIG_LOW = 0.02
EIG_HIGH = 2.0
TILE = 8
LANES = 128
HIGHEST = lax.Precision.HIGHEST
VMEM = pl.BlockSpec(memory_space=pltpu.VMEM)
SMEM = pl.BlockSpec(memory_space=pltpu.SMEM)
ANY = pl.BlockSpec(memory_space=pl.ANY)


def cheby_coefficients(count_sweeps):
    center_eig = 0.5 * (EIG_HIGH + EIG_LOW)
    half_width = 0.5 * (EIG_HIGH - EIG_LOW)
    ratio_eig = center_eig / half_width
    damping = 1.0 / ratio_eig
    coefficients = [(0.0, 1.0 / center_eig)]
    for sweep_no in range(1, count_sweeps):
        damping_new = 1.0 / (2.0 * ratio_eig - damping)
        coefficients.append((damping_new * damping, 2.0 * damping_new / half_width))
        damping = damping_new
    return coefficients


def ring(value, axis, step):
    count = lax.axis_size(axis)
    return lax.ppermute(value, axis, [(i, (i + step) % count) for i in range(count)])


def chain(value, axis, step):
    count = lax.axis_size(axis)
    pairs = [(i, i + step) for i in range(count) if 0 <= i + step < count]
    return lax.ppermute(value, axis, pairs)


def sides(axis):
    place = lax.axis_index(axis)
    return place > 0, place < lax.axis_size(axis) - 1


def lasts(micros):
    return pl.CostEstimate(flops=0, bytes_accessed=int(micros * 3.69e6), transcendentals=0)


def quick_reciprocal(value):
    guess = pl.reciprocal(value, approx=True)
    return guess * (2.0 - value * guess)


def lane_index(shape):
    return lax.broadcasted_iota(jnp.int32, shape, 1)


def row_index(shape):
    return lax.broadcasted_iota(jnp.int32, shape, 0)


def first_lane(value, at_first):
    head = value[:, :LANES]
    head = jnp.where(lane_index(head.shape) == 0, at_first, head)
    if value.shape[1] == LANES:
        return head
    return jnp.concatenate([head, value[:, LANES:]], axis=1)


def last_lane(value, at_last):
    tail = value[:, -LANES:]
    tail = jnp.where(lane_index(tail.shape) == LANES - 1, at_last, tail)
    if value.shape[1] == LANES:
        return tail
    return jnp.concatenate([value[:, :-LANES], tail], axis=1)


def from_above(value, row):
    return jnp.where(row_index(value.shape) == 0, row, pltpu.roll(value, 1, 0))


def from_below(value, row):
    count = value.shape[0]
    return jnp.where(row_index(value.shape) == count - 1, row, pltpu.roll(value, count - 1, 0))


def part_depths(depth):
    return [(0, LANES), (LANES, depth - LANES)] if depth > LANES else [(0, depth)]


class Copies:
    def __init__(self, sems):
        self.sems, self.count, self.waits = sems, 0, {}

    def start(self, key, src, dst):
        made = pltpu.make_async_copy(src, dst, self.sems.at[self.count])
        self.count += 1
        made.start()
        self.waits.setdefault(key, []).append(made)

    def wait(self, key):
        for made in self.waits.pop(key, []):
            made.wait()

    def wait_all(self):
        for key in list(self.waits):
            self.wait(key)


def x_fields(temp, velo, diff, side, cells_x, zs):
    two, one = (pl.ds(0, 2), pl.ds(0, 1)) if side == 0 else (pl.ds(cells_x - 2, 2), pl.ds(cells_x - 1, 1))
    return (
        (temp.at[two, :, zs], 0, 2),
        (diff.at[two, :, zs], 2, 2),
        (velo.at[0, two, :, zs], 4, 2),
        (velo.at[1, one, :, zs], 6, 1),
        (velo.at[2, one, :, zs], 7, 1),
    )


def x_pack_kernel(cells_x, start, depth, noted, *refs):
    temp, velo, diff = refs[:3]
    notes = refs[3] if noted else None
    outs, sems = refs[-3:-1], refs[-1]
    copies = Copies(sems)
    zs = pl.ds(start, depth)
    for side in range(2):
        for src, at, count in x_fields(temp, velo, diff, side, cells_x, zs):
            copies.start(0, src, outs[side].at[pl.ds(at, count)])
        if noted:
            copies.start(0, notes.at[side], outs[side].at[8])
    copies.wait_all()


def x_pack(temp, velo, diff, notes, start, depth):
    cells_x, cells_y, _ = temp.shape
    noted = notes is not None
    shape = jax.ShapeDtypeStruct((9 if noted else 8, cells_y, depth), temp.dtype)
    return pl.pallas_call(
        functools.partial(x_pack_kernel, cells_x, start, depth, noted),
        out_shape=(shape, shape),
        in_specs=[ANY] * (4 if noted else 3),
        out_specs=(VMEM, VMEM),
        scratch_shapes=[pltpu.SemaphoreType.DMA((12,))],
        compiler_params=pltpu.CompilerParams(vmem_limit_bytes=32 * 1024 * 1024),
        cost_estimate=lasts(2),
    )(*((temp, velo, diff, notes) if noted else (temp, velo, diff)))


def y_pack_kernel(cells_x, cells_y, start, depth, noted, *refs):
    temp, velo, diff, xlo, xhi = refs[:5]
    notes = refs[5] if noted else None
    outs, (tiles, sems) = refs[-4:-2], refs[-2:]
    copies = Copies(sems)
    zs = pl.ds(start, depth)
    sources = (temp.at[:], diff.at[:], velo.at[1], velo.at[0], velo.at[2])
    for side in range(2):
        rows = pl.ds(0 if side == 0 else cells_y - TILE, TILE)
        for number, src in enumerate(sources):
            copies.start((side, number), src.at[:, rows, zs], tiles.at[side, number])
    base = 9 * cells_x if noted else 8 * cells_x
    for side in range(2):
        out = outs[side]
        first, near = (0, 0) if side == 0 else (TILE - 2, TILE - 1)
        edge = 0 if side == 0 else cells_y - 1
        for at, halo, inner in ((base, xlo, 1), (base + 4, xhi, 0)):
            for j, plane in enumerate((inner, 2 + inner, 4 + inner, 6)):
                out[pl.ds(at + j, 1), :] = halo[plane, pl.ds(edge, 1), :]
        if noted:
            out[pl.ds(8 * cells_x, cells_x), :] = notes[2 + side]
        for number in range(5):
            copies.wait((side, number))
            if number < 3:
                picks = [(2 * number, first), (2 * number + 1, first + 1)]
            else:
                picks = [(3 + number, near)]
            for plane, row in picks:
                for x in range(cells_x):
                    out[pl.ds(plane * cells_x + x, 1), :] = tiles[side, number, x, pl.ds(row, 1), :]


def y_pack(temp, velo, diff, xlo, xhi, notes, start, depth):
    cells_x, cells_y, _ = temp.shape
    noted = notes is not None
    shape = jax.ShapeDtypeStruct(((9 if noted else 8) * cells_x + TILE, depth), temp.dtype)
    return pl.pallas_call(
        functools.partial(y_pack_kernel, cells_x, cells_y, start, depth, noted),
        out_shape=(shape, shape),
        in_specs=[ANY] * 3 + [VMEM] * (3 if noted else 2),
        out_specs=(VMEM, VMEM),
        scratch_shapes=[
            pltpu.VMEM((2, 5, cells_x, TILE, depth), jnp.float32),
            pltpu.SemaphoreType.DMA((10,)),
        ],
        compiler_params=pltpu.CompilerParams(vmem_limit_bytes=32 * 1024 * 1024),
        cost_estimate=lasts(2),
    )(temp, velo, diff, xlo, xhi, *((notes,) if noted else ()))


def face(a_low, a_high, u_low, u_high):
    a_two = a_low + a_high
    u_two = u_low + u_high
    plus = a_two + jnp.maximum(u_two, 0.0)
    return plus, plus - u_two


def relaxation(a, ut, uz, low, high, above, below, live_two, wall):
    depth = a.shape[1]
    p_above, q_above = face(from_above(a, above[0]), a, from_above(ut, above[1]), ut)
    p_below, q_below = face(a, from_below(a, below[0]), ut, from_below(ut, below[1]))
    p_down, q_down = face(pltpu.roll(a, 1, 1), a, pltpu.roll(uz, 1, 1), uz)
    p_up, q_up = pltpu.roll(p_down, depth - 1, 1), pltpu.roll(q_down, depth - 1, 1)
    a_first = 2.0 * a[:, :LANES]
    u_last = 2.0 * uz[:, -LANES:]
    plus_last = 2.0 * a[:, -LANES:] + jnp.maximum(u_last, 0.0)
    weight = (low[0] + low[1]) + (high[0] + high[1]) + (p_above + q_above) + (p_below + q_below)
    weight = weight + first_lane(p_down + q_down, 2.0 * a_first) + last_lane(p_up + q_up, 2.0 * plus_last - u_last)
    factor = (2.0 * RELAX_FACTOR) * quick_reciprocal(weight)
    gain = a_first * live_two
    p_down, q_down = first_lane(p_down, 0.0), first_lane(q_down, gain)
    p_up, q_up = last_lane(p_up, plus_last), last_lane(q_up, 0.0)
    leaving = (low[1] + high[0]) + (q_above + p_below) + (q_down + p_up)
    ghost = jnp.where(lane_index(gain.shape) == 0, gain * wall * factor[:, :LANES], 0.0)
    return (low[0] * factor, high[1] * factor, p_above * factor, q_below * factor, p_down * factor, q_up * factor,
            1.0 - leaving * factor, ghost)


def apply(factors, t, t_low, t_high, t_above, t_below):
    depth = t.shape[1]
    new = factors[6] * t + (factors[0] * t_low + factors[1] * t_high)
    new = new + (factors[2] * from_above(t, t_above) + factors[3] * from_below(t, t_below))
    new = new + (factors[4] * pltpu.roll(t, 1, 1) + factors[5] * pltpu.roll(t, depth - 1, 1))
    head = new[:, :LANES] + factors[7]
    return head if depth == LANES else jnp.concatenate([head, new[:, LANES:]], axis=1)


def fluid_kernel(cells_x, cells_y, depth, parts, at_wall, flags, temp, velo, diff, wall_t, *refs):
    halos, refs = refs[:4 * len(parts)], refs[4 * len(parts):]
    out, (ts, us, as_, vs, ws, t1, yl, yc, xn, yn, cs, ks, sems) = refs[:-13], refs[-13:]
    rows_total = flags[4]
    xlo, xhi, ylo, yhi = (halos[i::4] for i in range(4))
    mid = pl.ds(TILE, cells_y)
    copies = Copies(sems)
    for (start, size), *strips in zip(parts, xlo, xhi, ylo, yhi):
        zs = pl.ds(start, size)
        for side in range(2):
            halo, key = strips[2 + side], "y"
            noted = start == 0
            for plane in range(8):
                copies.start(key, halo.at[pl.ds(plane * cells_x, cells_x)],
                             yl.at[side, plane, pl.ds(TILE, cells_x), zs])
            copies.start(key, halo.at[pl.ds((9 if noted else 8) * cells_x, TILE)], yc.at[side, :, zs])
            if noted:
                copies.start(key, halo.at[pl.ds(8 * cells_x, cells_x), pl.ds(0, LANES)], yn.at[side])
        for side in range(2):
            halo, at = strips[side], 0 if side == 0 else cells_x + 2
            near = 0 if side == 0 else cells_x + 1
            key = "x"
            copies.start(key, halo.at[pl.ds(0, 2)], ts.at[pl.ds(at, 2), mid, zs])
            copies.start(key, halo.at[pl.ds(2, 2)], as_.at[pl.ds(at, 2), mid, zs])
            copies.start(key, halo.at[pl.ds(4, 2)], us.at[pl.ds(at, 2), :, zs])
            copies.start(key, halo.at[pl.ds(6, 1)], vs.at[pl.ds(near, 1), mid, zs])
            copies.start(key, halo.at[pl.ds(7, 1)], ws.at[pl.ds(near, 1), :, zs])
            if start == 0:
                copies.start(key, halo.at[8, :, pl.ds(0, LANES)], xn.at[side])
    zs = pl.ds(0, depth)
    step = TILE
    starts = list(range(0, cells_x, step))
    for start in starts:
        here = pl.ds(start, step)
        copies.start(start, temp.at[here, :, zs], ts.at[pl.ds(start + 2, step), mid])
        copies.start(start, diff.at[here, :, zs], as_.at[pl.ds(start + 2, step), mid])
        copies.start(start, velo.at[0, here, :, zs], us.at[pl.ds(start + 2, step)])
        copies.start(start, velo.at[1, here, :, zs], vs.at[pl.ds(start + 1, step), mid])
        copies.start(start, velo.at[2, here, :, zs], ws.at[pl.ds(start + 1, step)])

    copies.wait("y")
    copies.wait("x")
    for side, row in ((0, TILE - 1), (1, TILE + cells_y)):
        inner = 1 - side
        for corner, at in ((0, TILE - 1), (4, TILE + cells_x)):
            for j, plane in enumerate((inner, 2 + inner, 6, 4 + inner)):
                yl[side, plane, pl.ds(at, 1), :] = yc[side, pl.ds(corner + j, 1), :]
        for j in range(cells_x + 2):
            at = pl.ds(TILE - 1 + j, 1)
            ts[j + 1, pl.ds(row, 1), :] = yl[side, inner, at, :]
            as_[j + 1, pl.ds(row, 1), :] = yl[side, 2 + inner, at, :]
            vs[j, pl.ds(row, 1), :] = yl[side, 4 + inner, at, :]

    def plane_factors(i, live_two, wall):
        a, un = as_[i + 1, mid, :], us[i + 1]
        low = face(as_[i, mid, :], a, us[i], un)
        high = face(a, as_[i + 2, mid, :], un, us[i + 2])
        up, down = pl.ds(TILE - 1, 1), pl.ds(TILE + cells_y, 1)
        return relaxation(a, vs[i, mid, :], ws[i], low, high, (as_[i + 1, up, :], vs[i, up, :]),
                          (as_[i + 1, down, :], vs[i, down, :]), live_two, wall)

    def plane_apply(factors, ref, i):
        up, down = pl.ds(TILE - 1, 1), pl.ds(TILE + cells_y, 1)
        return apply(factors, ref[i, mid, :], ref[i - 1, mid, :], ref[i + 1, mid, :], ref[i, up, :], ref[i, down, :])

    def note_of(note):
        return note, pltpu.roll(note, LANES - 1, 1)

    def first_sweep(i, carry):
        place = (i - 1) * cells_y + row_index((cells_y, LANES))
        live_two = jnp.where(place < rows_total, 2.0, 0.0)
        factors = plane_factors(i, live_two, pltpu.roll(wall_t[...], LANES + 1 - i, 1))
        for j in range(7):
            cs[j, i - 1] = factors[j]
        ks[i - 1] = factors[7]
        t1[i, mid, :] = plane_apply(factors, ts, i + 1)
        return carry

    def halo_plane(i, side):
        factors = plane_factors(i, *note_of(xn[side]))
        t1[i, mid, :] = jnp.where(flags[side] > 0, plane_apply(factors, ts, i + 1), 0.0)

    for start in starts:
        copies.wait(start)
        if start == 0:
            halo_plane(0, 0)
        last = cells_x + 1 if start == starts[-1] else start + step
        lax.fori_loop(max(start, 1), last, first_sweep, 0, unroll=4 if at_wall else 1)
    halo_plane(cells_x + 1, 1)

    for side, row in ((0, TILE - 1), (1, TILE + cells_y)):
        inner = 1 - side
        own = TILE if side == 0 else TILE + cells_y - 1
        rows, up, down = pl.ds(TILE, cells_x), pl.ds(TILE - 1, 1), pl.ds(TILE + cells_x, 1)

        def own_rows(ref, off):
            return jnp.concatenate([ref[off + x, pl.ds(own, 1), :] for x in range(cells_x)], axis=0)

        t, a, un = yl[side, inner, rows, :], yl[side, 2 + inner, rows, :], yl[side, 4 + inner, rows, :]
        t_far, a_far, un_far = (yl[side, 1 - inner, rows, :], yl[side, 3 - inner, rows, :],
                                yl[side, 5 - inner, rows, :])
        t_own, a_own, un_own = own_rows(ts, 2), own_rows(as_, 2), own_rows(vs, 1)
        if side == 0:
            low, high = face(a_far, a, un_far, un), face(a, a_own, un, un_own)
            t_low, t_high = t_far, t_own
        else:
            low, high = face(a_own, a, un_own, un), face(a, a_far, un, un_far)
            t_low, t_high = t_own, t_far
        factors = relaxation(
            a, yl[side, 6, rows, :], yl[side, 7, rows, :], low, high,
            (yl[side, 2 + inner, up, :], yl[side, 6, up, :]), (yl[side, 2 + inner, down, :], yl[side, 6, down, :]),
            *note_of(yn[side]))
        new = apply(factors, t, t_low, t_high, yl[side, inner, up, :], yl[side, inner, down, :])
        new = jnp.where(flags[2 + side] > 0, new, 0.0)
        for x in range(cells_x):
            t1[1 + x, pl.ds(row, 1), :] = new[x:x + 1, :]

    if at_wall:
        gas, film = out
        gas[...] = jnp.zeros_like(gas)
        film[...] = jnp.zeros_like(film)

        def second_wall(i, carry):
            factors = [cs[j, i - 1] for j in range(7)] + [ks[i - 1]]
            lane = lane_index((cells_y, LANES))
            shift = i - 1
            new = pltpu.roll(plane_apply(factors, t1, i)[:, :LANES], shift, 1)
            wall_diff = pltpu.roll(as_[i + 1, mid, pl.ds(0, LANES)], shift, 1)
            place = shift * cells_y + row_index((cells_y, LANES))
            wall_film = jnp.where(place < rows_total, 2.0 * wall_diff, 0.0)
            gas[...] = jnp.where(lane == shift, new, gas[...])
            film[...] = jnp.where(lane == shift, wall_film, film[...])
            return carry

        lax.fori_loop(1, cells_x + 1, second_wall, 0, unroll=4)
    else:
        def second_sweep(i, carry):
            factors = [cs[j, i - 1] for j in range(7)] + [ks[i - 1]]
            ts[i - 1, mid, :] = plane_apply(factors, t1, i)
            return carry

        for start in starts:
            lax.fori_loop(start + 1, start + step + 1, second_sweep, 0)
            copies.start("out", ts.at[pl.ds(start, step), mid], out[0].at[pl.ds(start, step)])
        copies.wait("out")


def fluid_call(temp, velo, diff, wall_t, flags, halos, depth, parts, at_wall):
    cells_x, cells_y, _ = temp.shape
    wide = cells_y + 2 * TILE
    chunks = cells_x // TILE
    plane = jax.ShapeDtypeStruct((cells_y, LANES), temp.dtype)
    copy_count = len(parts) * 28 + 4 + 6 * chunks
    return pl.pallas_call(
        functools.partial(fluid_kernel, cells_x, cells_y, depth, parts, at_wall),
        out_shape=(plane, plane) if at_wall else jax.ShapeDtypeStruct(temp.shape, temp.dtype),
        in_specs=[SMEM, ANY, ANY, ANY, VMEM] + [ANY] * len(halos),
        out_specs=(VMEM, VMEM) if at_wall else ANY,
        scratch_shapes=[
            pltpu.VMEM((cells_x + 4, wide, depth), jnp.float32),
            pltpu.VMEM((cells_x + 4, cells_y, depth), jnp.float32),
            pltpu.VMEM((cells_x + 4, wide, depth), jnp.float32),
            pltpu.VMEM((cells_x + 2, wide, depth), jnp.float32),
            pltpu.VMEM((cells_x + 2, cells_y, depth), jnp.float32),
            pltpu.VMEM((cells_x + 2, wide, depth), jnp.float32),
            pltpu.VMEM((2, 8, cells_x + 2 * TILE, depth), jnp.float32),
            pltpu.VMEM((2, TILE, depth), jnp.float32),
            pltpu.VMEM((2, cells_y, LANES), jnp.float32),
            pltpu.VMEM((2, cells_x, LANES), jnp.float32),
            pltpu.VMEM((7, cells_x, cells_y, depth), jnp.float32),
            pltpu.VMEM((cells_x, cells_y, LANES), jnp.float32),
            pltpu.SemaphoreType.DMA((copy_count,)),
        ],
        compiler_params=pltpu.CompilerParams(vmem_limit_bytes=52 * 1024 * 1024),
        cost_estimate=lasts(6 if at_wall else 18),
    )(flags, temp, velo, diff, wall_t, *halos)


def solid_kernel(
    cells_x, cells_y, depth, pad, coefficients,
    flags, cond, sink, heat, temp, xlo, xhi, ylo, yhi, film, film_lo, film_hi,
    out, surface, ks, es, bs, us, vs, gx, gy, gz, ss, ps, fs, sems,
):
    wide_x, wide_y = cells_x + 2 * pad, cells_y + 2 * TILE
    copies = Copies(sems)
    own_x, own_y = pl.ds(pad, cells_x), pl.ds(TILE, cells_y)
    for field, (src, dst) in enumerate(((cond, ks), (sink, es), (heat, bs), (temp, us))):
        for s, d in (
            (src, dst.at[own_x, own_y]),
            (xlo.at[field], dst.at[pl.ds(0, pad), own_y]),
            (xhi.at[field], dst.at[pl.ds(pad + cells_x, pad), own_y]),
            (ylo.at[field], dst.at[:, pl.ds(0, TILE)]),
            (yhi.at[field], dst.at[:, pl.ds(TILE + cells_y, TILE)]),
        ):
            copies.start(field // 2, s, d)
    fs[:, pl.ds(0, TILE), :] = jnp.where(flags[2] > 0, film_lo[...], 0.0)
    fs[:, own_y, :] = film[...]
    fs[:, pl.ds(TILE + cells_y, TILE), :] = jnp.where(flags[3] > 0, film_hi[...], 0.0)

    def harmonic(k, near):
        total = jnp.maximum(k + near, 1e-30)
        return (2.0 * k * near) * quick_reciprocal(total)

    def film_of(kind, x):
        return pltpu.roll(fs[kind], 2 * LANES + pad - x, 1)

    def add_first(value, extra):
        head = value[:, :LANES]
        head = head + jnp.where(lane_index(head.shape) == 0, extra, 0.0)
        return jnp.concatenate([head, value[:, LANES:]], axis=1) if depth > LANES else head

    gx[0, :, :] = jnp.zeros((wide_y, depth), jnp.float32)
    edge = row_index((wide_y, depth)) == wide_y - 1
    top = lane_index((wide_y, depth)) == depth - 1

    def conductances(x, carry):
        keep = jnp.where(x < wide_x - 1, 1.0, 0.0)
        follow = jnp.minimum(x + 1, wide_x - 1)
        k = ks[x]
        face_x = harmonic(k, ks[follow]) * keep
        face_y = jnp.where(edge, 0.0, harmonic(k, pltpu.roll(k, wide_y - 1, 0)))
        face_z = jnp.where(top, 0.0, harmonic(k, pltpu.roll(k, depth - 1, 1)))
        diag = add_first(es[x], film_of(0, x))
        diag = diag + (gx[x] + face_x) + (face_y + pltpu.roll(face_y, 1, 0))
        diag = diag + (face_z + pltpu.roll(face_z, 1, 1))
        gx[x + 1] = face_x
        gy[x] = face_y
        gz[x] = face_z
        es[x] = diag
        ss[x] = lax.rsqrt(jnp.maximum(diag, 1e-30))
        return carry

    copies.wait(0)
    lax.fori_loop(0, wide_x, conductances, 0, unroll=2)

    def scale(x, carry):
        follow = jnp.minimum(x + 1, wide_x - 1)
        s = ss[x]
        gx[x + 1] = gx[x + 1] * s * ss[follow]
        gy[x] = gy[x] * s * pltpu.roll(s, wide_y - 1, 0)
        gz[x] = gz[x] * s * pltpu.roll(s, depth - 1, 1)
        bs[x] = add_first(bs[x], film_of(1, x)) * s
        us[x] = us[x] * es[x] * s
        return carry

    copies.wait(1)
    lax.fori_loop(0, wide_x, scale, 0, unroll=2)

    total = len(coefficients)
    src, dst = us, vs
    for number, (decay, gain) in enumerate(coefficients):
        last = number == total - 1
        margin = total - 1 - number

        def one(x, carry, src=src, dst=dst, decay=decay, gain=gain, number=number, last=last):
            here = src[x]
            g_y, g_z = gy[x], gz[x]
            total_in = gx[x] * src[x - 1] + gx[x + 1] * src[x + 1]
            total_in += g_y * pltpu.roll(here, wide_y - 1, 0) + pltpu.roll(g_y * here, 1, 0)
            total_in += g_z * pltpu.roll(here, depth - 1, 1) + pltpu.roll(g_z * here, 1, 1)
            step = gain * ((bs[x] - here) + total_in)
            if number > 0:
                step = step + decay * ps[x]
            fresh = here + step
            if last:
                final = (fresh * ss[x])[TILE:TILE + cells_y]
                out[x - pad] = final
                shift = x - pad
                lane = lane_index((cells_y, LANES))
                surface[...] = jnp.where(lane == shift, pltpu.roll(final[:, :LANES], shift, 1), surface[...])
            else:
                ps[x] = step
                dst[x] = fresh
            return carry

        if last:
            surface[...] = jnp.zeros_like(surface)
        lax.fori_loop(pad - margin, pad + cells_x + margin, one, 0, unroll=2)
        src, dst = dst, src


def solid_x_kernel(cells_x, pad, *refs):
    outs, sems = refs[4:6], refs[6]
    copies = Copies(sems)
    for field in range(4):
        copies.start(0, refs[field].at[pl.ds(0, pad)], outs[0].at[field])
        copies.start(0, refs[field].at[pl.ds(cells_x - pad, pad)], outs[1].at[field])
    copies.wait_all()


def solid_y_kernel(cells_x, cells_y, pad, *refs):
    xlo, xhi = refs[4:6]
    outs, sems = refs[6:8], refs[8]
    copies = Copies(sems)
    for field in range(4):
        for side in range(2):
            rows = pl.ds(0 if side == 0 else cells_y - TILE, TILE)
            out = outs[side]
            copies.start(0, refs[field].at[:, rows], out.at[field, pl.ds(pad, cells_x)])
            copies.start(0, xlo.at[field, :, rows], out.at[field, pl.ds(0, pad)])
            copies.start(0, xhi.at[field, :, rows], out.at[field, pl.ds(pad + cells_x, pad)])
    copies.wait_all()


def solid_halo(cond, sink, heat, temp, pad):
    cells_x, cells_y, depth = cond.shape
    fields = (cond, sink, heat, temp)
    x_shape = jax.ShapeDtypeStruct((4, pad, cells_y, depth), cond.dtype)
    low, high = pl.pallas_call(
        functools.partial(solid_x_kernel, cells_x, pad),
        out_shape=(x_shape, x_shape), in_specs=[ANY] * 4, out_specs=(VMEM, VMEM),
        scratch_shapes=[pltpu.SemaphoreType.DMA((8,))],
        compiler_params=pltpu.CompilerParams(vmem_limit_bytes=32 * 1024 * 1024),
        cost_estimate=lasts(2),
    )(*fields)
    xlo, xhi = chain(high, "blk", 1), chain(low, "blk", -1)
    y_shape = jax.ShapeDtypeStruct((4, cells_x + 2 * pad, TILE, depth), cond.dtype)
    low, high = pl.pallas_call(
        functools.partial(solid_y_kernel, cells_x, cells_y, pad),
        out_shape=(y_shape, y_shape), in_specs=[ANY] * 6, out_specs=(VMEM, VMEM),
        scratch_shapes=[pltpu.SemaphoreType.DMA((24,))],
        compiler_params=pltpu.CompilerParams(vmem_limit_bytes=32 * 1024 * 1024),
        cost_estimate=lasts(3),
    )(*fields, xlo, xhi)
    return xlo, xhi, chain(high, "sub", 1), chain(low, "sub", -1)


def solid_step(flags, cond, sink, heat, temp, halo, films, pad):
    cells_x, cells_y, depth = cond.shape
    wide_x, wide_y = cells_x + 2 * pad, cells_y + 2 * TILE
    area = pltpu.VMEM((wide_x, wide_y, depth), jnp.float32)
    return pl.pallas_call(
        functools.partial(solid_kernel, cells_x, cells_y, depth, pad, cheby_coefficients(SWEEPS)),
        out_shape=(jax.ShapeDtypeStruct((cells_x, cells_y, depth), cond.dtype),
                   jax.ShapeDtypeStruct((cells_y, LANES), cond.dtype)),
        in_specs=[SMEM] + [ANY] * 8 + [VMEM] * 3,
        out_specs=(VMEM, VMEM),
        scratch_shapes=[area] * 5
        + [pltpu.VMEM((wide_x + 1, wide_y, depth), jnp.float32)]
        + [area] * 4
        + [pltpu.VMEM((2, wide_y, LANES), jnp.float32), pltpu.SemaphoreType.DMA((20,))],
        compiler_params=pltpu.CompilerParams(vmem_limit_bytes=48 * 1024 * 1024),
        cost_estimate=lasts(30),
    )(flags, cond, sink, heat, temp, *halo, *films)


def ones_where(condition):
    return jnp.where(condition, 1.0, 0.0)


def route_kernel(group_total, slot_cap, owner, out):
    dirs = owner[...]
    row_total = group_total * slot_cap
    codes = row_index((TILE, group_total))
    matched = ones_where((codes >= 1) & (codes <= 4) & (dirs == codes))
    before = ones_where(row_index((group_total, group_total)) < lane_index((group_total, group_total)))
    rank = jnp.dot(matched, before, precision=HIGHEST)
    start = jnp.where(matched > 0.5, rank * slot_cap, -1.0 * row_total)
    start = jnp.where(codes == 0, ones_where(dirs == 0), start)
    spread = ones_where(row_index((group_total, row_total)) == lane_index((group_total, row_total)) // slot_cap)
    wide = jnp.dot(start, spread, precision=HIGHEST)
    within = (lane_index((TILE, row_total)) % slot_cap).astype(jnp.float32)
    out[...] = jnp.where(row_index((TILE, row_total)) == 0, wide, wide + within)


def cell_values(plane_t, cells_x, cells_y, cells):
    count = cells.shape[1]
    in_x = ones_where(row_index((cells_x, count)) == cells // cells_y)
    in_y = ones_where(row_index((cells_y, count)) == cells % cells_y)
    lines = jnp.dot(plane_t[:, :cells_x], in_x, precision=HIGHEST)
    return jnp.sum(lines * in_y, axis=0, keepdims=True)


def rows_kernel(cells_x, cells_y, near_rows, route, gas_t, film_t, pair, *outs):
    row_total = cells_x * cells_y
    cells = lane_index((1, row_total))
    film = cell_values(film_t[...], cells_x, cells_y, cells)
    gas = cell_values(gas_t[...], cells_x, cells_y, cells)
    values = jnp.concatenate([film, gas], axis=0)
    pair[...] = values
    for d in range(4):
        slots = route[d + 1:d + 2, :].astype(jnp.int32)
        pick = ones_where(row_index((near_rows, row_total)) == slots)
        outs[d][...] = lax.dot_general(values, pick, (((1,), (1,)), ((), ())), precision=HIGHEST)


def film_kernel(cells_x, cells_y, pad, flags, route, landing, pair, from_0, from_1, from_2, from_3, plane, low, high):
    cells = landing[...]
    slots = cells.shape[1]
    arrived = [jnp.where(flags[d] > 0, piece[...], 0.0) for d, piece in enumerate((from_0, from_1, from_2, from_3))]
    own = pair[...]
    film = jnp.concatenate([own[:1] * route[0:1, :]] + [piece[:1] for piece in arrived], axis=1)
    gas = jnp.concatenate([own[1:]] + [piece[1:] for piece in arrived], axis=1)
    in_x = ones_where(row_index((LANES, slots)) == cells // cells_y)
    in_y = ones_where(row_index((cells_y, slots)) == cells % cells_y)
    weighted = jnp.concatenate([in_y * film, in_y * (film * gas)], axis=0)
    total = lax.dot_general(weighted, in_x, (((1,), (1,)), ((), ())), precision=HIGHEST)
    lane = lane_index(total.shape)
    to_high = jnp.where(lane >= LANES - pad, pltpu.roll(total, LANES - cells_x, 1), 0.0)
    to_low = jnp.where((lane >= cells_x) & (lane < cells_x + pad), pltpu.roll(total, cells_x, 1), 0.0)
    for ref, value in ((plane, total), (low, to_low), (high, to_high)):
        ref[0] = value[:cells_y]
        ref[1] = value[cells_y:]


def widen_kernel(cells_y, flags, plane, low, high, out, first, last):
    total = plane[...] + jnp.where(flags[0] > 0, low[...], 0.0) + jnp.where(flags[1] > 0, high[...], 0.0)
    out[...] = total
    first[...] = total[:, :TILE]
    last[...] = total[:, cells_y - TILE:]


def gather_kernel(cells_x, cells_y, row_total, near_rows, landing, surface_t, own, *outs):
    values = cell_values(surface_t[...], cells_x, cells_y, landing[...])
    own[...] = values[:, :row_total]
    for d in range(4):
        outs[d][...] = values[:, row_total + d * near_rows:row_total + (d + 1) * near_rows]


def wall_kernel(near_rows, flags, route, own, from_0, from_1, from_2, from_3, out):
    row_total = own.shape[1]
    total = own[...] * route[0:1, :]
    for d, (piece, side) in enumerate(((from_0, 1), (from_1, 0), (from_2, 3), (from_3, 2))):
        slots = route[d + 1:d + 2, :].astype(jnp.int32)
        pick = ones_where(row_index((near_rows, row_total)) == slots)
        total = total + jnp.dot(jnp.where(flags[side] > 0, piece[...], 0.0), pick, precision=HIGHEST)
    out[...] = jnp.where(lane_index((1, row_total)) < flags[4], total, 0.0)


def small_call(kernel, shapes, flags, *args):
    lead = [] if flags is None else [flags]
    return pl.pallas_call(
        kernel,
        out_shape=tuple(jax.ShapeDtypeStruct(shape, jnp.float32) for shape in shapes),
        in_specs=[SMEM] * len(lead) + [VMEM] * len(args),
        out_specs=tuple(VMEM for _ in shapes),
        compiler_params=pltpu.CompilerParams(vmem_limit_bytes=32 * 1024 * 1024),
        cost_estimate=lasts(1),
    )(*lead, *args)


def on_device(
    fluid_temp, velocity, eddy_diff, wall_prev, row_count, owner_table, landing_cell,
    solid_temp, conductivity, sink, heat_source,
):
    cells_x, cells_y, cells_z = fluid_temp.shape
    solid_x, solid_y, solid_z = solid_temp.shape
    row_total = cells_x * cells_y
    group_total = owner_table.shape[1]
    slot_cap = row_total // group_total
    near_rows = group_total // 8 * slot_cap
    pad = SWEEPS
    wall_plane = wall_prev.reshape(cells_x, cells_y)
    live_two = jnp.where(jnp.arange(row_total, dtype=jnp.int32) < row_count[0], 2.0, 0.0).reshape(cells_x, cells_y)
    flags = jnp.concatenate([jnp.stack([*sides("blk"), *sides("sub")]).astype(jnp.int32), row_count])

    both = jnp.stack([live_two, wall_plane])
    edges = jnp.stack([both[:, 0], both[:, -1], both[:, :, 0], both[:, :, -1]])
    notes = jnp.pad(edges.transpose(0, 2, 1), ((0, 0), (0, 0), (0, LANES - 2)))
    wall_t = jnp.pad(wall_plane.T, ((0, 0), (0, LANES - cells_x)))

    parts = part_depths(cells_z)
    strips = []
    for start, size in parts:
        here = notes if start == 0 else None
        low, high = x_pack(fluid_temp, velocity, eddy_diff, here, start, size)
        xlo, xhi = chain(high, "blk", 1), chain(low, "blk", -1)
        low, high = y_pack(fluid_temp, velocity, eddy_diff, xlo, xhi, here, start, size)
        strips.append((xlo, xhi, chain(high, "sub", 1), chain(low, "sub", -1)))
    fluid = (fluid_temp, velocity, eddy_diff, wall_t, flags)
    gas_t, film_t = fluid_call(*fluid, strips[0], parts[0][1], parts[:1], True)
    halo = solid_halo(conductivity, sink, heat_source, solid_temp, pad)
    fluid_new = fluid_call(*fluid, sum(strips, ()), cells_z, parts, False)

    (route,) = small_call(
        functools.partial(route_kernel, group_total, slot_cap), [(TILE, row_total)], None, owner_table
    )
    pair, *bands = small_call(
        functools.partial(rows_kernel, cells_x, cells_y, near_rows),
        [(2, row_total)] + [(2, near_rows)] * 4, None, route, gas_t, film_t,
    )
    moves = (("blk", 1), ("blk", -1), ("sub", 1), ("sub", -1))
    arrived = [ring(band, axis, step) for band, (axis, step) in zip(bands, moves)]
    plane = (2, solid_y, LANES)
    film, low, high = small_call(
        functools.partial(film_kernel, solid_x, solid_y, pad), [plane] * 3, flags, route, landing_cell, pair, *arrived
    )
    film, first, last = small_call(
        functools.partial(widen_kernel, solid_y), [plane] + [(2, TILE, LANES)] * 2,
        flags, film, ring(high, "blk", 1), ring(low, "blk", -1),
    )
    films = (film, ring(last, "sub", 1), ring(first, "sub", -1))
    solid_new, surface_t = solid_step(flags, conductivity, sink, heat_source, solid_temp, halo, films, pad)

    own, *backs = small_call(
        functools.partial(gather_kernel, solid_x, solid_y, row_total, near_rows),
        [(1, row_total)] + [(1, near_rows)] * 4, None, landing_cell, surface_t,
    )
    returned = [ring(back, axis, -step) for back, (axis, step) in zip(backs, moves)]
    (wall_new,) = small_call(
        functools.partial(wall_kernel, near_rows), [(1, row_total)], flags, route, own, *returned
    )
    return fluid_new, solid_new, wall_new.reshape(row_total)


def solution(mesh):
    return jax.shard_map(
        on_device,
        mesh=mesh,
        in_specs=(
            P("blk", "sub", None),
            P(None, "blk", "sub", None),
            P("blk", "sub", None),
            P(("blk", "sub")),
            P(("blk", "sub")),
            P(("blk", "sub"), None),
            P(("blk", "sub"), None),
            P("blk", "sub", None),
            P("blk", "sub", None),
            P("blk", "sub", None),
            P("blk", "sub", None),
        ),
        out_specs=(P("blk", "sub", None), P("blk", "sub", None), P(("blk", "sub"))),
        check_vma=False,
    )
```

time: 299 us -> 205 us (0.69)
  the two profiles are of different devices: /device:TPU:27 before, /device:TPU:3 now
where the time goes in v1:
time: 205 us; the launch traced here: 203 us
  Pallas kernels  73 us (36%)
  waiting for transfers between devices  64.6 us (32%)
  starting transfers between devices  41.7 us (20%)
  local copies, waits for them, and re-layouts  18.2 us (9%)
  other arithmetic  4.26 us (2%)
    ppermute x12, waiting for transfers between devices, chain(): return lax.ppermute(value, axis, pairs)  41.5 us
    pallas_call x1, Pallas kernels, solid_step(): pl.pallas_call(functools.partial(solid_kernel, cells_x, cells_y, depth, p...  32.2 us
    ppermute x12, starting transfers between devices, chain(): return lax.ppermute(value, axis, pairs)  32.2 us
    pallas_call x2, Pallas kernels, fluid_call(): pl.pallas_call(functools.partial(fluid_kernel, cells_x, cells_y, depth, p...  25.6 us
    ppermute x12, waiting for transfers between devices, ring(): lax.ppermute(value, axis, [(i, (i + step) % count) for i in range(count)])  23.1 us
    unnamed x46, local copies, waits for them, and re-layouts  11.9 us
    ppermute x12, starting transfers between devices, ring(): lax.ppermute(value, axis, [(i, (i + step) % count) for i in range(count)])  9.58 us
    pallas_call x6, Pallas kernels, small_call(): pl.pallas_call(kernel, out_shape=tuple((jax.ShapeDtypeStruct(shape, jnp.f...  7.38 us
  transfers between devices with their start and end apart: 24, of which 13 were waited for; matrix products, arithmetic and copies ran while one was open for 5% of the time, Pallas kernels for 33%

profile of v1, /device:TPU:3, one launch (start us, length us, event | category | flops | bytes accessed | tf_op | source)
XLA Modules:
  0.0 203.4 jit_solution(14909699605067329067)
XLA Ops:
  5.8 3.9 %collective-permute-start.8 = (f32[4,8,32,256]{3,2,1,0:T(8,128)S(1)}, f32[4,8,32,256]{3,2,1,0:T(8,128)S(1)}, u32[]{:S(2)}, u32[]{:S(2)}) collective-permute-start(f32[4,8,32,256]{3,2,1,0:T(8,128)S(1)} %get-tuple-element.43), channel_id=1, source_target_pairs={{0,4},{4,8},{8,12},{12,16},{16,20},{20,24},{24,28},{1,5},{5,9},{9,... | collective-permute-start | bytes 3145736 | tf_op jit(solution)/shard_map/ppermute | solution.py:44
  9.7 2.3 %collective-permute-start.9 = (f32[4,8,32,256]{3,2,1,0:T(8,128)S(1)}, f32[4,8,32,256]{3,2,1,0:T(8,128)S(1)}, u32[]{:S(2)}, u32[]{:S(2)}) collective-permute-start(f32[4,8,32,256]{3,2,1,0:T(8,128)S(1)} %get-tuple-element.44), channel_id=1, source_target_pairs={{4,0},{8,4},{12,8},{16,12},{20,16},{24,20},{28,24},{5,1},{9,5},{13... | collective-permute-start | bytes 3145736 | tf_op jit(solution)/shard_map/ppermute | solution.py:44
  12.1 17.5 %collective-permute-done.8.refs_4_.xlo = f32[4,8,32,256]{3,2,1,0:T(8,128)S(1)} collective-permute-done((f32[4,8,32,256]{3,2,1,0:T(8,128)S(1)}, f32[4,8,32,256]{3,2,1,0:T(8,128)S(1)}, u32[]{:S(2)}, u32[]{:S(2)}) %collective-permute-start.8) | collective-permute-done | bytes 1048608 | tf_op jit(solution)/shard_map/ppermute | solution.py:44
  29.6 4.7 %collective-permute-done.9.refs_5_.xhi = f32[4,8,32,256]{3,2,1,0:T(8,128)S(1)} collective-permute-done((f32[4,8,32,256]{3,2,1,0:T(8,128)S(1)}, f32[4,8,32,256]{3,2,1,0:T(8,128)S(1)}, u32[]{:S(2)}, u32[]{:S(2)}) %collective-permute-start.9) | collective-permute-done | bytes 1048608 | tf_op jit(solution)/shard_map/ppermute | solution.py:44
  36.7 4.4 %collective-permute-start.10 = (f32[4,48,8,256]{3,2,1,0:T(8,128)}, f32[4,48,8,256]{3,2,1,0:T(8,128)}, u32[]{:S(2)}, u32[]{:S(2)}) collective-permute-start(f32[4,48,8,256]{3,2,1,0:T(8,128)} %get-tuple-element.45), channel_id=1, source_target_pairs={{0,1},{1,2},{2,3},{4,5},{5,6},{6,7},{8,9},{9,10},{10,11},{12,13},{... | collective-permute-start | bytes 4718600 | tf_op jit(solution)/shard_map/ppermute | solution.py:44
  58.8 2.8 %copy-done.1 = f32[3,32,32,512]{3,2,1,0:T(8,128)S(1)} copy-done((f32[3,32,32,512]{3,2,1,0:T(8,128)S(1)}, f32[3,32,32,512]{3,2,1,0:T(8,128)}, u32[]{:S(2)}) %copy-start.1) | copy-done | bytes 6291480
  63.4 4.2 %collective-permute-start = (f32[9,32,128]{2,1,0:T(8,128)S(1)}, f32[9,32,128]{2,1,0:T(8,128)S(1)}, u32[]{:S(2)}, u32[]{:S(2)}) collective-permute-start(f32[9,32,128]{2,1,0:T(8,128)S(1)} %get-tuple-element.35), channel_id=1, source_target_pairs={{0,4},{4,8},{8,12},{12,16},{16,20},{20,24},{24,28},{1,5},{5,9},{9,... | collective-permute-start | bytes 442376 | tf_op jit(solution)/shard_map/ppermute | solution.py:44
  69.7 2.7 %collective-permute-start.1 = (f32[9,32,128]{2,1,0:T(8,128)S(1)}, f32[9,32,128]{2,1,0:T(8,128)S(1)}, u32[]{:S(2)}, u32[]{:S(2)}) collective-permute-start(f32[9,32,128]{2,1,0:T(8,128)S(1)} %get-tuple-element.36), channel_id=1, source_target_pairs={{4,0},{8,4},{12,8},{16,12},{20,16},{24,20},{28,24},{5,1},{9,5},{13... | collective-permute-start | bytes 442376 | tf_op jit(solution)/shard_map/ppermute | solution.py:44
  72.3 5.4 %collective-permute-done.1.refs_4_.refs_1_ = f32[9,32,128]{2,1,0:T(8,128)S(1)} collective-permute-done((f32[9,32,128]{2,1,0:T(8,128)S(1)}, f32[9,32,128]{2,1,0:T(8,128)S(1)}, u32[]{:S(2)}, u32[]{:S(2)}) %collective-permute-start.1) | collective-permute-done | bytes 147488 | tf_op jit(solution)/shard_map/ppermute | solution.py:44
  79.0 5.1 %collective-permute-start.2 = (f32[296,128]{1,0:T(8,128)}, f32[296,128]{1,0:T(8,128)}, u32[]{:S(2)}, u32[]{:S(2)}) collective-permute-start(f32[296,128]{1,0:T(8,128)} %get-tuple-element.37), channel_id=1, source_target_pairs={{0,1},{1,2},{2,3},{4,5},{5,6},{6,7},{8,9},{9,10},{10,11},{12,13},{... | collective-permute-start | bytes 454664 | tf_op jit(solution)/shard_map/ppermute | solution.py:44
  84.1 2.6 %shard_map.133 = (f32[264,384]{1,0:T(8,128)}, f32[264,384]{1,0:T(8,128)}) custom-call(f32[32,32,512]{2,1,0:T(8,128)S(1)} %copy-done.2, f32[3,32,32,512]{3,2,1,0:T(8,128)S(1)} %copy-done.1, f32[32,32,512]{2,1,0:T(8,128)S(1)} %copy-done.4, f32[8,32,384]{2,1,0:T(8,128)S(1)} %collective-permute-done.4.refs_3_.refs_4_, ...), custom_call_target="tpu_custom_call" | custom-call | bytes 7380000 | tf_op jit(solution)/shard_map/pallas_call | solution.py:193
  91.6 11.7 %collective-permute-done.3.refs_3_ = f32[296,128]{1,0:T(8,128)S(1)} collective-permute-done((f32[296,128]{1,0:T(8,128)}, f32[296,128]{1,0:T(8,128)S(1)}, u32[]{:S(2)}, u32[]{:S(2)}) %collective-permute-start.3) | collective-permute-done | bytes 151584 | tf_op jit(solution)/shard_map/ppermute | solution.py:44
  105.1 7.0 %shard_map.138 = (f32[32,128]{1,0:T(8,128)S(1)}, f32[32,128]{1,0:T(8,128)S(1)}) custom-call(s32[5]{0:T(128)S(1)} %pad_add_fusion.flags, f32[32,32,512]{2,1,0:T(8,128)} %temp.4, f32[3,32,32,512]{3,2,1,0:T(8,128)} %velo.3, f32[32,32,512]{2,1,0:T(8,128)} %diff.3, f32[32,128]{1,0:T(8,128)S(1)} %pad.8.wall_t, f32[9,32,128]{2,1,0:T(8,128)S(1)} %copy-done.15, ...), custom_call_target="tpu_custom_call" | custom-call | bytes 22140000 | tf_op jit(solution)/shard_map/pallas_call | solution.py:397
  116.0 4.4 %collective-permute-done.13.from_1 = f32[2,128]{1,0:T(2,128)S(1)} collective-permute-done((f32[2,128]{1,0:T(2,128)S(1)}, f32[2,128]{1,0:T(2,128)S(1)}, u32[]{:S(2)}, u32[]{:S(2)}) %collective-permute-start.13) | collective-permute-done | bytes 1056 | tf_op jit(solution)/shard_map/ppermute | solution.py:38
  121.9 2.8 %collective-permute-done.14.from_2 = f32[2,128]{1,0:T(2,128)S(1)} collective-permute-done((f32[2,128]{1,0:T(2,128)S(1)}, f32[2,128]{1,0:T(2,128)S(1)}, u32[]{:S(2)}, u32[]{:S(2)}) %collective-permute-start.14) | collective-permute-done | bytes 1056 | tf_op jit(solution)/shard_map/ppermute | solution.py:38
  124.6 2.4 %collective-permute-done.15.from_3 = f32[2,128]{1,0:T(2,128)S(1)} collective-permute-done((f32[2,128]{1,0:T(2,128)S(1)}, f32[2,128]{1,0:T(2,128)S(1)}, u32[]{:S(2)}, u32[]{:S(2)}) %collective-permute-start.15) | collective-permute-done | bytes 1056 | tf_op jit(solution)/shard_map/ppermute | solution.py:38
  128.7 2.4 %collective-permute-start.16 = (f32[2,32,128]{2,1,0:T(8,128)S(1)}, f32[2,32,128]{2,1,0:T(8,128)S(1)}, u32[]{:S(2)}, u32[]{:S(2)}) collective-permute-start(f32[2,32,128]{2,1,0:T(8,128)S(1)} %get-tuple-element.55), channel_id=1, source_target_pairs={{0,4},{4,8},{8,12},{12,16},{16,20},{20,24},{24,28},{28,0},{1,5},{5... | collective-permute-start | bytes 98312 | tf_op jit(solution)/shard_map/ppermute | solution.py:38
  132.1 5.0 %collective-permute-done.17.high = f32[2,32,128]{2,1,0:T(8,128)S(1)} collective-permute-done((f32[2,32,128]{2,1,0:T(8,128)S(1)}, f32[2,32,128]{2,1,0:T(8,128)S(1)}, u32[]{:S(2)}, u32[]{:S(2)}) %collective-permute-start.17) | collective-permute-done | bytes 32800 | tf_op jit(solution)/shard_map/ppermute | solution.py:38
  137.7 4.3 %collective-permute-done.18.film_lo = f32[2,8,128]{2,1,0:T(8,128)S(1)} collective-permute-done((f32[2,8,128]{2,1,0:T(8,128)S(1)}, f32[2,8,128]{2,1,0:T(8,128)S(1)}, u32[]{:S(2)}, u32[]{:S(2)}) %collective-permute-start.18) | collective-permute-done | bytes 8224 | tf_op jit(solution)/shard_map/ppermute | solution.py:38
  142.0 2.5 %collective-permute-done.19.film_hi = f32[2,8,128]{2,1,0:T(8,128)S(1)} collective-permute-done((f32[2,8,128]{2,1,0:T(8,128)S(1)}, f32[2,8,128]{2,1,0:T(8,128)S(1)}, u32[]{:S(2)}, u32[]{:S(2)}) %collective-permute-start.19) | collective-permute-done | bytes 8224 | tf_op jit(solution)/shard_map/ppermute | solution.py:38
  144.5 32.2 %shard_map.142 = (f32[32,32,256]{2,1,0:T(8,128)}, f32[32,128]{1,0:T(8,128)S(1)}) custom-call(s32[5]{0:T(128)S(1)} %pad_add_fusion.flags, f32[32,32,256]{2,1,0:T(8,128)S(1)} %copy-done.6, f32[32,32,256]{2,1,0:T(8,128)S(1)} %copy-done.8, f32[32,32,256]{2,1,0:T(8,128)S(1)} %copy-done.10, f32[32,32,256]{2,1,0:T(8,128)S(1)} %copy-done.12, ...), custom_call_target="tpu_custom_call" | custom-call | bytes 110700000 | tf_op jit(solution)/shard_map/pallas_call | solution.py:575
  177.1 2.6 %collective-permute-start.21 = (f32[1,128]{1,0:T(1,128)S(1)}, f32[1,128]{1,0:T(1,128)S(1)}, u32[]{:S(2)}, u32[]{:S(2)}) collective-permute-start(f32[1,128]{1,0:T(1,128)S(1)} %get-tuple-element.64), channel_id=1, source_target_pairs={{0,4},{4,8},{8,12},{12,16},{16,20},{20,24},{24,28},{28,0},{1,5},{5... | collective-permute-start | bytes 1544 | tf_op jit(solution)/shard_map/ppermute | solution.py:38
  182.3 18.6 %shard_map.134 = f32[32,32,512]{2,1,0:T(8,128)} custom-call(s32[5]{0:T(128)S(1)} %pad_add_fusion.flags, f32[32,32,512]{2,1,0:T(8,128)} %temp.4, f32[3,32,32,512]{3,2,1,0:T(8,128)} %velo.3, f32[32,32,512]{2,1,0:T(8,128)} %diff.3, f32[32,128]{1,0:T(8,128)S(1)} %pad.8.wall_t, f32[9,32,128]{2,1,0:T(8,128)S(1)} %copy-done.15, f32[9,32,128]{2,1,0:T(8,128)S(1)} %copy-done.17, ...), custom_call_target="tpu_custom_call" | custom-call | bytes 66420000 | tf_op jit(solution)/shard_map/pallas_call | solution.py:397
  201.0 2.4 %shard_map.144 = f32[1,1024]{1,0:T(1,128)} custom-call(s32[5]{0:T(128)S(1)} %pad_add_fusion.flags, f32[8,1024]{1,0:T(8,128)S(1)} %shard_map.137.route, f32[1,1024]{1,0:T(1,128)S(1)} %get-tuple-element.62.own, f32[1,128]{1,0:T(1,128)S(1)} %collective-permute-done.20.from_0, f32[1,128]{1,0:T(1,128)S(1)} %collective-permute-done.21.from_1, ...), custom_call_target="tpu_custom_call" | custom-call | bytes 3690000 | tf_op jit(solution)/shard_map/pallas_call | solution.py:675
  (100 shorter events, 47.8 us)
Async XLA Ops:
  5.8 23.8 %collective-permute-start.8 = (f32[4,8,32,256]{3,2,1,0:T(8,128)S(1)}, f32[4,8,32,256]{3,2,1,0:T(8,128)S(1)}, u32[]{:S(2)}, u32[]{:S(2)}) collective-permute-start(f32[4,8,32,256]{3,2,1,0:T(8,128)S(1)} %get-tuple-element.43), channel_id=1, source_target_pairs={{0,4},{4,8},{8,12},{12,16},{16,20},{20,24},{24,28},{1,5},{5,9},{9,... | collective-permute-start | bytes 3145736 | tf_op jit(solution)/shard_map/ppermute | solution.py:44
  9.7 24.6 %collective-permute-start.9 = (f32[4,8,32,256]{3,2,1,0:T(8,128)S(1)}, f32[4,8,32,256]{3,2,1,0:T(8,128)S(1)}, u32[]{:S(2)}, u32[]{:S(2)}) collective-permute-start(f32[4,8,32,256]{3,2,1,0:T(8,128)S(1)} %get-tuple-element.44), channel_id=1, source_target_pairs={{4,0},{8,4},{12,8},{16,12},{20,16},{24,20},{28,24},{5,1},{9,5},{13... | collective-permute-start | bytes 3145736 | tf_op jit(solution)/shard_map/ppermute | solution.py:44
  36.7 107.8 %collective-permute-start.10 = (f32[4,48,8,256]{3,2,1,0:T(8,128)}, f32[4,48,8,256]{3,2,1,0:T(8,128)}, u32[]{:S(2)}, u32[]{:S(2)}) collective-permute-start(f32[4,48,8,256]{3,2,1,0:T(8,128)} %get-tuple-element.45), channel_id=1, source_target_pairs={{0,1},{1,2},{2,3},{4,5},{5,6},{6,7},{8,9},{9,10},{10,11},{12,13},{... | collective-permute-start | bytes 4718600 | tf_op jit(solution)/shard_map/ppermute | solution.py:44
  41.1 103.4 %collective-permute-start.11 = (f32[4,48,8,256]{3,2,1,0:T(8,128)}, f32[4,48,8,256]{3,2,1,0:T(8,128)}, u32[]{:S(2)}, u32[]{:S(2)}) collective-permute-start(f32[4,48,8,256]{3,2,1,0:T(8,128)} %get-tuple-element.46), channel_id=1, source_target_pairs={{1,0},{2,1},{3,2},{5,4},{6,5},{7,6},{9,8},{10,9},{11,10},{13,12},{... | collective-permute-start | bytes 4718600 | tf_op jit(solution)/shard_map/ppermute | solution.py:44
  43.5 40.5 %collective-permute-start.4 = (f32[8,32,384]{2,1,0:T(8,128)}, f32[8,32,384]{2,1,0:T(8,128)S(1)}, u32[]{:S(2)}, u32[]{:S(2)}) collective-permute-start(f32[8,32,384]{2,1,0:T(8,128)} %get-tuple-element.39), channel_id=1, source_target_pairs={{0,4},{4,8},{8,12},{12,16},{16,20},{20,24},{24,28},{1,5},{5,9},{9,... | collective-permute-start | bytes 1179656 | tf_op jit(solution)/shard_map/ppermute | solution.py:44
  45.6 38.5 %collective-permute-start.5 = (f32[8,32,384]{2,1,0:T(8,128)}, f32[8,32,384]{2,1,0:T(8,128)}, u32[]{:S(2)}, u32[]{:S(2)}) collective-permute-start(f32[8,32,384]{2,1,0:T(8,128)} %get-tuple-element.40), channel_id=1, source_target_pairs={{4,0},{8,4},{12,8},{16,12},{20,16},{24,20},{28,24},{5,1},{9,5},{13... | collective-permute-start | bytes 1179656 | tf_op jit(solution)/shard_map/ppermute | solution.py:44
  63.4 6.2 %collective-permute-start = (f32[9,32,128]{2,1,0:T(8,128)S(1)}, f32[9,32,128]{2,1,0:T(8,128)S(1)}, u32[]{:S(2)}, u32[]{:S(2)}) collective-permute-start(f32[9,32,128]{2,1,0:T(8,128)S(1)} %get-tuple-element.35), channel_id=1, source_target_pairs={{0,4},{4,8},{8,12},{12,16},{16,20},{20,24},{24,28},{1,5},{5,9},{9,... | collective-permute-start | bytes 442376 | tf_op jit(solution)/shard_map/ppermute | solution.py:44
  69.7 8.1 %collective-permute-start.1 = (f32[9,32,128]{2,1,0:T(8,128)S(1)}, f32[9,32,128]{2,1,0:T(8,128)S(1)}, u32[]{:S(2)}, u32[]{:S(2)}) collective-permute-start(f32[9,32,128]{2,1,0:T(8,128)S(1)} %get-tuple-element.36), channel_id=1, source_target_pairs={{4,0},{8,4},{12,8},{16,12},{20,16},{24,20},{28,24},{5,1},{9,5},{13... | collective-permute-start | bytes 442376 | tf_op jit(solution)/shard_map/ppermute | solution.py:44
  79.0 10.5 %collective-permute-start.2 = (f32[296,128]{1,0:T(8,128)}, f32[296,128]{1,0:T(8,128)}, u32[]{:S(2)}, u32[]{:S(2)}) collective-permute-start(f32[296,128]{1,0:T(8,128)} %get-tuple-element.37), channel_id=1, source_target_pairs={{0,1},{1,2},{2,3},{4,5},{5,6},{6,7},{8,9},{9,10},{10,11},{12,13},{... | collective-permute-start | bytes 454664 | tf_op jit(solution)/shard_map/ppermute | solution.py:44
  86.7 94.8 %collective-permute-start.6 = (f32[264,384]{1,0:T(8,128)}, f32[264,384]{1,0:T(8,128)S(1)}, u32[]{:S(2)}, u32[]{:S(2)}) collective-permute-start(f32[264,384]{1,0:T(8,128)} %get-tuple-element.41), channel_id=1, source_target_pairs={{0,1},{1,2},{2,3},{4,5},{5,6},{6,7},{8,9},{9,10},{10,11},{12,13},{... | collective-permute-start | bytes 1216520 | tf_op jit(solution)/shard_map/ppermute | solution.py:44
  88.1 93.4 %collective-permute-start.7 = (f32[264,384]{1,0:T(8,128)}, f32[264,384]{1,0:T(8,128)S(1)}, u32[]{:S(2)}, u32[]{:S(2)}) collective-permute-start(f32[264,384]{1,0:T(8,128)} %get-tuple-element.42), channel_id=1, source_target_pairs={{1,0},{2,1},{3,2},{5,4},{6,5},{7,6},{9,8},{10,9},{11,10},{13,12},{... | collective-permute-start | bytes 1216520 | tf_op jit(solution)/shard_map/ppermute | solution.py:44
  89.5 13.8 %collective-permute-start.3 = (f32[296,128]{1,0:T(8,128)}, f32[296,128]{1,0:T(8,128)S(1)}, u32[]{:S(2)}, u32[]{:S(2)}) collective-permute-start(f32[296,128]{1,0:T(8,128)} %copy-done.20), channel_id=1, source_target_pairs={{1,0},{2,1},{3,2},{5,4},{6,5},{7,6},{9,8},{10,9},{11,10},{13,12},{... | collective-permute-start | bytes 454664 | tf_op jit(solution)/shard_map/ppermute | solution.py:44
  114.1 1.9 collective-permute-start.12
  116.0 4.4 %collective-permute-start.13 = (f32[2,128]{1,0:T(2,128)S(1)}, f32[2,128]{1,0:T(2,128)S(1)}, u32[]{:S(2)}, u32[]{:S(2)}) collective-permute-start(f32[2,128]{1,0:T(2,128)S(1)} %get-tuple-element.51), channel_id=1, source_target_pairs={{0,28},{4,0},{8,4},{12,8},{16,12},{20,16},{24,20},{28,24},{1,29},{... | collective-permute-start | bytes 3080 | tf_op jit(solution)/shard_map/ppermute | solution.py:38
  120.4 4.2 %collective-permute-start.14 = (f32[2,128]{1,0:T(2,128)S(1)}, f32[2,128]{1,0:T(2,128)S(1)}, u32[]{:S(2)}, u32[]{:S(2)}) collective-permute-start(f32[2,128]{1,0:T(2,128)S(1)} %get-tuple-element.52), channel_id=1, source_target_pairs={{0,1},{1,2},{2,3},{3,0},{4,5},{5,6},{6,7},{7,4},{8,9},{9,10},{10,1... | collective-permute-start | bytes 3080 | tf_op jit(solution)/shard_map/ppermute | solution.py:38
  124.6 2.4 %collective-permute-start.15 = (f32[2,128]{1,0:T(2,128)S(1)}, f32[2,128]{1,0:T(2,128)S(1)}, u32[]{:S(2)}, u32[]{:S(2)}) collective-permute-start(f32[2,128]{1,0:T(2,128)S(1)} %get-tuple-element.53), channel_id=1, source_target_pairs={{0,3},{1,0},{2,1},{3,2},{4,7},{5,4},{6,5},{7,6},{8,11},{9,8},{10,9... | collective-permute-start | bytes 3080 | tf_op jit(solution)/shard_map/ppermute | solution.py:38
  128.7 3.4 %collective-permute-start.16 = (f32[2,32,128]{2,1,0:T(8,128)S(1)}, f32[2,32,128]{2,1,0:T(8,128)S(1)}, u32[]{:S(2)}, u32[]{:S(2)}) collective-permute-start(f32[2,32,128]{2,1,0:T(8,128)S(1)} %get-tuple-element.55), channel_id=1, source_target_pairs={{0,4},{4,8},{8,12},{12,16},{16,20},{20,24},{24,28},{28,0},{1,5},{5... | collective-permute-start | bytes 98312 | tf_op jit(solution)/shard_map/ppermute | solution.py:38
  132.1 5.0 %collective-permute-start.17 = (f32[2,32,128]{2,1,0:T(8,128)S(1)}, f32[2,32,128]{2,1,0:T(8,128)S(1)}, u32[]{:S(2)}, u32[]{:S(2)}) collective-permute-start(f32[2,32,128]{2,1,0:T(8,128)S(1)} %get-tuple-element.56), channel_id=1, source_target_pairs={{0,28},{4,0},{8,4},{12,8},{16,12},{20,16},{24,20},{28,24},{1,29},{... | collective-permute-start | bytes 98312 | tf_op jit(solution)/shard_map/ppermute | solution.py:38
  137.6 4.4 %collective-permute-start.18 = (f32[2,8,128]{2,1,0:T(8,128)S(1)}, f32[2,8,128]{2,1,0:T(8,128)S(1)}, u32[]{:S(2)}, u32[]{:S(2)}) collective-permute-start(f32[2,8,128]{2,1,0:T(8,128)S(1)} %get-tuple-element.58), channel_id=1, source_target_pairs={{0,1},{1,2},{2,3},{3,0},{4,5},{5,6},{6,7},{7,4},{8,9},{9,10},{10,1... | collective-permute-start | bytes 24584 | tf_op jit(solution)/shard_map/ppermute | solution.py:38
  142.0 2.5 %collective-permute-start.19 = (f32[2,8,128]{2,1,0:T(8,128)S(1)}, f32[2,8,128]{2,1,0:T(8,128)S(1)}, u32[]{:S(2)}, u32[]{:S(2)}) collective-permute-start(f32[2,8,128]{2,1,0:T(8,128)S(1)} %get-tuple-element.59), channel_id=1, source_target_pairs={{0,3},{1,0},{2,1},{3,2},{4,7},{5,4},{6,5},{7,6},{8,11},{9,8},{10,9... | collective-permute-start | bytes 24584 | tf_op jit(solution)/shard_map/ppermute | solution.py:38
  177.1 23.9 %collective-permute-start.20 = (f32[1,128]{1,0:T(1,128)S(1)}, f32[1,128]{1,0:T(1,128)S(1)}, u32[]{:S(2)}, u32[]{:S(2)}) collective-permute-start(f32[1,128]{1,0:T(1,128)S(1)} %get-tuple-element.63), channel_id=1, source_target_pairs={{0,28},{4,0},{8,4},{12,8},{16,12},{20,16},{24,20},{28,24},{1,29},{... | collective-permute-start | bytes 1544 | tf_op jit(solution)/shard_map/ppermute | solution.py:38
  177.1 23.8 %collective-permute-start.21 = (f32[1,128]{1,0:T(1,128)S(1)}, f32[1,128]{1,0:T(1,128)S(1)}, u32[]{:S(2)}, u32[]{:S(2)}) collective-permute-start(f32[1,128]{1,0:T(1,128)S(1)} %get-tuple-element.64), channel_id=1, source_target_pairs={{0,4},{4,8},{8,12},{12,16},{16,20},{20,24},{24,28},{28,0},{1,5},{5... | collective-permute-start | bytes 1544 | tf_op jit(solution)/shard_map/ppermute | solution.py:38
  179.8 21.2 %collective-permute-start.22 = (f32[1,128]{1,0:T(1,128)S(1)}, f32[1,128]{1,0:T(1,128)S(1)}, u32[]{:S(2)}, u32[]{:S(2)}) collective-permute-start(f32[1,128]{1,0:T(1,128)S(1)} %get-tuple-element.65), channel_id=1, source_target_pairs={{0,3},{1,0},{2,1},{3,2},{4,7},{5,4},{6,5},{7,6},{8,11},{9,8},{10,9... | collective-permute-start | bytes 1544 | tf_op jit(solution)/shard_map/ppermute | solution.py:38
  181.6 19.4 %collective-permute-start.23 = (f32[1,128]{1,0:T(1,128)S(1)}, f32[1,128]{1,0:T(1,128)S(1)}, u32[]{:S(2)}, u32[]{:S(2)}) collective-permute-start(f32[1,128]{1,0:T(1,128)S(1)} %get-tuple-element.66), channel_id=1, source_target_pairs={{0,1},{1,2},{2,3},{3,0},{4,5},{5,6},{6,7},{7,4},{8,9},{9,10},{10,1... | collective-permute-start | bytes 1544 | tf_op jit(solution)/shard_map/ppermute | solution.py:38
  (23 other events, 396.3 us)

commit v2 on v1

--- a/solution.py
+++ b/solution.py
@@ -14,10 +14,12 @@
 EIG_HIGH = 2.0
 TILE = 8
 LANES = 128
+VMEM_ALL = 60 * 1024 * 1024
+BATCH = 8
 HIGHEST = lax.Precision.HIGHEST
 VMEM = pl.BlockSpec(memory_space=pltpu.VMEM)
 SMEM = pl.BlockSpec(memory_space=pltpu.SMEM)
-ANY = pl.BlockSpec(memory_space=pl.ANY)
+HBM = pl.BlockSpec(memory_space=pltpu.HBM)
 
 
 def cheby_coefficients(count_sweeps):
@@ -91,10 +93,6 @@
     return jnp.where(row_index(value.shape) == count - 1, row, pltpu.roll(value, count - 1, 0))
 
 
-def part_depths(depth):
-    return [(0, LANES), (LANES, depth - LANES)] if depth > LANES else [(0, depth)]
-
-
 class Copies:
     def __init__(self, sems):
         self.sems, self.count, self.waits = sems, 0, {}
@@ -125,83 +123,126 @@
     )
 
 
-def x_pack_kernel(cells_x, start, depth, noted, *refs):
-    temp, velo, diff = refs[:3]
-    notes = refs[3] if noted else None
-    outs, sems = refs[-3:-1], refs[-1]
+def near_kernel(cells_x, cells_y, depth, flags, wall, temp, velo, diff, xlow, xhigh, ylow, yhigh, wall_t, tiles, sems):
     copies = Copies(sems)
-    zs = pl.ds(start, depth)
-    for side in range(2):
-        for src, at, count in x_fields(temp, velo, diff, side, cells_x, zs):
-            copies.start(0, src, outs[side].at[pl.ds(at, count)])
-        if noted:
-            copies.start(0, notes.at[side], outs[side].at[8])
-    copies.wait_all()
-
-
-def x_pack(temp, velo, diff, notes, start, depth):
-    cells_x, cells_y, _ = temp.shape
-    noted = notes is not None
-    shape = jax.ShapeDtypeStruct((9 if noted else 8, cells_y, depth), temp.dtype)
-    return pl.pallas_call(
-        functools.partial(x_pack_kernel, cells_x, start, depth, noted),
-        out_shape=(shape, shape),
-        in_specs=[ANY] * (4 if noted else 3),
-        out_specs=(VMEM, VMEM),
-        scratch_shapes=[pltpu.SemaphoreType.DMA((12,))],
-        compiler_params=pltpu.CompilerParams(vmem_limit_bytes=32 * 1024 * 1024),
-        cost_estimate=lasts(2),
-    )(*((temp, velo, diff, notes) if noted else (temp, velo, diff)))
-
-
-def y_pack_kernel(cells_x, cells_y, start, depth, noted, *refs):
-    temp, velo, diff, xlo, xhi = refs[:5]
-    notes = refs[5] if noted else None
-    outs, (tiles, sems) = refs[-4:-2], refs[-2:]
-    copies = Copies(sems)
-    zs = pl.ds(start, depth)
-    sources = (temp.at[:], diff.at[:], velo.at[1], velo.at[0], velo.at[2])
+    count = depth // LANES
+    sources = (temp, diff, velo.at[1], velo.at[0], velo.at[2])
     for side in range(2):
         rows = pl.ds(0 if side == 0 else cells_y - TILE, TILE)
         for number, src in enumerate(sources):
-            copies.start((side, number), src.at[:, rows, zs], tiles.at[side, number])
-    base = 9 * cells_x if noted else 8 * cells_x
+            copies.start((side, number), src.at[:, rows, :], tiles.at[side, number])
+    for side, out in ((0, xlow), (1, xhigh)):
+        for tile in range(count):
+            for src, at, planes in x_fields(temp, velo, diff, side, cells_x, pl.ds(tile * LANES, LANES)):
+                copies.start("x", src, out.at[pl.ds(8 * tile + at, planes)])
+    same = ones_where(row_index((cells_x, LANES)) == lane_index((cells_x, LANES)))
+    turned = lax.dot_general(wall[...], same, (((0,), (0,)), ((), ())), precision=HIGHEST)
+    same = ones_where(row_index((cells_y, LANES)) == lane_index((cells_y, LANES)))
+    plain = jnp.dot(wall[...], same, precision=HIGHEST)
+    wall_t[...] = turned
+
+    def note(plane, place, at):
+        lane = lane_index(plane.shape)
+        live_two = jnp.where(place < flags[4], 2.0, 0.0)
+        return jnp.where(lane == 0, live_two, jnp.where(lane == 1, pltpu.roll(plane, (LANES + 1 - at) % LANES, 1), 0.0))
+
     for side in range(2):
-        out = outs[side]
+        x, y = side * (cells_x - 1), side * (cells_y - 1)
+        (xlow, xhigh)[side][8 * count] = note(turned, x * cells_y + row_index(turned.shape), x)
+        (ylow, yhigh)[side][8 * count] = note(plain, row_index(plain.shape) * cells_y + y, y)
+    for side, out in ((0, ylow), (1, yhigh)):
         first, near = (0, 0) if side == 0 else (TILE - 2, TILE - 1)
-        edge = 0 if side == 0 else cells_y - 1
-        for at, halo, inner in ((base, xlo, 1), (base + 4, xhi, 0)):
-            for j, plane in enumerate((inner, 2 + inner, 4 + inner, 6)):
-                out[pl.ds(at + j, 1), :] = halo[plane, pl.ds(edge, 1), :]
-        if noted:
-            out[pl.ds(8 * cells_x, cells_x), :] = notes[2 + side]
         for number in range(5):
             copies.wait((side, number))
-            if number < 3:
-                picks = [(2 * number, first), (2 * number + 1, first + 1)]
-            else:
-                picks = [(3 + number, near)]
+            picks = [(2 * number, first), (2 * number + 1, first + 1)] if number < 3 else [(3 + number, near)]
             for plane, row in picks:
                 for x in range(cells_x):
-                    out[pl.ds(plane * cells_x + x, 1), :] = tiles[side, number, x, pl.ds(row, 1), :]
-
-
-def y_pack(temp, velo, diff, xlo, xhi, notes, start, depth):
-    cells_x, cells_y, _ = temp.shape
-    noted = notes is not None
-    shape = jax.ShapeDtypeStruct(((9 if noted else 8) * cells_x + TILE, depth), temp.dtype)
+                    line = tiles[side, number, x, pl.ds(row, 1), :]
+                    for tile in range(count):
+                        out[8 * tile + plane, pl.ds(x, 1), :] = line[:, tile * LANES:(tile + 1) * LANES]
+    copies.wait_all()
+
+
+def near_step(flags, wall, temp, velo, diff):
+    cells_x, cells_y, depth = temp.shape
+    planes = 8 * (depth // LANES) + 1
+    x_strip = jax.ShapeDtypeStruct((planes, cells_y, LANES), temp.dtype)
+    y_strip = jax.ShapeDtypeStruct((planes, cells_x, LANES), temp.dtype)
     return pl.pallas_call(
-        functools.partial(y_pack_kernel, cells_x, cells_y, start, depth, noted),
-        out_shape=(shape, shape),
-        in_specs=[ANY] * 3 + [VMEM] * (3 if noted else 2),
-        out_specs=(VMEM, VMEM),
+        functools.partial(near_kernel, cells_x, cells_y, depth),
+        out_shape=(x_strip, x_strip, y_strip, y_strip, jax.ShapeDtypeStruct((cells_y, LANES), temp.dtype)),
+        in_specs=[SMEM, VMEM, HBM, HBM, HBM],
+        out_specs=(VMEM,) * 5,
         scratch_shapes=[
             pltpu.VMEM((2, 5, cells_x, TILE, depth), jnp.float32),
-            pltpu.SemaphoreType.DMA((10,)),
+            pltpu.SemaphoreType.DMA((10 + 10 * (depth // LANES),)),
         ],
-        compiler_params=pltpu.CompilerParams(vmem_limit_bytes=32 * 1024 * 1024),
-        cost_estimate=lasts(2),
-    )(temp, velo, diff, xlo, xhi, *((notes,) if noted else ()))
+        compiler_params=pltpu.CompilerParams(vmem_limit_bytes=VMEM_ALL),
+        cost_estimate=lasts(4),
+    )(flags, wall, temp, velo, diff)
+
+
+def corner_kernel(cells_x, count, ylo, yhi, low, high):
+    for out, x in ((low, 0), (high, cells_x - 1)):
+        for half, (strip, inner) in enumerate(((ylo, 1), (yhi, 0))):
+            for j, plane in enumerate((inner, 2 + inner, 6, 4 + inner)):
+                for tile in range(count):
+                    out[pl.ds(4 * half + j, 1), pl.ds(tile * LANES, LANES)] = strip[8 * tile + plane, pl.ds(x, 1), :]
+
+
+def solid_pack_kernel(cells_x, cells_y, pad, depth, *refs):
+    xlow, xhigh, ylow, yhigh, sems = refs[4:]
+    copies = Copies(sems)
+    for field, src in enumerate(refs[:4]):
+        for tile in range(depth // LANES):
+            number, zs = field * (depth // LANES) + tile, pl.ds(tile * LANES, LANES)
+            for side, out in ((0, xlow), (1, xhigh)):
+                here = pl.ds(side * (cells_x - pad), pad)
+                copies.start(0, src.at[here, :, zs], out.at[pl.ds(number * pad, pad)])
+            for side, out in ((0, ylow), (1, yhigh)):
+                here = pl.ds(side * (cells_y - TILE), TILE)
+                copies.start(0, src.at[:, here, zs], out.at[pl.ds(number * cells_x, cells_x)])
+    copies.wait_all()
+
+
+def solid_corner_kernel(cells_x, pad, numbers, ylo, yhi, low, high, sems):
+    copies = Copies(sems)
+    for out, x in ((low, 0), (high, cells_x - pad)):
+        for half, strip in enumerate((ylo, yhi)):
+            for number in range(numbers):
+                copies.start(0, strip.at[pl.ds(number * cells_x + x, pad)],
+                             out.at[pl.ds((half * numbers + number) * pad, pad)])
+    copies.wait_all()
+
+
+def packing(kernel, shapes, copies, micros, *args):
+    return pl.pallas_call(
+        kernel,
+        out_shape=tuple(jax.ShapeDtypeStruct(shape, jnp.float32) for shape in shapes),
+        in_specs=[HBM if copies else VMEM] * len(args),
+        out_specs=(VMEM,) * len(shapes),
+        scratch_shapes=[pltpu.SemaphoreType.DMA((copies,))] if copies else [],
+        compiler_params=pltpu.CompilerParams(vmem_limit_bytes=VMEM_ALL if copies else VMEM_ALL // 2),
+        cost_estimate=lasts(micros),
+    )(*args)
+
+
+def exchange(low, high, axis, move):
+    return move(high, axis, 1), move(low, axis, -1)
+
+
+def solid_strips(solids, pad):
+    cells_x, cells_y, depth = solids[0].shape
+    numbers = 4 * (depth // LANES)
+    x_shape, y_shape = (numbers * pad, cells_y, LANES), (numbers * cells_x, TILE, LANES)
+    return packing(functools.partial(solid_pack_kernel, cells_x, cells_y, pad, depth),
+                   (x_shape, x_shape, y_shape, y_shape), 4 * numbers, 3, *solids)
+
+
+def solid_corners(ylo, yhi, cells_x, numbers, pad):
+    shape = (2 * numbers * pad, TILE, LANES)
+    return packing(functools.partial(solid_corner_kernel, cells_x, pad, numbers), (shape, shape), 4 * numbers, 1,
+                   ylo, yhi)
 
 
 def face(a_low, a_high, u_low, u_high):
@@ -241,53 +282,49 @@
     return head if depth == LANES else jnp.concatenate([head, new[:, LANES:]], axis=1)
 
 
-def fluid_kernel(cells_x, cells_y, depth, parts, at_wall, flags, temp, velo, diff, wall_t, *refs):
-    halos, refs = refs[:4 * len(parts)], refs[4 * len(parts):]
-    out, (ts, us, as_, vs, ws, t1, yl, yc, xn, yn, cs, ks, sems) = refs[:-13], refs[-13:]
+def fluid_kernel(cells_x, cells_y, depth, flags, wall_t, xlo, xhi, ylo, yhi, clo, chi, temp, velo, diff,
+                 out, gas, ts, us, as_, vs, ws, t1, yl, cs, ks, sems):
     rows_total = flags[4]
-    xlo, xhi, ylo, yhi = (halos[i::4] for i in range(4))
     mid = pl.ds(TILE, cells_y)
+    tiles = [(tile, pl.ds(tile * LANES, LANES)) for tile in range(depth // LANES)]
     copies = Copies(sems)
-    for (start, size), *strips in zip(parts, xlo, xhi, ylo, yhi):
-        zs = pl.ds(start, size)
-        for side in range(2):
-            halo, key = strips[2 + side], "y"
-            noted = start == 0
-            for plane in range(8):
-                copies.start(key, halo.at[pl.ds(plane * cells_x, cells_x)],
-                             yl.at[side, plane, pl.ds(TILE, cells_x), zs])
-            copies.start(key, halo.at[pl.ds((9 if noted else 8) * cells_x, TILE)], yc.at[side, :, zs])
-            if noted:
-                copies.start(key, halo.at[pl.ds(8 * cells_x, cells_x), pl.ds(0, LANES)], yn.at[side])
-        for side in range(2):
-            halo, at = strips[side], 0 if side == 0 else cells_x + 2
-            near = 0 if side == 0 else cells_x + 1
-            key = "x"
-            copies.start(key, halo.at[pl.ds(0, 2)], ts.at[pl.ds(at, 2), mid, zs])
-            copies.start(key, halo.at[pl.ds(2, 2)], as_.at[pl.ds(at, 2), mid, zs])
-            copies.start(key, halo.at[pl.ds(4, 2)], us.at[pl.ds(at, 2), :, zs])
-            copies.start(key, halo.at[pl.ds(6, 1)], vs.at[pl.ds(near, 1), mid, zs])
-            copies.start(key, halo.at[pl.ds(7, 1)], ws.at[pl.ds(near, 1), :, zs])
-            if start == 0:
-                copies.start(key, halo.at[8, :, pl.ds(0, LANES)], xn.at[side])
-    zs = pl.ds(0, depth)
     step = TILE
     starts = list(range(0, cells_x, step))
-    for start in starts:
+
+    def load(start):
         here = pl.ds(start, step)
-        copies.start(start, temp.at[here, :, zs], ts.at[pl.ds(start + 2, step), mid])
-        copies.start(start, diff.at[here, :, zs], as_.at[pl.ds(start + 2, step), mid])
-        copies.start(start, velo.at[0, here, :, zs], us.at[pl.ds(start + 2, step)])
-        copies.start(start, velo.at[1, here, :, zs], vs.at[pl.ds(start + 1, step), mid])
-        copies.start(start, velo.at[2, here, :, zs], ws.at[pl.ds(start + 1, step)])
-
-    copies.wait("y")
-    copies.wait("x")
-    for side, row in ((0, TILE - 1), (1, TILE + cells_y)):
+        copies.start(start, temp.at[here], ts.at[pl.ds(start + 2, step), mid])
+        copies.start(start, diff.at[here], as_.at[pl.ds(start + 2, step), mid])
+        copies.start(start, velo.at[0, here], us.at[pl.ds(start + 2, step)])
+        copies.start(start, velo.at[1, here], vs.at[pl.ds(start + 1, step), mid])
+        copies.start(start, velo.at[2, here], ws.at[pl.ds(start + 1, step)])
+
+    for start in starts[:2]:
+        load(start)
+    for side, halo in enumerate((xlo, xhi)):
+        at, beside = (0, 0) if side == 0 else (cells_x + 2, cells_x + 1)
+        for tile, zs in tiles:
+            for j in range(2):
+                ts[at + j, mid, zs] = halo[8 * tile + j]
+                as_[at + j, mid, zs] = halo[8 * tile + 2 + j]
+                us[at + j, :, zs] = halo[8 * tile + 4 + j]
+            vs[beside, mid, zs] = halo[8 * tile + 6]
+            ws[beside, :, zs] = halo[8 * tile + 7]
+
+        @pl.when(flags[side] == 0)
+        def _():
+            for ref, first, count in ((ts, at, 2), (as_, at, 2), (us, at, 2), (vs, beside, 1), (ws, beside, 1)):
+                for j in range(count):
+                    ref[first + j] = jnp.zeros(ref.shape[1:], jnp.float32)
+
+    for side, (halo, row) in enumerate(((ylo, TILE - 1), (yhi, TILE + cells_y))):
         inner = 1 - side
-        for corner, at in ((0, TILE - 1), (4, TILE + cells_x)):
+        for plane in range(8):
+            for tile, zs in tiles:
+                yl[side, plane, pl.ds(TILE, cells_x), zs] = halo[8 * tile + plane]
+        for end, (corner, at) in enumerate(((clo, TILE - 1), (chi, TILE + cells_x))):
             for j, plane in enumerate((inner, 2 + inner, 6, 4 + inner)):
-                yl[side, plane, pl.ds(at, 1), :] = yc[side, pl.ds(corner + j, 1), :]
+                yl[side, plane, pl.ds(at, 1), :] = jnp.where(flags[end] > 0, corner[pl.ds(4 * side + j, 1), :], 0.0)
         for j in range(cells_x + 2):
             at = pl.ds(TILE - 1 + j, 1)
             ts[j + 1, pl.ds(row, 1), :] = yl[side, inner, at, :]
@@ -320,15 +357,17 @@
         return carry
 
     def halo_plane(i, side):
-        factors = plane_factors(i, *note_of(xn[side]))
+        factors = plane_factors(i, *note_of((xlo, xhi)[side][8 * len(tiles)]))
         t1[i, mid, :] = jnp.where(flags[side] > 0, plane_apply(factors, ts, i + 1), 0.0)
 
-    for start in starts:
+    for number, start in enumerate(starts):
         copies.wait(start)
+        if number + 2 < len(starts):
+            load(starts[number + 2])
         if start == 0:
             halo_plane(0, 0)
         last = cells_x + 1 if start == starts[-1] else start + step
-        lax.fori_loop(max(start, 1), last, first_sweep, 0, unroll=4 if at_wall else 1)
+        lax.fori_loop(max(start, 1), last, first_sweep, 0, unroll=2)
     halo_plane(cells_x + 1, 1)
 
     for side, row in ((0, TILE - 1), (1, TILE + cells_y)):
@@ -352,53 +391,62 @@
         factors = relaxation(
             a, yl[side, 6, rows, :], yl[side, 7, rows, :], low, high,
             (yl[side, 2 + inner, up, :], yl[side, 6, up, :]), (yl[side, 2 + inner, down, :], yl[side, 6, down, :]),
-            *note_of(yn[side]))
+            *note_of((ylo, yhi)[side][8 * len(tiles)]))
         new = apply(factors, t, t_low, t_high, yl[side, inner, up, :], yl[side, inner, down, :])
         new = jnp.where(flags[2 + side] > 0, new, 0.0)
         for x in range(cells_x):
             t1[1 + x, pl.ds(row, 1), :] = new[x:x + 1, :]
 
-    if at_wall:
-        gas, film = out
-        gas[...] = jnp.zeros_like(gas)
-        film[...] = jnp.zeros_like(film)
-
-        def second_wall(i, carry):
-            factors = [cs[j, i - 1] for j in range(7)] + [ks[i - 1]]
-            lane = lane_index((cells_y, LANES))
-            shift = i - 1
-            new = pltpu.roll(plane_apply(factors, t1, i)[:, :LANES], shift, 1)
-            wall_diff = pltpu.roll(as_[i + 1, mid, pl.ds(0, LANES)], shift, 1)
-            place = shift * cells_y + row_index((cells_y, LANES))
-            wall_film = jnp.where(place < rows_total, 2.0 * wall_diff, 0.0)
-            gas[...] = jnp.where(lane == shift, new, gas[...])
-            film[...] = jnp.where(lane == shift, wall_film, film[...])
-            return carry
-
-        lax.fori_loop(1, cells_x + 1, second_wall, 0, unroll=4)
-    else:
-        def second_sweep(i, carry):
-            factors = [cs[j, i - 1] for j in range(7)] + [ks[i - 1]]
-            ts[i - 1, mid, :] = plane_apply(factors, t1, i)
-            return carry
-
-        for start in starts:
-            lax.fori_loop(start + 1, start + step + 1, second_sweep, 0)
-            copies.start("out", ts.at[pl.ds(start, step), mid], out[0].at[pl.ds(start, step)])
-        copies.wait("out")
-
-
-def fluid_call(temp, velo, diff, wall_t, flags, halos, depth, parts, at_wall):
-    cells_x, cells_y, _ = temp.shape
+    def second_sweep(i, carry):
+        factors = [cs[j, i - 1] for j in range(7)] + [ks[i - 1]]
+        new = plane_apply(factors, t1, i)
+        ts[i - 1, mid, :] = new
+        shift = i - 1
+        return jnp.where(lane_index((cells_y, LANES)) == shift, pltpu.roll(new[:, :LANES], shift, 1), carry)
+
+    plane = jnp.zeros((cells_y, LANES), jnp.float32)
+    for start in starts:
+        plane = lax.fori_loop(start + 1, start + step + 1, second_sweep, plane, unroll=4)
+        copies.start("out", ts.at[pl.ds(start, step), mid], out.at[pl.ds(start, step)])
+    gas[...] = plane
+    copies.wait("out")
+
+
+def film_coefficients_kernel(cells_x, cells_y, flags, diff, out, tile, sem):
+    copy = pltpu.make_async_copy(diff.at[:, :, pl.ds(0, LANES)], tile, sem)
+    copy.start()
+    copy.wait()
+    shape = (cells_y, LANES)
+    total = jnp.zeros(shape, jnp.float32)
+    for x in range(cells_x):
+        total = jnp.where(lane_index(shape) == x, pltpu.roll(tile[x], x, 1), total)
+    place = lane_index(shape) * cells_y + row_index(shape)
+    out[...] = jnp.where(place < flags[4], 2.0 * total, 0.0)
+
+
+def film_coefficients(flags, diff):
+    cells_x, cells_y, _ = diff.shape
+    return pl.pallas_call(
+        functools.partial(film_coefficients_kernel, cells_x, cells_y),
+        out_shape=(jax.ShapeDtypeStruct((cells_y, LANES), diff.dtype),),
+        in_specs=[SMEM, HBM],
+        out_specs=(VMEM,),
+        scratch_shapes=[pltpu.VMEM((cells_x, cells_y, LANES), jnp.float32), pltpu.SemaphoreType.DMA],
+        compiler_params=pltpu.CompilerParams(vmem_limit_bytes=VMEM_ALL),
+        cost_estimate=lasts(1),
+    )(flags, diff)
+
+
+def fluid_call(flags, wall_t, strips, temp, velo, diff):
+    cells_x, cells_y, depth = temp.shape
     wide = cells_y + 2 * TILE
     chunks = cells_x // TILE
     plane = jax.ShapeDtypeStruct((cells_y, LANES), temp.dtype)
-    copy_count = len(parts) * 28 + 4 + 6 * chunks
     return pl.pallas_call(
-        functools.partial(fluid_kernel, cells_x, cells_y, depth, parts, at_wall),
-        out_shape=(plane, plane) if at_wall else jax.ShapeDtypeStruct(temp.shape, temp.dtype),
-        in_specs=[SMEM, ANY, ANY, ANY, VMEM] + [ANY] * len(halos),
-        out_specs=(VMEM, VMEM) if at_wall else ANY,
+        functools.partial(fluid_kernel, cells_x, cells_y, depth),
+        out_shape=(jax.ShapeDtypeStruct(temp.shape, temp.dtype), plane),
+        in_specs=[SMEM] + [VMEM] * 7 + [HBM] * 3,
+        out_specs=(HBM, VMEM),
         scratch_shapes=[
             pltpu.VMEM((cells_x + 4, wide, depth), jnp.float32),
             pltpu.VMEM((cells_x + 4, cells_y, depth), jnp.float32),
@@ -407,35 +455,39 @@
             pltpu.VMEM((cells_x + 2, cells_y, depth), jnp.float32),
             pltpu.VMEM((cells_x + 2, wide, depth), jnp.float32),
             pltpu.VMEM((2, 8, cells_x + 2 * TILE, depth), jnp.float32),
-            pltpu.VMEM((2, TILE, depth), jnp.float32),
-            pltpu.VMEM((2, cells_y, LANES), jnp.float32),
-            pltpu.VMEM((2, cells_x, LANES), jnp.float32),
             pltpu.VMEM((7, cells_x, cells_y, depth), jnp.float32),
             pltpu.VMEM((cells_x, cells_y, LANES), jnp.float32),
-            pltpu.SemaphoreType.DMA((copy_count,)),
+            pltpu.SemaphoreType.DMA((6 * chunks,)),
         ],
-        compiler_params=pltpu.CompilerParams(vmem_limit_bytes=52 * 1024 * 1024),
-        cost_estimate=lasts(6 if at_wall else 18),
-    )(flags, temp, velo, diff, wall_t, *halos)
+        compiler_params=pltpu.CompilerParams(vmem_limit_bytes=VMEM_ALL),
+        cost_estimate=lasts(13),
+    )(flags, wall_t, *strips, temp, velo, diff)
 
 
 def solid_kernel(
     cells_x, cells_y, depth, pad, coefficients,
-    flags, cond, sink, heat, temp, xlo, xhi, ylo, yhi, film, film_lo, film_hi,
+    flags, cond, sink, heat, temp, xlo, xhi, ylo, yhi, clo, chi, film, film_lo, film_hi,
     out, surface, ks, es, bs, us, vs, gx, gy, gz, ss, ps, fs, sems,
 ):
     wide_x, wide_y = cells_x + 2 * pad, cells_y + 2 * TILE
     copies = Copies(sems)
     own_x, own_y = pl.ds(pad, cells_x), pl.ds(TILE, cells_y)
     for field, (src, dst) in enumerate(((cond, ks), (sink, es), (heat, bs), (temp, us))):
-        for s, d in (
-            (src, dst.at[own_x, own_y]),
-            (xlo.at[field], dst.at[pl.ds(0, pad), own_y]),
-            (xhi.at[field], dst.at[pl.ds(pad + cells_x, pad), own_y]),
-            (ylo.at[field], dst.at[:, pl.ds(0, TILE)]),
-            (yhi.at[field], dst.at[:, pl.ds(TILE + cells_y, TILE)]),
-        ):
-            copies.start(field // 2, s, d)
+        copies.start(field // 2, src, dst.at[own_x, own_y])
+        for tile in range(depth // LANES):
+            zs, number = pl.ds(tile * LANES, LANES), field * (depth // LANES) + tile
+            key, numbers = field // 2, 4 * (depth // LANES)
+            x_from, y_from = pl.ds(number * pad, pad), pl.ds(number * cells_x, cells_x)
+            x_low, x_high = pl.ds(0, pad), pl.ds(pad + cells_x, pad)
+            y_low, y_high = pl.ds(0, TILE), pl.ds(TILE + cells_y, TILE)
+            copies.start(key, xlo.at[x_from], dst.at[x_low, own_y, zs])
+            copies.start(key, xhi.at[x_from], dst.at[x_high, own_y, zs])
+            copies.start(key, ylo.at[y_from], dst.at[own_x, y_low, zs])
+            copies.start(key, yhi.at[y_from], dst.at[own_x, y_high, zs])
+            for half, y_at in enumerate((y_low, y_high)):
+                c_from = pl.ds((half * numbers + number) * pad, pad)
+                copies.start(key, clo.at[c_from], dst.at[x_low, y_at, zs])
+                copies.start(key, chi.at[c_from], dst.at[x_high, y_at, zs])
     fs[:, pl.ds(0, TILE), :] = jnp.where(flags[2] > 0, film_lo[...], 0.0)
     fs[:, own_y, :] = film[...]
     fs[:, pl.ds(TILE + cells_y, TILE), :] = jnp.where(flags[3] > 0, film_hi[...], 0.0)
@@ -474,7 +526,13 @@
         return carry
 
     copies.wait(0)
-    lax.fori_loop(0, wide_x, conductances, 0, unroll=2)
+    for side in range(2):
+        @pl.when(flags[side] == 0)
+        def _():
+            for j in range(pad):
+                ks[side * (pad + cells_x) + j] = jnp.zeros((wide_y, depth), jnp.float32)
+
+    lax.fori_loop(0, wide_x, conductances, 0, unroll=4)
 
     def scale(x, carry):
         follow = jnp.minimum(x + 1, wide_x - 1)
@@ -487,7 +545,7 @@
         return carry
 
     copies.wait(1)
-    lax.fori_loop(0, wide_x, scale, 0, unroll=2)
+    lax.fori_loop(0, wide_x, scale, 0, unroll=4)
 
     total = len(coefficients)
     src, dst = us, vs
@@ -495,94 +553,56 @@
         last = number == total - 1
         margin = total - 1 - number
 
-        def one(x, carry, src=src, dst=dst, decay=decay, gain=gain, number=number, last=last):
-            here = src[x]
-            g_y, g_z = gy[x], gz[x]
-            total_in = gx[x] * src[x - 1] + gx[x + 1] * src[x + 1]
-            total_in += g_y * pltpu.roll(here, wide_y - 1, 0) + pltpu.roll(g_y * here, 1, 0)
-            total_in += g_z * pltpu.roll(here, depth - 1, 1) + pltpu.roll(g_z * here, 1, 1)
-            step = gain * ((bs[x] - here) + total_in)
-            if number > 0:
-                step = step + decay * ps[x]
-            fresh = here + step
-            if last:
-                final = (fresh * ss[x])[TILE:TILE + cells_y]
-                out[x - pad] = final
-                shift = x - pad
-                lane = lane_index((cells_y, LANES))
-                surface[...] = jnp.where(lane == shift, pltpu.roll(final[:, :LANES], shift, 1), surface[...])
-            else:
-                ps[x] = step
-                dst[x] = fresh
+        def some(block, carry, src=src, dst=dst, decay=decay, gain=gain, number=number, last=last, margin=margin):
+            planes = [pad - margin + block * BATCH + j for j in range(BATCH)]
+            here = [src[x] for x in planes]
+            before = [src[planes[0] - 1]] + here[:-1]
+            after = here[1:] + [src[planes[-1] + 1]]
+            g_x = [gx[planes[0]]] + [gx[x + 1] for x in planes]
+            results = []
+            for j, x in enumerate(planes):
+                g_y, g_z, value = gy[x], gz[x], here[j]
+                total_in = g_x[j] * before[j] + g_x[j + 1] * after[j]
+                total_in += g_y * pltpu.roll(value, wide_y - 1, 0) + pltpu.roll(g_y * value, 1, 0)
+                total_in += g_z * pltpu.roll(value, depth - 1, 1) + pltpu.roll(g_z * value, 1, 1)
+                step = gain * ((bs[x] - value) + total_in)
+                if number > 0:
+                    step = step + decay * ps[x]
+                results.append((step, value + step))
+            for j, x in enumerate(planes):
+                step, fresh = results[j]
+                if last:
+                    final = (fresh * ss[x])[TILE:TILE + cells_y]
+                    out[x - pad] = final
+                    shift = x - pad
+                    lane = lane_index((cells_y, LANES))
+                    surface[...] = jnp.where(lane == shift, pltpu.roll(final[:, :LANES], shift, 1), surface[...])
+                else:
+                    ps[x] = step
+                    dst[x] = fresh
             return carry
 
         if last:
             surface[...] = jnp.zeros_like(surface)
-        lax.fori_loop(pad - margin, pad + cells_x + margin, one, 0, unroll=2)
+        lax.fori_loop(0, -(-(cells_x + 2 * margin) // BATCH), some, 0)
         src, dst = dst, src
-
-
-def solid_x_kernel(cells_x, pad, *refs):
-    outs, sems = refs[4:6], refs[6]
-    copies = Copies(sems)
-    for field in range(4):
-        copies.start(0, refs[field].at[pl.ds(0, pad)], outs[0].at[field])
-        copies.start(0, refs[field].at[pl.ds(cells_x - pad, pad)], outs[1].at[field])
-    copies.wait_all()
-
-
-def solid_y_kernel(cells_x, cells_y, pad, *refs):
-    xlo, xhi = refs[4:6]
-    outs, sems = refs[6:8], refs[8]
-    copies = Copies(sems)
-    for field in range(4):
-        for side in range(2):
-            rows = pl.ds(0 if side == 0 else cells_y - TILE, TILE)
-            out = outs[side]
-            copies.start(0, refs[field].at[:, rows], out.at[field, pl.ds(pad, cells_x)])
-            copies.start(0, xlo.at[field, :, rows], out.at[field, pl.ds(0, pad)])
-            copies.start(0, xhi.at[field, :, rows], out.at[field, pl.ds(pad + cells_x, pad)])
-    copies.wait_all()
-
-
-def solid_halo(cond, sink, heat, temp, pad):
-    cells_x, cells_y, depth = cond.shape
-    fields = (cond, sink, heat, temp)
-    x_shape = jax.ShapeDtypeStruct((4, pad, cells_y, depth), cond.dtype)
-    low, high = pl.pallas_call(
-        functools.partial(solid_x_kernel, cells_x, pad),
-        out_shape=(x_shape, x_shape), in_specs=[ANY] * 4, out_specs=(VMEM, VMEM),
-        scratch_shapes=[pltpu.SemaphoreType.DMA((8,))],
-        compiler_params=pltpu.CompilerParams(vmem_limit_bytes=32 * 1024 * 1024),
-        cost_estimate=lasts(2),
-    )(*fields)
-    xlo, xhi = chain(high, "blk", 1), chain(low, "blk", -1)
-    y_shape = jax.ShapeDtypeStruct((4, cells_x + 2 * pad, TILE, depth), cond.dtype)
-    low, high = pl.pallas_call(
-        functools.partial(solid_y_kernel, cells_x, cells_y, pad),
-        out_shape=(y_shape, y_shape), in_specs=[ANY] * 6, out_specs=(VMEM, VMEM),
-        scratch_shapes=[pltpu.SemaphoreType.DMA((24,))],
-        compiler_params=pltpu.CompilerParams(vmem_limit_bytes=32 * 1024 * 1024),
-        cost_estimate=lasts(3),
-    )(*fields, xlo, xhi)
-    return xlo, xhi, chain(high, "sub", 1), chain(low, "sub", -1)
 
 
 def solid_step(flags, cond, sink, heat, temp, halo, films, pad):
     cells_x, cells_y, depth = cond.shape
     wide_x, wide_y = cells_x + 2 * pad, cells_y + 2 * TILE
-    area = pltpu.VMEM((wide_x, wide_y, depth), jnp.float32)
+    area = pltpu.VMEM((wide_x + BATCH, wide_y, depth), jnp.float32)
     return pl.pallas_call(
         functools.partial(solid_kernel, cells_x, cells_y, depth, pad, cheby_coefficients(SWEEPS)),
         out_shape=(jax.ShapeDtypeStruct((cells_x, cells_y, depth), cond.dtype),
                    jax.ShapeDtypeStruct((cells_y, LANES), cond.dtype)),
-        in_specs=[SMEM] + [ANY] * 8 + [VMEM] * 3,
+        in_specs=[SMEM] + [HBM] * 10 + [VMEM] * 3,
         out_specs=(VMEM, VMEM),
         scratch_shapes=[area] * 5
-        + [pltpu.VMEM((wide_x + 1, wide_y, depth), jnp.float32)]
+        + [area]
         + [area] * 4
-        + [pltpu.VMEM((2, wide_y, LANES), jnp.float32), pltpu.SemaphoreType.DMA((20,))],
-        compiler_params=pltpu.CompilerParams(vmem_limit_bytes=48 * 1024 * 1024),
+        + [pltpu.VMEM((2, wide_y, LANES), jnp.float32), pltpu.SemaphoreType.DMA((4 + 32 * (depth // LANES),))],
+        compiler_params=pltpu.CompilerParams(vmem_limit_bytes=VMEM_ALL),
         cost_estimate=lasts(30),
     )(flags, cond, sink, heat, temp, *halo, *films)
 
@@ -694,36 +714,38 @@
     near_rows = group_total // 8 * slot_cap
     pad = SWEEPS
     wall_plane = wall_prev.reshape(cells_x, cells_y)
-    live_two = jnp.where(jnp.arange(row_total, dtype=jnp.int32) < row_count[0], 2.0, 0.0).reshape(cells_x, cells_y)
     flags = jnp.concatenate([jnp.stack([*sides("blk"), *sides("sub")]).astype(jnp.int32), row_count])
-
-    both = jnp.stack([live_two, wall_plane])
-    edges = jnp.stack([both[:, 0], both[:, -1], both[:, :, 0], both[:, :, -1]])
-    notes = jnp.pad(edges.transpose(0, 2, 1), ((0, 0), (0, 0), (0, LANES - 2)))
-    wall_t = jnp.pad(wall_plane.T, ((0, 0), (0, LANES - cells_x)))
-
-    parts = part_depths(cells_z)
-    strips = []
-    for start, size in parts:
-        here = notes if start == 0 else None
-        low, high = x_pack(fluid_temp, velocity, eddy_diff, here, start, size)
-        xlo, xhi = chain(high, "blk", 1), chain(low, "blk", -1)
-        low, high = y_pack(fluid_temp, velocity, eddy_diff, xlo, xhi, here, start, size)
-        strips.append((xlo, xhi, chain(high, "sub", 1), chain(low, "sub", -1)))
-    fluid = (fluid_temp, velocity, eddy_diff, wall_t, flags)
-    gas_t, film_t = fluid_call(*fluid, strips[0], parts[0][1], parts[:1], True)
-    halo = solid_halo(conductivity, sink, heat_source, solid_temp, pad)
-    fluid_new = fluid_call(*fluid, sum(strips, ()), cells_z, parts, False)
-
+    fluid = (fluid_temp, velocity, eddy_diff)
+    solids = (conductivity, sink, heat_source, solid_temp)
+
+    xlow, xhigh, ylow, yhigh, wall_t = near_step(flags, wall_plane, *fluid)
+    xlo, xhi = exchange(xlow, xhigh, "blk", ring)
+    ylo, yhi = exchange(ylow, yhigh, "sub", chain)
+    after_near = lax.optimization_barrier((xlow, *solids, eddy_diff, owner_table))[1:]
+    strips = solid_strips(after_near[:4], pad)
+    (film_t,) = film_coefficients(flags, after_near[4])
     (route,) = small_call(
-        functools.partial(route_kernel, group_total, slot_cap), [(TILE, row_total)], None, owner_table
+        functools.partial(route_kernel, group_total, slot_cap), [(TILE, row_total)], None, after_near[5]
     )
+    xlo, xhi, ylo, yhi, film_t, route, *strips = lax.optimization_barrier((xlo, xhi, ylo, yhi, film_t, route, *strips))
+    corner = (TILE, cells_z)
+    low, high = packing(functools.partial(corner_kernel, cells_x, cells_z // LANES), (corner, corner), 0, 1, ylo, yhi)
+    clo, chi = exchange(low, high, "blk", ring)
+    clo, chi, *strips = lax.optimization_barrier((clo, chi, *strips))
+    xlow, xhigh, ylow, yhigh = strips
+    halo = [*exchange(xlow, xhigh, "blk", ring), *exchange(ylow, yhigh, "sub", chain)]
+    fluid_new, gas_t = fluid_call(flags, wall_t, (xlo, xhi, ylo, yhi, clo, chi), *fluid)
+    gas_t, *halo = lax.optimization_barrier((gas_t, *halo))
+    low, high = solid_corners(halo[2], halo[3], solid_x, 4 * (solid_z // LANES), pad)
+
     pair, *bands = small_call(
         functools.partial(rows_kernel, cells_x, cells_y, near_rows),
         [(2, row_total)] + [(2, near_rows)] * 4, None, route, gas_t, film_t,
     )
     moves = (("blk", 1), ("blk", -1), ("sub", 1), ("sub", -1))
     arrived = [ring(band, axis, step) for band, (axis, step) in zip(bands, moves)]
+    *arrived, low, high = lax.optimization_barrier((*arrived, low, high))
+    halo += exchange(low, high, "blk", ring)
     plane = (2, solid_y, LANES)
     film, low, high = small_call(
         functools.partial(film_kernel, solid_x, solid_y, pad), [plane] * 3, flags, route, landing_cell, pair, *arrived
@@ -733,7 +755,7 @@
         flags, film, ring(high, "blk", 1), ring(low, "blk", -1),
     )
     films = (film, ring(last, "sub", 1), ring(first, "sub", -1))
-    solid_new, surface_t = solid_step(flags, conductivity, sink, heat_source, solid_temp, halo, films, pad)
+    solid_new, surface_t = solid_step(flags, *solids, halo, films, pad)
 
     own, *backs = small_call(
         functools.partial(gather_kernel, solid_x, solid_y, row_total, near_rows),

time: 205 us -> 140 us (0.68)
  the two profiles are of different devices: /device:TPU:3 before, /device:TPU:0 now
where the time goes in v2:
time: 140 us; the launch traced here: 139 us
  Pallas kernels  64.7 us (46%)
  starting transfers between devices  39 us (28%)
  waiting for transfers between devices  29 us (21%)
  local copies, waits for them, and re-layouts  4.42 us (3%)
  between operations  1.61 us (1%)
    ppermute x20, starting transfers between devices, ring(): lax.ppermute(value, axis, [(i, (i + step) % count) for i in range(count)])  28.3 us
    pallas_call x1, Pallas kernels, solid_step(): pl.pallas_call(functools.partial(solid_kernel, cells_x, cells_y, depth, p...  25.4 us
    ppermute x20, waiting for transfers between devices, ring(): lax.ppermute(value, axis, [(i, (i + step) % count) for i in range(count)])  17.9 us
    pallas_call x1, Pallas kernels, fluid_call(): pl.pallas_call(functools.partial(fluid_kernel, cells_x, cells_y, depth),...  17.3 us
    ppermute x4, waiting for transfers between devices, chain(): return lax.ppermute(value, axis, pairs)  11.1 us
    ppermute x4, starting transfers between devices, chain(): return lax.ppermute(value, axis, pairs)  10.6 us
    pallas_call x6, Pallas kernels, small_call(): pl.pallas_call(kernel, out_shape=tuple((jax.ShapeDtypeStruct(shape, jnp.f...  7.37 us
    pallas_call x3, Pallas kernels, packing(): pl.pallas_call(kernel, out_shape=tuple((jax.ShapeDtypeStruct(shape, jnp.f...  7 us
  transfers between devices with their start and end apart: 24, of which 11 were waited for; matrix products, arithmetic and copies ran while one was open for 0% of the time, Pallas kernels for 21%

profile of v2, /device:TPU:0, one launch (start us, length us, event | category | flops | bytes accessed | tf_op | source)
XLA Modules:
  0.0 139.4 jit_solution(17902841544438499136)
XLA Ops:
  3.3 5.2 %shard_map.130 = (f32[33,32,128]{2,1,0:T(8,128)}, f32[33,32,128]{2,1,0:T(8,128)}, f32[33,32,128]{2,1,0:T(8,128)}, f32[33,32,128]{2,1,0:T(8,128)}, f32[32,128]{1,0:T(8,128)}) custom-call(s32[5]{0:T(128)} %pad_add_fusion.flags, f32[32,32]{1,0:T(8,128)} %reshape.12.wall, f32[32,32,512]{2,1,0:T(8,128)} %temp.4, f32[3,32,32,512]{3,2,1,0:T(8,128)} %velo.3, ...), custom_call_target="tpu_custom_call" | custom-call | bytes 14760000 | tf_op jit(solution)/shard_map/pallas_call | solution.py:171
  9.0 4.5 %collective-permute-start.2 = (f32[33,32,128]{2,1,0:T(8,128)}, f32[33,32,128]{2,1,0:T(8,128)S(1)}, u32[]{:S(2)}, u32[]{:S(2)}) collective-permute-start(f32[33,32,128]{2,1,0:T(8,128)} %get-tuple-element.72), channel_id=1, source_target_pairs={{0,1},{1,2},{2,3},{4,5},{5,6},{6,7},{8,9},{9,10},{10,11},{12,13},{... | collective-permute-start | bytes 1622024 | tf_op jit(solution)/shard_map/ppermute | solution.py:46
  14.9 2.4 %collective-permute-start.1 = (f32[33,32,128]{2,1,0:T(8,128)}, f32[33,32,128]{2,1,0:T(8,128)S(1)}, u32[]{:S(2)}, u32[]{:S(2)}) collective-permute-start(f32[33,32,128]{2,1,0:T(8,128)} %get-tuple-element.71), channel_id=1, source_target_pairs={{0,28},{4,0},{8,4},{12,8},{16,12},{20,16},{24,20},{28,24},{1,29},{... | collective-permute-start | bytes 1622024 | tf_op jit(solution)/shard_map/ppermute | solution.py:40
  17.3 2.5 %shard_map.131.film_t = f32[32,128]{1,0:T(8,128)} custom-call(s32[5]{0:T(128)} %pad_add_fusion.flags, f32[32,32,512]{2,1,0:T(8,128)} %diff.4), custom_call_target="tpu_custom_call" | custom-call | bytes 3690000 | tf_op jit(solution)/shard_map/pallas_call | solution.py:429
  20.2 4.6 %shard_map.133 = (f32[64,32,128]{2,1,0:T(8,128)}, f32[64,32,128]{2,1,0:T(8,128)}, f32[256,8,128]{2,1,0:T(8,128)}, f32[256,8,128]{2,1,0:T(8,128)}) custom-call(f32[32,32,256]{2,1,0:T(8,128)} %cond.1, f32[32,32,256]{2,1,0:T(8,128)} %sink.1, f32[32,32,256]{2,1,0:T(8,128)} %heat.1, f32[32,32,256]{2,1,0:T(8,128)} %temp.5), custom_call_target="tpu_custom_call" | custom-call | bytes 11070000 | tf_op jit(solution)/shard_map/pallas_call | solution.py:219
  25.9 4.5 %collective-permute-done.3.yhi = f32[33,32,128]{2,1,0:T(8,128)S(1)} collective-permute-done((f32[33,32,128]{2,1,0:T(8,128)}, f32[33,32,128]{2,1,0:T(8,128)S(1)}, u32[]{:S(2)}, u32[]{:S(2)}) %collective-permute-start.3) | collective-permute-done | bytes 540704 | tf_op jit(solution)/shard_map/ppermute | solution.py:46
  30.7 2.5 %collective-permute-start.5 = (f32[8,512]{1,0:T(8,128)S(1)}, f32[8,512]{1,0:T(8,128)S(1)}, u32[]{:S(2)}, u32[]{:S(2)}) collective-permute-start(f32[8,512]{1,0:T(8,128)S(1)} %get-tuple-element.89), channel_id=1, source_target_pairs={{0,28},{4,0},{8,4},{12,8},{16,12},{20,16},{24,20},{28,24},{1,29},{... | collective-permute-start | bytes 49160 | tf_op jit(solution)/shard_map/ppermute | solution.py:40
  35.4 2.0 %collective-permute-start.7 = (f32[64,32,128]{2,1,0:T(8,128)}, f32[64,32,128]{2,1,0:T(8,128)}, u32[]{:S(2)}, u32[]{:S(2)}) collective-permute-start(f32[64,32,128]{2,1,0:T(8,128)} %get-tuple-element.99), channel_id=1, source_target_pairs={{0,28},{4,0},{8,4},{12,8},{16,12},{20,16},{24,20},{28,24},{1,29},{... | collective-permute-start | bytes 3145736 | tf_op jit(solution)/shard_map/ppermute | solution.py:40
  37.3 3.5 %collective-permute-start.8 = (f32[256,8,128]{2,1,0:T(8,128)}, f32[256,8,128]{2,1,0:T(8,128)S(1)}, u32[]{:S(2)}, u32[]{:S(2)}) collective-permute-start(f32[256,8,128]{2,1,0:T(8,128)} %get-tuple-element.100), channel_id=1, source_target_pairs={{0,1},{1,2},{2,3},{4,5},{5,6},{6,7},{8,9},{9,10},{10,11},{12,13},{... | collective-permute-start | bytes 3145736 | tf_op jit(solution)/shard_map/ppermute | solution.py:46
  42.2 17.3 %shard_map.135 = (f32[32,32,512]{2,1,0:T(8,128)}, f32[32,128]{1,0:T(8,128)}) custom-call(s32[5]{0:T(128)} %pad_add_fusion.flags, f32[32,128]{1,0:T(8,128)} %get-tuple-element.69.wall_t, f32[33,32,128]{2,1,0:T(8,128)} %copy-done.12, f32[33,32,128]{2,1,0:T(8,128)} %copy-done.13, f32[33,32,128]{2,1,0:T(8,128)} %copy-done, f32[33,32,128]{2,1,0:T(8,128)} %copy-done.1, ...), custom_call_target="tpu_custom_call" | custom-call | bytes 47970000 | tf_op jit(solution)/shard_map/pallas_call | solution.py:445
  62.2 4.1 %collective-permute-done.9.yhi = f32[256,8,128]{2,1,0:T(8,128)S(1)} collective-permute-done((f32[256,8,128]{2,1,0:T(8,128)}, f32[256,8,128]{2,1,0:T(8,128)S(1)}, u32[]{:S(2)}, u32[]{:S(2)}) %collective-permute-start.9) | collective-permute-done | bytes 1048608 | tf_op jit(solution)/shard_map/ppermute | solution.py:46
  67.0 2.0 %shard_map.136 = (f32[2,1024]{1,0:T(2,128)S(1)}, f32[2,128]{1,0:T(2,128)S(1)}, f32[2,128]{1,0:T(2,128)S(1)}, f32[2,128]{1,0:T(2,128)S(1)}, f32[2,128]{1,0:T(2,128)S(1)}) custom-call(f32[8,1024]{1,0:T(8,128)S(1)} %shard_map.132.route, f32[32,128]{1,0:T(8,128)S(1)} %copy-done.8, f32[32,128]{1,0:T(8,128)S(1)} %copy-done.2), custom_call_target="tpu_custom_call" | custom-call | bytes 3690000 | tf_op jit(solution)/shard_map/pallas_call | solution.py:695
  69.0 2.7 %collective-permute-start.11 = (f32[2,128]{1,0:T(2,128)S(1)}, f32[2,128]{1,0:T(2,128)S(1)}, u32[]{:S(2)}, u32[]{:S(2)}) collective-permute-start(f32[2,128]{1,0:T(2,128)S(1)} %get-tuple-element.110), channel_id=1, source_target_pairs={{0,28},{4,0},{8,4},{12,8},{16,12},{20,16},{24,20},{28,24},{1,29},{... | collective-permute-start | bytes 3080 | tf_op jit(solution)/shard_map/ppermute | solution.py:40
  73.2 2.3 %collective-permute-start.13 = (f32[2,128]{1,0:T(2,128)S(1)}, f32[2,128]{1,0:T(2,128)S(1)}, u32[]{:S(2)}, u32[]{:S(2)}) collective-permute-start(f32[2,128]{1,0:T(2,128)S(1)} %get-tuple-element.112), channel_id=1, source_target_pairs={{0,3},{1,0},{2,1},{3,2},{4,7},{5,4},{6,5},{7,6},{8,11},{9,8},{10,9... | collective-permute-start | bytes 3080 | tf_op jit(solution)/shard_map/ppermute | solution.py:40
  75.5 2.4 %shard_map.137 = (f32[128,8,128]{2,1,0:T(8,128)}, f32[128,8,128]{2,1,0:T(8,128)}) custom-call(f32[256,8,128]{2,1,0:T(8,128)} %copy-done.10, f32[256,8,128]{2,1,0:T(8,128)} %copy-done.11), custom_call_target="tpu_custom_call" | custom-call | bytes 3690000 | tf_op jit(solution)/shard_map/pallas_call | solution.py:219
  78.0 2.6 %collective-permute-start.15 = (f32[128,8,128]{2,1,0:T(8,128)}, f32[128,8,128]{2,1,0:T(8,128)S(1)}, u32[]{:S(2)}, u32[]{:S(2)}) collective-permute-start(f32[128,8,128]{2,1,0:T(8,128)} %get-tuple-element.116), channel_id=1, source_target_pairs={{0,28},{4,0},{8,4},{12,8},{16,12},{20,16},{24,20},{28,24},{1,29},{... | collective-permute-start | bytes 1572872 | tf_op jit(solution)/shard_map/ppermute | solution.py:40
  80.7 1.6 %shard_map.138 = (f32[2,32,128]{2,1,0:T(8,128)S(1)}, f32[2,32,128]{2,1,0:T(8,128)S(1)}, f32[2,32,128]{2,1,0:T(8,128)S(1)}) custom-call(s32[5]{0:T(128)S(1)} %copy-done.4, f32[8,1024]{1,0:T(8,128)S(1)} %shard_map.132.route, s32[1,1536]{1,0:T(1,128)S(1)} %copy-done.6, f32[2,1024]{1,0:T(2,128)S(1)} %get-tuple-element.117.pair, ...), custom_call_target="tpu_custom_call" | custom-call | bytes 3690000 | tf_op jit(solution)/shard_map/pallas_call | solution.py:695
  82.4 2.6 %collective-permute-start.17 = (f32[2,32,128]{2,1,0:T(8,128)S(1)}, f32[2,32,128]{2,1,0:T(8,128)S(1)}, u32[]{:S(2)}, u32[]{:S(2)}) collective-permute-start(f32[2,32,128]{2,1,0:T(8,128)S(1)} %get-tuple-element.124), channel_id=1, source_target_pairs={{0,28},{4,0},{8,4},{12,8},{16,12},{20,16},{24,20},{28,24},{1,29},{... | collective-permute-start | bytes 98312 | tf_op jit(solution)/shard_map/ppermute | solution.py:40
  85.0 8.3 %collective-permute-done.16.low = f32[2,32,128]{2,1,0:T(8,128)S(1)} collective-permute-done((f32[2,32,128]{2,1,0:T(8,128)S(1)}, f32[2,32,128]{2,1,0:T(8,128)S(1)}, u32[]{:S(2)}, u32[]{:S(2)}) %collective-permute-start.16) | collective-permute-done | bytes 32800 | tf_op jit(solution)/shard_map/ppermute | solution.py:40
  94.4 3.8 %collective-permute-start.19 = (f32[2,8,128]{2,1,0:T(8,128)S(1)}, f32[2,8,128]{2,1,0:T(8,128)S(1)}, u32[]{:S(2)}, u32[]{:S(2)}) collective-permute-start(f32[2,8,128]{2,1,0:T(8,128)S(1)} %get-tuple-element.127), channel_id=1, source_target_pairs={{0,3},{1,0},{2,1},{3,2},{4,7},{5,4},{6,5},{7,6},{8,11},{9,8},{10,9... | collective-permute-start | bytes 24584 | tf_op jit(solution)/shard_map/ppermute | solution.py:40
  100.9 25.4 %shard_map.140 = (f32[32,32,256]{2,1,0:T(8,128)}, f32[32,128]{1,0:T(8,128)}) custom-call(s32[5]{0:T(128)} %pad_add_fusion.flags, f32[32,32,256]{2,1,0:T(8,128)} %cond.1, f32[32,32,256]{2,1,0:T(8,128)} %sink.1, f32[32,32,256]{2,1,0:T(8,128)} %heat.1, f32[32,32,256]{2,1,0:T(8,128)} %temp.5, f32[64,32,128]{2,1,0:T(8,128)} %collective-permute-done.6.xlo, ...), custom_call_target="tpu_custom_call" | custom-call | bytes 110700000 | tf_op jit(solution)/shard_map/pallas_call | solution.py:595
  127.9 3.8 %collective-permute-start.22 = (f32[1,128]{1,0:T(1,128)S(1)}, f32[1,128]{1,0:T(1,128)S(1)}, u32[]{:S(2)}, u32[]{:S(2)}) collective-permute-start(f32[1,128]{1,0:T(1,128)S(1)} %get-tuple-element.133), channel_id=1, source_target_pairs={{0,3},{1,0},{2,1},{3,2},{4,7},{5,4},{6,5},{7,6},{8,11},{9,8},{10,9... | collective-permute-start | bytes 1544 | tf_op jit(solution)/shard_map/ppermute | solution.py:40
  133.0 4.0 %collective-permute-done.23.from_3 = f32[1,128]{1,0:T(1,128)S(1)} collective-permute-done((f32[1,128]{1,0:T(1,128)S(1)}, f32[1,128]{1,0:T(1,128)S(1)}, u32[]{:S(2)}, u32[]{:S(2)}) %collective-permute-start.23) | collective-permute-done | bytes 544 | tf_op jit(solution)/shard_map/ppermute | solution.py:40
  137.0 2.4 %shard_map.142 = f32[1,1024]{1,0:T(1,128)} custom-call(s32[5]{0:T(128)S(1)} %copy-done.5, f32[8,1024]{1,0:T(8,128)S(1)} %shard_map.132.route, f32[1,1024]{1,0:T(1,128)S(1)} %get-tuple-element.130.own, f32[1,128]{1,0:T(1,128)S(1)} %collective-permute-done.20.from_0, f32[1,128]{1,0:T(1,128)S(1)} %collective-permute-done.21.from_1, ...), custom_call_target="tpu_custom_call" | custom-call | bytes 3690000 | tf_op jit(solution)/shard_map/pallas_call | solution.py:695
  (80 shorter events, 20.8 us)
Async XLA Ops:
  8.5 16.3 %collective-permute-start = (f32[33,32,128]{2,1,0:T(8,128)}, f32[33,32,128]{2,1,0:T(8,128)S(1)}, u32[]{:S(2)}, u32[]{:S(2)}) collective-permute-start(f32[33,32,128]{2,1,0:T(8,128)} %get-tuple-element.70), channel_id=1, source_target_pairs={{0,4},{4,8},{8,12},{12,16},{16,20},{20,24},{24,28},{28,0},{1,5},{5... | collective-permute-start | bytes 1622024 | tf_op jit(solution)/shard_map/ppermute | solution.py:40
  9.0 16.9 %collective-permute-start.2 = (f32[33,32,128]{2,1,0:T(8,128)}, f32[33,32,128]{2,1,0:T(8,128)S(1)}, u32[]{:S(2)}, u32[]{:S(2)}) collective-permute-start(f32[33,32,128]{2,1,0:T(8,128)} %get-tuple-element.72), channel_id=1, source_target_pairs={{0,1},{1,2},{2,3},{4,5},{5,6},{6,7},{8,9},{9,10},{10,11},{12,13},{... | collective-permute-start | bytes 1622024 | tf_op jit(solution)/shard_map/ppermute | solution.py:46
  13.6 16.9 %collective-permute-start.3 = (f32[33,32,128]{2,1,0:T(8,128)}, f32[33,32,128]{2,1,0:T(8,128)S(1)}, u32[]{:S(2)}, u32[]{:S(2)}) collective-permute-start(f32[33,32,128]{2,1,0:T(8,128)} %get-tuple-element.73), channel_id=1, source_target_pairs={{1,0},{2,1},{3,2},{5,4},{6,5},{7,6},{9,8},{10,9},{11,10},{13,12},{... | collective-permute-start | bytes 1622024 | tf_op jit(solution)/shard_map/ppermute | solution.py:46
  14.9 15.6 %collective-permute-start.1 = (f32[33,32,128]{2,1,0:T(8,128)}, f32[33,32,128]{2,1,0:T(8,128)S(1)}, u32[]{:S(2)}, u32[]{:S(2)}) collective-permute-start(f32[33,32,128]{2,1,0:T(8,128)} %get-tuple-element.71), channel_id=1, source_target_pairs={{0,28},{4,0},{8,4},{12,8},{16,12},{20,16},{24,20},{28,24},{1,29},{... | collective-permute-start | bytes 1622024 | tf_op jit(solution)/shard_map/ppermute | solution.py:40
  30.5 4.1 %collective-permute-start.4 = (f32[8,512]{1,0:T(8,128)S(1)}, f32[8,512]{1,0:T(8,128)S(1)}, u32[]{:S(2)}, u32[]{:S(2)}) collective-permute-start(f32[8,512]{1,0:T(8,128)S(1)} %get-tuple-element.88), channel_id=1, source_target_pairs={{0,4},{4,8},{8,12},{12,16},{16,20},{20,24},{24,28},{28,0},{1,5},{5... | collective-permute-start | bytes 49160 | tf_op jit(solution)/shard_map/ppermute | solution.py:40
  30.7 3.9 %collective-permute-start.5 = (f32[8,512]{1,0:T(8,128)S(1)}, f32[8,512]{1,0:T(8,128)S(1)}, u32[]{:S(2)}, u32[]{:S(2)}) collective-permute-start(f32[8,512]{1,0:T(8,128)S(1)} %get-tuple-element.89), channel_id=1, source_target_pairs={{0,28},{4,0},{8,4},{12,8},{16,12},{20,16},{24,20},{28,24},{1,29},{... | collective-permute-start | bytes 49160 | tf_op jit(solution)/shard_map/ppermute | solution.py:40
  34.7 26.1 %collective-permute-start.6 = (f32[64,32,128]{2,1,0:T(8,128)}, f32[64,32,128]{2,1,0:T(8,128)}, u32[]{:S(2)}, u32[]{:S(2)}) collective-permute-start(f32[64,32,128]{2,1,0:T(8,128)} %get-tuple-element.98), channel_id=1, source_target_pairs={{0,4},{4,8},{8,12},{12,16},{16,20},{20,24},{24,28},{28,0},{1,5},{5... | collective-permute-start | bytes 3145736 | tf_op jit(solution)/shard_map/ppermute | solution.py:40
  35.4 25.4 %collective-permute-start.7 = (f32[64,32,128]{2,1,0:T(8,128)}, f32[64,32,128]{2,1,0:T(8,128)}, u32[]{:S(2)}, u32[]{:S(2)}) collective-permute-start(f32[64,32,128]{2,1,0:T(8,128)} %get-tuple-element.99), channel_id=1, source_target_pairs={{0,28},{4,0},{8,4},{12,8},{16,12},{20,16},{24,20},{28,24},{1,29},{... | collective-permute-start | bytes 3145736 | tf_op jit(solution)/shard_map/ppermute | solution.py:40
  37.3 24.8 %collective-permute-start.8 = (f32[256,8,128]{2,1,0:T(8,128)}, f32[256,8,128]{2,1,0:T(8,128)S(1)}, u32[]{:S(2)}, u32[]{:S(2)}) collective-permute-start(f32[256,8,128]{2,1,0:T(8,128)} %get-tuple-element.100), channel_id=1, source_target_pairs={{0,1},{1,2},{2,3},{4,5},{5,6},{6,7},{8,9},{9,10},{10,11},{12,13},{... | collective-permute-start | bytes 3145736 | tf_op jit(solution)/shard_map/ppermute | solution.py:46
  40.9 25.4 %collective-permute-start.9 = (f32[256,8,128]{2,1,0:T(8,128)}, f32[256,8,128]{2,1,0:T(8,128)S(1)}, u32[]{:S(2)}, u32[]{:S(2)}) collective-permute-start(f32[256,8,128]{2,1,0:T(8,128)} %get-tuple-element.101), channel_id=1, source_target_pairs={{1,0},{2,1},{3,2},{5,4},{6,5},{7,6},{9,8},{10,9},{11,10},{13,12},{... | collective-permute-start | bytes 3145736 | tf_op jit(solution)/shard_map/ppermute | solution.py:46
  69.0 8.9 %collective-permute-start.10 = (f32[2,128]{1,0:T(2,128)S(1)}, f32[2,128]{1,0:T(2,128)S(1)}, u32[]{:S(2)}, u32[]{:S(2)}) collective-permute-start(f32[2,128]{1,0:T(2,128)S(1)} %get-tuple-element.109), channel_id=1, source_target_pairs={{0,4},{4,8},{8,12},{12,16},{16,20},{20,24},{24,28},{28,0},{1,5},{5... | collective-permute-start | bytes 3080 | tf_op jit(solution)/shard_map/ppermute | solution.py:40
  69.0 8.9 %collective-permute-start.11 = (f32[2,128]{1,0:T(2,128)S(1)}, f32[2,128]{1,0:T(2,128)S(1)}, u32[]{:S(2)}, u32[]{:S(2)}) collective-permute-start(f32[2,128]{1,0:T(2,128)S(1)} %get-tuple-element.110), channel_id=1, source_target_pairs={{0,28},{4,0},{8,4},{12,8},{16,12},{20,16},{24,20},{28,24},{1,29},{... | collective-permute-start | bytes 3080 | tf_op jit(solution)/shard_map/ppermute | solution.py:40
  71.7 6.3 %collective-permute-start.12 = (f32[2,128]{1,0:T(2,128)S(1)}, f32[2,128]{1,0:T(2,128)S(1)}, u32[]{:S(2)}, u32[]{:S(2)}) collective-permute-start(f32[2,128]{1,0:T(2,128)S(1)} %get-tuple-element.111), channel_id=1, source_target_pairs={{0,1},{1,2},{2,3},{3,0},{4,5},{5,6},{6,7},{7,4},{8,9},{9,10},{10,1... | collective-permute-start | bytes 3080 | tf_op jit(solution)/shard_map/ppermute | solution.py:40
  73.2 4.8 %collective-permute-start.13 = (f32[2,128]{1,0:T(2,128)S(1)}, f32[2,128]{1,0:T(2,128)S(1)}, u32[]{:S(2)}, u32[]{:S(2)}) collective-permute-start(f32[2,128]{1,0:T(2,128)S(1)} %get-tuple-element.112), channel_id=1, source_target_pairs={{0,3},{1,0},{2,1},{3,2},{4,7},{5,4},{6,5},{7,6},{8,11},{9,8},{10,9... | collective-permute-start | bytes 3080 | tf_op jit(solution)/shard_map/ppermute | solution.py:40
  78.0 21.9 %collective-permute-start.14 = (f32[128,8,128]{2,1,0:T(8,128)}, f32[128,8,128]{2,1,0:T(8,128)S(1)}, u32[]{:S(2)}, u32[]{:S(2)}) collective-permute-start(f32[128,8,128]{2,1,0:T(8,128)} %get-tuple-element.115), channel_id=1, source_target_pairs={{0,4},{4,8},{8,12},{12,16},{16,20},{20,24},{24,28},{28,0},{1,5},{5... | collective-permute-start | bytes 1572872 | tf_op jit(solution)/shard_map/ppermute | solution.py:40
  78.0 21.9 %collective-permute-start.15 = (f32[128,8,128]{2,1,0:T(8,128)}, f32[128,8,128]{2,1,0:T(8,128)S(1)}, u32[]{:S(2)}, u32[]{:S(2)}) collective-permute-start(f32[128,8,128]{2,1,0:T(8,128)} %get-tuple-element.116), channel_id=1, source_target_pairs={{0,28},{4,0},{8,4},{12,8},{16,12},{20,16},{24,20},{28,24},{1,29},{... | collective-permute-start | bytes 1572872 | tf_op jit(solution)/shard_map/ppermute | solution.py:40
  82.3 10.9 %collective-permute-start.16 = (f32[2,32,128]{2,1,0:T(8,128)S(1)}, f32[2,32,128]{2,1,0:T(8,128)S(1)}, u32[]{:S(2)}, u32[]{:S(2)}) collective-permute-start(f32[2,32,128]{2,1,0:T(8,128)S(1)} %get-tuple-element.123), channel_id=1, source_target_pairs={{0,4},{4,8},{8,12},{12,16},{16,20},{20,24},{24,28},{28,0},{1,5},{5... | collective-permute-start | bytes 98312 | tf_op jit(solution)/shard_map/ppermute | solution.py:40
  82.4 10.9 %collective-permute-start.17 = (f32[2,32,128]{2,1,0:T(8,128)S(1)}, f32[2,32,128]{2,1,0:T(8,128)S(1)}, u32[]{:S(2)}, u32[]{:S(2)}) collective-permute-start(f32[2,32,128]{2,1,0:T(8,128)S(1)} %get-tuple-element.124), channel_id=1, source_target_pairs={{0,28},{4,0},{8,4},{12,8},{16,12},{20,16},{24,20},{28,24},{1,29},{... | collective-permute-start | bytes 98312 | tf_op jit(solution)/shard_map/ppermute | solution.py:40
  94.4 5.4 %collective-permute-start.18 = (f32[2,8,128]{2,1,0:T(8,128)S(1)}, f32[2,8,128]{2,1,0:T(8,128)S(1)}, u32[]{:S(2)}, u32[]{:S(2)}) collective-permute-start(f32[2,8,128]{2,1,0:T(8,128)S(1)} %get-tuple-element.126), channel_id=1, source_target_pairs={{0,1},{1,2},{2,3},{3,0},{4,5},{5,6},{6,7},{7,4},{8,9},{9,10},{10,1... | collective-permute-start | bytes 24584 | tf_op jit(solution)/shard_map/ppermute | solution.py:40
  94.4 5.5 %collective-permute-start.19 = (f32[2,8,128]{2,1,0:T(8,128)S(1)}, f32[2,8,128]{2,1,0:T(8,128)S(1)}, u32[]{:S(2)}, u32[]{:S(2)}) collective-permute-start(f32[2,8,128]{2,1,0:T(8,128)S(1)} %get-tuple-element.127), channel_id=1, source_target_pairs={{0,3},{1,0},{2,1},{3,2},{4,7},{5,4},{6,5},{7,6},{8,11},{9,8},{10,9... | collective-permute-start | bytes 24584 | tf_op jit(solution)/shard_map/ppermute | solution.py:40
  127.3 4.4 %collective-permute-start.20 = (f32[1,128]{1,0:T(1,128)S(1)}, f32[1,128]{1,0:T(1,128)S(1)}, u32[]{:S(2)}, u32[]{:S(2)}) collective-permute-start(f32[1,128]{1,0:T(1,128)S(1)} %get-tuple-element.131), channel_id=1, source_target_pairs={{0,28},{4,0},{8,4},{12,8},{16,12},{20,16},{24,20},{28,24},{1,29},{... | collective-permute-start | bytes 1544 | tf_op jit(solution)/shard_map/ppermute | solution.py:40
  127.9 3.9 %collective-permute-start.21 = (f32[1,128]{1,0:T(1,128)S(1)}, f32[1,128]{1,0:T(1,128)S(1)}, u32[]{:S(2)}, u32[]{:S(2)}) collective-permute-start(f32[1,128]{1,0:T(1,128)S(1)} %get-tuple-element.132), channel_id=1, source_target_pairs={{0,4},{4,8},{8,12},{12,16},{16,20},{20,24},{24,28},{28,0},{1,5},{5... | collective-permute-start | bytes 1544 | tf_op jit(solution)/shard_map/ppermute | solution.py:40
  127.9 5.1 %collective-permute-start.22 = (f32[1,128]{1,0:T(1,128)S(1)}, f32[1,128]{1,0:T(1,128)S(1)}, u32[]{:S(2)}, u32[]{:S(2)}) collective-permute-start(f32[1,128]{1,0:T(1,128)S(1)} %get-tuple-element.133), channel_id=1, source_target_pairs={{0,3},{1,0},{2,1},{3,2},{4,7},{5,4},{6,5},{7,6},{8,11},{9,8},{10,9... | collective-permute-start | bytes 1544 | tf_op jit(solution)/shard_map/ppermute | solution.py:40
  131.7 5.3 %collective-permute-start.23 = (f32[1,128]{1,0:T(1,128)S(1)}, f32[1,128]{1,0:T(1,128)S(1)}, u32[]{:S(2)}, u32[]{:S(2)}) collective-permute-start(f32[1,128]{1,0:T(1,128)S(1)} %get-tuple-element.134), channel_id=1, source_target_pairs={{0,1},{1,2},{2,3},{3,0},{4,5},{5,6},{6,7},{7,4},{8,9},{9,10},{10,1... | collective-permute-start | bytes 1544 | tf_op jit(solution)/shard_map/ppermute | solution.py:40
  (20 other events, 206.4 us)

commit v3 on v2

--- a/solution.py
+++ b/solution.py
@@ -85,12 +85,15 @@
 
 
 def from_above(value, row):
-    return jnp.where(row_index(value.shape) == 0, row, pltpu.roll(value, 1, 0))
+    moved = pltpu.roll(value, 1, 0)
+    head = jnp.where(row_index((TILE, value.shape[1])) == 0, row, moved[:TILE])
+    return jnp.concatenate([head, moved[TILE:]], axis=0)
 
 
 def from_below(value, row):
-    count = value.shape[0]
-    return jnp.where(row_index(value.shape) == count - 1, row, pltpu.roll(value, count - 1, 0))
+    moved = pltpu.roll(value, value.shape[0] - 1, 0)
+    tail = jnp.where(row_index((TILE, value.shape[1])) == TILE - 1, row, moved[-TILE:])
+    return jnp.concatenate([moved[:-TILE], tail], axis=0)
 
 
 class Copies:
@@ -123,47 +126,46 @@
     )
 
 
-def near_kernel(cells_x, cells_y, depth, flags, wall, temp, velo, diff, xlow, xhigh, ylow, yhigh, wall_t, tiles, sems):
+def near_kernel(cells_x, cells_y, depth, count_ref, wall, temp, velo, diff, xlow, xhigh, ylow, yhigh, wall_t, sems):
     copies = Copies(sems)
     count = depth // LANES
-    sources = (temp, diff, velo.at[1], velo.at[0], velo.at[2])
-    for side in range(2):
-        rows = pl.ds(0 if side == 0 else cells_y - TILE, TILE)
-        for number, src in enumerate(sources):
-            copies.start((side, number), src.at[:, rows, :], tiles.at[side, number])
+    for side, out in ((0, ylow), (1, yhigh)):
+        first, near = (0, 0) if side == 0 else (cells_y - 2, cells_y - 1)
+        picks = ((temp, first), (temp, first + 1), (diff, first), (diff, first + 1), (velo.at[1], first),
+                 (velo.at[1], first + 1), (velo.at[0], near), (velo.at[2], near))
+        for tile in range(count):
+            for plane, (src, row) in enumerate(picks):
+                copies.start("y", src.at[:, row, pl.ds(tile * LANES, LANES)], out.at[8 * tile + plane])
     for side, out in ((0, xlow), (1, xhigh)):
         for tile in range(count):
             for src, at, planes in x_fields(temp, velo, diff, side, cells_x, pl.ds(tile * LANES, LANES)):
                 copies.start("x", src, out.at[pl.ds(8 * tile + at, planes)])
+    lines = wall[...]
+    group = LANES // cells_y
+    shape = (cells_x, lines.shape[0])
+    plain = jnp.zeros((cells_x, LANES), jnp.float32)
+    for j in range(group):
+        pick = ones_where(row_index(shape) == lane_index(shape) * group + j)
+        spread = jnp.dot(pick, lines, precision=HIGHEST)
+        plain = plain + (pltpu.roll(spread, LANES - j * cells_y, 1) if j else spread)
+    plain = jnp.where(lane_index(plain.shape) < cells_y, plain, 0.0)
     same = ones_where(row_index((cells_x, LANES)) == lane_index((cells_x, LANES)))
-    turned = lax.dot_general(wall[...], same, (((0,), (0,)), ((), ())), precision=HIGHEST)
-    same = ones_where(row_index((cells_y, LANES)) == lane_index((cells_y, LANES)))
-    plain = jnp.dot(wall[...], same, precision=HIGHEST)
+    turned = lax.dot_general(plain, same, (((0,), (0,)), ((), ())), precision=HIGHEST)[:cells_y]
     wall_t[...] = turned
 
     def note(plane, place, at):
         lane = lane_index(plane.shape)
-        live_two = jnp.where(place < flags[4], 2.0, 0.0)
+        live_two = jnp.where(place < count_ref[0], 2.0, 0.0)
         return jnp.where(lane == 0, live_two, jnp.where(lane == 1, pltpu.roll(plane, (LANES + 1 - at) % LANES, 1), 0.0))
 
     for side in range(2):
         x, y = side * (cells_x - 1), side * (cells_y - 1)
         (xlow, xhigh)[side][8 * count] = note(turned, x * cells_y + row_index(turned.shape), x)
         (ylow, yhigh)[side][8 * count] = note(plain, row_index(plain.shape) * cells_y + y, y)
-    for side, out in ((0, ylow), (1, yhigh)):
-        first, near = (0, 0) if side == 0 else (TILE - 2, TILE - 1)
-        for number in range(5):
-            copies.wait((side, number))
-            picks = [(2 * number, first), (2 * number + 1, first + 1)] if number < 3 else [(3 + number, near)]
-            for plane, row in picks:
-                for x in range(cells_x):
-                    line = tiles[side, number, x, pl.ds(row, 1), :]
-                    for tile in range(count):
-                        out[8 * tile + plane, pl.ds(x, 1), :] = line[:, tile * LANES:(tile + 1) * LANES]
     copies.wait_all()
 
 
-def near_step(flags, wall, temp, velo, diff):
+def near_step(row_count, wall, temp, velo, diff):
     cells_x, cells_y, depth = temp.shape
     planes = 8 * (depth // LANES) + 1
     x_strip = jax.ShapeDtypeStruct((planes, cells_y, LANES), temp.dtype)
@@ -173,21 +175,18 @@
         out_shape=(x_strip, x_strip, y_strip, y_strip, jax.ShapeDtypeStruct((cells_y, LANES), temp.dtype)),
         in_specs=[SMEM, VMEM, HBM, HBM, HBM],
         out_specs=(VMEM,) * 5,
-        scratch_shapes=[
-            pltpu.VMEM((2, 5, cells_x, TILE, depth), jnp.float32),
-            pltpu.SemaphoreType.DMA((10 + 10 * (depth // LANES),)),
-        ],
+        scratch_shapes=[pltpu.SemaphoreType.DMA((26 * (depth // LANES),))],
         compiler_params=pltpu.CompilerParams(vmem_limit_bytes=VMEM_ALL),
         cost_estimate=lasts(4),
-    )(flags, wall, temp, velo, diff)
-
-
-def corner_kernel(cells_x, count, ylo, yhi, low, high):
-    for out, x in ((low, 0), (high, cells_x - 1)):
-        for half, (strip, inner) in enumerate(((ylo, 1), (yhi, 0))):
-            for j, plane in enumerate((inner, 2 + inner, 6, 4 + inner)):
+    )(row_count, wall, temp, velo, diff)
+
+
+def corner_kernel(cells_y, count, xlo, xhi, low, high):
+    for out, y in ((low, 0), (high, cells_y - 1)):
+        for end, (strip, inner) in enumerate(((xlo, 1), (xhi, 0))):
+            for j, plane in enumerate((inner, 2 + inner, 4 + inner, 6)):
                 for tile in range(count):
-                    out[pl.ds(4 * half + j, 1), pl.ds(tile * LANES, LANES)] = strip[8 * tile + plane, pl.ds(x, 1), :]
+                    out[pl.ds(4 * end + j, 1), pl.ds(tile * LANES, LANES)] = strip[8 * tile + plane, pl.ds(y, 1), :]
 
 
 def solid_pack_kernel(cells_x, cells_y, pad, depth, *refs):
@@ -205,14 +204,26 @@
     copies.wait_all()
 
 
-def solid_corner_kernel(cells_x, pad, numbers, ylo, yhi, low, high, sems):
+def solid_corner_kernel(cells_y, numbers, xlo, xhi, low, high, tiles, sems):
     copies = Copies(sems)
-    for out, x in ((low, 0), (high, cells_x - pad)):
-        for half, strip in enumerate((ylo, yhi)):
+    for side in range(2):
+        rows = pl.ds(side * (cells_y - TILE), TILE)
+        for end, strip in enumerate((xlo, xhi)):
+            copies.start((side, end), strip.at[:, rows], tiles.at[side, end])
+    for side, out in enumerate((low, high)):
+        for end in range(2):
+            copies.wait((side, end))
             for number in range(numbers):
-                copies.start(0, strip.at[pl.ds(number * cells_x + x, pad)],
-                             out.at[pl.ds((half * numbers + number) * pad, pad)])
-    copies.wait_all()
+                for i in range(1, TILE // 2 + 1):
+                    near, far = (TILE - i, i) if end == 0 else (i - 1, TILE - 1 - i)
+                    tile = tiles[side, end, number * TILE + near]
+                    other = tiles[side, end, number * TILE + far]
+                    row = row_index(tile.shape)
+                    if side == 1:
+                        tile = jnp.where(row >= i, tile, pltpu.roll(other, i, 0))
+                    else:
+                        tile = jnp.where(row < TILE - i, tile, pltpu.roll(other, TILE - i, 0))
+                    out[(end * numbers + number) * (TILE // 2) + i - 1] = tile
 
 
 def packing(kernel, shapes, copies, micros, *args):
@@ -239,10 +250,18 @@
                    (x_shape, x_shape, y_shape, y_shape), 4 * numbers, 3, *solids)
 
 
-def solid_corners(ylo, yhi, cells_x, numbers, pad):
-    shape = (2 * numbers * pad, TILE, LANES)
-    return packing(functools.partial(solid_corner_kernel, cells_x, pad, numbers), (shape, shape), 4 * numbers, 1,
-                   ylo, yhi)
+def solid_corners(xlo, xhi, numbers):
+    cells_y = xlo.shape[1]
+    shape = jax.ShapeDtypeStruct((numbers * TILE, TILE, LANES), jnp.float32)
+    return pl.pallas_call(
+        functools.partial(solid_corner_kernel, cells_y, numbers),
+        out_shape=(shape, shape),
+        in_specs=[HBM, HBM],
+        out_specs=(VMEM, VMEM),
+        scratch_shapes=[pltpu.VMEM((2, 2, numbers * TILE, TILE, LANES), jnp.float32), pltpu.SemaphoreType.DMA((4,))],
+        compiler_params=pltpu.CompilerParams(vmem_limit_bytes=VMEM_ALL),
+        cost_estimate=lasts(2),
+    )(xlo, xhi)
 
 
 def face(a_low, a_high, u_low, u_high):
@@ -261,13 +280,16 @@
     a_first = 2.0 * a[:, :LANES]
     u_last = 2.0 * uz[:, -LANES:]
     plus_last = 2.0 * a[:, -LANES:] + jnp.maximum(u_last, 0.0)
-    weight = (low[0] + low[1]) + (high[0] + high[1]) + (p_above + q_above) + (p_below + q_below)
-    weight = weight + first_lane(p_down + q_down, 2.0 * a_first) + last_lane(p_up + q_up, 2.0 * plus_last - u_last)
-    factor = (2.0 * RELAX_FACTOR) * quick_reciprocal(weight)
     gain = a_first * live_two
     p_down, q_down = first_lane(p_down, 0.0), first_lane(q_down, gain)
     p_up, q_up = last_lane(p_up, plus_last), last_lane(q_up, 0.0)
     leaving = (low[1] + high[0]) + (q_above + p_below) + (q_down + p_up)
+    weight = leaving + ((low[0] + high[1]) + (p_above + q_below) + (p_down + q_up))
+    head = weight[:, :LANES] + jnp.where(lane_index(gain.shape) == 0, 2.0 * a_first - gain, 0.0)
+    weight = head if depth == LANES else jnp.concatenate([head, weight[:, LANES:]], axis=1)
+    tail = weight[:, -LANES:] + jnp.where(lane_index(gain.shape) == LANES - 1, plus_last - u_last, 0.0)
+    weight = tail if depth == LANES else jnp.concatenate([weight[:, :-LANES], tail], axis=1)
+    factor = (2.0 * RELAX_FACTOR) * quick_reciprocal(weight)
     ghost = jnp.where(lane_index(gain.shape) == 0, gain * wall * factor[:, :LANES], 0.0)
     return (low[0] * factor, high[1] * factor, p_above * factor, q_below * factor, p_down * factor, q_up * factor,
             1.0 - leaving * factor, ghost)
@@ -282,10 +304,9 @@
     return head if depth == LANES else jnp.concatenate([head, new[:, LANES:]], axis=1)
 
 
-def fluid_kernel(cells_x, cells_y, depth, flags, wall_t, xlo, xhi, ylo, yhi, clo, chi, temp, velo, diff,
-                 out, gas, ts, us, as_, vs, ws, t1, yl, cs, ks, sems):
+def fluid_kernel(cells_x, cells_y, depth, flags, wall_t, xlo, xhi, ylo, yhi, clo, chi, own_lo, own_hi,
+                 temp, velo, diff, out, gas, ts, us, as_, vs, ws, t1, yl, yt, cs, ks, sems):
     rows_total = flags[4]
-    mid = pl.ds(TILE, cells_y)
     tiles = [(tile, pl.ds(tile * LANES, LANES)) for tile in range(depth // LANES)]
     copies = Copies(sems)
     step = TILE
@@ -293,10 +314,10 @@
 
     def load(start):
         here = pl.ds(start, step)
-        copies.start(start, temp.at[here], ts.at[pl.ds(start + 2, step), mid])
-        copies.start(start, diff.at[here], as_.at[pl.ds(start + 2, step), mid])
+        copies.start(start, temp.at[here], ts.at[pl.ds(start + 2, step)])
+        copies.start(start, diff.at[here], as_.at[pl.ds(start + 2, step)])
         copies.start(start, velo.at[0, here], us.at[pl.ds(start + 2, step)])
-        copies.start(start, velo.at[1, here], vs.at[pl.ds(start + 1, step), mid])
+        copies.start(start, velo.at[1, here], vs.at[pl.ds(start + 1, step)])
         copies.start(start, velo.at[2, here], ws.at[pl.ds(start + 1, step)])
 
     for start in starts[:2]:
@@ -305,10 +326,10 @@
         at, beside = (0, 0) if side == 0 else (cells_x + 2, cells_x + 1)
         for tile, zs in tiles:
             for j in range(2):
-                ts[at + j, mid, zs] = halo[8 * tile + j]
-                as_[at + j, mid, zs] = halo[8 * tile + 2 + j]
+                ts[at + j, :, zs] = halo[8 * tile + j]
+                as_[at + j, :, zs] = halo[8 * tile + 2 + j]
                 us[at + j, :, zs] = halo[8 * tile + 4 + j]
-            vs[beside, mid, zs] = halo[8 * tile + 6]
+            vs[beside, :, zs] = halo[8 * tile + 6]
             ws[beside, :, zs] = halo[8 * tile + 7]
 
         @pl.when(flags[side] == 0)
@@ -317,71 +338,84 @@
                 for j in range(count):
                     ref[first + j] = jnp.zeros(ref.shape[1:], jnp.float32)
 
-    for side, (halo, row) in enumerate(((ylo, TILE - 1), (yhi, TILE + cells_y))):
+    for side, halo in enumerate((ylo, yhi)):
         inner = 1 - side
         for plane in range(8):
             for tile, zs in tiles:
                 yl[side, plane, pl.ds(TILE, cells_x), zs] = halo[8 * tile + plane]
-        for end, (corner, at) in enumerate(((clo, TILE - 1), (chi, TILE + cells_x))):
+        for end, at in enumerate((TILE - 1, TILE + cells_x)):
+            good = flags[end] * flags[2 + side] > 0
             for j, plane in enumerate((inner, 2 + inner, 6, 4 + inner)):
-                yl[side, plane, pl.ds(at, 1), :] = jnp.where(flags[end] > 0, corner[pl.ds(4 * side + j, 1), :], 0.0)
-        for j in range(cells_x + 2):
-            at = pl.ds(TILE - 1 + j, 1)
-            ts[j + 1, pl.ds(row, 1), :] = yl[side, inner, at, :]
-            as_[j + 1, pl.ds(row, 1), :] = yl[side, 2 + inner, at, :]
-            vs[j, pl.ds(row, 1), :] = yl[side, 4 + inner, at, :]
-
-    def plane_factors(i, live_two, wall):
-        a, un = as_[i + 1, mid, :], us[i + 1]
-        low = face(as_[i, mid, :], a, us[i], un)
-        high = face(a, as_[i + 2, mid, :], un, us[i + 2])
-        up, down = pl.ds(TILE - 1, 1), pl.ds(TILE + cells_y, 1)
-        return relaxation(a, vs[i, mid, :], ws[i], low, high, (as_[i + 1, up, :], vs[i, up, :]),
-                          (as_[i + 1, down, :], vs[i, down, :]), live_two, wall)
-
-    def plane_apply(factors, ref, i):
-        up, down = pl.ds(TILE - 1, 1), pl.ds(TILE + cells_y, 1)
-        return apply(factors, ref[i, mid, :], ref[i - 1, mid, :], ref[i + 1, mid, :], ref[i, up, :], ref[i, down, :])
+                yl[side, plane, pl.ds(at, 1), :] = jnp.where(good, (clo, chi)[side][pl.ds(4 * end + j, 1), :], 0.0)
+
+    def batch_factors(first, count, notes):
+        a = [as_[first + j] for j in range(count + 2)]
+        un = [us[first + j] for j in range(count + 2)]
+        faces = [face(a[j], a[j + 1], un[j], un[j + 1]) for j in range(count + 1)]
+        results = []
+        for j in range(count):
+            row = pl.ds(TILE - 1 + first + j, 1)
+            results.append(relaxation(
+                a[j + 1], vs[first + j], ws[first + j], faces[j], faces[j + 1], (yl[0, 3, row, :], yl[0, 5, row, :]),
+                (yl[1, 2, row, :], yl[1, 4, row, :]), *notes[j]))
+        return results
+
+    def batch_apply(factors, ref, offset, first, rows_above, rows_below):
+        t = [ref[first + offset - 1 + j] for j in range(len(factors) + 2)]
+        results = []
+        for j, plane in enumerate(factors):
+            row = pl.ds(TILE - 1 + first + j, 1)
+            results.append(apply(plane, t[j + 1], t[j], t[j + 2], rows_above[row, :], rows_below[row, :]))
+        return results
 
     def note_of(note):
         return note, pltpu.roll(note, LANES - 1, 1)
 
-    def first_sweep(i, carry):
+    def own_note(i):
         place = (i - 1) * cells_y + row_index((cells_y, LANES))
-        live_two = jnp.where(place < rows_total, 2.0, 0.0)
-        factors = plane_factors(i, live_two, pltpu.roll(wall_t[...], LANES + 1 - i, 1))
-        for j in range(7):
-            cs[j, i - 1] = factors[j]
-        ks[i - 1] = factors[7]
-        t1[i, mid, :] = plane_apply(factors, ts, i + 1)
-        return carry
+        return jnp.where(place < rows_total, 2.0, 0.0), pltpu.roll(wall_t[...], LANES + 1 - i, 1)
+
+    pair = 2
+
+    def first_sweep(block, first):
+        i = first + pair * block
+        factors = batch_factors(i, pair, [own_note(i + j) for j in range(pair)])
+        new = batch_apply(factors, ts, 1, i, yl.at[0, 1], yl.at[1, 0])
+        for j in range(pair):
+            for number in range(7):
+                cs[number, i + j - 1] = factors[j][number]
+            ks[i + j - 1] = factors[j][7]
+            t1[i + j] = new[j]
+        return first
 
     def halo_plane(i, side):
-        factors = plane_factors(i, *note_of((xlo, xhi)[side][8 * len(tiles)]))
-        t1[i, mid, :] = jnp.where(flags[side] > 0, plane_apply(factors, ts, i + 1), 0.0)
-
+        factors = batch_factors(i, 1, [note_of((xlo, xhi)[side][8 * len(tiles)])])
+        (new,) = batch_apply(factors, ts, 1, i, yl.at[0, 1], yl.at[1, 0])
+        t1[i] = jnp.where(flags[side] > 0, new, 0.0)
+
+    following = 1
     for number, start in enumerate(starts):
         copies.wait(start)
         if number + 2 < len(starts):
             load(starts[number + 2])
         if start == 0:
             halo_plane(0, 0)
-        last = cells_x + 1 if start == starts[-1] else start + step
-        lax.fori_loop(max(start, 1), last, first_sweep, 0, unroll=2)
+        last = cells_x + 1 if start == starts[-1] else start + step - 1
+        lax.fori_loop(0, (last - following) // pair, first_sweep, following)
+        following = last
     halo_plane(cells_x + 1, 1)
 
-    for side, row in ((0, TILE - 1), (1, TILE + cells_y)):
+    for side, own in enumerate((own_lo, own_hi)):
         inner = 1 - side
-        own = TILE if side == 0 else TILE + cells_y - 1
         rows, up, down = pl.ds(TILE, cells_x), pl.ds(TILE - 1, 1), pl.ds(TILE + cells_x, 1)
 
-        def own_rows(ref, off):
-            return jnp.concatenate([ref[off + x, pl.ds(own, 1), :] for x in range(cells_x)], axis=0)
+        def own_plane(plane):
+            return jnp.concatenate([own[8 * tile + plane] for tile, _ in tiles], axis=1)
 
         t, a, un = yl[side, inner, rows, :], yl[side, 2 + inner, rows, :], yl[side, 4 + inner, rows, :]
         t_far, a_far, un_far = (yl[side, 1 - inner, rows, :], yl[side, 3 - inner, rows, :],
                                 yl[side, 5 - inner, rows, :])
-        t_own, a_own, un_own = own_rows(ts, 2), own_rows(as_, 2), own_rows(vs, 1)
+        t_own, a_own, un_own = own_plane(side), own_plane(2 + side), own_plane(4 + side)
         if side == 0:
             low, high = face(a_far, a, un_far, un), face(a, a_own, un, un_own)
             t_low, t_high = t_far, t_own
@@ -393,21 +427,25 @@
             (yl[side, 2 + inner, up, :], yl[side, 6, up, :]), (yl[side, 2 + inner, down, :], yl[side, 6, down, :]),
             *note_of((ylo, yhi)[side][8 * len(tiles)]))
         new = apply(factors, t, t_low, t_high, yl[side, inner, up, :], yl[side, inner, down, :])
-        new = jnp.where(flags[2 + side] > 0, new, 0.0)
-        for x in range(cells_x):
-            t1[1 + x, pl.ds(row, 1), :] = new[x:x + 1, :]
-
-    def second_sweep(i, carry):
-        factors = [cs[j, i - 1] for j in range(7)] + [ks[i - 1]]
-        new = plane_apply(factors, t1, i)
-        ts[i - 1, mid, :] = new
-        shift = i - 1
-        return jnp.where(lane_index((cells_y, LANES)) == shift, pltpu.roll(new[:, :LANES], shift, 1), carry)
+        yt[side, rows, :] = jnp.where(flags[2 + side] > 0, new, 0.0)
+
+    group = 4
+
+    def second_sweep(block, carry):
+        first, plane = carry
+        i = first + group * block
+        factors = [[cs[number, i + j - 1] for number in range(7)] + [ks[i + j - 1]] for j in range(group)]
+        new = batch_apply(factors, t1, 0, i, yt.at[0], yt.at[1])
+        for j in range(group):
+            ts[i + j - 1] = new[j]
+            shift = i + j - 1
+            plane = jnp.where(lane_index((cells_y, LANES)) == shift, pltpu.roll(new[j][:, :LANES], shift, 1), plane)
+        return first, plane
 
     plane = jnp.zeros((cells_y, LANES), jnp.float32)
     for start in starts:
-        plane = lax.fori_loop(start + 1, start + step + 1, second_sweep, plane, unroll=4)
-        copies.start("out", ts.at[pl.ds(start, step), mid], out.at[pl.ds(start, step)])
+        _, plane = lax.fori_loop(0, step // group, second_sweep, (start + 1, plane))
+        copies.start("out", ts.at[pl.ds(start, step)], out.at[pl.ds(start, step)])
     gas[...] = plane
     copies.wait("out")
 
@@ -439,22 +477,26 @@
 
 def fluid_call(flags, wall_t, strips, temp, velo, diff):
     cells_x, cells_y, depth = temp.shape
-    wide = cells_y + 2 * TILE
     chunks = cells_x // TILE
     plane = jax.ShapeDtypeStruct((cells_y, LANES), temp.dtype)
+
+    def planes(count):
+        return pltpu.VMEM((count, cells_y, depth), jnp.float32)
+
     return pl.pallas_call(
         functools.partial(fluid_kernel, cells_x, cells_y, depth),
         out_shape=(jax.ShapeDtypeStruct(temp.shape, temp.dtype), plane),
-        in_specs=[SMEM] + [VMEM] * 7 + [HBM] * 3,
+        in_specs=[SMEM] + [VMEM] * 9 + [HBM] * 3,
         out_specs=(HBM, VMEM),
         scratch_shapes=[
-            pltpu.VMEM((cells_x + 4, wide, depth), jnp.float32),
-            pltpu.VMEM((cells_x + 4, cells_y, depth), jnp.float32),
-            pltpu.VMEM((cells_x + 4, wide, depth), jnp.float32),
-            pltpu.VMEM((cells_x + 2, wide, depth), jnp.float32),
-            pltpu.VMEM((cells_x + 2, cells_y, depth), jnp.float32),
-            pltpu.VMEM((cells_x + 2, wide, depth), jnp.float32),
+            planes(cells_x + 4),
+            planes(cells_x + 4),
+            planes(cells_x + 4),
+            planes(cells_x + 2),
+            planes(cells_x + 2),
+            planes(cells_x + 2),
             pltpu.VMEM((2, 8, cells_x + 2 * TILE, depth), jnp.float32),
+            pltpu.VMEM((2, cells_x + 2 * TILE, depth), jnp.float32),
             pltpu.VMEM((7, cells_x, cells_y, depth), jnp.float32),
             pltpu.VMEM((cells_x, cells_y, LANES), jnp.float32),
             pltpu.SemaphoreType.DMA((6 * chunks,)),
@@ -467,12 +509,14 @@
 def solid_kernel(
     cells_x, cells_y, depth, pad, coefficients,
     flags, cond, sink, heat, temp, xlo, xhi, ylo, yhi, clo, chi, film, film_lo, film_hi,
-    out, surface, ks, es, bs, us, vs, gx, gy, gz, ss, ps, fs, sems,
+    out, surface, ks, es, bs, us, vs, gx, gy, gz, ss, fs, sems,
 ):
     wide_x, wide_y = cells_x + 2 * pad, cells_y + 2 * TILE
     copies = Copies(sems)
     own_x, own_y = pl.ds(pad, cells_x), pl.ds(TILE, cells_y)
-    for field, (src, dst) in enumerate(((cond, ks), (sink, es), (heat, bs), (temp, us))):
+
+    def load(field):
+        src, dst = ((cond, ks), (sink, es), (heat, bs), (temp, us))[field]
         copies.start(field // 2, src, dst.at[own_x, own_y])
         for tile in range(depth // LANES):
             zs, number = pl.ds(tile * LANES, LANES), field * (depth // LANES) + tile
@@ -484,10 +528,16 @@
             copies.start(key, xhi.at[x_from], dst.at[x_high, own_y, zs])
             copies.start(key, ylo.at[y_from], dst.at[own_x, y_low, zs])
             copies.start(key, yhi.at[y_from], dst.at[own_x, y_high, zs])
-            for half, y_at in enumerate((y_low, y_high)):
-                c_from = pl.ds((half * numbers + number) * pad, pad)
-                copies.start(key, clo.at[c_from], dst.at[x_low, y_at, zs])
-                copies.start(key, chi.at[c_from], dst.at[x_high, y_at, zs])
+            for side, (strip, y_at) in enumerate(((clo, y_low), (chi, y_high))):
+                for end in range(2):
+                    for i in range(1, TILE + 1):
+                        shared = min(i, TILE - i) or 1
+                        tile = strip[(end * numbers + number) * (TILE // 2) + shared - 1]
+                        if i > TILE // 2:
+                            tile = pltpu.roll(tile, TILE - shared if side == 0 else shared, 0)
+                        dst[pad - i if end == 0 else pad + cells_x + i - 1, y_at, zs] = tile
+    load(0)
+    load(1)
     fs[:, pl.ds(0, TILE), :] = jnp.where(flags[2] > 0, film_lo[...], 0.0)
     fs[:, own_y, :] = film[...]
     fs[:, pl.ds(TILE + cells_y, TILE), :] = jnp.where(flags[3] > 0, film_hi[...], 0.0)
@@ -526,6 +576,8 @@
         return carry
 
     copies.wait(0)
+    load(2)
+    load(3)
     for side in range(2):
         @pl.when(flags[side] == 0)
         def _():
@@ -565,12 +617,12 @@
                 total_in = g_x[j] * before[j] + g_x[j + 1] * after[j]
                 total_in += g_y * pltpu.roll(value, wide_y - 1, 0) + pltpu.roll(g_y * value, 1, 0)
                 total_in += g_z * pltpu.roll(value, depth - 1, 1) + pltpu.roll(g_z * value, 1, 1)
-                step = gain * ((bs[x] - value) + total_in)
+                fresh = value + gain * ((bs[x] - value) + total_in)
                 if number > 0:
-                    step = step + decay * ps[x]
-                results.append((step, value + step))
+                    fresh = fresh + decay * (value - dst[x])
+                results.append(fresh)
             for j, x in enumerate(planes):
-                step, fresh = results[j]
+                fresh = results[j]
                 if last:
                     final = (fresh * ss[x])[TILE:TILE + cells_y]
                     out[x - pad] = final
@@ -578,7 +630,6 @@
                     lane = lane_index((cells_y, LANES))
                     surface[...] = jnp.where(lane == shift, pltpu.roll(final[:, :LANES], shift, 1), surface[...])
                 else:
-                    ps[x] = step
                     dst[x] = fresh
             return carry
 
@@ -596,12 +647,11 @@
         functools.partial(solid_kernel, cells_x, cells_y, depth, pad, cheby_coefficients(SWEEPS)),
         out_shape=(jax.ShapeDtypeStruct((cells_x, cells_y, depth), cond.dtype),
                    jax.ShapeDtypeStruct((cells_y, LANES), cond.dtype)),
-        in_specs=[SMEM] + [HBM] * 10 + [VMEM] * 3,
+        in_specs=[SMEM] + [HBM] * 8 + [VMEM] * 5,
         out_specs=(VMEM, VMEM),
         scratch_shapes=[area] * 5
-        + [area]
         + [area] * 4
-        + [pltpu.VMEM((2, wide_y, LANES), jnp.float32), pltpu.SemaphoreType.DMA((4 + 32 * (depth // LANES),))],
+        + [pltpu.VMEM((2, wide_y, LANES), jnp.float32), pltpu.SemaphoreType.DMA((4 + 16 * (depth // LANES),))],
         compiler_params=pltpu.CompilerParams(vmem_limit_bytes=VMEM_ALL),
         cost_estimate=lasts(30),
     )(flags, cond, sink, heat, temp, *halo, *films)
@@ -609,6 +659,23 @@
 
 def ones_where(condition):
     return jnp.where(condition, 1.0, 0.0)
+
+
+def pick_dot(values, picks, dims):
+    parts, rest = [], values
+    for _ in range(2):
+        scaled = rest * 65537.0
+        parts.append(scaled - (scaled - rest))
+        rest = rest - parts[-1]
+    parts.append(rest)
+    count = values.shape[0]
+    if count % TILE:
+        parts = [jnp.pad(part, ((0, TILE - count), (0, 0))) for part in parts]
+    total = lax.dot_general(jnp.concatenate(parts, axis=0), picks, (dims, ((), ())),
+                            precision=lax.Precision.DEFAULT, preferred_element_type=jnp.float32)
+    size = parts[0].shape[0]
+    total = total[:size] + (total[size:2 * size] + total[2 * size:])
+    return total[:count]
 
 
 def route_kernel(group_total, slot_cap, owner, out):
@@ -630,7 +697,7 @@
     count = cells.shape[1]
     in_x = ones_where(row_index((cells_x, count)) == cells // cells_y)
     in_y = ones_where(row_index((cells_y, count)) == cells % cells_y)
-    lines = jnp.dot(plane_t[:, :cells_x], in_x, precision=HIGHEST)
+    lines = pick_dot(plane_t[:, :cells_x], in_x, ((1,), (0,)))
     return jnp.sum(lines * in_y, axis=0, keepdims=True)
 
 
@@ -644,7 +711,7 @@
     for d in range(4):
         slots = route[d + 1:d + 2, :].astype(jnp.int32)
         pick = ones_where(row_index((near_rows, row_total)) == slots)
-        outs[d][...] = lax.dot_general(values, pick, (((1,), (1,)), ((), ())), precision=HIGHEST)
+        outs[d][...] = pick_dot(values, pick, ((1,), (1,)))
 
 
 def film_kernel(cells_x, cells_y, pad, flags, route, landing, pair, from_0, from_1, from_2, from_3, plane, low, high):
@@ -657,7 +724,7 @@
     in_x = ones_where(row_index((LANES, slots)) == cells // cells_y)
     in_y = ones_where(row_index((cells_y, slots)) == cells % cells_y)
     weighted = jnp.concatenate([in_y * film, in_y * (film * gas)], axis=0)
-    total = lax.dot_general(weighted, in_x, (((1,), (1,)), ((), ())), precision=HIGHEST)
+    total = pick_dot(weighted, in_x, ((1,), (1,)))
     lane = lane_index(total.shape)
     to_high = jnp.where(lane >= LANES - pad, pltpu.roll(total, LANES - cells_x, 1), 0.0)
     to_low = jnp.where((lane >= cells_x) & (lane < cells_x + pad), pltpu.roll(total, cells_x, 1), 0.0)
@@ -686,7 +753,7 @@
     for d, (piece, side) in enumerate(((from_0, 1), (from_1, 0), (from_2, 3), (from_3, 2))):
         slots = route[d + 1:d + 2, :].astype(jnp.int32)
         pick = ones_where(row_index((near_rows, row_total)) == slots)
-        total = total + jnp.dot(jnp.where(flags[side] > 0, piece[...], 0.0), pick, precision=HIGHEST)
+        total = total + pick_dot(jnp.where(flags[side] > 0, piece[...], 0.0), pick, ((1,), (0,)))
     out[...] = jnp.where(lane_index((1, row_total)) < flags[4], total, 0.0)
 
 
@@ -713,12 +780,11 @@
     slot_cap = row_total // group_total
     near_rows = group_total // 8 * slot_cap
     pad = SWEEPS
-    wall_plane = wall_prev.reshape(cells_x, cells_y)
     flags = jnp.concatenate([jnp.stack([*sides("blk"), *sides("sub")]).astype(jnp.int32), row_count])
     fluid = (fluid_temp, velocity, eddy_diff)
     solids = (conductivity, sink, heat_source, solid_temp)
 
-    xlow, xhigh, ylow, yhigh, wall_t = near_step(flags, wall_plane, *fluid)
+    xlow, xhigh, ylow, yhigh, wall_t = near_step(row_count, wall_prev.reshape(row_total // LANES, LANES), *fluid)
     xlo, xhi = exchange(xlow, xhigh, "blk", ring)
     ylo, yhi = exchange(ylow, yhigh, "sub", chain)
     after_near = lax.optimization_barrier((xlow, *solids, eddy_diff, owner_table))[1:]
@@ -727,25 +793,24 @@
     (route,) = small_call(
         functools.partial(route_kernel, group_total, slot_cap), [(TILE, row_total)], None, after_near[5]
     )
-    xlo, xhi, ylo, yhi, film_t, route, *strips = lax.optimization_barrier((xlo, xhi, ylo, yhi, film_t, route, *strips))
+    xlo, xhi, film_t, route, *strips = lax.optimization_barrier((xlo, xhi, film_t, route, *strips))
+    blk_halo = exchange(*strips[:2], "blk", ring)
     corner = (TILE, cells_z)
-    low, high = packing(functools.partial(corner_kernel, cells_x, cells_z // LANES), (corner, corner), 0, 1, ylo, yhi)
-    clo, chi = exchange(low, high, "blk", ring)
-    clo, chi, *strips = lax.optimization_barrier((clo, chi, *strips))
-    xlow, xhigh, ylow, yhigh = strips
-    halo = [*exchange(xlow, xhigh, "blk", ring), *exchange(ylow, yhigh, "sub", chain)]
-    fluid_new, gas_t = fluid_call(flags, wall_t, (xlo, xhi, ylo, yhi, clo, chi), *fluid)
-    gas_t, *halo = lax.optimization_barrier((gas_t, *halo))
-    low, high = solid_corners(halo[2], halo[3], solid_x, 4 * (solid_z // LANES), pad)
-
+    low, high = packing(functools.partial(corner_kernel, cells_y, cells_z // LANES), (corner, corner), 0, 1, xlo, xhi)
+    clo, chi = exchange(low, high, "sub", ring)
+    ylo, yhi, clo, chi, *sub_strips = lax.optimization_barrier((ylo, yhi, clo, chi, *strips[2:]))
+    sub_halo = exchange(*sub_strips, "sub", chain)
+    fluid_new, gas_t = fluid_call(flags, wall_t, (xlo, xhi, ylo, yhi, clo, chi, ylow, yhigh), *fluid)
     pair, *bands = small_call(
         functools.partial(rows_kernel, cells_x, cells_y, near_rows),
         [(2, row_total)] + [(2, near_rows)] * 4, None, route, gas_t, film_t,
     )
     moves = (("blk", 1), ("blk", -1), ("sub", 1), ("sub", -1))
+    *bands, blk_low, blk_high, sub_low, sub_high = lax.optimization_barrier((*bands, *blk_halo, *sub_halo))
     arrived = [ring(band, axis, step) for band, (axis, step) in zip(bands, moves)]
+    low, high = solid_corners(blk_low, blk_high, 4 * (solid_z // LANES))
     *arrived, low, high = lax.optimization_barrier((*arrived, low, high))
-    halo += exchange(low, high, "blk", ring)
+    halo = (blk_low, blk_high, sub_low, sub_high, *exchange(low, high, "sub", chain))
     plane = (2, solid_y, LANES)
     film, low, high = small_call(
         functools.partial(film_kernel, solid_x, solid_y, pad), [plane] * 3, flags, route, landing_cell, pair, *arrived

time: 140 us -> 126 us (0.900)
  waiting for transfers between devices: 29 us -> 14.2 us
  starting transfers between devices: 39 us -> 45 us
  Pallas kernels: 64.7 us -> 60.6 us
  local copies, waits for them, and re-layouts: 4.42 us -> 2.83 us
    ppermute x20 -> x18, waiting for transfers between devices: 17.9 us -> 9.07 us  [ring(): lax.ppermute(value, axis, [(i, (i + step) % count) for i in range(count)])]
    ppermute x4 -> x6, waiting for transfers between devices: 11.1 us -> 5.18 us  [chain(): return lax.ppermute(value, axis, pairs)]
    ppermute x20 -> x18, starting transfers between devices: 28.3 us -> 31.6 us  [ring(): lax.ppermute(value, axis, [(i, (i + step) % count) for i in range(count)])]
    pallas_call x6, Pallas kernels: 7.37 us -> 4.25 us  [small_call(): pl.pallas_call(kernel, out_shape=tuple((jax.ShapeDtypeStruct(shape, jnp.f...]
    ppermute x4 -> x6, starting transfers between devices: 10.6 us -> 13.4 us  [chain(): return lax.ppermute(value, axis, pairs)]
    pallas_call x3 -> x2, Pallas kernels: 7 us -> 4.58 us  [packing(): pl.pallas_call(kernel, out_shape=tuple((jax.ShapeDtypeStruct(shape, jnp.f...]
    pallas_call x0 -> x1, Pallas kernels: none -> 2.04 us  [solid_corners(): pl.pallas_call(functools.partial(solid_corner_kernel, cells_y, numbers),...]
    unnamed x40 -> x36, local copies, waits for them, and re-layouts: 3.06 us -> 2.83 us
  transfers between devices with their start and end apart: 24 -> 24, of which waited for: 11 -> 8; matrix products, arithmetic and copies ran while one was open for 0% -> 1% of each run, Pallas kernels for 21% -> 23%
where the time goes in v3:
time: 126 us; the launch traced here: 125 us
  Pallas kernels  60.6 us (48%)
  starting transfers between devices  45 us (36%)
  waiting for transfers between devices  14.2 us (11%)
  local copies, waits for them, and re-layouts  2.83 us (2%)
  between operations  1.66 us (1%)
    ppermute x18, starting transfers between devices, ring(): lax.ppermute(value, axis, [(i, (i + step) % count) for i in range(count)])  31.6 us
    pallas_call x1, Pallas kernels, solid_step(): pl.pallas_call(functools.partial(solid_kernel, cells_x, cells_y, depth, p...  25.7 us
    pallas_call x1, Pallas kernels, fluid_call(): pl.pallas_call(functools.partial(fluid_kernel, cells_x, cells_y, depth),...  16.8 us
    ppermute x6, starting transfers between devices, chain(): return lax.ppermute(value, axis, pairs)  13.4 us
    ppermute x18, waiting for transfers between devices, ring(): lax.ppermute(value, axis, [(i, (i + step) % count) for i in range(count)])  9.07 us
    ppermute x6, waiting for transfers between devices, chain(): return lax.ppermute(value, axis, pairs)  5.18 us
    pallas_call x1, Pallas kernels, near_step(): pl.pallas_call(functools.partial(near_kernel, cells_x, cells_y, depth), o...  4.78 us
    pallas_call x2, Pallas kernels, packing(): pl.pallas_call(kernel, out_shape=tuple((jax.ShapeDtypeStruct(shape, jnp.f...  4.58 us
  transfers between devices with their start and end apart: 24, of which 8 were waited for; matrix products, arithmetic and copies ran while one was open for 1% of the time, Pallas kernels for 23%

profile of v3, /device:TPU:0, one launch (start us, length us, event | category | flops | bytes accessed | tf_op | source)
XLA Modules:
  0.0 125.1 jit_solution(17100804189964194067)
XLA Ops:
  1.3 4.8 %shard_map.130 = (f32[33,32,128]{2,1,0:T(8,128)}, f32[33,32,128]{2,1,0:T(8,128)}, f32[33,32,128]{2,1,0:T(8,128)}, f32[33,32,128]{2,1,0:T(8,128)}, f32[32,128]{1,0:T(8,128)}) custom-call(s32[1]{0:T(128)S(6)} %copy.14.count_ref, f32[8,128]{1,0:T(8,128)} %bitcast.6, f32[32,32,512]{2,1,0:T(8,128)} %temp.4, f32[3,32,32,512]{3,2,1,0:T(8,128)} %velo.3, ...), custom_call_target="tpu_custom_call" | custom-call | bytes 14760000 | tf_op jit(solution)/shard_map/pallas_call | solution.py:173
  6.6 2.9 %collective-permute-start.1 = (f32[33,32,128]{2,1,0:T(8,128)}, f32[33,32,128]{2,1,0:T(8,128)S(1)}, u32[]{:S(2)}, u32[]{:S(2)}) collective-permute-start(f32[33,32,128]{2,1,0:T(8,128)} %get-tuple-element.72), channel_id=1, source_target_pairs={{0,28},{4,0},{8,4},{12,8},{16,12},{20,16},{24,20},{28,24},{1,29},{... | collective-permute-start | bytes 1622024 | tf_op jit(solution)/shard_map/ppermute | solution.py:40
  9.5 5.0 %collective-permute-start.2 = (f32[33,32,128]{2,1,0:T(8,128)}, f32[33,32,128]{2,1,0:T(8,128)}, u32[]{:S(2)}, u32[]{:S(2)}) collective-permute-start(f32[33,32,128]{2,1,0:T(8,128)} %get-tuple-element.85.own_hi), channel_id=1, source_target_pairs={{0,1},{1,2},{2,3},{4,5},{5,6},{6,7},{8,9},{9,10},{10,11},{12,13},{... | collective-permute-start | bytes 1622024 | tf_op jit(solution)/shard_map/ppermute | solution.py:46
  16.9 2.5 %shard_map.131.film_t = f32[32,128]{1,0:T(8,128)} custom-call(s32[5]{0:T(128)} %pad_add_fusion.flags, f32[32,32,512]{2,1,0:T(8,128)} %diff.4), custom_call_target="tpu_custom_call" | custom-call | bytes 3690000 | tf_op jit(solution)/shard_map/pallas_call | solution.py:467
  19.5 4.6 %shard_map.133 = (f32[64,32,128]{2,1,0:T(8,128)}, f32[64,32,128]{2,1,0:T(8,128)}, f32[256,8,128]{2,1,0:T(8,128)}, f32[256,8,128]{2,1,0:T(8,128)}) custom-call(f32[32,32,256]{2,1,0:T(8,128)} %cond.1, f32[32,32,256]{2,1,0:T(8,128)} %sink.1, f32[32,32,256]{2,1,0:T(8,128)} %heat.1, f32[32,32,256]{2,1,0:T(8,128)} %temp.5), custom_call_target="tpu_custom_call" | custom-call | bytes 11070000 | tf_op jit(solution)/shard_map/pallas_call | solution.py:230
  24.1 2.7 %collective-permute-start.4 = (f32[8,512]{1,0:T(8,128)S(1)}, f32[8,512]{1,0:T(8,128)S(1)}, u32[]{:S(2)}, u32[]{:S(2)}) collective-permute-start(f32[8,512]{1,0:T(8,128)S(1)} %get-tuple-element.87), channel_id=1, source_target_pairs={{0,1},{1,2},{2,3},{3,0},{4,5},{5,6},{6,7},{7,4},{8,9},{9,10},{10,1... | collective-permute-start | bytes 49160 | tf_op jit(solution)/shard_map/ppermute | solution.py:40
  26.8 2.1 %collective-permute-start.5 = (f32[8,512]{1,0:T(8,128)S(1)}, f32[8,512]{1,0:T(8,128)S(1)}, u32[]{:S(2)}, u32[]{:S(2)}) collective-permute-start(f32[8,512]{1,0:T(8,128)S(1)} %get-tuple-element.88), channel_id=1, source_target_pairs={{0,3},{1,0},{2,1},{3,2},{4,7},{5,4},{6,5},{7,6},{8,11},{9,8},{10,9... | collective-permute-start | bytes 49160 | tf_op jit(solution)/shard_map/ppermute | solution.py:40
  28.9 2.6 %collective-permute-start.7 = (f32[64,32,128]{2,1,0:T(8,128)}, f32[64,32,128]{2,1,0:T(8,128)S(1)}, u32[]{:S(2)}, u32[]{:S(2)}) collective-permute-start(f32[64,32,128]{2,1,0:T(8,128)} %get-tuple-element.104), channel_id=1, source_target_pairs={{0,28},{4,0},{8,4},{12,8},{16,12},{20,16},{24,20},{28,24},{1,29},{... | collective-permute-start | bytes 3145736 | tf_op jit(solution)/shard_map/ppermute | solution.py:40
  31.6 3.0 %collective-permute-start.8 = (f32[256,8,128]{2,1,0:T(8,128)}, f32[256,8,128]{2,1,0:T(8,128)}, u32[]{:S(2)}, u32[]{:S(2)}) collective-permute-start(f32[256,8,128]{2,1,0:T(8,128)} %get-tuple-element.105), channel_id=1, source_target_pairs={{0,1},{1,2},{2,3},{4,5},{5,6},{6,7},{8,9},{9,10},{10,11},{12,13},{... | collective-permute-start | bytes 3145736 | tf_op jit(solution)/shard_map/ppermute | solution.py:46
  35.9 16.8 %shard_map.135 = (f32[32,32,512]{2,1,0:T(8,128)}, f32[32,128]{1,0:T(8,128)}) custom-call(s32[5]{0:T(128)} %pad_add_fusion.flags, f32[32,128]{1,0:T(8,128)} %get-tuple-element.70.wall_t, f32[33,32,128]{2,1,0:T(8,128)} %copy-done, f32[33,32,128]{2,1,0:T(8,128)} %copy-done.1, f32[33,32,128]{2,1,0:T(8,128)} %collective-permute-done.2.ylo, ...), custom_call_target="tpu_custom_call" | custom-call | bytes 47970000 | tf_op jit(solution)/shard_map/pallas_call | solution.py:486
  54.6 5.1 %collective-permute-done.9.yhi = f32[256,8,128]{2,1,0:T(8,128)} collective-permute-done((f32[256,8,128]{2,1,0:T(8,128)}, f32[256,8,128]{2,1,0:T(8,128)}, u32[]{:S(2)}, u32[]{:S(2)}) %collective-permute-start.9) | collective-permute-done | bytes 1048608 | tf_op jit(solution)/shard_map/ppermute | solution.py:46
  59.7 2.6 %collective-permute-start.11 = (f32[2,128]{1,0:T(2,128)S(1)}, f32[2,128]{1,0:T(2,128)S(1)}, u32[]{:S(2)}, u32[]{:S(2)}) collective-permute-start(f32[2,128]{1,0:T(2,128)S(1)} %get-tuple-element.112), channel_id=1, source_target_pairs={{0,28},{4,0},{8,4},{12,8},{16,12},{20,16},{24,20},{28,24},{1,29},{... | collective-permute-start | bytes 3080 | tf_op jit(solution)/shard_map/ppermute | solution.py:40
  62.9 3.3 %collective-permute-start.13 = (f32[2,128]{1,0:T(2,128)S(1)}, f32[2,128]{1,0:T(2,128)S(1)}, u32[]{:S(2)}, u32[]{:S(2)}) collective-permute-start(f32[2,128]{1,0:T(2,128)S(1)} %get-tuple-element.114), channel_id=1, source_target_pairs={{0,3},{1,0},{2,1},{3,2},{4,7},{5,4},{6,5},{7,6},{8,11},{9,8},{10,9... | collective-permute-start | bytes 3080 | tf_op jit(solution)/shard_map/ppermute | solution.py:40
  66.2 2.0 %shard_map.137 = (f32[64,8,128]{2,1,0:T(8,128)}, f32[64,8,128]{2,1,0:T(8,128)}) custom-call(f32[64,32,128]{2,1,0:T(8,128)} %copy-done.10, f32[64,32,128]{2,1,0:T(8,128)} %copy-done.11), custom_call_target="tpu_custom_call" | custom-call | bytes 7380000 | tf_op jit(solution)/shard_map/pallas_call | solution.py:256
  68.3 1.6 %collective-permute-start.14 = (f32[64,8,128]{2,1,0:T(8,128)}, f32[64,8,128]{2,1,0:T(8,128)S(1)}, u32[]{:S(2)}, u32[]{:S(2)}) collective-permute-start(f32[64,8,128]{2,1,0:T(8,128)} %get-tuple-element.117), channel_id=1, source_target_pairs={{0,1},{1,2},{2,3},{4,5},{5,6},{6,7},{8,9},{9,10},{10,11},{12,13},{... | collective-permute-start | bytes 786440 | tf_op jit(solution)/shard_map/ppermute | solution.py:46
  72.2 2.6 %collective-permute-start.17 = (f32[2,32,128]{2,1,0:T(8,128)S(1)}, f32[2,32,128]{2,1,0:T(8,128)S(1)}, u32[]{:S(2)}, u32[]{:S(2)}) collective-permute-start(f32[2,32,128]{2,1,0:T(8,128)S(1)} %get-tuple-element.126), channel_id=1, source_target_pairs={{0,28},{4,0},{8,4},{12,8},{16,12},{20,16},{24,20},{28,24},{1,29},{... | collective-permute-start | bytes 98312 | tf_op jit(solution)/shard_map/ppermute | solution.py:40
  74.8 1.6 %collective-permute-done.16.low = f32[2,32,128]{2,1,0:T(8,128)S(1)} collective-permute-done((f32[2,32,128]{2,1,0:T(8,128)S(1)}, f32[2,32,128]{2,1,0:T(8,128)S(1)}, u32[]{:S(2)}, u32[]{:S(2)}) %collective-permute-start.16) | collective-permute-done | bytes 32800 | tf_op jit(solution)/shard_map/ppermute | solution.py:40
  77.6 2.6 %collective-permute-start.18 = (f32[2,8,128]{2,1,0:T(8,128)S(1)}, f32[2,8,128]{2,1,0:T(8,128)S(1)}, u32[]{:S(2)}, u32[]{:S(2)}) collective-permute-start(f32[2,8,128]{2,1,0:T(8,128)S(1)} %get-tuple-element.128), channel_id=1, source_target_pairs={{0,1},{1,2},{2,3},{3,0},{4,5},{5,6},{6,7},{7,4},{8,9},{9,10},{10,1... | collective-permute-start | bytes 24584 | tf_op jit(solution)/shard_map/ppermute | solution.py:40
  80.2 3.6 %collective-permute-start.19 = (f32[2,8,128]{2,1,0:T(8,128)S(1)}, f32[2,8,128]{2,1,0:T(8,128)S(1)}, u32[]{:S(2)}, u32[]{:S(2)}) collective-permute-start(f32[2,8,128]{2,1,0:T(8,128)S(1)} %get-tuple-element.129), channel_id=1, source_target_pairs={{0,3},{1,0},{2,1},{3,2},{4,7},{5,4},{6,5},{7,6},{8,11},{9,8},{10,9... | collective-permute-start | bytes 24584 | tf_op jit(solution)/shard_map/ppermute | solution.py:40
  83.8 1.6 %collective-permute-done.18.film_lo = f32[2,8,128]{2,1,0:T(8,128)S(1)} collective-permute-done((f32[2,8,128]{2,1,0:T(8,128)S(1)}, f32[2,8,128]{2,1,0:T(8,128)S(1)}, u32[]{:S(2)}, u32[]{:S(2)}) %collective-permute-start.18) | collective-permute-done | bytes 8224 | tf_op jit(solution)/shard_map/ppermute | solution.py:40
  86.3 25.7 %shard_map.140 = (f32[32,32,256]{2,1,0:T(8,128)}, f32[32,128]{1,0:T(8,128)}) custom-call(s32[5]{0:T(128)} %pad_add_fusion.flags, f32[32,32,256]{2,1,0:T(8,128)} %cond.1, f32[32,32,256]{2,1,0:T(8,128)} %sink.1, f32[32,32,256]{2,1,0:T(8,128)} %heat.1, f32[32,32,256]{2,1,0:T(8,128)} %temp.5, f32[64,32,128]{2,1,0:T(8,128)} %copy-done.10, ...), custom_call_target="tpu_custom_call" | custom-call | bytes 110700000 | tf_op jit(solution)/shard_map/pallas_call | solution.py:646
  112.9 1.9 %collective-permute-start.20 = (f32[1,128]{1,0:T(1,128)S(1)}, f32[1,128]{1,0:T(1,128)S(1)}, u32[]{:S(2)}, u32[]{:S(2)}) collective-permute-start(f32[1,128]{1,0:T(1,128)S(1)} %get-tuple-element.133), channel_id=1, source_target_pairs={{0,28},{4,0},{8,4},{12,8},{16,12},{20,16},{24,20},{28,24},{1,29},{... | collective-permute-start | bytes 1544 | tf_op jit(solution)/shard_map/ppermute | solution.py:40
  114.8 3.4 %collective-permute-start.22 = (f32[1,128]{1,0:T(1,128)S(1)}, f32[1,128]{1,0:T(1,128)S(1)}, u32[]{:S(2)}, u32[]{:S(2)}) collective-permute-start(f32[1,128]{1,0:T(1,128)S(1)} %get-tuple-element.135), channel_id=1, source_target_pairs={{0,3},{1,0},{2,1},{3,2},{4,7},{5,4},{6,5},{7,6},{8,11},{9,8},{10,9... | collective-permute-start | bytes 1544 | tf_op jit(solution)/shard_map/ppermute | solution.py:40
  119.6 4.0 %collective-permute-done.23.from_3 = f32[1,128]{1,0:T(1,128)S(1)} collective-permute-done((f32[1,128]{1,0:T(1,128)S(1)}, f32[1,128]{1,0:T(1,128)S(1)}, u32[]{:S(2)}, u32[]{:S(2)}) %collective-permute-start.23) | collective-permute-done | bytes 544 | tf_op jit(solution)/shard_map/ppermute | solution.py:40
  (75 shorter events, 14.6 us)
Async XLA Ops:
  6.1 18.0 %collective-permute-start = (f32[33,32,128]{2,1,0:T(8,128)}, f32[33,32,128]{2,1,0:T(8,128)S(1)}, u32[]{:S(2)}, u32[]{:S(2)}) collective-permute-start(f32[33,32,128]{2,1,0:T(8,128)} %get-tuple-element.71), channel_id=1, source_target_pairs={{0,4},{4,8},{8,12},{12,16},{16,20},{20,24},{24,28},{28,0},{1,5},{5... | collective-permute-start | bytes 1622024 | tf_op jit(solution)/shard_map/ppermute | solution.py:40
  6.6 17.5 %collective-permute-start.1 = (f32[33,32,128]{2,1,0:T(8,128)}, f32[33,32,128]{2,1,0:T(8,128)S(1)}, u32[]{:S(2)}, u32[]{:S(2)}) collective-permute-start(f32[33,32,128]{2,1,0:T(8,128)} %get-tuple-element.72), channel_id=1, source_target_pairs={{0,28},{4,0},{8,4},{12,8},{16,12},{20,16},{24,20},{28,24},{1,29},{... | collective-permute-start | bytes 1622024 | tf_op jit(solution)/shard_map/ppermute | solution.py:40
  9.5 19.4 %collective-permute-start.2 = (f32[33,32,128]{2,1,0:T(8,128)}, f32[33,32,128]{2,1,0:T(8,128)}, u32[]{:S(2)}, u32[]{:S(2)}) collective-permute-start(f32[33,32,128]{2,1,0:T(8,128)} %get-tuple-element.85.own_hi), channel_id=1, source_target_pairs={{0,1},{1,2},{2,3},{4,5},{5,6},{6,7},{8,9},{9,10},{10,11},{12,13},{... | collective-permute-start | bytes 1622024 | tf_op jit(solution)/shard_map/ppermute | solution.py:46
  14.5 17.0 %collective-permute-start.3 = (f32[33,32,128]{2,1,0:T(8,128)}, f32[33,32,128]{2,1,0:T(8,128)}, u32[]{:S(2)}, u32[]{:S(2)}) collective-permute-start(f32[33,32,128]{2,1,0:T(8,128)} %get-tuple-element.86.own_lo), channel_id=1, source_target_pairs={{1,0},{2,1},{3,2},{5,4},{6,5},{7,6},{9,8},{10,9},{11,10},{13,12},{... | collective-permute-start | bytes 1622024 | tf_op jit(solution)/shard_map/ppermute | solution.py:46
  24.1 7.4 %collective-permute-start.4 = (f32[8,512]{1,0:T(8,128)S(1)}, f32[8,512]{1,0:T(8,128)S(1)}, u32[]{:S(2)}, u32[]{:S(2)}) collective-permute-start(f32[8,512]{1,0:T(8,128)S(1)} %get-tuple-element.87), channel_id=1, source_target_pairs={{0,1},{1,2},{2,3},{3,0},{4,5},{5,6},{6,7},{7,4},{8,9},{9,10},{10,1... | collective-permute-start | bytes 49160 | tf_op jit(solution)/shard_map/ppermute | solution.py:40
  26.8 4.7 %collective-permute-start.5 = (f32[8,512]{1,0:T(8,128)S(1)}, f32[8,512]{1,0:T(8,128)S(1)}, u32[]{:S(2)}, u32[]{:S(2)}) collective-permute-start(f32[8,512]{1,0:T(8,128)S(1)} %get-tuple-element.88), channel_id=1, source_target_pairs={{0,3},{1,0},{2,1},{3,2},{4,7},{5,4},{6,5},{7,6},{8,11},{9,8},{10,9... | collective-permute-start | bytes 49160 | tf_op jit(solution)/shard_map/ppermute | solution.py:40
  28.9 25.6 %collective-permute-start.6 = (f32[64,32,128]{2,1,0:T(8,128)}, f32[64,32,128]{2,1,0:T(8,128)S(1)}, u32[]{:S(2)}, u32[]{:S(2)}) collective-permute-start(f32[64,32,128]{2,1,0:T(8,128)} %get-tuple-element.103), channel_id=1, source_target_pairs={{0,4},{4,8},{8,12},{12,16},{16,20},{20,24},{24,28},{28,0},{1,5},{5... | collective-permute-start | bytes 3145736 | tf_op jit(solution)/shard_map/ppermute | solution.py:40
  28.9 25.6 %collective-permute-start.7 = (f32[64,32,128]{2,1,0:T(8,128)}, f32[64,32,128]{2,1,0:T(8,128)S(1)}, u32[]{:S(2)}, u32[]{:S(2)}) collective-permute-start(f32[64,32,128]{2,1,0:T(8,128)} %get-tuple-element.104), channel_id=1, source_target_pairs={{0,28},{4,0},{8,4},{12,8},{16,12},{20,16},{24,20},{28,24},{1,29},{... | collective-permute-start | bytes 3145736 | tf_op jit(solution)/shard_map/ppermute | solution.py:40
  31.6 23.0 %collective-permute-start.8 = (f32[256,8,128]{2,1,0:T(8,128)}, f32[256,8,128]{2,1,0:T(8,128)}, u32[]{:S(2)}, u32[]{:S(2)}) collective-permute-start(f32[256,8,128]{2,1,0:T(8,128)} %get-tuple-element.105), channel_id=1, source_target_pairs={{0,1},{1,2},{2,3},{4,5},{5,6},{6,7},{8,9},{9,10},{10,11},{12,13},{... | collective-permute-start | bytes 3145736 | tf_op jit(solution)/shard_map/ppermute | solution.py:46
  34.6 25.1 %collective-permute-start.9 = (f32[256,8,128]{2,1,0:T(8,128)}, f32[256,8,128]{2,1,0:T(8,128)}, u32[]{:S(2)}, u32[]{:S(2)}) collective-permute-start(f32[256,8,128]{2,1,0:T(8,128)} %get-tuple-element.106), channel_id=1, source_target_pairs={{1,0},{2,1},{3,2},{5,4},{6,5},{7,6},{9,8},{10,9},{11,10},{13,12},{... | collective-permute-start | bytes 3145736 | tf_op jit(solution)/shard_map/ppermute | solution.py:46
  59.7 8.5 %collective-permute-start.10 = (f32[2,128]{1,0:T(2,128)S(1)}, f32[2,128]{1,0:T(2,128)S(1)}, u32[]{:S(2)}, u32[]{:S(2)}) collective-permute-start(f32[2,128]{1,0:T(2,128)S(1)} %get-tuple-element.111), channel_id=1, source_target_pairs={{0,4},{4,8},{8,12},{12,16},{16,20},{20,24},{24,28},{28,0},{1,5},{5... | collective-permute-start | bytes 3080 | tf_op jit(solution)/shard_map/ppermute | solution.py:40
  59.7 8.5 %collective-permute-start.11 = (f32[2,128]{1,0:T(2,128)S(1)}, f32[2,128]{1,0:T(2,128)S(1)}, u32[]{:S(2)}, u32[]{:S(2)}) collective-permute-start(f32[2,128]{1,0:T(2,128)S(1)} %get-tuple-element.112), channel_id=1, source_target_pairs={{0,28},{4,0},{8,4},{12,8},{16,12},{20,16},{24,20},{28,24},{1,29},{... | collective-permute-start | bytes 3080 | tf_op jit(solution)/shard_map/ppermute | solution.py:40
  62.3 5.9 %collective-permute-start.12 = (f32[2,128]{1,0:T(2,128)S(1)}, f32[2,128]{1,0:T(2,128)S(1)}, u32[]{:S(2)}, u32[]{:S(2)}) collective-permute-start(f32[2,128]{1,0:T(2,128)S(1)} %get-tuple-element.113), channel_id=1, source_target_pairs={{0,1},{1,2},{2,3},{3,0},{4,5},{5,6},{6,7},{7,4},{8,9},{9,10},{10,1... | collective-permute-start | bytes 3080 | tf_op jit(solution)/shard_map/ppermute | solution.py:40
  62.9 5.4 %collective-permute-start.13 = (f32[2,128]{1,0:T(2,128)S(1)}, f32[2,128]{1,0:T(2,128)S(1)}, u32[]{:S(2)}, u32[]{:S(2)}) collective-permute-start(f32[2,128]{1,0:T(2,128)S(1)} %get-tuple-element.114), channel_id=1, source_target_pairs={{0,3},{1,0},{2,1},{3,2},{4,7},{5,4},{6,5},{7,6},{8,11},{9,8},{10,9... | collective-permute-start | bytes 3080 | tf_op jit(solution)/shard_map/ppermute | solution.py:40
  68.3 17.2 %collective-permute-start.14 = (f32[64,8,128]{2,1,0:T(8,128)}, f32[64,8,128]{2,1,0:T(8,128)S(1)}, u32[]{:S(2)}, u32[]{:S(2)}) collective-permute-start(f32[64,8,128]{2,1,0:T(8,128)} %get-tuple-element.117), channel_id=1, source_target_pairs={{0,1},{1,2},{2,3},{4,5},{5,6},{6,7},{8,9},{9,10},{10,11},{12,13},{... | collective-permute-start | bytes 786440 | tf_op jit(solution)/shard_map/ppermute | solution.py:46
  69.8 15.6 %collective-permute-start.15 = (f32[64,8,128]{2,1,0:T(8,128)}, f32[64,8,128]{2,1,0:T(8,128)S(1)}, u32[]{:S(2)}, u32[]{:S(2)}) collective-permute-start(f32[64,8,128]{2,1,0:T(8,128)} %get-tuple-element.118), channel_id=1, source_target_pairs={{1,0},{2,1},{3,2},{5,4},{6,5},{7,6},{9,8},{10,9},{11,10},{13,12},{... | collective-permute-start | bytes 786440 | tf_op jit(solution)/shard_map/ppermute | solution.py:46
  72.1 4.3 %collective-permute-start.16 = (f32[2,32,128]{2,1,0:T(8,128)S(1)}, f32[2,32,128]{2,1,0:T(8,128)S(1)}, u32[]{:S(2)}, u32[]{:S(2)}) collective-permute-start(f32[2,32,128]{2,1,0:T(8,128)S(1)} %get-tuple-element.125), channel_id=1, source_target_pairs={{0,4},{4,8},{8,12},{12,16},{16,20},{20,24},{24,28},{28,0},{1,5},{5... | collective-permute-start | bytes 98312 | tf_op jit(solution)/shard_map/ppermute | solution.py:40
  72.2 4.2 %collective-permute-start.17 = (f32[2,32,128]{2,1,0:T(8,128)S(1)}, f32[2,32,128]{2,1,0:T(8,128)S(1)}, u32[]{:S(2)}, u32[]{:S(2)}) collective-permute-start(f32[2,32,128]{2,1,0:T(8,128)S(1)} %get-tuple-element.126), channel_id=1, source_target_pairs={{0,28},{4,0},{8,4},{12,8},{16,12},{20,16},{24,20},{28,24},{1,29},{... | collective-permute-start | bytes 98312 | tf_op jit(solution)/shard_map/ppermute | solution.py:40
  77.6 7.9 %collective-permute-start.18 = (f32[2,8,128]{2,1,0:T(8,128)S(1)}, f32[2,8,128]{2,1,0:T(8,128)S(1)}, u32[]{:S(2)}, u32[]{:S(2)}) collective-permute-start(f32[2,8,128]{2,1,0:T(8,128)S(1)} %get-tuple-element.128), channel_id=1, source_target_pairs={{0,1},{1,2},{2,3},{3,0},{4,5},{5,6},{6,7},{7,4},{8,9},{9,10},{10,1... | collective-permute-start | bytes 24584 | tf_op jit(solution)/shard_map/ppermute | solution.py:40
  80.2 5.2 %collective-permute-start.19 = (f32[2,8,128]{2,1,0:T(8,128)S(1)}, f32[2,8,128]{2,1,0:T(8,128)S(1)}, u32[]{:S(2)}, u32[]{:S(2)}) collective-permute-start(f32[2,8,128]{2,1,0:T(8,128)S(1)} %get-tuple-element.129), channel_id=1, source_target_pairs={{0,3},{1,0},{2,1},{3,2},{4,7},{5,4},{6,5},{7,6},{8,11},{9,8},{10,9... | collective-permute-start | bytes 24584 | tf_op jit(solution)/shard_map/ppermute | solution.py:40
  112.9 5.4 %collective-permute-start.20 = (f32[1,128]{1,0:T(1,128)S(1)}, f32[1,128]{1,0:T(1,128)S(1)}, u32[]{:S(2)}, u32[]{:S(2)}) collective-permute-start(f32[1,128]{1,0:T(1,128)S(1)} %get-tuple-element.133), channel_id=1, source_target_pairs={{0,28},{4,0},{8,4},{12,8},{16,12},{20,16},{24,20},{28,24},{1,29},{... | collective-permute-start | bytes 1544 | tf_op jit(solution)/shard_map/ppermute | solution.py:40
  114.8 3.9 %collective-permute-start.21 = (f32[1,128]{1,0:T(1,128)S(1)}, f32[1,128]{1,0:T(1,128)S(1)}, u32[]{:S(2)}, u32[]{:S(2)}) collective-permute-start(f32[1,128]{1,0:T(1,128)S(1)} %get-tuple-element.134), channel_id=1, source_target_pairs={{0,4},{4,8},{8,12},{12,16},{16,20},{20,24},{24,28},{28,0},{1,5},{5... | collective-permute-start | bytes 1544 | tf_op jit(solution)/shard_map/ppermute | solution.py:40
  114.8 4.7 %collective-permute-start.22 = (f32[1,128]{1,0:T(1,128)S(1)}, f32[1,128]{1,0:T(1,128)S(1)}, u32[]{:S(2)}, u32[]{:S(2)}) collective-permute-start(f32[1,128]{1,0:T(1,128)S(1)} %get-tuple-element.135), channel_id=1, source_target_pairs={{0,3},{1,0},{2,1},{3,2},{4,7},{5,4},{6,5},{7,6},{8,11},{9,8},{10,9... | collective-permute-start | bytes 1544 | tf_op jit(solution)/shard_map/ppermute | solution.py:40
  118.3 5.3 %collective-permute-start.23 = (f32[1,128]{1,0:T(1,128)S(1)}, f32[1,128]{1,0:T(1,128)S(1)}, u32[]{:S(2)}, u32[]{:S(2)}) collective-permute-start(f32[1,128]{1,0:T(1,128)S(1)} %get-tuple-element.136), channel_id=1, source_target_pairs={{0,1},{1,2},{2,3},{3,0},{4,5},{5,6},{6,7},{7,4},{8,9},{9,10},{10,1... | collective-permute-start | bytes 1544 | tf_op jit(solution)/shard_map/ppermute | solution.py:40
  (18 other events, 165.9 us)

commit v4 on v3

--- a/solution.py
+++ b/solution.py
@@ -15,6 +15,8 @@
 TILE = 8
 LANES = 128
 VMEM_ALL = 60 * 1024 * 1024
+VMEM_FLUID = 53 * 1024 * 1024
+VMEM_SOLID = 53 * 1024 * 1024
 BATCH = 8
 HIGHEST = lax.Precision.HIGHEST
 VMEM = pl.BlockSpec(memory_space=pltpu.VMEM)
@@ -204,20 +206,15 @@
     copies.wait_all()
 
 
-def solid_corner_kernel(cells_y, numbers, xlo, xhi, low, high, tiles, sems):
-    copies = Copies(sems)
-    for side in range(2):
+def solid_corner_kernel(cells_y, numbers, xlo, xhi, low, high):
+    for side, out in enumerate((low, high)):
         rows = pl.ds(side * (cells_y - TILE), TILE)
         for end, strip in enumerate((xlo, xhi)):
-            copies.start((side, end), strip.at[:, rows], tiles.at[side, end])
-    for side, out in enumerate((low, high)):
-        for end in range(2):
-            copies.wait((side, end))
             for number in range(numbers):
                 for i in range(1, TILE // 2 + 1):
                     near, far = (TILE - i, i) if end == 0 else (i - 1, TILE - 1 - i)
-                    tile = tiles[side, end, number * TILE + near]
-                    other = tiles[side, end, number * TILE + far]
+                    tile = strip[number * TILE + near, rows, :]
+                    other = strip[number * TILE + far, rows, :]
                     row = row_index(tile.shape)
                     if side == 1:
                         tile = jnp.where(row >= i, tile, pltpu.roll(other, i, 0))
@@ -251,17 +248,8 @@
 
 
 def solid_corners(xlo, xhi, numbers):
-    cells_y = xlo.shape[1]
-    shape = jax.ShapeDtypeStruct((numbers * TILE, TILE, LANES), jnp.float32)
-    return pl.pallas_call(
-        functools.partial(solid_corner_kernel, cells_y, numbers),
-        out_shape=(shape, shape),
-        in_specs=[HBM, HBM],
-        out_specs=(VMEM, VMEM),
-        scratch_shapes=[pltpu.VMEM((2, 2, numbers * TILE, TILE, LANES), jnp.float32), pltpu.SemaphoreType.DMA((4,))],
-        compiler_params=pltpu.CompilerParams(vmem_limit_bytes=VMEM_ALL),
-        cost_estimate=lasts(2),
-    )(xlo, xhi)
+    shape = (numbers * TILE, TILE, LANES)
+    return packing(functools.partial(solid_corner_kernel, xlo.shape[1], numbers), (shape, shape), 0, 1, xlo, xhi)
 
 
 def face(a_low, a_high, u_low, u_high):
@@ -304,8 +292,8 @@
     return head if depth == LANES else jnp.concatenate([head, new[:, LANES:]], axis=1)
 
 
-def fluid_kernel(cells_x, cells_y, depth, flags, wall_t, xlo, xhi, ylo, yhi, clo, chi, own_lo, own_hi,
-                 temp, velo, diff, out, gas, ts, us, as_, vs, ws, t1, yl, yt, cs, ks, sems):
+def fluid_kernel(cells_x, cells_y, depth, near_rows, flags, wall_t, xlo, xhi, ylo, yhi, clo, chi, own_lo, own_hi,
+                 route, film_t, temp, velo, diff, out, pair_out, to_0, to_1, to_2, to_3, ts, us, as_, vs, ws, t1, yl, yt, cs, ks, sems):
     rows_total = flags[4]
     tiles = [(tile, pl.ds(tile * LANES, LANES)) for tile in range(depth // LANES)]
     copies = Copies(sems)
@@ -446,7 +434,7 @@
     for start in starts:
         _, plane = lax.fori_loop(0, step // group, second_sweep, (start + 1, plane))
         copies.start("out", ts.at[pl.ds(start, step)], out.at[pl.ds(start, step)])
-    gas[...] = plane
+    rows_out(cells_x, cells_y, near_rows, route, plane, film_t, pair_out, to_0, to_1, to_2, to_3)
     copies.wait("out")
 
 
@@ -475,19 +463,20 @@
     )(flags, diff)
 
 
-def fluid_call(flags, wall_t, strips, temp, velo, diff):
+def fluid_call(flags, wall_t, strips, route, film_t, near_rows, temp, velo, diff):
     cells_x, cells_y, depth = temp.shape
     chunks = cells_x // TILE
-    plane = jax.ShapeDtypeStruct((cells_y, LANES), temp.dtype)
+    pair = jax.ShapeDtypeStruct((2, cells_x * cells_y), temp.dtype)
+    band = jax.ShapeDtypeStruct((2, near_rows), temp.dtype)
 
     def planes(count):
         return pltpu.VMEM((count, cells_y, depth), jnp.float32)
 
     return pl.pallas_call(
-        functools.partial(fluid_kernel, cells_x, cells_y, depth),
-        out_shape=(jax.ShapeDtypeStruct(temp.shape, temp.dtype), plane),
-        in_specs=[SMEM] + [VMEM] * 9 + [HBM] * 3,
-        out_specs=(HBM, VMEM),
+        functools.partial(fluid_kernel, cells_x, cells_y, depth, near_rows),
+        out_shape=(jax.ShapeDtypeStruct(temp.shape, temp.dtype), pair) + (band,) * 4,
+        in_specs=[SMEM] + [VMEM] * 11 + [HBM] * 3,
+        out_specs=(HBM,) + (VMEM,) * 5,
         scratch_shapes=[
             planes(cells_x + 4),
             planes(cells_x + 4),
@@ -501,15 +490,15 @@
             pltpu.VMEM((cells_x, cells_y, LANES), jnp.float32),
             pltpu.SemaphoreType.DMA((6 * chunks,)),
         ],
-        compiler_params=pltpu.CompilerParams(vmem_limit_bytes=VMEM_ALL),
+        compiler_params=pltpu.CompilerParams(vmem_limit_bytes=VMEM_FLUID),
         cost_estimate=lasts(13),
-    )(flags, wall_t, *strips, temp, velo, diff)
+    )(flags, wall_t, *strips, route, film_t, temp, velo, diff)
 
 
 def solid_kernel(
     cells_x, cells_y, depth, pad, coefficients,
-    flags, cond, sink, heat, temp, xlo, xhi, ylo, yhi, clo, chi, film, film_lo, film_hi,
-    out, surface, ks, es, bs, us, vs, gx, gy, gz, ss, fs, sems,
+    near_rows, flags, cond, sink, heat, temp, xlo, xhi, ylo, yhi, clo, chi, film, film_lo, film_hi, landing,
+    out, own_rows, to_0, to_1, to_2, to_3, ks, es, bs, us, vs, gx, gy, gz, ss, fs, sems,
 ):
     wide_x, wide_y = cells_x + 2 * pad, cells_y + 2 * TILE
     copies = Copies(sems)
@@ -605,7 +594,7 @@
         last = number == total - 1
         margin = total - 1 - number
 
-        def some(block, carry, src=src, dst=dst, decay=decay, gain=gain, number=number, last=last, margin=margin):
+        def some(block, surface, src=src, dst=dst, decay=decay, gain=gain, number=number, last=last, margin=margin):
             planes = [pad - margin + block * BATCH + j for j in range(BATCH)]
             here = [src[x] for x in planes]
             before = [src[planes[0] - 1]] + here[:-1]
@@ -625,36 +614,43 @@
                 fresh = results[j]
                 if last:
                     final = (fresh * ss[x])[TILE:TILE + cells_y]
-                    out[x - pad] = final
+                    es[x, pl.ds(0, cells_y), :] = final
                     shift = x - pad
                     lane = lane_index((cells_y, LANES))
-                    surface[...] = jnp.where(lane == shift, pltpu.roll(final[:, :LANES], shift, 1), surface[...])
+                    surface = jnp.where(lane == shift, pltpu.roll(final[:, :LANES], shift, 1), surface)
                 else:
                     dst[x] = fresh
-            return carry
+            return surface
 
         if last:
-            surface[...] = jnp.zeros_like(surface)
+            surface = jnp.zeros((cells_y, LANES), jnp.float32)
+            for block in range(cells_x // BATCH):
+                surface = some(block, surface)
+                here = pl.ds(block * BATCH, BATCH)
+                copies.start("out", es.at[pl.ds(pad + block * BATCH, BATCH), pl.ds(0, cells_y)], out.at[here])
+            gather_out(cells_x, cells_y, near_rows, landing, surface, own_rows, to_0, to_1, to_2, to_3)
+            copies.wait("out")
+            break
         lax.fori_loop(0, -(-(cells_x + 2 * margin) // BATCH), some, 0)
         src, dst = dst, src
 
 
-def solid_step(flags, cond, sink, heat, temp, halo, films, pad):
+def solid_step(flags, cond, sink, heat, temp, halo, films, landing, row_total, near_rows, pad):
     cells_x, cells_y, depth = cond.shape
     wide_x, wide_y = cells_x + 2 * pad, cells_y + 2 * TILE
     area = pltpu.VMEM((wide_x + BATCH, wide_y, depth), jnp.float32)
     return pl.pallas_call(
-        functools.partial(solid_kernel, cells_x, cells_y, depth, pad, cheby_coefficients(SWEEPS)),
-        out_shape=(jax.ShapeDtypeStruct((cells_x, cells_y, depth), cond.dtype),
-                   jax.ShapeDtypeStruct((cells_y, LANES), cond.dtype)),
-        in_specs=[SMEM] + [HBM] * 8 + [VMEM] * 5,
-        out_specs=(VMEM, VMEM),
+        functools.partial(solid_kernel, cells_x, cells_y, depth, pad, cheby_coefficients(SWEEPS), near_rows),
+        out_shape=tuple(jax.ShapeDtypeStruct(shape, cond.dtype)
+                        for shape in [(cells_x, cells_y, depth), (1, row_total)] + [(1, near_rows)] * 4),
+        in_specs=[SMEM] + [HBM] * 8 + [VMEM] * 6,
+        out_specs=(HBM,) + (VMEM,) * 5,
         scratch_shapes=[area] * 5
         + [area] * 4
-        + [pltpu.VMEM((2, wide_y, LANES), jnp.float32), pltpu.SemaphoreType.DMA((4 + 16 * (depth // LANES),))],
-        compiler_params=pltpu.CompilerParams(vmem_limit_bytes=VMEM_ALL),
+        + [pltpu.VMEM((2, wide_y, LANES), jnp.float32), pltpu.SemaphoreType.DMA((4 + 16 * (depth // LANES) + cells_x // BATCH,))],
+        compiler_params=pltpu.CompilerParams(vmem_limit_bytes=VMEM_SOLID),
         cost_estimate=lasts(30),
-    )(flags, cond, sink, heat, temp, *halo, *films)
+    )(flags, cond, sink, heat, temp, *halo, *films, landing)
 
 
 def ones_where(condition):
@@ -701,11 +697,11 @@
     return jnp.sum(lines * in_y, axis=0, keepdims=True)
 
 
-def rows_kernel(cells_x, cells_y, near_rows, route, gas_t, film_t, pair, *outs):
+def rows_out(cells_x, cells_y, near_rows, route, gas_t, film_t, pair, *outs):
     row_total = cells_x * cells_y
     cells = lane_index((1, row_total))
     film = cell_values(film_t[...], cells_x, cells_y, cells)
-    gas = cell_values(gas_t[...], cells_x, cells_y, cells)
+    gas = cell_values(gas_t, cells_x, cells_y, cells)
     values = jnp.concatenate([film, gas], axis=0)
     pair[...] = values
     for d in range(4):
@@ -740,8 +736,9 @@
     last[...] = total[:, cells_y - TILE:]
 
 
-def gather_kernel(cells_x, cells_y, row_total, near_rows, landing, surface_t, own, *outs):
-    values = cell_values(surface_t[...], cells_x, cells_y, landing[...])
+def gather_out(cells_x, cells_y, near_rows, landing, surface_t, own, *outs):
+    values = cell_values(surface_t, cells_x, cells_y, landing[...])
+    row_total = own.shape[1]
     own[...] = values[:, :row_total]
     for d in range(4):
         outs[d][...] = values[:, row_total + d * near_rows:row_total + (d + 1) * near_rows]
@@ -787,26 +784,26 @@
     xlow, xhigh, ylow, yhigh, wall_t = near_step(row_count, wall_prev.reshape(row_total // LANES, LANES), *fluid)
     xlo, xhi = exchange(xlow, xhigh, "blk", ring)
     ylo, yhi = exchange(ylow, yhigh, "sub", chain)
-    after_near = lax.optimization_barrier((xlow, *solids, eddy_diff, owner_table))[1:]
+    after_near = lax.optimization_barrier((xlow, *solids, eddy_diff))[1:]
     strips = solid_strips(after_near[:4], pad)
     (film_t,) = film_coefficients(flags, after_near[4])
+    xlo, xhi, owners, film_t, *strips = lax.optimization_barrier((xlo, xhi, owner_table, film_t, *strips))
+    blk_halo = exchange(*strips[:2], "blk", ring)
     (route,) = small_call(
-        functools.partial(route_kernel, group_total, slot_cap), [(TILE, row_total)], None, after_near[5]
+        functools.partial(route_kernel, group_total, slot_cap), [(TILE, row_total)], None, owners
     )
-    xlo, xhi, film_t, route, *strips = lax.optimization_barrier((xlo, xhi, film_t, route, *strips))
-    blk_halo = exchange(*strips[:2], "blk", ring)
+    xlo, xhi, route = lax.optimization_barrier((xlo, xhi, route))
     corner = (TILE, cells_z)
     low, high = packing(functools.partial(corner_kernel, cells_y, cells_z // LANES), (corner, corner), 0, 1, xlo, xhi)
     clo, chi = exchange(low, high, "sub", ring)
     ylo, yhi, clo, chi, *sub_strips = lax.optimization_barrier((ylo, yhi, clo, chi, *strips[2:]))
     sub_halo = exchange(*sub_strips, "sub", chain)
-    fluid_new, gas_t = fluid_call(flags, wall_t, (xlo, xhi, ylo, yhi, clo, chi, ylow, yhigh), *fluid)
-    pair, *bands = small_call(
-        functools.partial(rows_kernel, cells_x, cells_y, near_rows),
-        [(2, row_total)] + [(2, near_rows)] * 4, None, route, gas_t, film_t,
+    fluid_new, pair, *bands = fluid_call(
+        flags, wall_t, (xlo, xhi, ylo, yhi, clo, chi, ylow, yhigh), route, film_t, near_rows, *fluid
     )
     moves = (("blk", 1), ("blk", -1), ("sub", 1), ("sub", -1))
-    *bands, blk_low, blk_high, sub_low, sub_high = lax.optimization_barrier((*bands, *blk_halo, *sub_halo))
+    *bands, blk_low, blk_high = lax.optimization_barrier((*bands, *blk_halo))
+    bands[2], bands[3], sub_low, sub_high = lax.optimization_barrier((bands[2], bands[3], *sub_halo))
     arrived = [ring(band, axis, step) for band, (axis, step) in zip(bands, moves)]
     low, high = solid_corners(blk_low, blk_high, 4 * (solid_z // LANES))
     *arrived, low, high = lax.optimization_barrier((*arrived, low, high))
@@ -820,12 +817,7 @@
         flags, film, ring(high, "blk", 1), ring(low, "blk", -1),
     )
     films = (film, ring(last, "sub", 1), ring(first, "sub", -1))
-    solid_new, surface_t = solid_step(flags, *solids, halo, films, pad)
-
-    own, *backs = small_call(
-        functools.partial(gather_kernel, solid_x, solid_y, row_total, near_rows),
-        [(1, row_total)] + [(1, near_rows)] * 4, None, landing_cell, surface_t,
-    )
+    solid_new, own, *backs = solid_step(flags, *solids, halo, films, landing_cell, row_total, near_rows, pad)
     returned = [ring(back, axis, -step) for back, (axis, step) in zip(backs, moves)]
     (wall_new,) = small_call(
         functools.partial(wall_kernel, near_rows), [(1, row_total)], flags, route, own, *returned

time: 126 us -> 119 us (0.944)
  Pallas kernels: 60.6 us -> 56.2 us
  local copies, waits for them, and re-layouts: 2.83 us -> 0.05 us
  waiting for transfers between devices: 14.2 us -> 15.8 us
    ppermute x18, waiting for transfers between devices: 9.07 us -> 13.4 us  [ring(): lax.ppermute(value, axis, [(i, (i + step) % count) for i in range(count)])]
    pallas_call x2 -> x1, Pallas kernels: 18.8 us -> 16 us  [fluid_call(): pl.pallas_call(functools.partial(fluid_kernel, cells_x, cells_y, depth, n...]
    ppermute x6, waiting for transfers between devices: 5.18 us -> 2.36 us  [chain(): return lax.ppermute(value, axis, pairs)]
    unnamed x36 -> x24, local copies, waits for them, and re-layouts: 2.83 us -> 0.05 us
    pallas_call x6 -> x4, Pallas kernels: 4.25 us -> 3.43 us  [small_call(): pl.pallas_call(kernel, out_shape=tuple((jax.ShapeDtypeStruct(shape, jnp.f...]
    pallas_call x2 -> x3, Pallas kernels: 4.58 us -> 4.7 us  [packing(): pl.pallas_call(kernel, out_shape=tuple((jax.ShapeDtypeStruct(shape, jnp.f...]
  transfers between devices with their start and end apart: 24 -> 24, of which waited for: 8 -> 9; matrix products, arithmetic and copies ran while one was open for 1% -> 1% of each run, Pallas kernels for 23% -> 21%
where the time goes in v4:
time: 119 us; the launch traced here: 118 us
  Pallas kernels  56.2 us (47%)
  starting transfers between devices  44.2 us (37%)
  waiting for transfers between devices  15.8 us (13%)
  between operations  1.61 us (1%)
    ppermute x18, starting transfers between devices, ring(): lax.ppermute(value, axis, [(i, (i + step) % count) for i in range(count)])  30.7 us
    pallas_call x1, Pallas kernels, solid_step(): pl.pallas_call(functools.partial(solid_kernel, cells_x, cells_y, depth, p...  24.8 us
    pallas_call x1, Pallas kernels, fluid_call(): pl.pallas_call(functools.partial(fluid_kernel, cells_x, cells_y, depth, n...  16 us
    ppermute x18, waiting for transfers between devices, ring(): lax.ppermute(value, axis, [(i, (i + step) % count) for i in range(count)])  13.4 us
    ppermute x6, starting transfers between devices, chain(): return lax.ppermute(value, axis, pairs)  13.4 us
    pallas_call x1, Pallas kernels, near_step(): pl.pallas_call(functools.partial(near_kernel, cells_x, cells_y, depth), o...  4.77 us
    pallas_call x3, Pallas kernels, packing(): pl.pallas_call(kernel, out_shape=tuple((jax.ShapeDtypeStruct(shape, jnp.f...  4.7 us
    pallas_call x4, Pallas kernels, small_call(): pl.pallas_call(kernel, out_shape=tuple((jax.ShapeDtypeStruct(shape, jnp.f...  3.43 us
  transfers between devices with their start and end apart: 24, of which 9 were waited for; matrix products, arithmetic and copies ran while one was open for 1% of the time, Pallas kernels for 21%

profile of v4, /device:TPU:0, one launch (start us, length us, event | category | flops | bytes accessed | tf_op | source)
XLA Modules:
  0.0 118.5 jit_solution(13446588997185877792)
XLA Ops:
  1.3 4.8 %shard_map.130 = (f32[33,32,128]{2,1,0:T(8,128)}, f32[33,32,128]{2,1,0:T(8,128)}, f32[33,32,128]{2,1,0:T(8,128)}, f32[33,32,128]{2,1,0:T(8,128)}, f32[32,128]{1,0:T(8,128)}) custom-call(s32[1]{0:T(128)S(6)} %copy.14.count_ref, f32[8,128]{1,0:T(8,128)} %bitcast.6, f32[32,32,512]{2,1,0:T(8,128)} %temp.4, f32[3,32,32,512]{3,2,1,0:T(8,128)} %velo.3, ...), custom_call_target="tpu_custom_call" | custom-call | bytes 14760000 | tf_op jit(solution)/shard_map/pallas_call | solution.py:175
  6.6 2.9 %collective-permute-start.1 = (f32[33,32,128]{2,1,0:T(8,128)}, f32[33,32,128]{2,1,0:T(8,128)S(1)}, u32[]{:S(2)}, u32[]{:S(2)}) collective-permute-start(f32[33,32,128]{2,1,0:T(8,128)} %get-tuple-element.74), channel_id=1, source_target_pairs={{0,28},{4,0},{8,4},{12,8},{16,12},{20,16},{24,20},{28,24},{1,29},{... | collective-permute-start | bytes 1622024 | tf_op jit(solution)/shard_map/ppermute | solution.py:42
  9.5 4.2 %collective-permute-start.2 = (f32[33,32,128]{2,1,0:T(8,128)}, f32[33,32,128]{2,1,0:T(8,128)S(1)}, u32[]{:S(2)}, u32[]{:S(2)}) collective-permute-start(f32[33,32,128]{2,1,0:T(8,128)} %get-tuple-element.89.own_hi), channel_id=1, source_target_pairs={{0,1},{1,2},{2,3},{4,5},{5,6},{6,7},{8,9},{9,10},{10,11},{12,13},{... | collective-permute-start | bytes 1622024 | tf_op jit(solution)/shard_map/ppermute | solution.py:48
  15.7 2.5 %shard_map.131.film_t = f32[32,128]{1,0:T(8,128)} custom-call(s32[5]{0:T(128)} %pad_add_fusion.flags, f32[32,32,512]{2,1,0:T(8,128)} %diff.4), custom_call_target="tpu_custom_call" | custom-call | bytes 3690000 | tf_op jit(solution)/shard_map/pallas_call | solution.py:455
  18.2 4.6 %shard_map.132 = (f32[64,32,128]{2,1,0:T(8,128)}, f32[64,32,128]{2,1,0:T(8,128)}, f32[256,8,128]{2,1,0:T(8,128)}, f32[256,8,128]{2,1,0:T(8,128)}) custom-call(f32[32,32,256]{2,1,0:T(8,128)} %cond.1, f32[32,32,256]{2,1,0:T(8,128)} %sink.1, f32[32,32,256]{2,1,0:T(8,128)} %heat.1, f32[32,32,256]{2,1,0:T(8,128)} %temp.5), custom_call_target="tpu_custom_call" | custom-call | bytes 11070000 | tf_op jit(solution)/shard_map/pallas_call | solution.py:227
  23.4 2.7 %collective-permute-start.4 = (f32[8,512]{1,0:T(8,128)S(1)}, f32[8,512]{1,0:T(8,128)S(1)}, u32[]{:S(2)}, u32[]{:S(2)}) collective-permute-start(f32[8,512]{1,0:T(8,128)S(1)} %get-tuple-element.91), channel_id=1, source_target_pairs={{0,1},{1,2},{2,3},{3,0},{4,5},{5,6},{6,7},{7,4},{8,9},{9,10},{10,1... | collective-permute-start | bytes 49160 | tf_op jit(solution)/shard_map/ppermute | solution.py:42
  26.1 2.1 %collective-permute-start.5 = (f32[8,512]{1,0:T(8,128)S(1)}, f32[8,512]{1,0:T(8,128)S(1)}, u32[]{:S(2)}, u32[]{:S(2)}) collective-permute-start(f32[8,512]{1,0:T(8,128)S(1)} %get-tuple-element.92), channel_id=1, source_target_pairs={{0,3},{1,0},{2,1},{3,2},{4,7},{5,4},{6,5},{7,6},{8,11},{9,8},{10,9... | collective-permute-start | bytes 49160 | tf_op jit(solution)/shard_map/ppermute | solution.py:42
  28.2 2.6 %collective-permute-start.7 = (f32[64,32,128]{2,1,0:T(8,128)}, f32[64,32,128]{2,1,0:T(8,128)S(1)}, u32[]{:S(2)}, u32[]{:S(2)}) collective-permute-start(f32[64,32,128]{2,1,0:T(8,128)} %get-tuple-element.107), channel_id=1, source_target_pairs={{0,28},{4,0},{8,4},{12,8},{16,12},{20,16},{24,20},{28,24},{1,29},{... | collective-permute-start | bytes 3145736 | tf_op jit(solution)/shard_map/ppermute | solution.py:42
  31.2 2.1 %collective-permute-start.8 = (f32[256,8,128]{2,1,0:T(8,128)}, f32[256,8,128]{2,1,0:T(8,128)S(1)}, u32[]{:S(2)}, u32[]{:S(2)}) collective-permute-start(f32[256,8,128]{2,1,0:T(8,128)} %get-tuple-element.112), channel_id=1, source_target_pairs={{0,1},{1,2},{2,3},{4,5},{5,6},{6,7},{8,9},{9,10},{10,11},{12,13},{... | collective-permute-start | bytes 3145736 | tf_op jit(solution)/shard_map/ppermute | solution.py:48
  34.7 16.0 %shard_map.135 = (f32[32,32,512]{2,1,0:T(8,128)}, f32[2,1024]{1,0:T(2,128)S(1)}, f32[2,128]{1,0:T(2,128)S(1)}, f32[2,128]{1,0:T(2,128)S(1)}, f32[2,128]{1,0:T(2,128)S(1)}, /*index=5*/f32[2,128]{1,0:T(2,128)S(1)}) custom-call(s32[5]{0:T(128)S(1)} %copy-done.5, f32[32,128]{1,0:T(8,128)S(1)} %copy-done.6, f32[33,32,128]{2,1,0:T(8,128)S(1)} %collective-permute-done.xlo, ...), custom_call_target="tpu_custom_call" | custom-call | bytes 47970000 | tf_op jit(solution)/shard_map/pallas_call | solution.py:475
  50.7 3.1 %collective-permute-done.6.xlo = f32[64,32,128]{2,1,0:T(8,128)S(1)} collective-permute-done((f32[64,32,128]{2,1,0:T(8,128)}, f32[64,32,128]{2,1,0:T(8,128)S(1)}, u32[]{:S(2)}, u32[]{:S(2)}) %collective-permute-start.6) | collective-permute-done | bytes 1048608 | tf_op jit(solution)/shard_map/ppermute | solution.py:42
  54.8 1.7 %collective-permute-start.11 = (f32[2,128]{1,0:T(2,128)S(1)}, f32[2,128]{1,0:T(2,128)S(1)}, u32[]{:S(2)}, u32[]{:S(2)}) collective-permute-start(f32[2,128]{1,0:T(2,128)S(1)} %get-tuple-element.117), channel_id=1, source_target_pairs={{0,28},{4,0},{8,4},{12,8},{16,12},{20,16},{24,20},{28,24},{1,29},{... | collective-permute-start | bytes 3080 | tf_op jit(solution)/shard_map/ppermute | solution.py:42
  56.5 2.3 %collective-permute-done.9.yhi = f32[256,8,128]{2,1,0:T(8,128)S(1)} collective-permute-done((f32[256,8,128]{2,1,0:T(8,128)}, f32[256,8,128]{2,1,0:T(8,128)S(1)}, u32[]{:S(2)}, u32[]{:S(2)}) %collective-permute-start.9) | collective-permute-done | bytes 1048608 | tf_op jit(solution)/shard_map/ppermute | solution.py:48
  60.3 2.3 %collective-permute-start.13 = (f32[2,128]{1,0:T(2,128)S(1)}, f32[2,128]{1,0:T(2,128)S(1)}, u32[]{:S(2)}, u32[]{:S(2)}) collective-permute-start(f32[2,128]{1,0:T(2,128)S(1)} %get-tuple-element.119), channel_id=1, source_target_pairs={{0,3},{1,0},{2,1},{3,2},{4,7},{5,4},{6,5},{7,6},{8,11},{9,8},{10,9... | collective-permute-start | bytes 3080 | tf_op jit(solution)/shard_map/ppermute | solution.py:42
  64.2 3.2 %collective-permute-start.14 = (f32[64,8,128]{2,1,0:T(8,128)S(1)}, f32[64,8,128]{2,1,0:T(8,128)S(1)}, u32[]{:S(2)}, u32[]{:S(2)}) collective-permute-start(f32[64,8,128]{2,1,0:T(8,128)S(1)} %get-tuple-element.122), channel_id=1, source_target_pairs={{0,1},{1,2},{2,3},{4,5},{5,6},{6,7},{8,9},{9,10},{10,11},{12,13},{... | collective-permute-start | bytes 786440 | tf_op jit(solution)/shard_map/ppermute | solution.py:48
  69.8 2.6 %collective-permute-start.17 = (f32[2,32,128]{2,1,0:T(8,128)S(1)}, f32[2,32,128]{2,1,0:T(8,128)S(1)}, u32[]{:S(2)}, u32[]{:S(2)}) collective-permute-start(f32[2,32,128]{2,1,0:T(8,128)S(1)} %get-tuple-element.131), channel_id=1, source_target_pairs={{0,28},{4,0},{8,4},{12,8},{16,12},{20,16},{24,20},{28,24},{1,29},{... | collective-permute-start | bytes 98312 | tf_op jit(solution)/shard_map/ppermute | solution.py:42
  72.4 1.6 %collective-permute-done.16.low = f32[2,32,128]{2,1,0:T(8,128)S(1)} collective-permute-done((f32[2,32,128]{2,1,0:T(8,128)S(1)}, f32[2,32,128]{2,1,0:T(8,128)S(1)}, u32[]{:S(2)}, u32[]{:S(2)}) %collective-permute-start.16) | collective-permute-done | bytes 32800 | tf_op jit(solution)/shard_map/ppermute | solution.py:42
  74.6 2.7 %collective-permute-start.18 = (f32[2,8,128]{2,1,0:T(8,128)S(1)}, f32[2,8,128]{2,1,0:T(8,128)S(1)}, u32[]{:S(2)}, u32[]{:S(2)}) collective-permute-start(f32[2,8,128]{2,1,0:T(8,128)S(1)} %get-tuple-element.133), channel_id=1, source_target_pairs={{0,1},{1,2},{2,3},{3,0},{4,5},{5,6},{6,7},{7,4},{8,9},{9,10},{10,1... | collective-permute-start | bytes 24584 | tf_op jit(solution)/shard_map/ppermute | solution.py:42
  77.3 2.6 %collective-permute-start.19 = (f32[2,8,128]{2,1,0:T(8,128)S(1)}, f32[2,8,128]{2,1,0:T(8,128)S(1)}, u32[]{:S(2)}, u32[]{:S(2)}) collective-permute-start(f32[2,8,128]{2,1,0:T(8,128)S(1)} %get-tuple-element.134), channel_id=1, source_target_pairs={{0,3},{1,0},{2,1},{3,2},{4,7},{5,4},{6,5},{7,6},{8,11},{9,8},{10,9... | collective-permute-start | bytes 24584 | tf_op jit(solution)/shard_map/ppermute | solution.py:42
  79.8 1.6 %collective-permute-done.18.film_lo = f32[2,8,128]{2,1,0:T(8,128)S(1)} collective-permute-done((f32[2,8,128]{2,1,0:T(8,128)S(1)}, f32[2,8,128]{2,1,0:T(8,128)S(1)}, u32[]{:S(2)}, u32[]{:S(2)}) %collective-permute-start.18) | collective-permute-done | bytes 8224 | tf_op jit(solution)/shard_map/ppermute | solution.py:42
  81.5 24.8 %shard_map.139 = (f32[32,32,256]{2,1,0:T(8,128)}, f32[1,1024]{1,0:T(1,128)S(1)}, f32[1,128]{1,0:T(1,128)S(1)}, f32[1,128]{1,0:T(1,128)S(1)}, f32[1,128]{1,0:T(1,128)S(1)}, /*index=5*/f32[1,128]{1,0:T(1,128)S(1)}) custom-call(s32[5]{0:T(128)S(1)} %copy-done.5, f32[32,32,256]{2,1,0:T(8,128)} %cond.1, f32[32,32,256]{2,1,0:T(8,128)} %sink.1, ...), custom_call_target="tpu_custom_call" | custom-call | bytes 110700000 | tf_op jit(solution)/shard_map/pallas_call | solution.py:642
  106.3 1.9 %collective-permute-start.20 = (f32[1,128]{1,0:T(1,128)S(1)}, f32[1,128]{1,0:T(1,128)S(1)}, u32[]{:S(2)}, u32[]{:S(2)}) collective-permute-start(f32[1,128]{1,0:T(1,128)S(1)} %get-tuple-element.137), channel_id=1, source_target_pairs={{0,28},{4,0},{8,4},{12,8},{16,12},{20,16},{24,20},{28,24},{1,29},{... | collective-permute-start | bytes 1544 | tf_op jit(solution)/shard_map/ppermute | solution.py:42
  108.2 3.5 %collective-permute-start.22 = (f32[1,128]{1,0:T(1,128)S(1)}, f32[1,128]{1,0:T(1,128)S(1)}, u32[]{:S(2)}, u32[]{:S(2)}) collective-permute-start(f32[1,128]{1,0:T(1,128)S(1)} %get-tuple-element.139), channel_id=1, source_target_pairs={{0,3},{1,0},{2,1},{3,2},{4,7},{5,4},{6,5},{7,6},{8,11},{9,8},{10,9... | collective-permute-start | bytes 1544 | tf_op jit(solution)/shard_map/ppermute | solution.py:42
  113.0 4.0 %collective-permute-done.23.from_3 = f32[1,128]{1,0:T(1,128)S(1)} collective-permute-done((f32[1,128]{1,0:T(1,128)S(1)}, f32[1,128]{1,0:T(1,128)S(1)}, u32[]{:S(2)}, u32[]{:S(2)}) %collective-permute-start.23) | collective-permute-done | bytes 544 | tf_op jit(solution)/shard_map/ppermute | solution.py:42
  (61 shorter events, 14.4 us)
Async XLA Ops:
  6.1 16.8 %collective-permute-start = (f32[33,32,128]{2,1,0:T(8,128)}, f32[33,32,128]{2,1,0:T(8,128)S(1)}, u32[]{:S(2)}, u32[]{:S(2)}) collective-permute-start(f32[33,32,128]{2,1,0:T(8,128)} %get-tuple-element.73), channel_id=1, source_target_pairs={{0,4},{4,8},{8,12},{12,16},{16,20},{20,24},{24,28},{28,0},{1,5},{5... | collective-permute-start | bytes 1622024 | tf_op jit(solution)/shard_map/ppermute | solution.py:42
  6.6 16.3 %collective-permute-start.1 = (f32[33,32,128]{2,1,0:T(8,128)}, f32[33,32,128]{2,1,0:T(8,128)S(1)}, u32[]{:S(2)}, u32[]{:S(2)}) collective-permute-start(f32[33,32,128]{2,1,0:T(8,128)} %get-tuple-element.74), channel_id=1, source_target_pairs={{0,28},{4,0},{8,4},{12,8},{16,12},{20,16},{24,20},{28,24},{1,29},{... | collective-permute-start | bytes 1622024 | tf_op jit(solution)/shard_map/ppermute | solution.py:42
  9.5 18.6 %collective-permute-start.2 = (f32[33,32,128]{2,1,0:T(8,128)}, f32[33,32,128]{2,1,0:T(8,128)S(1)}, u32[]{:S(2)}, u32[]{:S(2)}) collective-permute-start(f32[33,32,128]{2,1,0:T(8,128)} %get-tuple-element.89.own_hi), channel_id=1, source_target_pairs={{0,1},{1,2},{2,3},{4,5},{5,6},{6,7},{8,9},{9,10},{10,11},{12,13},{... | collective-permute-start | bytes 1622024 | tf_op jit(solution)/shard_map/ppermute | solution.py:48
  13.7 17.1 %collective-permute-start.3 = (f32[33,32,128]{2,1,0:T(8,128)}, f32[33,32,128]{2,1,0:T(8,128)S(1)}, u32[]{:S(2)}, u32[]{:S(2)}) collective-permute-start(f32[33,32,128]{2,1,0:T(8,128)} %get-tuple-element.90.own_lo), channel_id=1, source_target_pairs={{1,0},{2,1},{3,2},{5,4},{6,5},{7,6},{9,8},{10,9},{11,10},{13,12},{... | collective-permute-start | bytes 1622024 | tf_op jit(solution)/shard_map/ppermute | solution.py:48
  23.4 7.8 %collective-permute-start.4 = (f32[8,512]{1,0:T(8,128)S(1)}, f32[8,512]{1,0:T(8,128)S(1)}, u32[]{:S(2)}, u32[]{:S(2)}) collective-permute-start(f32[8,512]{1,0:T(8,128)S(1)} %get-tuple-element.91), channel_id=1, source_target_pairs={{0,1},{1,2},{2,3},{3,0},{4,5},{5,6},{6,7},{7,4},{8,9},{9,10},{10,1... | collective-permute-start | bytes 49160 | tf_op jit(solution)/shard_map/ppermute | solution.py:42
  26.1 5.2 %collective-permute-start.5 = (f32[8,512]{1,0:T(8,128)S(1)}, f32[8,512]{1,0:T(8,128)S(1)}, u32[]{:S(2)}, u32[]{:S(2)}) collective-permute-start(f32[8,512]{1,0:T(8,128)S(1)} %get-tuple-element.92), channel_id=1, source_target_pairs={{0,3},{1,0},{2,1},{3,2},{4,7},{5,4},{6,5},{7,6},{8,11},{9,8},{10,9... | collective-permute-start | bytes 49160 | tf_op jit(solution)/shard_map/ppermute | solution.py:42
  28.1 25.6 %collective-permute-start.6 = (f32[64,32,128]{2,1,0:T(8,128)}, f32[64,32,128]{2,1,0:T(8,128)S(1)}, u32[]{:S(2)}, u32[]{:S(2)}) collective-permute-start(f32[64,32,128]{2,1,0:T(8,128)} %get-tuple-element.106), channel_id=1, source_target_pairs={{0,4},{4,8},{8,12},{12,16},{16,20},{20,24},{24,28},{28,0},{1,5},{5... | collective-permute-start | bytes 3145736 | tf_op jit(solution)/shard_map/ppermute | solution.py:42
  28.2 25.6 %collective-permute-start.7 = (f32[64,32,128]{2,1,0:T(8,128)}, f32[64,32,128]{2,1,0:T(8,128)S(1)}, u32[]{:S(2)}, u32[]{:S(2)}) collective-permute-start(f32[64,32,128]{2,1,0:T(8,128)} %get-tuple-element.107), channel_id=1, source_target_pairs={{0,28},{4,0},{8,4},{12,8},{16,12},{20,16},{24,20},{28,24},{1,29},{... | collective-permute-start | bytes 3145736 | tf_op jit(solution)/shard_map/ppermute | solution.py:42
  31.2 25.3 %collective-permute-start.8 = (f32[256,8,128]{2,1,0:T(8,128)}, f32[256,8,128]{2,1,0:T(8,128)S(1)}, u32[]{:S(2)}, u32[]{:S(2)}) collective-permute-start(f32[256,8,128]{2,1,0:T(8,128)} %get-tuple-element.112), channel_id=1, source_target_pairs={{0,1},{1,2},{2,3},{4,5},{5,6},{6,7},{8,9},{9,10},{10,11},{12,13},{... | collective-permute-start | bytes 3145736 | tf_op jit(solution)/shard_map/ppermute | solution.py:48
  33.3 25.5 %collective-permute-start.9 = (f32[256,8,128]{2,1,0:T(8,128)}, f32[256,8,128]{2,1,0:T(8,128)S(1)}, u32[]{:S(2)}, u32[]{:S(2)}) collective-permute-start(f32[256,8,128]{2,1,0:T(8,128)} %get-tuple-element.113), channel_id=1, source_target_pairs={{1,0},{2,1},{3,2},{5,4},{6,5},{7,6},{9,8},{10,9},{11,10},{13,12},{... | collective-permute-start | bytes 3145736 | tf_op jit(solution)/shard_map/ppermute | solution.py:48
  53.8 9.0 %collective-permute-start.10 = (f32[2,128]{1,0:T(2,128)S(1)}, f32[2,128]{1,0:T(2,128)S(1)}, u32[]{:S(2)}, u32[]{:S(2)}) collective-permute-start(f32[2,128]{1,0:T(2,128)S(1)} %get-tuple-element.116), channel_id=1, source_target_pairs={{0,4},{4,8},{8,12},{12,16},{16,20},{20,24},{24,28},{28,0},{1,5},{5... | collective-permute-start | bytes 3080 | tf_op jit(solution)/shard_map/ppermute | solution.py:42
  54.8 8.0 %collective-permute-start.11 = (f32[2,128]{1,0:T(2,128)S(1)}, f32[2,128]{1,0:T(2,128)S(1)}, u32[]{:S(2)}, u32[]{:S(2)}) collective-permute-start(f32[2,128]{1,0:T(2,128)S(1)} %get-tuple-element.117), channel_id=1, source_target_pairs={{0,28},{4,0},{8,4},{12,8},{16,12},{20,16},{24,20},{28,24},{1,29},{... | collective-permute-start | bytes 3080 | tf_op jit(solution)/shard_map/ppermute | solution.py:42
  58.8 5.4 %collective-permute-start.12 = (f32[2,128]{1,0:T(2,128)S(1)}, f32[2,128]{1,0:T(2,128)S(1)}, u32[]{:S(2)}, u32[]{:S(2)}) collective-permute-start(f32[2,128]{1,0:T(2,128)S(1)} %get-tuple-element.118), channel_id=1, source_target_pairs={{0,1},{1,2},{2,3},{3,0},{4,5},{5,6},{6,7},{7,4},{8,9},{9,10},{10,1... | collective-permute-start | bytes 3080 | tf_op jit(solution)/shard_map/ppermute | solution.py:42
  60.3 3.9 %collective-permute-start.13 = (f32[2,128]{1,0:T(2,128)S(1)}, f32[2,128]{1,0:T(2,128)S(1)}, u32[]{:S(2)}, u32[]{:S(2)}) collective-permute-start(f32[2,128]{1,0:T(2,128)S(1)} %get-tuple-element.119), channel_id=1, source_target_pairs={{0,3},{1,0},{2,1},{3,2},{4,7},{5,4},{6,5},{7,6},{8,11},{9,8},{10,9... | collective-permute-start | bytes 3080 | tf_op jit(solution)/shard_map/ppermute | solution.py:42
  64.2 17.2 %collective-permute-start.14 = (f32[64,8,128]{2,1,0:T(8,128)S(1)}, f32[64,8,128]{2,1,0:T(8,128)S(1)}, u32[]{:S(2)}, u32[]{:S(2)}) collective-permute-start(f32[64,8,128]{2,1,0:T(8,128)S(1)} %get-tuple-element.122), channel_id=1, source_target_pairs={{0,1},{1,2},{2,3},{4,5},{5,6},{6,7},{8,9},{9,10},{10,11},{12,13},{... | collective-permute-start | bytes 786440 | tf_op jit(solution)/shard_map/ppermute | solution.py:48
  67.5 14.0 %collective-permute-start.15 = (f32[64,8,128]{2,1,0:T(8,128)S(1)}, f32[64,8,128]{2,1,0:T(8,128)S(1)}, u32[]{:S(2)}, u32[]{:S(2)}) collective-permute-start(f32[64,8,128]{2,1,0:T(8,128)S(1)} %get-tuple-element.123), channel_id=1, source_target_pairs={{1,0},{2,1},{3,2},{5,4},{6,5},{7,6},{9,8},{10,9},{11,10},{13,12},{... | collective-permute-start | bytes 786440 | tf_op jit(solution)/shard_map/ppermute | solution.py:48
  69.7 4.3 %collective-permute-start.16 = (f32[2,32,128]{2,1,0:T(8,128)S(1)}, f32[2,32,128]{2,1,0:T(8,128)S(1)}, u32[]{:S(2)}, u32[]{:S(2)}) collective-permute-start(f32[2,32,128]{2,1,0:T(8,128)S(1)} %get-tuple-element.130), channel_id=1, source_target_pairs={{0,4},{4,8},{8,12},{12,16},{16,20},{20,24},{24,28},{28,0},{1,5},{5... | collective-permute-start | bytes 98312 | tf_op jit(solution)/shard_map/ppermute | solution.py:42
  69.8 4.2 %collective-permute-start.17 = (f32[2,32,128]{2,1,0:T(8,128)S(1)}, f32[2,32,128]{2,1,0:T(8,128)S(1)}, u32[]{:S(2)}, u32[]{:S(2)}) collective-permute-start(f32[2,32,128]{2,1,0:T(8,128)S(1)} %get-tuple-element.131), channel_id=1, source_target_pairs={{0,28},{4,0},{8,4},{12,8},{16,12},{20,16},{24,20},{28,24},{1,29},{... | collective-permute-start | bytes 98312 | tf_op jit(solution)/shard_map/ppermute | solution.py:42
  74.6 6.8 %collective-permute-start.18 = (f32[2,8,128]{2,1,0:T(8,128)S(1)}, f32[2,8,128]{2,1,0:T(8,128)S(1)}, u32[]{:S(2)}, u32[]{:S(2)}) collective-permute-start(f32[2,8,128]{2,1,0:T(8,128)S(1)} %get-tuple-element.133), channel_id=1, source_target_pairs={{0,1},{1,2},{2,3},{3,0},{4,5},{5,6},{6,7},{7,4},{8,9},{9,10},{10,1... | collective-permute-start | bytes 24584 | tf_op jit(solution)/shard_map/ppermute | solution.py:42
  77.3 4.1 %collective-permute-start.19 = (f32[2,8,128]{2,1,0:T(8,128)S(1)}, f32[2,8,128]{2,1,0:T(8,128)S(1)}, u32[]{:S(2)}, u32[]{:S(2)}) collective-permute-start(f32[2,8,128]{2,1,0:T(8,128)S(1)} %get-tuple-element.134), channel_id=1, source_target_pairs={{0,3},{1,0},{2,1},{3,2},{4,7},{5,4},{6,5},{7,6},{8,11},{9,8},{10,9... | collective-permute-start | bytes 24584 | tf_op jit(solution)/shard_map/ppermute | solution.py:42
  106.3 5.4 %collective-permute-start.20 = (f32[1,128]{1,0:T(1,128)S(1)}, f32[1,128]{1,0:T(1,128)S(1)}, u32[]{:S(2)}, u32[]{:S(2)}) collective-permute-start(f32[1,128]{1,0:T(1,128)S(1)} %get-tuple-element.137), channel_id=1, source_target_pairs={{0,28},{4,0},{8,4},{12,8},{16,12},{20,16},{24,20},{28,24},{1,29},{... | collective-permute-start | bytes 1544 | tf_op jit(solution)/shard_map/ppermute | solution.py:42
  108.2 3.9 %collective-permute-start.21 = (f32[1,128]{1,0:T(1,128)S(1)}, f32[1,128]{1,0:T(1,128)S(1)}, u32[]{:S(2)}, u32[]{:S(2)}) collective-permute-start(f32[1,128]{1,0:T(1,128)S(1)} %get-tuple-element.138), channel_id=1, source_target_pairs={{0,4},{4,8},{8,12},{12,16},{16,20},{20,24},{24,28},{28,0},{1,5},{5... | collective-permute-start | bytes 1544 | tf_op jit(solution)/shard_map/ppermute | solution.py:42
  108.2 4.8 %collective-permute-start.22 = (f32[1,128]{1,0:T(1,128)S(1)}, f32[1,128]{1,0:T(1,128)S(1)}, u32[]{:S(2)}, u32[]{:S(2)}) collective-permute-start(f32[1,128]{1,0:T(1,128)S(1)} %get-tuple-element.139), channel_id=1, source_target_pairs={{0,3},{1,0},{2,1},{3,2},{4,7},{5,4},{6,5},{7,6},{8,11},{9,8},{10,9... | collective-permute-start | bytes 1544 | tf_op jit(solution)/shard_map/ppermute | solution.py:42
  111.7 5.3 %collective-permute-start.23 = (f32[1,128]{1,0:T(1,128)S(1)}, f32[1,128]{1,0:T(1,128)S(1)}, u32[]{:S(2)}, u32[]{:S(2)}) collective-permute-start(f32[1,128]{1,0:T(1,128)S(1)} %get-tuple-element.140), channel_id=1, source_target_pairs={{0,1},{1,2},{2,3},{3,0},{4,5},{5,6},{6,7},{7,4},{8,9},{9,10},{10,1... | collective-permute-start | bytes 1544 | tf_op jit(solution)/shard_map/ppermute | solution.py:42
  (12 other events, 197.0 us)

commit v5 on v4

--- a/solution.py
+++ b/solution.py
@@ -117,31 +117,46 @@
             self.wait(key)
 
 
-def x_fields(temp, velo, diff, side, cells_x, zs):
-    two, one = (pl.ds(0, 2), pl.ds(0, 1)) if side == 0 else (pl.ds(cells_x - 2, 2), pl.ds(cells_x - 1, 1))
-    return (
-        (temp.at[two, :, zs], 0, 2),
-        (diff.at[two, :, zs], 2, 2),
-        (velo.at[0, two, :, zs], 4, 2),
-        (velo.at[1, one, :, zs], 6, 1),
-        (velo.at[2, one, :, zs], 7, 1),
-    )
-
-
-def near_kernel(cells_x, cells_y, depth, count_ref, wall, temp, velo, diff, xlow, xhigh, ylow, yhigh, wall_t, sems):
+PLANES = 6
+
+
+def strip_sums(side, t, a, un, uz, t_far, a_far, un_far, live_two, wall):
+    depth = t.shape[1]
+    if side == 0:
+        plus, minus = face(a, a_far, un, un_far)
+        total = minus * t_far - plus * t
+    else:
+        plus, minus = face(a_far, a, un_far, un)
+        total = plus * t_far - minus * t
+    p_down, q_down = face(pltpu.roll(a, 1, 1), a, pltpu.roll(uz, 1, 1), uz)
+    p_up, q_up = pltpu.roll(p_down, depth - 1, 1), pltpu.roll(q_down, depth - 1, 1)
+    a_first, a_last, u_last = 2.0 * a[:, :LANES], 2.0 * a[:, -LANES:], 2.0 * uz[:, -LANES:]
+    plus_last = a_last + jnp.maximum(u_last, 0.0)
+    weight = (plus + minus) + first_lane(p_down + q_down, 2.0 * a_first)
+    weight = weight + last_lane(p_up + q_up, 2.0 * plus_last - u_last)
+    gain = a_first * live_two
+    p_down, q_down = first_lane(p_down, 0.0), first_lane(q_down, gain)
+    p_up, q_up = last_lane(p_up, plus_last), last_lane(q_up, 0.0)
+    total = total + (p_down * pltpu.roll(t, 1, 1) + q_up * pltpu.roll(t, depth - 1, 1)) - (q_down + p_up) * t
+    head = total[:, :LANES] + jnp.where(lane_index(gain.shape) == 0, gain * wall, 0.0)
+    return (head if depth == LANES else jnp.concatenate([head, total[:, LANES:]], axis=1)), weight
+
+
+def near_kernel(cells_x, cells_y, depth, count_ref, wall, temp, velo, diff, xlow, xhigh, ylow, yhigh, wall_t,
+                sx, sy, sems):
     copies = Copies(sems)
-    count = depth // LANES
-    for side, out in ((0, ylow), (1, yhigh)):
-        first, near = (0, 0) if side == 0 else (cells_y - 2, cells_y - 1)
-        picks = ((temp, first), (temp, first + 1), (diff, first), (diff, first + 1), (velo.at[1], first),
-                 (velo.at[1], first + 1), (velo.at[0], near), (velo.at[2], near))
-        for tile in range(count):
-            for plane, (src, row) in enumerate(picks):
-                copies.start("y", src.at[:, row, pl.ds(tile * LANES, LANES)], out.at[8 * tile + plane])
-    for side, out in ((0, xlow), (1, xhigh)):
-        for tile in range(count):
-            for src, at, planes in x_fields(temp, velo, diff, side, cells_x, pl.ds(tile * LANES, LANES)):
-                copies.start("x", src, out.at[pl.ds(8 * tile + at, planes)])
+    for side in range(2):
+        edge, far = (0, 1) if side == 0 else (cells_y - 1, cells_y - 2)
+        sources = ((temp, edge), (diff, edge), (velo.at[1], edge), (velo.at[0], edge), (velo.at[2], edge),
+                   (temp, far), (diff, far), (velo.at[1], far))
+        for plane, (src, y) in enumerate(sources):
+            copies.start(("y", side), src.at[:, y, :], sy.at[side, plane])
+    for side in range(2):
+        edge, far = (0, 1) if side == 0 else (cells_x - 1, cells_x - 2)
+        sources = ((temp, edge), (diff, edge), (velo.at[0], edge), (velo.at[1], edge), (velo.at[2], edge),
+                   (temp, far), (diff, far), (velo.at[0], far))
+        for plane, (src, x) in enumerate(sources):
+            copies.start(("x", side), src.at[x], sx.at[side, plane])
     lines = wall[...]
     group = LANES // cells_y
     shape = (cells_x, lines.shape[0])
@@ -154,22 +169,25 @@
     same = ones_where(row_index((cells_x, LANES)) == lane_index((cells_x, LANES)))
     turned = lax.dot_general(plain, same, (((0,), (0,)), ((), ())), precision=HIGHEST)[:cells_y]
     wall_t[...] = turned
-
-    def note(plane, place, at):
-        lane = lane_index(plane.shape)
-        live_two = jnp.where(place < count_ref[0], 2.0, 0.0)
-        return jnp.where(lane == 0, live_two, jnp.where(lane == 1, pltpu.roll(plane, (LANES + 1 - at) % LANES, 1), 0.0))
-
     for side in range(2):
         x, y = side * (cells_x - 1), side * (cells_y - 1)
-        (xlow, xhigh)[side][8 * count] = note(turned, x * cells_y + row_index(turned.shape), x)
-        (ylow, yhigh)[side][8 * count] = note(plain, row_index(plain.shape) * cells_y + y, y)
-    copies.wait_all()
+        for key, ref, out, plane, place, at in (
+            ("x", sx, (xlow, xhigh)[side], turned, x * cells_y + row_index(turned.shape), x),
+            ("y", sy, (ylow, yhigh)[side], plain, row_index(plain.shape) * cells_y + y, y),
+        ):
+            copies.wait((key, side))
+            t, a, un, ut, uz, t_far, a_far, un_far = [ref[side, number] for number in range(8)]
+            live_two = jnp.where(place < count_ref[0], 2.0, 0.0)
+            sums = strip_sums(side, t, a, un, uz, t_far, a_far, un_far, live_two,
+                              pltpu.roll(plane, LANES - at, 1) if at else plane)
+            for number, value in enumerate((t, a, un, ut) + sums):
+                for tile in range(depth // LANES):
+                    out[PLANES * tile + number] = value[:, tile * LANES:(tile + 1) * LANES]
 
 
 def near_step(row_count, wall, temp, velo, diff):
     cells_x, cells_y, depth = temp.shape
-    planes = 8 * (depth // LANES) + 1
+    planes = PLANES * (depth // LANES)
     x_strip = jax.ShapeDtypeStruct((planes, cells_y, LANES), temp.dtype)
     y_strip = jax.ShapeDtypeStruct((planes, cells_x, LANES), temp.dtype)
     return pl.pallas_call(
@@ -177,7 +195,11 @@
         out_shape=(x_strip, x_strip, y_strip, y_strip, jax.ShapeDtypeStruct((cells_y, LANES), temp.dtype)),
         in_specs=[SMEM, VMEM, HBM, HBM, HBM],
         out_specs=(VMEM,) * 5,
-        scratch_shapes=[pltpu.SemaphoreType.DMA((26 * (depth // LANES),))],
+        scratch_shapes=[
+            pltpu.VMEM((2, 8, cells_y, depth), jnp.float32),
+            pltpu.VMEM((2, 8, cells_x, depth), jnp.float32),
+            pltpu.SemaphoreType.DMA((32,)),
+        ],
         compiler_params=pltpu.CompilerParams(vmem_limit_bytes=VMEM_ALL),
         cost_estimate=lasts(4),
     )(row_count, wall, temp, velo, diff)
@@ -185,10 +207,18 @@
 
 def corner_kernel(cells_y, count, xlo, xhi, low, high):
     for out, y in ((low, 0), (high, cells_y - 1)):
-        for end, (strip, inner) in enumerate(((xlo, 1), (xhi, 0))):
-            for j, plane in enumerate((inner, 2 + inner, 4 + inner, 6)):
+        for end, strip in enumerate((xlo, xhi)):
+            for j in range(4):
                 for tile in range(count):
-                    out[pl.ds(4 * end + j, 1), pl.ds(tile * LANES, LANES)] = strip[8 * tile + plane, pl.ds(y, 1), :]
+                    out[pl.ds(4 * end + j, 1), pl.ds(tile * LANES, LANES)] = strip[PLANES * tile + j, pl.ds(y, 1), :]
+
+
+def layers_of(field, pad):
+    return pad
+
+
+def layers_before(field, tile, tiles, pad):
+    return sum(tiles * layers_of(other, pad) for other in range(field)) + tile * layers_of(field, pad)
 
 
 def solid_pack_kernel(cells_x, cells_y, pad, depth, *refs):
@@ -197,9 +227,10 @@
     for field, src in enumerate(refs[:4]):
         for tile in range(depth // LANES):
             number, zs = field * (depth // LANES) + tile, pl.ds(tile * LANES, LANES)
+            layers, before = layers_of(field, pad), layers_before(field, tile, depth // LANES, pad)
             for side, out in ((0, xlow), (1, xhigh)):
-                here = pl.ds(side * (cells_x - pad), pad)
-                copies.start(0, src.at[here, :, zs], out.at[pl.ds(number * pad, pad)])
+                here = pl.ds(side * (cells_x - layers), layers)
+                copies.start(0, src.at[here, :, zs], out.at[pl.ds(before, layers)])
             for side, out in ((0, ylow), (1, yhigh)):
                 here = pl.ds(side * (cells_y - TILE), TILE)
                 copies.start(0, src.at[:, here, zs], out.at[pl.ds(number * cells_x, cells_x)])
@@ -211,10 +242,12 @@
         rows = pl.ds(side * (cells_y - TILE), TILE)
         for end, strip in enumerate((xlo, xhi)):
             for number in range(numbers):
+                field, part = divmod(number, numbers // 4)
+                layers, before = layers_of(field, TILE), layers_before(field, part, numbers // 4, TILE)
                 for i in range(1, TILE // 2 + 1):
-                    near, far = (TILE - i, i) if end == 0 else (i - 1, TILE - 1 - i)
-                    tile = strip[number * TILE + near, rows, :]
-                    other = strip[number * TILE + far, rows, :]
+                    near, far = (layers - i, layers - TILE + i) if end == 0 else (i - 1, TILE - 1 - i)
+                    tile = strip[before + near, rows, :]
+                    other = strip[before + far, rows, :]
                     row = row_index(tile.shape)
                     if side == 1:
                         tile = jnp.where(row >= i, tile, pltpu.roll(other, i, 0))
@@ -242,7 +275,8 @@
 def solid_strips(solids, pad):
     cells_x, cells_y, depth = solids[0].shape
     numbers = 4 * (depth // LANES)
-    x_shape, y_shape = (numbers * pad, cells_y, LANES), (numbers * cells_x, TILE, LANES)
+    planes = layers_before(4, 0, depth // LANES, pad)
+    x_shape, y_shape = (planes, cells_y, LANES), (numbers * cells_x, TILE, LANES)
     return packing(functools.partial(solid_pack_kernel, cells_x, cells_y, pad, depth),
                    (x_shape, x_shape, y_shape, y_shape), 4 * numbers, 3, *solids)
 
@@ -293,7 +327,7 @@
 
 
 def fluid_kernel(cells_x, cells_y, depth, near_rows, flags, wall_t, xlo, xhi, ylo, yhi, clo, chi, own_lo, own_hi,
-                 route, film_t, temp, velo, diff, out, pair_out, to_0, to_1, to_2, to_3, ts, us, as_, vs, ws, t1, yl, yt, cs, ks, sems):
+                 route, temp, velo, diff, out, pair_out, to_0, to_1, to_2, to_3, ts, us, as_, vs, ws, t1, yl, yt, cs, ks, sems):
     rows_total = flags[4]
     tiles = [(tile, pl.ds(tile * LANES, LANES)) for tile in range(depth // LANES)]
     copies = Copies(sems)
@@ -311,30 +345,42 @@
     for start in starts[:2]:
         load(start)
     for side, halo in enumerate((xlo, xhi)):
-        at, beside = (0, 0) if side == 0 else (cells_x + 2, cells_x + 1)
+        at = 1 if side == 0 else cells_x + 2
         for tile, zs in tiles:
-            for j in range(2):
-                ts[at + j, :, zs] = halo[8 * tile + j]
-                as_[at + j, :, zs] = halo[8 * tile + 2 + j]
-                us[at + j, :, zs] = halo[8 * tile + 4 + j]
-            vs[beside, :, zs] = halo[8 * tile + 6]
-            ws[beside, :, zs] = halo[8 * tile + 7]
+            for number, ref in enumerate((ts, as_, us)):
+                ref[at, :, zs] = halo[PLANES * tile + number]
 
         @pl.when(flags[side] == 0)
         def _():
-            for ref, first, count in ((ts, at, 2), (as_, at, 2), (us, at, 2), (vs, beside, 1), (ws, beside, 1)):
-                for j in range(count):
-                    ref[first + j] = jnp.zeros(ref.shape[1:], jnp.float32)
+            for ref in (ts, as_, us):
+                ref[at] = jnp.zeros(ref.shape[1:], jnp.float32)
 
     for side, halo in enumerate((ylo, yhi)):
-        inner = 1 - side
-        for plane in range(8):
+        for number in range(PLANES):
             for tile, zs in tiles:
-                yl[side, plane, pl.ds(TILE, cells_x), zs] = halo[8 * tile + plane]
+                yl[side, number, pl.ds(TILE, cells_x), zs] = halo[PLANES * tile + number]
         for end, at in enumerate((TILE - 1, TILE + cells_x)):
             good = flags[end] * flags[2 + side] > 0
-            for j, plane in enumerate((inner, 2 + inner, 6, 4 + inner)):
-                yl[side, plane, pl.ds(at, 1), :] = jnp.where(good, (clo, chi)[side][pl.ds(4 * end + j, 1), :], 0.0)
+            for j, number in enumerate((0, 1, 3, 2)):
+                yl[side, number, pl.ds(at, 1), :] = jnp.where(good, (clo, chi)[side][pl.ds(4 * end + j, 1), :], 0.0)
+
+    def strip_plane(strip, number):
+        return jnp.concatenate([strip[PLANES * tile + number] for tile, _ in tiles], axis=1)
+
+    def beside(side, t, a, un, ut, total, weight, own, above, below):
+        low, high = (t, a, un), own
+        if side == 1:
+            low, high = high, low
+        plus, minus = face(low[1], high[1], low[2], high[2])
+        total = total + (minus * own[0] - plus * t if side == 0 else plus * own[0] - minus * t)
+        weight = weight + (plus + minus)
+        plus, minus = face(from_above(a, above[1]), a, from_above(ut, above[2]), ut)
+        total = total + (plus * from_above(t, above[0]) - minus * t)
+        weight = weight + (plus + minus)
+        plus, minus = face(a, from_below(a, below[1]), ut, from_below(ut, below[2]))
+        total = total + (minus * from_below(t, below[0]) - plus * t)
+        weight = weight + (plus + minus)
+        return t + (2.0 * RELAX_FACTOR) * total * quick_reciprocal(weight)
 
     def batch_factors(first, count, notes):
         a = [as_[first + j] for j in range(count + 2)]
@@ -344,8 +390,8 @@
         for j in range(count):
             row = pl.ds(TILE - 1 + first + j, 1)
             results.append(relaxation(
-                a[j + 1], vs[first + j], ws[first + j], faces[j], faces[j + 1], (yl[0, 3, row, :], yl[0, 5, row, :]),
-                (yl[1, 2, row, :], yl[1, 4, row, :]), *notes[j]))
+                a[j + 1], vs[first + j], ws[first + j], faces[j], faces[j + 1], (yl[0, 1, row, :], yl[0, 2, row, :]),
+                (yl[1, 1, row, :], yl[1, 2, row, :]), *notes[j]))
         return results
 
     def batch_apply(factors, ref, offset, first, rows_above, rows_below):
@@ -356,9 +402,6 @@
             results.append(apply(plane, t[j + 1], t[j], t[j + 2], rows_above[row, :], rows_below[row, :]))
         return results
 
-    def note_of(note):
-        return note, pltpu.roll(note, LANES - 1, 1)
-
     def own_note(i):
         place = (i - 1) * cells_y + row_index((cells_y, LANES))
         return jnp.where(place < rows_total, 2.0, 0.0), pltpu.roll(wall_t[...], LANES + 1 - i, 1)
@@ -368,7 +411,7 @@
     def first_sweep(block, first):
         i = first + pair * block
         factors = batch_factors(i, pair, [own_note(i + j) for j in range(pair)])
-        new = batch_apply(factors, ts, 1, i, yl.at[0, 1], yl.at[1, 0])
+        new = batch_apply(factors, ts, 1, i, yl.at[0, 0], yl.at[1, 0])
         for j in range(pair):
             for number in range(7):
                 cs[number, i + j - 1] = factors[j][number]
@@ -376,10 +419,13 @@
             t1[i + j] = new[j]
         return first
 
-    def halo_plane(i, side):
-        factors = batch_factors(i, 1, [note_of((xlo, xhi)[side][8 * len(tiles)])])
-        (new,) = batch_apply(factors, ts, 1, i, yl.at[0, 1], yl.at[1, 0])
-        t1[i] = jnp.where(flags[side] > 0, new, 0.0)
+    def halo_plane(side):
+        at, inside, row = (1, 2, TILE - 1) if side == 0 else (cells_x + 2, cells_x + 1, TILE + cells_x)
+        strip, row = (xlo, xhi)[side], pl.ds(row, 1)
+        new = beside(side, ts[at], as_[at], us[at], strip_plane(strip, 3), strip_plane(strip, 4), strip_plane(strip, 5),
+                     (ts[inside], as_[inside], us[inside]), [yl[0, number, row, :] for number in range(3)],
+                     [yl[1, number, row, :] for number in range(3)])
+        t1[0 if side == 0 else cells_x + 1] = jnp.where(flags[side] > 0, new, 0.0)
 
     following = 1
     for number, start in enumerate(starts):
@@ -387,34 +433,18 @@
         if number + 2 < len(starts):
             load(starts[number + 2])
         if start == 0:
-            halo_plane(0, 0)
+            halo_plane(0)
         last = cells_x + 1 if start == starts[-1] else start + step - 1
         lax.fori_loop(0, (last - following) // pair, first_sweep, following)
         following = last
-    halo_plane(cells_x + 1, 1)
+    halo_plane(1)
 
     for side, own in enumerate((own_lo, own_hi)):
-        inner = 1 - side
         rows, up, down = pl.ds(TILE, cells_x), pl.ds(TILE - 1, 1), pl.ds(TILE + cells_x, 1)
-
-        def own_plane(plane):
-            return jnp.concatenate([own[8 * tile + plane] for tile, _ in tiles], axis=1)
-
-        t, a, un = yl[side, inner, rows, :], yl[side, 2 + inner, rows, :], yl[side, 4 + inner, rows, :]
-        t_far, a_far, un_far = (yl[side, 1 - inner, rows, :], yl[side, 3 - inner, rows, :],
-                                yl[side, 5 - inner, rows, :])
-        t_own, a_own, un_own = own_plane(side), own_plane(2 + side), own_plane(4 + side)
-        if side == 0:
-            low, high = face(a_far, a, un_far, un), face(a, a_own, un, un_own)
-            t_low, t_high = t_far, t_own
-        else:
-            low, high = face(a_own, a, un_own, un), face(a, a_far, un, un_far)
-            t_low, t_high = t_own, t_far
-        factors = relaxation(
-            a, yl[side, 6, rows, :], yl[side, 7, rows, :], low, high,
-            (yl[side, 2 + inner, up, :], yl[side, 6, up, :]), (yl[side, 2 + inner, down, :], yl[side, 6, down, :]),
-            *note_of((ylo, yhi)[side][8 * len(tiles)]))
-        new = apply(factors, t, t_low, t_high, yl[side, inner, up, :], yl[side, inner, down, :])
+        new = beside(side, *[yl[side, number, rows, :] for number in range(PLANES)],
+                     [strip_plane(own, number) for number in range(3)],
+                     [yl[side, number, up, :] for number in (0, 1, 3)],
+                     [yl[side, number, down, :] for number in (0, 1, 3)])
         yt[side, rows, :] = jnp.where(flags[2 + side] > 0, new, 0.0)
 
     group = 4
@@ -434,36 +464,16 @@
     for start in starts:
         _, plane = lax.fori_loop(0, step // group, second_sweep, (start + 1, plane))
         copies.start("out", ts.at[pl.ds(start, step)], out.at[pl.ds(start, step)])
-    rows_out(cells_x, cells_y, near_rows, route, plane, film_t, pair_out, to_0, to_1, to_2, to_3)
+    film = jnp.zeros((cells_y, LANES), jnp.float32)
+    lane = lane_index(film.shape)
+    for x in range(cells_x):
+        film = jnp.where(lane == x, pltpu.roll(as_[x + 2, :, pl.ds(0, LANES)], x, 1), film)
+    film = jnp.where(lane * cells_y + row_index(film.shape) < rows_total, 2.0 * film, 0.0)
+    rows_out(cells_x, cells_y, near_rows, route, plane, film, pair_out, to_0, to_1, to_2, to_3)
     copies.wait("out")
 
 
-def film_coefficients_kernel(cells_x, cells_y, flags, diff, out, tile, sem):
-    copy = pltpu.make_async_copy(diff.at[:, :, pl.ds(0, LANES)], tile, sem)
-    copy.start()
-    copy.wait()
-    shape = (cells_y, LANES)
-    total = jnp.zeros(shape, jnp.float32)
-    for x in range(cells_x):
-        total = jnp.where(lane_index(shape) == x, pltpu.roll(tile[x], x, 1), total)
-    place = lane_index(shape) * cells_y + row_index(shape)
-    out[...] = jnp.where(place < flags[4], 2.0 * total, 0.0)
-
-
-def film_coefficients(flags, diff):
-    cells_x, cells_y, _ = diff.shape
-    return pl.pallas_call(
-        functools.partial(film_coefficients_kernel, cells_x, cells_y),
-        out_shape=(jax.ShapeDtypeStruct((cells_y, LANES), diff.dtype),),
-        in_specs=[SMEM, HBM],
-        out_specs=(VMEM,),
-        scratch_shapes=[pltpu.VMEM((cells_x, cells_y, LANES), jnp.float32), pltpu.SemaphoreType.DMA],
-        compiler_params=pltpu.CompilerParams(vmem_limit_bytes=VMEM_ALL),
-        cost_estimate=lasts(1),
-    )(flags, diff)
-
-
-def fluid_call(flags, wall_t, strips, route, film_t, near_rows, temp, velo, diff):
+def fluid_call(flags, wall_t, strips, route, near_rows, temp, velo, diff):
     cells_x, cells_y, depth = temp.shape
     chunks = cells_x // TILE
     pair = jax.ShapeDtypeStruct((2, cells_x * cells_y), temp.dtype)
@@ -475,7 +485,7 @@
     return pl.pallas_call(
         functools.partial(fluid_kernel, cells_x, cells_y, depth, near_rows),
         out_shape=(jax.ShapeDtypeStruct(temp.shape, temp.dtype), pair) + (band,) * 4,
-        in_specs=[SMEM] + [VMEM] * 11 + [HBM] * 3,
+        in_specs=[SMEM] + [VMEM] * 10 + [HBM] * 3,
         out_specs=(HBM,) + (VMEM,) * 5,
         scratch_shapes=[
             planes(cells_x + 4),
@@ -484,15 +494,15 @@
             planes(cells_x + 2),
             planes(cells_x + 2),
             planes(cells_x + 2),
-            pltpu.VMEM((2, 8, cells_x + 2 * TILE, depth), jnp.float32),
+            pltpu.VMEM((2, PLANES, cells_x + 2 * TILE, depth), jnp.float32),
             pltpu.VMEM((2, cells_x + 2 * TILE, depth), jnp.float32),
             pltpu.VMEM((7, cells_x, cells_y, depth), jnp.float32),
             pltpu.VMEM((cells_x, cells_y, LANES), jnp.float32),
             pltpu.SemaphoreType.DMA((6 * chunks,)),
         ],
         compiler_params=pltpu.CompilerParams(vmem_limit_bytes=VMEM_FLUID),
-        cost_estimate=lasts(13),
-    )(flags, wall_t, *strips, route, film_t, temp, velo, diff)
+        cost_estimate=lasts(1),
+    )(flags, wall_t, *strips, route, temp, velo, diff)
 
 
 def solid_kernel(
@@ -506,12 +516,17 @@
 
     def load(field):
         src, dst = ((cond, ks), (sink, es), (heat, bs), (temp, us))[field]
+        if layers_of(field, pad) < pad:
+            for x in (0, wide_x - 1):
+                dst[x] = jnp.ones((wide_y, depth), jnp.float32)
         copies.start(field // 2, src, dst.at[own_x, own_y])
         for tile in range(depth // LANES):
             zs, number = pl.ds(tile * LANES, LANES), field * (depth // LANES) + tile
             key, numbers = field // 2, 4 * (depth // LANES)
-            x_from, y_from = pl.ds(number * pad, pad), pl.ds(number * cells_x, cells_x)
-            x_low, x_high = pl.ds(0, pad), pl.ds(pad + cells_x, pad)
+            layers = layers_of(field, pad)
+            x_from = pl.ds(layers_before(field, tile, depth // LANES, pad), layers)
+            y_from = pl.ds(number * cells_x, cells_x)
+            x_low, x_high = pl.ds(pad - layers, layers), pl.ds(pad + cells_x, layers)
             y_low, y_high = pl.ds(0, TILE), pl.ds(TILE + cells_y, TILE)
             copies.start(key, xlo.at[x_from], dst.at[x_low, own_y, zs])
             copies.start(key, xhi.at[x_from], dst.at[x_high, own_y, zs])
@@ -700,7 +715,7 @@
 def rows_out(cells_x, cells_y, near_rows, route, gas_t, film_t, pair, *outs):
     row_total = cells_x * cells_y
     cells = lane_index((1, row_total))
-    film = cell_values(film_t[...], cells_x, cells_y, cells)
+    film = cell_values(film_t, cells_x, cells_y, cells)
     gas = cell_values(gas_t, cells_x, cells_y, cells)
     values = jnp.concatenate([film, gas], axis=0)
     pair[...] = values
@@ -784,10 +799,9 @@
     xlow, xhigh, ylow, yhigh, wall_t = near_step(row_count, wall_prev.reshape(row_total // LANES, LANES), *fluid)
     xlo, xhi = exchange(xlow, xhigh, "blk", ring)
     ylo, yhi = exchange(ylow, yhigh, "sub", chain)
-    after_near = lax.optimization_barrier((xlow, *solids, eddy_diff))[1:]
+    after_near = lax.optimization_barrier((xlow, *solids))[1:]
     strips = solid_strips(after_near[:4], pad)
-    (film_t,) = film_coefficients(flags, after_near[4])
-    xlo, xhi, owners, film_t, *strips = lax.optimization_barrier((xlo, xhi, owner_table, film_t, *strips))
+    xlo, xhi, owners, *strips = lax.optimization_barrier((xlo, xhi, owner_table, *strips))
     blk_halo = exchange(*strips[:2], "blk", ring)
     (route,) = small_call(
         functools.partial(route_kernel, group_total, slot_cap), [(TILE, row_total)], None, owners
@@ -799,7 +813,7 @@
     ylo, yhi, clo, chi, *sub_strips = lax.optimization_barrier((ylo, yhi, clo, chi, *strips[2:]))
     sub_halo = exchange(*sub_strips, "sub", chain)
     fluid_new, pair, *bands = fluid_call(
-        flags, wall_t, (xlo, xhi, ylo, yhi, clo, chi, ylow, yhigh), route, film_t, near_rows, *fluid
+        flags, wall_t, (xlo, xhi, ylo, yhi, clo, chi, ylow, yhigh), route, near_rows, *fluid
     )
     moves = (("blk", 1), ("blk", -1), ("sub", 1), ("sub", -1))
     *bands, blk_low, blk_high = lax.optimization_barrier((*bands, *blk_halo))

time: 119 us -> 117 us (0.983)
  Pallas kernels: 56.2 us -> 53.2 us
    pallas_call x1 -> x0, Pallas kernels: 2.51 us -> none  [film_coefficients(): pl.pallas_call(functools.partial(film_coefficients_kernel, cells_x, cells...]
  transfers between devices with their start and end apart: 24 -> 24, of which waited for: 9 -> 9; matrix products, arithmetic and copies ran while one was open for 1% -> 0% of each run, Pallas kernels for 21% -> 19%
where the time goes in v5:
time: 117 us; the launch traced here: 116 us
  Pallas kernels  53.2 us (45%)
  starting transfers between devices  45.1 us (39%)
  waiting for transfers between devices  15.9 us (14%)
  between operations  1.51 us (1%)
    ppermute x18, starting transfers between devices, ring(): lax.ppermute(value, axis, [(i, (i + step) % count) for i in range(count)])  31.7 us
    pallas_call x1, Pallas kernels, solid_step(): pl.pallas_call(functools.partial(solid_kernel, cells_x, cells_y, depth, p...  24.8 us
    pallas_call x1, Pallas kernels, fluid_call(): pl.pallas_call(functools.partial(fluid_kernel, cells_x, cells_y, depth, n...  15.7 us
    ppermute x6, starting transfers between devices, chain(): return lax.ppermute(value, axis, pairs)  13.3 us
    ppermute x18, waiting for transfers between devices, ring(): lax.ppermute(value, axis, [(i, (i + step) % count) for i in range(count)])  12.6 us
    pallas_call x3, Pallas kernels, packing(): pl.pallas_call(kernel, out_shape=tuple((jax.ShapeDtypeStruct(shape, jnp.f...  4.69 us
    pallas_call x1, Pallas kernels, near_step(): pl.pallas_call(functools.partial(near_kernel, cells_x, cells_y, depth), o...  4.56 us
    pallas_call x4, Pallas kernels, small_call(): pl.pallas_call(kernel, out_shape=tuple((jax.ShapeDtypeStruct(shape, jnp.f...  3.43 us
  transfers between devices with their start and end apart: 24, of which 9 were waited for; matrix products, arithmetic and copies ran while one was open for 0% of the time, Pallas kernels for 19%

profile of v5, /device:TPU:0, one launch (start us, length us, event | category | flops | bytes accessed | tf_op | source)
XLA Modules:
  0.0 116.2 jit_solution(13716150941105822618)
XLA Ops:
  1.3 4.6 %shard_map.130 = (f32[24,32,128]{2,1,0:T(8,128)}, f32[24,32,128]{2,1,0:T(8,128)}, f32[24,32,128]{2,1,0:T(8,128)}, f32[24,32,128]{2,1,0:T(8,128)}, f32[32,128]{1,0:T(8,128)}) custom-call(s32[1]{0:T(128)S(6)} %copy.14.count_ref, f32[8,128]{1,0:T(8,128)} %bitcast.6, f32[32,32,512]{2,1,0:T(8,128)} %temp.4, f32[3,32,32,512]{3,2,1,0:T(8,128)} %velo.3, ...), custom_call_target="tpu_custom_call" | custom-call | bytes 14760000 | tf_op jit(solution)/shard_map/pallas_call | solution.py:193
  6.3 2.9 %collective-permute-start.1 = (f32[24,32,128]{2,1,0:T(8,128)}, f32[24,32,128]{2,1,0:T(8,128)S(1)}, u32[]{:S(2)}, u32[]{:S(2)}) collective-permute-start(f32[24,32,128]{2,1,0:T(8,128)} %get-tuple-element.72), channel_id=1, source_target_pairs={{0,28},{4,0},{8,4},{12,8},{16,12},{20,16},{24,20},{28,24},{1,29},{... | collective-permute-start | bytes 1179656 | tf_op jit(solution)/shard_map/ppermute | solution.py:42
  9.3 4.2 %collective-permute-start.2 = (f32[24,32,128]{2,1,0:T(8,128)}, f32[24,32,128]{2,1,0:T(8,128)S(1)}, u32[]{:S(2)}, u32[]{:S(2)}) collective-permute-start(f32[24,32,128]{2,1,0:T(8,128)} %get-tuple-element.86.own_hi), channel_id=1, source_target_pairs={{0,1},{1,2},{2,3},{4,5},{5,6},{6,7},{8,9},{9,10},{10,11},{12,13},{... | collective-permute-start | bytes 1179656 | tf_op jit(solution)/shard_map/ppermute | solution.py:48
  14.9 4.6 %shard_map.131 = (f32[64,32,128]{2,1,0:T(8,128)}, f32[64,32,128]{2,1,0:T(8,128)}, f32[256,8,128]{2,1,0:T(8,128)}, f32[256,8,128]{2,1,0:T(8,128)}) custom-call(f32[32,32,256]{2,1,0:T(8,128)} %cond.1, f32[32,32,256]{2,1,0:T(8,128)} %sink.1, f32[32,32,256]{2,1,0:T(8,128)} %heat.1, f32[32,32,256]{2,1,0:T(8,128)} %temp.5), custom_call_target="tpu_custom_call" | custom-call | bytes 11070000 | tf_op jit(solution)/shard_map/pallas_call | solution.py:260
  20.0 2.7 %collective-permute-start.4 = (f32[8,512]{1,0:T(8,128)S(1)}, f32[8,512]{1,0:T(8,128)S(1)}, u32[]{:S(2)}, u32[]{:S(2)}) collective-permute-start(f32[8,512]{1,0:T(8,128)S(1)} %get-tuple-element.88), channel_id=1, source_target_pairs={{0,1},{1,2},{2,3},{3,0},{4,5},{5,6},{6,7},{7,4},{8,9},{9,10},{10,1... | collective-permute-start | bytes 49160 | tf_op jit(solution)/shard_map/ppermute | solution.py:42
  22.7 2.1 %collective-permute-start.5 = (f32[8,512]{1,0:T(8,128)S(1)}, f32[8,512]{1,0:T(8,128)S(1)}, u32[]{:S(2)}, u32[]{:S(2)}) collective-permute-start(f32[8,512]{1,0:T(8,128)S(1)} %get-tuple-element.89), channel_id=1, source_target_pairs={{0,3},{1,0},{2,1},{3,2},{4,7},{5,4},{6,5},{7,6},{8,11},{9,8},{10,9... | collective-permute-start | bytes 49160 | tf_op jit(solution)/shard_map/ppermute | solution.py:42
  24.8 2.6 %collective-permute-start.7 = (f32[64,32,128]{2,1,0:T(8,128)}, f32[64,32,128]{2,1,0:T(8,128)S(1)}, u32[]{:S(2)}, u32[]{:S(2)}) collective-permute-start(f32[64,32,128]{2,1,0:T(8,128)} %get-tuple-element.103), channel_id=1, source_target_pairs={{0,28},{4,0},{8,4},{12,8},{16,12},{20,16},{24,20},{28,24},{1,29},{... | collective-permute-start | bytes 3145736 | tf_op jit(solution)/shard_map/ppermute | solution.py:42
  28.2 2.8 %collective-permute-start.8 = (f32[256,8,128]{2,1,0:T(8,128)}, f32[256,8,128]{2,1,0:T(8,128)}, u32[]{:S(2)}, u32[]{:S(2)}) collective-permute-start(f32[256,8,128]{2,1,0:T(8,128)} %get-tuple-element.108), channel_id=1, source_target_pairs={{0,1},{1,2},{2,3},{4,5},{5,6},{6,7},{8,9},{9,10},{10,11},{12,13},{... | collective-permute-start | bytes 3145736 | tf_op jit(solution)/shard_map/ppermute | solution.py:48
  32.5 15.7 %shard_map.134 = (f32[32,32,512]{2,1,0:T(8,128)}, f32[2,1024]{1,0:T(2,128)S(1)}, f32[2,128]{1,0:T(2,128)S(1)}, f32[2,128]{1,0:T(2,128)S(1)}, f32[2,128]{1,0:T(2,128)S(1)}, /*index=5*/f32[2,128]{1,0:T(2,128)S(1)}) custom-call(s32[5]{0:T(128)S(1)} %pad_add_fusion.flags, f32[32,128]{1,0:T(8,128)S(1)} %copy-done.3, f32[24,32,128]{2,1,0:T(8,128)S(1)} %collective-permute-done.xlo, ...), custom_call_target="tpu_custom_call" | custom-call | bytes 3690000 | tf_op jit(solution)/shard_map/pallas_call | solution.py:485
  48.3 2.2 %collective-permute-done.6.xlo = f32[64,32,128]{2,1,0:T(8,128)S(1)} collective-permute-done((f32[64,32,128]{2,1,0:T(8,128)}, f32[64,32,128]{2,1,0:T(8,128)S(1)}, u32[]{:S(2)}, u32[]{:S(2)}) %collective-permute-start.6) | collective-permute-done | bytes 1048608 | tf_op jit(solution)/shard_map/ppermute | solution.py:42
  51.6 1.6 %collective-permute-start.11 = (f32[2,128]{1,0:T(2,128)S(1)}, f32[2,128]{1,0:T(2,128)S(1)}, u32[]{:S(2)}, u32[]{:S(2)}) collective-permute-start(f32[2,128]{1,0:T(2,128)S(1)} %get-tuple-element.113), channel_id=1, source_target_pairs={{0,28},{4,0},{8,4},{12,8},{16,12},{20,16},{24,20},{28,24},{1,29},{... | collective-permute-start | bytes 3080 | tf_op jit(solution)/shard_map/ppermute | solution.py:42
  53.2 3.3 %collective-permute-done.9.yhi = f32[256,8,128]{2,1,0:T(8,128)} collective-permute-done((f32[256,8,128]{2,1,0:T(8,128)}, f32[256,8,128]{2,1,0:T(8,128)}, u32[]{:S(2)}, u32[]{:S(2)}) %collective-permute-start.9) | collective-permute-done | bytes 1048608 | tf_op jit(solution)/shard_map/ppermute | solution.py:48
  57.1 3.2 %collective-permute-start.13 = (f32[2,128]{1,0:T(2,128)S(1)}, f32[2,128]{1,0:T(2,128)S(1)}, u32[]{:S(2)}, u32[]{:S(2)}) collective-permute-start(f32[2,128]{1,0:T(2,128)S(1)} %get-tuple-element.115), channel_id=1, source_target_pairs={{0,3},{1,0},{2,1},{3,2},{4,7},{5,4},{6,5},{7,6},{8,11},{9,8},{10,9... | collective-permute-start | bytes 3080 | tf_op jit(solution)/shard_map/ppermute | solution.py:42
  61.8 2.3 %collective-permute-start.14 = (f32[64,8,128]{2,1,0:T(8,128)S(1)}, f32[64,8,128]{2,1,0:T(8,128)S(1)}, u32[]{:S(2)}, u32[]{:S(2)}) collective-permute-start(f32[64,8,128]{2,1,0:T(8,128)S(1)} %get-tuple-element.118), channel_id=1, source_target_pairs={{0,1},{1,2},{2,3},{4,5},{5,6},{6,7},{8,9},{9,10},{10,11},{12,13},{... | collective-permute-start | bytes 786440 | tf_op jit(solution)/shard_map/ppermute | solution.py:48
  66.5 2.6 %collective-permute-start.17 = (f32[2,32,128]{2,1,0:T(8,128)S(1)}, f32[2,32,128]{2,1,0:T(8,128)S(1)}, u32[]{:S(2)}, u32[]{:S(2)}) collective-permute-start(f32[2,32,128]{2,1,0:T(8,128)S(1)} %get-tuple-element.127), channel_id=1, source_target_pairs={{0,28},{4,0},{8,4},{12,8},{16,12},{20,16},{24,20},{28,24},{1,29},{... | collective-permute-start | bytes 98312 | tf_op jit(solution)/shard_map/ppermute | solution.py:42
  69.2 1.6 %collective-permute-done.16.low = f32[2,32,128]{2,1,0:T(8,128)S(1)} collective-permute-done((f32[2,32,128]{2,1,0:T(8,128)S(1)}, f32[2,32,128]{2,1,0:T(8,128)S(1)}, u32[]{:S(2)}, u32[]{:S(2)}) %collective-permute-start.16) | collective-permute-done | bytes 32800 | tf_op jit(solution)/shard_map/ppermute | solution.py:42
  71.3 2.7 %collective-permute-start.18 = (f32[2,8,128]{2,1,0:T(8,128)S(1)}, f32[2,8,128]{2,1,0:T(8,128)S(1)}, u32[]{:S(2)}, u32[]{:S(2)}) collective-permute-start(f32[2,8,128]{2,1,0:T(8,128)S(1)} %get-tuple-element.129), channel_id=1, source_target_pairs={{0,1},{1,2},{2,3},{3,0},{4,5},{5,6},{6,7},{7,4},{8,9},{9,10},{10,1... | collective-permute-start | bytes 24584 | tf_op jit(solution)/shard_map/ppermute | solution.py:42
  74.0 3.5 %collective-permute-start.19 = (f32[2,8,128]{2,1,0:T(8,128)S(1)}, f32[2,8,128]{2,1,0:T(8,128)S(1)}, u32[]{:S(2)}, u32[]{:S(2)}) collective-permute-start(f32[2,8,128]{2,1,0:T(8,128)S(1)} %get-tuple-element.130), channel_id=1, source_target_pairs={{0,3},{1,0},{2,1},{3,2},{4,7},{5,4},{6,5},{7,6},{8,11},{9,8},{10,9... | collective-permute-start | bytes 24584 | tf_op jit(solution)/shard_map/ppermute | solution.py:42
  77.5 1.6 %collective-permute-done.18.film_lo = f32[2,8,128]{2,1,0:T(8,128)S(1)} collective-permute-done((f32[2,8,128]{2,1,0:T(8,128)S(1)}, f32[2,8,128]{2,1,0:T(8,128)S(1)}, u32[]{:S(2)}, u32[]{:S(2)}) %collective-permute-start.18) | collective-permute-done | bytes 8224 | tf_op jit(solution)/shard_map/ppermute | solution.py:42
  79.1 24.8 %shard_map.138 = (f32[32,32,256]{2,1,0:T(8,128)}, f32[1,1024]{1,0:T(1,128)S(1)}, f32[1,128]{1,0:T(1,128)S(1)}, f32[1,128]{1,0:T(1,128)S(1)}, f32[1,128]{1,0:T(1,128)S(1)}, /*index=5*/f32[1,128]{1,0:T(1,128)S(1)}) custom-call(s32[5]{0:T(128)S(1)} %pad_add_fusion.flags, f32[32,32,256]{2,1,0:T(8,128)} %cond.1, f32[32,32,256]{2,1,0:T(8,128)} %sink.1, ...), custom_call_target="tpu_custom_call" | custom-call | bytes 110700000 | tf_op jit(solution)/shard_map/pallas_call | solution.py:657
  104.0 1.8 %collective-permute-start.20 = (f32[1,128]{1,0:T(1,128)S(1)}, f32[1,128]{1,0:T(1,128)S(1)}, u32[]{:S(2)}, u32[]{:S(2)}) collective-permute-start(f32[1,128]{1,0:T(1,128)S(1)} %get-tuple-element.133), channel_id=1, source_target_pairs={{0,28},{4,0},{8,4},{12,8},{16,12},{20,16},{24,20},{28,24},{1,29},{... | collective-permute-start | bytes 1544 | tf_op jit(solution)/shard_map/ppermute | solution.py:42
  105.8 3.6 %collective-permute-start.22 = (f32[1,128]{1,0:T(1,128)S(1)}, f32[1,128]{1,0:T(1,128)S(1)}, u32[]{:S(2)}, u32[]{:S(2)}) collective-permute-start(f32[1,128]{1,0:T(1,128)S(1)} %get-tuple-element.135), channel_id=1, source_target_pairs={{0,3},{1,0},{2,1},{3,2},{4,7},{5,4},{6,5},{7,6},{8,11},{9,8},{10,9... | collective-permute-start | bytes 1544 | tf_op jit(solution)/shard_map/ppermute | solution.py:42
  110.7 4.0 %collective-permute-done.23.from_3 = f32[1,128]{1,0:T(1,128)S(1)} collective-permute-done((f32[1,128]{1,0:T(1,128)S(1)}, f32[1,128]{1,0:T(1,128)S(1)}, u32[]{:S(2)}, u32[]{:S(2)}) %collective-permute-start.23) | collective-permute-done | bytes 544 | tf_op jit(solution)/shard_map/ppermute | solution.py:42
  114.7 1.4 %shard_map.139 = f32[1,1024]{1,0:T(1,128)} custom-call(s32[5]{0:T(128)S(1)} %pad_add_fusion.flags, f32[8,1024]{1,0:T(8,128)S(1)} %shard_map.132.route, f32[1,1024]{1,0:T(1,128)S(1)} %get-tuple-element.132.own, f32[1,128]{1,0:T(1,128)S(1)} %collective-permute-done.20.from_0, f32[1,128]{1,0:T(1,128)S(1)} %collective-permute-done.21.from_1, ...), custom_call_target="tpu_custom_call" | custom-call | bytes 3690000 | tf_op jit(solution)/shard_map/pallas_call | solution.py:774
  (50 shorter events, 12.1 us)
Async XLA Ops:
  5.8 13.7 %collective-permute-start = (f32[24,32,128]{2,1,0:T(8,128)}, f32[24,32,128]{2,1,0:T(8,128)S(1)}, u32[]{:S(2)}, u32[]{:S(2)}) collective-permute-start(f32[24,32,128]{2,1,0:T(8,128)} %get-tuple-element.71), channel_id=1, source_target_pairs={{0,4},{4,8},{8,12},{12,16},{16,20},{20,24},{24,28},{28,0},{1,5},{5... | collective-permute-start | bytes 1179656 | tf_op jit(solution)/shard_map/ppermute | solution.py:42
  6.3 13.2 %collective-permute-start.1 = (f32[24,32,128]{2,1,0:T(8,128)}, f32[24,32,128]{2,1,0:T(8,128)S(1)}, u32[]{:S(2)}, u32[]{:S(2)}) collective-permute-start(f32[24,32,128]{2,1,0:T(8,128)} %get-tuple-element.72), channel_id=1, source_target_pairs={{0,28},{4,0},{8,4},{12,8},{16,12},{20,16},{24,20},{28,24},{1,29},{... | collective-permute-start | bytes 1179656 | tf_op jit(solution)/shard_map/ppermute | solution.py:42
  9.3 15.5 %collective-permute-start.2 = (f32[24,32,128]{2,1,0:T(8,128)}, f32[24,32,128]{2,1,0:T(8,128)S(1)}, u32[]{:S(2)}, u32[]{:S(2)}) collective-permute-start(f32[24,32,128]{2,1,0:T(8,128)} %get-tuple-element.86.own_hi), channel_id=1, source_target_pairs={{0,1},{1,2},{2,3},{4,5},{5,6},{6,7},{8,9},{9,10},{10,11},{12,13},{... | collective-permute-start | bytes 1179656 | tf_op jit(solution)/shard_map/ppermute | solution.py:48
  13.5 14.0 %collective-permute-start.3 = (f32[24,32,128]{2,1,0:T(8,128)}, f32[24,32,128]{2,1,0:T(8,128)S(1)}, u32[]{:S(2)}, u32[]{:S(2)}) collective-permute-start(f32[24,32,128]{2,1,0:T(8,128)} %get-tuple-element.87.own_lo), channel_id=1, source_target_pairs={{1,0},{2,1},{3,2},{5,4},{6,5},{7,6},{9,8},{10,9},{11,10},{13,12},{... | collective-permute-start | bytes 1179656 | tf_op jit(solution)/shard_map/ppermute | solution.py:48
  20.0 7.9 %collective-permute-start.4 = (f32[8,512]{1,0:T(8,128)S(1)}, f32[8,512]{1,0:T(8,128)S(1)}, u32[]{:S(2)}, u32[]{:S(2)}) collective-permute-start(f32[8,512]{1,0:T(8,128)S(1)} %get-tuple-element.88), channel_id=1, source_target_pairs={{0,1},{1,2},{2,3},{3,0},{4,5},{5,6},{6,7},{7,4},{8,9},{9,10},{10,1... | collective-permute-start | bytes 49160 | tf_op jit(solution)/shard_map/ppermute | solution.py:42
  22.7 5.3 %collective-permute-start.5 = (f32[8,512]{1,0:T(8,128)S(1)}, f32[8,512]{1,0:T(8,128)S(1)}, u32[]{:S(2)}, u32[]{:S(2)}) collective-permute-start(f32[8,512]{1,0:T(8,128)S(1)} %get-tuple-element.89), channel_id=1, source_target_pairs={{0,3},{1,0},{2,1},{3,2},{4,7},{5,4},{6,5},{7,6},{8,11},{9,8},{10,9... | collective-permute-start | bytes 49160 | tf_op jit(solution)/shard_map/ppermute | solution.py:42
  24.8 25.6 %collective-permute-start.6 = (f32[64,32,128]{2,1,0:T(8,128)}, f32[64,32,128]{2,1,0:T(8,128)S(1)}, u32[]{:S(2)}, u32[]{:S(2)}) collective-permute-start(f32[64,32,128]{2,1,0:T(8,128)} %get-tuple-element.102), channel_id=1, source_target_pairs={{0,4},{4,8},{8,12},{12,16},{16,20},{20,24},{24,28},{28,0},{1,5},{5... | collective-permute-start | bytes 3145736 | tf_op jit(solution)/shard_map/ppermute | solution.py:42
  24.8 25.6 %collective-permute-start.7 = (f32[64,32,128]{2,1,0:T(8,128)}, f32[64,32,128]{2,1,0:T(8,128)S(1)}, u32[]{:S(2)}, u32[]{:S(2)}) collective-permute-start(f32[64,32,128]{2,1,0:T(8,128)} %get-tuple-element.103), channel_id=1, source_target_pairs={{0,28},{4,0},{8,4},{12,8},{16,12},{20,16},{24,20},{28,24},{1,29},{... | collective-permute-start | bytes 3145736 | tf_op jit(solution)/shard_map/ppermute | solution.py:42
  28.2 24.9 %collective-permute-start.8 = (f32[256,8,128]{2,1,0:T(8,128)}, f32[256,8,128]{2,1,0:T(8,128)}, u32[]{:S(2)}, u32[]{:S(2)}) collective-permute-start(f32[256,8,128]{2,1,0:T(8,128)} %get-tuple-element.108), channel_id=1, source_target_pairs={{0,1},{1,2},{2,3},{4,5},{5,6},{6,7},{8,9},{9,10},{10,11},{12,13},{... | collective-permute-start | bytes 3145736 | tf_op jit(solution)/shard_map/ppermute | solution.py:48
  31.1 25.4 %collective-permute-start.9 = (f32[256,8,128]{2,1,0:T(8,128)}, f32[256,8,128]{2,1,0:T(8,128)}, u32[]{:S(2)}, u32[]{:S(2)}) collective-permute-start(f32[256,8,128]{2,1,0:T(8,128)} %get-tuple-element.109), channel_id=1, source_target_pairs={{1,0},{2,1},{3,2},{5,4},{6,5},{7,6},{9,8},{10,9},{11,10},{13,12},{... | collective-permute-start | bytes 3145736 | tf_op jit(solution)/shard_map/ppermute | solution.py:48
  50.5 9.9 %collective-permute-start.10 = (f32[2,128]{1,0:T(2,128)S(1)}, f32[2,128]{1,0:T(2,128)S(1)}, u32[]{:S(2)}, u32[]{:S(2)}) collective-permute-start(f32[2,128]{1,0:T(2,128)S(1)} %get-tuple-element.112), channel_id=1, source_target_pairs={{0,4},{4,8},{8,12},{12,16},{16,20},{20,24},{24,28},{28,0},{1,5},{5... | collective-permute-start | bytes 3080 | tf_op jit(solution)/shard_map/ppermute | solution.py:42
  51.6 8.9 %collective-permute-start.11 = (f32[2,128]{1,0:T(2,128)S(1)}, f32[2,128]{1,0:T(2,128)S(1)}, u32[]{:S(2)}, u32[]{:S(2)}) collective-permute-start(f32[2,128]{1,0:T(2,128)S(1)} %get-tuple-element.113), channel_id=1, source_target_pairs={{0,28},{4,0},{8,4},{12,8},{16,12},{20,16},{24,20},{28,24},{1,29},{... | collective-permute-start | bytes 3080 | tf_op jit(solution)/shard_map/ppermute | solution.py:42
  56.5 5.4 %collective-permute-start.12 = (f32[2,128]{1,0:T(2,128)S(1)}, f32[2,128]{1,0:T(2,128)S(1)}, u32[]{:S(2)}, u32[]{:S(2)}) collective-permute-start(f32[2,128]{1,0:T(2,128)S(1)} %get-tuple-element.114), channel_id=1, source_target_pairs={{0,1},{1,2},{2,3},{3,0},{4,5},{5,6},{6,7},{7,4},{8,9},{9,10},{10,1... | collective-permute-start | bytes 3080 | tf_op jit(solution)/shard_map/ppermute | solution.py:42
  57.1 4.8 %collective-permute-start.13 = (f32[2,128]{1,0:T(2,128)S(1)}, f32[2,128]{1,0:T(2,128)S(1)}, u32[]{:S(2)}, u32[]{:S(2)}) collective-permute-start(f32[2,128]{1,0:T(2,128)S(1)} %get-tuple-element.115), channel_id=1, source_target_pairs={{0,3},{1,0},{2,1},{3,2},{4,7},{5,4},{6,5},{7,6},{8,11},{9,8},{10,9... | collective-permute-start | bytes 3080 | tf_op jit(solution)/shard_map/ppermute | solution.py:42
  61.8 17.3 %collective-permute-start.14 = (f32[64,8,128]{2,1,0:T(8,128)S(1)}, f32[64,8,128]{2,1,0:T(8,128)S(1)}, u32[]{:S(2)}, u32[]{:S(2)}) collective-permute-start(f32[64,8,128]{2,1,0:T(8,128)S(1)} %get-tuple-element.118), channel_id=1, source_target_pairs={{0,1},{1,2},{2,3},{4,5},{5,6},{6,7},{8,9},{9,10},{10,11},{12,13},{... | collective-permute-start | bytes 786440 | tf_op jit(solution)/shard_map/ppermute | solution.py:48
  64.2 14.9 %collective-permute-start.15 = (f32[64,8,128]{2,1,0:T(8,128)S(1)}, f32[64,8,128]{2,1,0:T(8,128)S(1)}, u32[]{:S(2)}, u32[]{:S(2)}) collective-permute-start(f32[64,8,128]{2,1,0:T(8,128)S(1)} %get-tuple-element.119), channel_id=1, source_target_pairs={{1,0},{2,1},{3,2},{5,4},{6,5},{7,6},{9,8},{10,9},{11,10},{13,12},{... | collective-permute-start | bytes 786440 | tf_op jit(solution)/shard_map/ppermute | solution.py:48
  66.5 4.3 %collective-permute-start.16 = (f32[2,32,128]{2,1,0:T(8,128)S(1)}, f32[2,32,128]{2,1,0:T(8,128)S(1)}, u32[]{:S(2)}, u32[]{:S(2)}) collective-permute-start(f32[2,32,128]{2,1,0:T(8,128)S(1)} %get-tuple-element.126), channel_id=1, source_target_pairs={{0,4},{4,8},{8,12},{12,16},{16,20},{20,24},{24,28},{28,0},{1,5},{5... | collective-permute-start | bytes 98312 | tf_op jit(solution)/shard_map/ppermute | solution.py:42
  66.5 4.2 %collective-permute-start.17 = (f32[2,32,128]{2,1,0:T(8,128)S(1)}, f32[2,32,128]{2,1,0:T(8,128)S(1)}, u32[]{:S(2)}, u32[]{:S(2)}) collective-permute-start(f32[2,32,128]{2,1,0:T(8,128)S(1)} %get-tuple-element.127), channel_id=1, source_target_pairs={{0,28},{4,0},{8,4},{12,8},{16,12},{20,16},{24,20},{28,24},{1,29},{... | collective-permute-start | bytes 98312 | tf_op jit(solution)/shard_map/ppermute | solution.py:42
  71.3 7.8 %collective-permute-start.18 = (f32[2,8,128]{2,1,0:T(8,128)S(1)}, f32[2,8,128]{2,1,0:T(8,128)S(1)}, u32[]{:S(2)}, u32[]{:S(2)}) collective-permute-start(f32[2,8,128]{2,1,0:T(8,128)S(1)} %get-tuple-element.129), channel_id=1, source_target_pairs={{0,1},{1,2},{2,3},{3,0},{4,5},{5,6},{6,7},{7,4},{8,9},{9,10},{10,1... | collective-permute-start | bytes 24584 | tf_op jit(solution)/shard_map/ppermute | solution.py:42
  74.0 5.1 %collective-permute-start.19 = (f32[2,8,128]{2,1,0:T(8,128)S(1)}, f32[2,8,128]{2,1,0:T(8,128)S(1)}, u32[]{:S(2)}, u32[]{:S(2)}) collective-permute-start(f32[2,8,128]{2,1,0:T(8,128)S(1)} %get-tuple-element.130), channel_id=1, source_target_pairs={{0,3},{1,0},{2,1},{3,2},{4,7},{5,4},{6,5},{7,6},{8,11},{9,8},{10,9... | collective-permute-start | bytes 24584 | tf_op jit(solution)/shard_map/ppermute | solution.py:42
  104.0 5.4 %collective-permute-start.20 = (f32[1,128]{1,0:T(1,128)S(1)}, f32[1,128]{1,0:T(1,128)S(1)}, u32[]{:S(2)}, u32[]{:S(2)}) collective-permute-start(f32[1,128]{1,0:T(1,128)S(1)} %get-tuple-element.133), channel_id=1, source_target_pairs={{0,28},{4,0},{8,4},{12,8},{16,12},{20,16},{24,20},{28,24},{1,29},{... | collective-permute-start | bytes 1544 | tf_op jit(solution)/shard_map/ppermute | solution.py:42
  105.8 3.9 %collective-permute-start.21 = (f32[1,128]{1,0:T(1,128)S(1)}, f32[1,128]{1,0:T(1,128)S(1)}, u32[]{:S(2)}, u32[]{:S(2)}) collective-permute-start(f32[1,128]{1,0:T(1,128)S(1)} %get-tuple-element.134), channel_id=1, source_target_pairs={{0,4},{4,8},{8,12},{12,16},{16,20},{20,24},{24,28},{28,0},{1,5},{5... | collective-permute-start | bytes 1544 | tf_op jit(solution)/shard_map/ppermute | solution.py:42
  105.8 4.9 %collective-permute-start.22 = (f32[1,128]{1,0:T(1,128)S(1)}, f32[1,128]{1,0:T(1,128)S(1)}, u32[]{:S(2)}, u32[]{:S(2)}) collective-permute-start(f32[1,128]{1,0:T(1,128)S(1)} %get-tuple-element.135), channel_id=1, source_target_pairs={{0,3},{1,0},{2,1},{3,2},{4,7},{5,4},{6,5},{7,6},{8,11},{9,8},{10,9... | collective-permute-start | bytes 1544 | tf_op jit(solution)/shard_map/ppermute | solution.py:42
  109.4 5.3 %collective-permute-start.23 = (f32[1,128]{1,0:T(1,128)S(1)}, f32[1,128]{1,0:T(1,128)S(1)}, u32[]{:S(2)}, u32[]{:S(2)}) collective-permute-start(f32[1,128]{1,0:T(1,128)S(1)} %get-tuple-element.136), channel_id=1, source_target_pairs={{0,1},{1,2},{2,3},{3,0},{4,5},{5,6},{6,7},{7,4},{8,9},{9,10},{10,1... | collective-permute-start | bytes 1544 | tf_op jit(solution)/shard_map/ppermute | solution.py:42
  (7 other events, 108.1 us)

commit v6 on v5

--- a/solution.py
+++ b/solution.py
@@ -588,7 +588,7 @@
             for j in range(pad):
                 ks[side * (pad + cells_x) + j] = jnp.zeros((wide_y, depth), jnp.float32)
 
-    lax.fori_loop(0, wide_x, conductances, 0, unroll=4)
+    lax.fori_loop(0, wide_x, conductances, 0, unroll=6)
 
     def scale(x, carry):
         follow = jnp.minimum(x + 1, wide_x - 1)
@@ -601,7 +601,7 @@
         return carry
 
     copies.wait(1)
-    lax.fori_loop(0, wide_x, scale, 0, unroll=4)
+    lax.fori_loop(0, wide_x, scale, 0, unroll=8)
 
     total = len(coefficients)
     src, dst = us, vs
@@ -832,7 +832,8 @@
     )
     films = (film, ring(last, "sub", 1), ring(first, "sub", -1))
     solid_new, own, *backs = solid_step(flags, *solids, halo, films, landing_cell, row_total, near_rows, pad)
-    returned = [ring(back, axis, -step) for back, (axis, step) in zip(backs, moves)]
+    returned = {d: ring(backs[d], moves[d][0], -moves[d][1]) for d in (2, 3, 0, 1)}
+    returned = [returned[d] for d in range(4)]
     (wall_new,) = small_call(
         functools.partial(wall_kernel, near_rows), [(1, row_total)], flags, route, own, *returned
     )

time: 117 us -> 116 us (level)
  no operation moved by 1% of the time
where the time goes in v6:
time: 116 us
  Pallas kernels  52.7 us (45%)
  starting transfers between devices  45.1 us (39%)
  waiting for transfers between devices  15.9 us (14%)
  between operations  1.51 us (1%)
    ppermute x18, starting transfers between devices, ring(): lax.ppermute(value, axis, [(i, (i + step) % count) for i in range(count)])  31.7 us
    pallas_call x1, Pallas kernels, solid_step(): pl.pallas_call(functools.partial(solid_kernel, cells_x, cells_y, depth, p...  24.3 us
    pallas_call x1, Pallas kernels, fluid_call(): pl.pallas_call(functools.partial(fluid_kernel, cells_x, cells_y, depth, n...  15.7 us
    ppermute x6, starting transfers between devices, chain(): return lax.ppermute(value, axis, pairs)  13.3 us
    ppermute x18, waiting for transfers between devices, ring(): lax.ppermute(value, axis, [(i, (i + step) % count) for i in range(count)])  12.6 us
    pallas_call x3, Pallas kernels, packing(): pl.pallas_call(kernel, out_shape=tuple((jax.ShapeDtypeStruct(shape, jnp.f...  4.69 us
    pallas_call x1, Pallas kernels, near_step(): pl.pallas_call(functools.partial(near_kernel, cells_x, cells_y, depth), o...  4.56 us
    pallas_call x4, Pallas kernels, small_call(): pl.pallas_call(kernel, out_shape=tuple((jax.ShapeDtypeStruct(shape, jnp.f...  3.43 us
  transfers between devices with their start and end apart: 24, of which 9 were waited for; matrix products, arithmetic and copies ran while one was open for 0% of the time, Pallas kernels for 19%

profile of v6, /device:TPU:0, one launch (start us, length us, event | category | flops | bytes accessed | tf_op | source)
XLA Modules:
  0.0 115.6 jit_solution(9797364215861858707)
XLA Ops:
  1.3 4.6 %shard_map.130 = (f32[24,32,128]{2,1,0:T(8,128)}, f32[24,32,128]{2,1,0:T(8,128)}, f32[24,32,128]{2,1,0:T(8,128)}, f32[24,32,128]{2,1,0:T(8,128)}, f32[32,128]{1,0:T(8,128)}) custom-call(s32[1]{0:T(128)S(6)} %copy.14.count_ref, f32[8,128]{1,0:T(8,128)} %bitcast.6, f32[32,32,512]{2,1,0:T(8,128)} %temp.4, f32[3,32,32,512]{3,2,1,0:T(8,128)} %velo.3, ...), custom_call_target="tpu_custom_call" | custom-call | bytes 14760000 | tf_op jit(solution)/shard_map/pallas_call | solution.py:193
  6.3 2.9 %collective-permute-start.1 = (f32[24,32,128]{2,1,0:T(8,128)}, f32[24,32,128]{2,1,0:T(8,128)S(1)}, u32[]{:S(2)}, u32[]{:S(2)}) collective-permute-start(f32[24,32,128]{2,1,0:T(8,128)} %get-tuple-element.72), channel_id=1, source_target_pairs={{0,28},{4,0},{8,4},{12,8},{16,12},{20,16},{24,20},{28,24},{1,29},{... | collective-permute-start | bytes 1179656 | tf_op jit(solution)/shard_map/ppermute | solution.py:42
  9.3 4.2 %collective-permute-start.2 = (f32[24,32,128]{2,1,0:T(8,128)}, f32[24,32,128]{2,1,0:T(8,128)S(1)}, u32[]{:S(2)}, u32[]{:S(2)}) collective-permute-start(f32[24,32,128]{2,1,0:T(8,128)} %get-tuple-element.86.own_hi), channel_id=1, source_target_pairs={{0,1},{1,2},{2,3},{4,5},{5,6},{6,7},{8,9},{9,10},{10,11},{12,13},{... | collective-permute-start | bytes 1179656 | tf_op jit(solution)/shard_map/ppermute | solution.py:48
  14.9 4.6 %shard_map.131 = (f32[64,32,128]{2,1,0:T(8,128)}, f32[64,32,128]{2,1,0:T(8,128)}, f32[256,8,128]{2,1,0:T(8,128)}, f32[256,8,128]{2,1,0:T(8,128)}) custom-call(f32[32,32,256]{2,1,0:T(8,128)} %cond.1, f32[32,32,256]{2,1,0:T(8,128)} %sink.1, f32[32,32,256]{2,1,0:T(8,128)} %heat.1, f32[32,32,256]{2,1,0:T(8,128)} %temp.5), custom_call_target="tpu_custom_call" | custom-call | bytes 11070000 | tf_op jit(solution)/shard_map/pallas_call | solution.py:260
  20.0 2.7 %collective-permute-start.4 = (f32[8,512]{1,0:T(8,128)S(1)}, f32[8,512]{1,0:T(8,128)S(1)}, u32[]{:S(2)}, u32[]{:S(2)}) collective-permute-start(f32[8,512]{1,0:T(8,128)S(1)} %get-tuple-element.88), channel_id=1, source_target_pairs={{0,1},{1,2},{2,3},{3,0},{4,5},{5,6},{6,7},{7,4},{8,9},{9,10},{10,1... | collective-permute-start | bytes 49160 | tf_op jit(solution)/shard_map/ppermute | solution.py:42
  22.7 2.1 %collective-permute-start.5 = (f32[8,512]{1,0:T(8,128)S(1)}, f32[8,512]{1,0:T(8,128)S(1)}, u32[]{:S(2)}, u32[]{:S(2)}) collective-permute-start(f32[8,512]{1,0:T(8,128)S(1)} %get-tuple-element.89), channel_id=1, source_target_pairs={{0,3},{1,0},{2,1},{3,2},{4,7},{5,4},{6,5},{7,6},{8,11},{9,8},{10,9... | collective-permute-start | bytes 49160 | tf_op jit(solution)/shard_map/ppermute | solution.py:42
  24.8 2.6 %collective-permute-start.7 = (f32[64,32,128]{2,1,0:T(8,128)}, f32[64,32,128]{2,1,0:T(8,128)S(1)}, u32[]{:S(2)}, u32[]{:S(2)}) collective-permute-start(f32[64,32,128]{2,1,0:T(8,128)} %get-tuple-element.103), channel_id=1, source_target_pairs={{0,28},{4,0},{8,4},{12,8},{16,12},{20,16},{24,20},{28,24},{1,29},{... | collective-permute-start | bytes 3145736 | tf_op jit(solution)/shard_map/ppermute | solution.py:42
  28.2 2.8 %collective-permute-start.8 = (f32[256,8,128]{2,1,0:T(8,128)}, f32[256,8,128]{2,1,0:T(8,128)}, u32[]{:S(2)}, u32[]{:S(2)}) collective-permute-start(f32[256,8,128]{2,1,0:T(8,128)} %get-tuple-element.108), channel_id=1, source_target_pairs={{0,1},{1,2},{2,3},{4,5},{5,6},{6,7},{8,9},{9,10},{10,11},{12,13},{... | collective-permute-start | bytes 3145736 | tf_op jit(solution)/shard_map/ppermute | solution.py:48
  32.5 15.7 %shard_map.134 = (f32[32,32,512]{2,1,0:T(8,128)}, f32[2,1024]{1,0:T(2,128)S(1)}, f32[2,128]{1,0:T(2,128)S(1)}, f32[2,128]{1,0:T(2,128)S(1)}, f32[2,128]{1,0:T(2,128)S(1)}, /*index=5*/f32[2,128]{1,0:T(2,128)S(1)}) custom-call(s32[5]{0:T(128)S(1)} %pad_add_fusion.flags, f32[32,128]{1,0:T(8,128)S(1)} %copy-done.3, f32[24,32,128]{2,1,0:T(8,128)S(1)} %collective-permute-done.xlo, ...), custom_call_target="tpu_custom_call" | custom-call | bytes 3690000 | tf_op jit(solution)/shard_map/pallas_call | solution.py:485
  48.3 2.2 %collective-permute-done.6.xlo = f32[64,32,128]{2,1,0:T(8,128)S(1)} collective-permute-done((f32[64,32,128]{2,1,0:T(8,128)}, f32[64,32,128]{2,1,0:T(8,128)S(1)}, u32[]{:S(2)}, u32[]{:S(2)}) %collective-permute-start.6) | collective-permute-done | bytes 1048608 | tf_op jit(solution)/shard_map/ppermute | solution.py:42
  51.6 1.6 %collective-permute-start.11 = (f32[2,128]{1,0:T(2,128)S(1)}, f32[2,128]{1,0:T(2,128)S(1)}, u32[]{:S(2)}, u32[]{:S(2)}) collective-permute-start(f32[2,128]{1,0:T(2,128)S(1)} %get-tuple-element.113), channel_id=1, source_target_pairs={{0,28},{4,0},{8,4},{12,8},{16,12},{20,16},{24,20},{28,24},{1,29},{... | collective-permute-start | bytes 3080 | tf_op jit(solution)/shard_map/ppermute | solution.py:42
  53.2 3.3 %collective-permute-done.9.yhi = f32[256,8,128]{2,1,0:T(8,128)} collective-permute-done((f32[256,8,128]{2,1,0:T(8,128)}, f32[256,8,128]{2,1,0:T(8,128)}, u32[]{:S(2)}, u32[]{:S(2)}) %collective-permute-start.9) | collective-permute-done | bytes 1048608 | tf_op jit(solution)/shard_map/ppermute | solution.py:48
  57.1 3.2 %collective-permute-start.13 = (f32[2,128]{1,0:T(2,128)S(1)}, f32[2,128]{1,0:T(2,128)S(1)}, u32[]{:S(2)}, u32[]{:S(2)}) collective-permute-start(f32[2,128]{1,0:T(2,128)S(1)} %get-tuple-element.115), channel_id=1, source_target_pairs={{0,3},{1,0},{2,1},{3,2},{4,7},{5,4},{6,5},{7,6},{8,11},{9,8},{10,9... | collective-permute-start | bytes 3080 | tf_op jit(solution)/shard_map/ppermute | solution.py:42
  61.8 2.3 %collective-permute-start.14 = (f32[64,8,128]{2,1,0:T(8,128)S(1)}, f32[64,8,128]{2,1,0:T(8,128)S(1)}, u32[]{:S(2)}, u32[]{:S(2)}) collective-permute-start(f32[64,8,128]{2,1,0:T(8,128)S(1)} %get-tuple-element.118), channel_id=1, source_target_pairs={{0,1},{1,2},{2,3},{4,5},{5,6},{6,7},{8,9},{9,10},{10,11},{12,13},{... | collective-permute-start | bytes 786440 | tf_op jit(solution)/shard_map/ppermute | solution.py:48
  66.5 2.6 %collective-permute-start.17 = (f32[2,32,128]{2,1,0:T(8,128)S(1)}, f32[2,32,128]{2,1,0:T(8,128)S(1)}, u32[]{:S(2)}, u32[]{:S(2)}) collective-permute-start(f32[2,32,128]{2,1,0:T(8,128)S(1)} %get-tuple-element.127), channel_id=1, source_target_pairs={{0,28},{4,0},{8,4},{12,8},{16,12},{20,16},{24,20},{28,24},{1,29},{... | collective-permute-start | bytes 98312 | tf_op jit(solution)/shard_map/ppermute | solution.py:42
  69.2 1.6 %collective-permute-done.16.low = f32[2,32,128]{2,1,0:T(8,128)S(1)} collective-permute-done((f32[2,32,128]{2,1,0:T(8,128)S(1)}, f32[2,32,128]{2,1,0:T(8,128)S(1)}, u32[]{:S(2)}, u32[]{:S(2)}) %collective-permute-start.16) | collective-permute-done | bytes 32800 | tf_op jit(solution)/shard_map/ppermute | solution.py:42
  71.3 2.7 %collective-permute-start.18 = (f32[2,8,128]{2,1,0:T(8,128)S(1)}, f32[2,8,128]{2,1,0:T(8,128)S(1)}, u32[]{:S(2)}, u32[]{:S(2)}) collective-permute-start(f32[2,8,128]{2,1,0:T(8,128)S(1)} %get-tuple-element.129), channel_id=1, source_target_pairs={{0,1},{1,2},{2,3},{3,0},{4,5},{5,6},{6,7},{7,4},{8,9},{9,10},{10,1... | collective-permute-start | bytes 24584 | tf_op jit(solution)/shard_map/ppermute | solution.py:42
  74.0 3.5 %collective-permute-start.19 = (f32[2,8,128]{2,1,0:T(8,128)S(1)}, f32[2,8,128]{2,1,0:T(8,128)S(1)}, u32[]{:S(2)}, u32[]{:S(2)}) collective-permute-start(f32[2,8,128]{2,1,0:T(8,128)S(1)} %get-tuple-element.130), channel_id=1, source_target_pairs={{0,3},{1,0},{2,1},{3,2},{4,7},{5,4},{6,5},{7,6},{8,11},{9,8},{10,9... | collective-permute-start | bytes 24584 | tf_op jit(solution)/shard_map/ppermute | solution.py:42
  77.5 1.6 %collective-permute-done.18.film_lo = f32[2,8,128]{2,1,0:T(8,128)S(1)} collective-permute-done((f32[2,8,128]{2,1,0:T(8,128)S(1)}, f32[2,8,128]{2,1,0:T(8,128)S(1)}, u32[]{:S(2)}, u32[]{:S(2)}) %collective-permute-start.18) | collective-permute-done | bytes 8224 | tf_op jit(solution)/shard_map/ppermute | solution.py:42
  79.1 24.3 %shard_map.138 = (f32[32,32,256]{2,1,0:T(8,128)}, f32[1,1024]{1,0:T(1,128)S(1)}, f32[1,128]{1,0:T(1,128)S(1)}, f32[1,128]{1,0:T(1,128)S(1)}, f32[1,128]{1,0:T(1,128)S(1)}, /*index=5*/f32[1,128]{1,0:T(1,128)S(1)}) custom-call(s32[5]{0:T(128)S(1)} %pad_add_fusion.flags, f32[32,32,256]{2,1,0:T(8,128)} %cond.1, f32[32,32,256]{2,1,0:T(8,128)} %sink.1, ...), custom_call_target="tpu_custom_call" | custom-call | bytes 110700000 | tf_op jit(solution)/shard_map/pallas_call | solution.py:657
  103.4 1.8 %collective-permute-start.20 = (f32[1,128]{1,0:T(1,128)S(1)}, f32[1,128]{1,0:T(1,128)S(1)}, u32[]{:S(2)}, u32[]{:S(2)}) collective-permute-start(f32[1,128]{1,0:T(1,128)S(1)} %get-tuple-element.133), channel_id=1, source_target_pairs={{0,28},{4,0},{8,4},{12,8},{16,12},{20,16},{24,20},{28,24},{1,29},{... | collective-permute-start | bytes 1544 | tf_op jit(solution)/shard_map/ppermute | solution.py:42
  105.3 3.6 %collective-permute-start.22 = (f32[1,128]{1,0:T(1,128)S(1)}, f32[1,128]{1,0:T(1,128)S(1)}, u32[]{:S(2)}, u32[]{:S(2)}) collective-permute-start(f32[1,128]{1,0:T(1,128)S(1)} %get-tuple-element.135), channel_id=1, source_target_pairs={{0,3},{1,0},{2,1},{3,2},{4,7},{5,4},{6,5},{7,6},{8,11},{9,8},{10,9... | collective-permute-start | bytes 1544 | tf_op jit(solution)/shard_map/ppermute | solution.py:42
  110.1 4.0 %collective-permute-done.23.from_3 = f32[1,128]{1,0:T(1,128)S(1)} collective-permute-done((f32[1,128]{1,0:T(1,128)S(1)}, f32[1,128]{1,0:T(1,128)S(1)}, u32[]{:S(2)}, u32[]{:S(2)}) %collective-permute-start.23) | collective-permute-done | bytes 544 | tf_op jit(solution)/shard_map/ppermute | solution.py:42
  114.2 1.4 %shard_map.139 = f32[1,1024]{1,0:T(1,128)} custom-call(s32[5]{0:T(128)S(1)} %pad_add_fusion.flags, f32[8,1024]{1,0:T(8,128)S(1)} %shard_map.132.route, f32[1,1024]{1,0:T(1,128)S(1)} %get-tuple-element.132.own, f32[1,128]{1,0:T(1,128)S(1)} %collective-permute-done.20.from_0, f32[1,128]{1,0:T(1,128)S(1)} %collective-permute-done.21.from_1, ...), custom_call_target="tpu_custom_call" | custom-call | bytes 3690000 | tf_op jit(solution)/shard_map/pallas_call | solution.py:774
  (50 shorter events, 12.1 us)
Async XLA Ops:
  5.8 13.7 %collective-permute-start = (f32[24,32,128]{2,1,0:T(8,128)}, f32[24,32,128]{2,1,0:T(8,128)S(1)}, u32[]{:S(2)}, u32[]{:S(2)}) collective-permute-start(f32[24,32,128]{2,1,0:T(8,128)} %get-tuple-element.71), channel_id=1, source_target_pairs={{0,4},{4,8},{8,12},{12,16},{16,20},{20,24},{24,28},{28,0},{1,5},{5... | collective-permute-start | bytes 1179656 | tf_op jit(solution)/shard_map/ppermute | solution.py:42
  6.3 13.2 %collective-permute-start.1 = (f32[24,32,128]{2,1,0:T(8,128)}, f32[24,32,128]{2,1,0:T(8,128)S(1)}, u32[]{:S(2)}, u32[]{:S(2)}) collective-permute-start(f32[24,32,128]{2,1,0:T(8,128)} %get-tuple-element.72), channel_id=1, source_target_pairs={{0,28},{4,0},{8,4},{12,8},{16,12},{20,16},{24,20},{28,24},{1,29},{... | collective-permute-start | bytes 1179656 | tf_op jit(solution)/shard_map/ppermute | solution.py:42
  9.3 15.5 %collective-permute-start.2 = (f32[24,32,128]{2,1,0:T(8,128)}, f32[24,32,128]{2,1,0:T(8,128)S(1)}, u32[]{:S(2)}, u32[]{:S(2)}) collective-permute-start(f32[24,32,128]{2,1,0:T(8,128)} %get-tuple-element.86.own_hi), channel_id=1, source_target_pairs={{0,1},{1,2},{2,3},{4,5},{5,6},{6,7},{8,9},{9,10},{10,11},{12,13},{... | collective-permute-start | bytes 1179656 | tf_op jit(solution)/shard_map/ppermute | solution.py:48
  13.5 14.0 %collective-permute-start.3 = (f32[24,32,128]{2,1,0:T(8,128)}, f32[24,32,128]{2,1,0:T(8,128)S(1)}, u32[]{:S(2)}, u32[]{:S(2)}) collective-permute-start(f32[24,32,128]{2,1,0:T(8,128)} %get-tuple-element.87.own_lo), channel_id=1, source_target_pairs={{1,0},{2,1},{3,2},{5,4},{6,5},{7,6},{9,8},{10,9},{11,10},{13,12},{... | collective-permute-start | bytes 1179656 | tf_op jit(solution)/shard_map/ppermute | solution.py:48
  20.0 7.9 %collective-permute-start.4 = (f32[8,512]{1,0:T(8,128)S(1)}, f32[8,512]{1,0:T(8,128)S(1)}, u32[]{:S(2)}, u32[]{:S(2)}) collective-permute-start(f32[8,512]{1,0:T(8,128)S(1)} %get-tuple-element.88), channel_id=1, source_target_pairs={{0,1},{1,2},{2,3},{3,0},{4,5},{5,6},{6,7},{7,4},{8,9},{9,10},{10,1... | collective-permute-start | bytes 49160 | tf_op jit(solution)/shard_map/ppermute | solution.py:42
  22.7 5.3 %collective-permute-start.5 = (f32[8,512]{1,0:T(8,128)S(1)}, f32[8,512]{1,0:T(8,128)S(1)}, u32[]{:S(2)}, u32[]{:S(2)}) collective-permute-start(f32[8,512]{1,0:T(8,128)S(1)} %get-tuple-element.89), channel_id=1, source_target_pairs={{0,3},{1,0},{2,1},{3,2},{4,7},{5,4},{6,5},{7,6},{8,11},{9,8},{10,9... | collective-permute-start | bytes 49160 | tf_op jit(solution)/shard_map/ppermute | solution.py:42
  24.8 25.6 %collective-permute-start.6 = (f32[64,32,128]{2,1,0:T(8,128)}, f32[64,32,128]{2,1,0:T(8,128)S(1)}, u32[]{:S(2)}, u32[]{:S(2)}) collective-permute-start(f32[64,32,128]{2,1,0:T(8,128)} %get-tuple-element.102), channel_id=1, source_target_pairs={{0,4},{4,8},{8,12},{12,16},{16,20},{20,24},{24,28},{28,0},{1,5},{5... | collective-permute-start | bytes 3145736 | tf_op jit(solution)/shard_map/ppermute | solution.py:42
  24.8 25.6 %collective-permute-start.7 = (f32[64,32,128]{2,1,0:T(8,128)}, f32[64,32,128]{2,1,0:T(8,128)S(1)}, u32[]{:S(2)}, u32[]{:S(2)}) collective-permute-start(f32[64,32,128]{2,1,0:T(8,128)} %get-tuple-element.103), channel_id=1, source_target_pairs={{0,28},{4,0},{8,4},{12,8},{16,12},{20,16},{24,20},{28,24},{1,29},{... | collective-permute-start | bytes 3145736 | tf_op jit(solution)/shard_map/ppermute | solution.py:42
  28.2 24.9 %collective-permute-start.8 = (f32[256,8,128]{2,1,0:T(8,128)}, f32[256,8,128]{2,1,0:T(8,128)}, u32[]{:S(2)}, u32[]{:S(2)}) collective-permute-start(f32[256,8,128]{2,1,0:T(8,128)} %get-tuple-element.108), channel_id=1, source_target_pairs={{0,1},{1,2},{2,3},{4,5},{5,6},{6,7},{8,9},{9,10},{10,11},{12,13},{... | collective-permute-start | bytes 3145736 | tf_op jit(solution)/shard_map/ppermute | solution.py:48
  31.1 25.4 %collective-permute-start.9 = (f32[256,8,128]{2,1,0:T(8,128)}, f32[256,8,128]{2,1,0:T(8,128)}, u32[]{:S(2)}, u32[]{:S(2)}) collective-permute-start(f32[256,8,128]{2,1,0:T(8,128)} %get-tuple-element.109), channel_id=1, source_target_pairs={{1,0},{2,1},{3,2},{5,4},{6,5},{7,6},{9,8},{10,9},{11,10},{13,12},{... | collective-permute-start | bytes 3145736 | tf_op jit(solution)/shard_map/ppermute | solution.py:48
  50.5 9.9 %collective-permute-start.10 = (f32[2,128]{1,0:T(2,128)S(1)}, f32[2,128]{1,0:T(2,128)S(1)}, u32[]{:S(2)}, u32[]{:S(2)}) collective-permute-start(f32[2,128]{1,0:T(2,128)S(1)} %get-tuple-element.112), channel_id=1, source_target_pairs={{0,4},{4,8},{8,12},{12,16},{16,20},{20,24},{24,28},{28,0},{1,5},{5... | collective-permute-start | bytes 3080 | tf_op jit(solution)/shard_map/ppermute | solution.py:42
  51.6 8.9 %collective-permute-start.11 = (f32[2,128]{1,0:T(2,128)S(1)}, f32[2,128]{1,0:T(2,128)S(1)}, u32[]{:S(2)}, u32[]{:S(2)}) collective-permute-start(f32[2,128]{1,0:T(2,128)S(1)} %get-tuple-element.113), channel_id=1, source_target_pairs={{0,28},{4,0},{8,4},{12,8},{16,12},{20,16},{24,20},{28,24},{1,29},{... | collective-permute-start | bytes 3080 | tf_op jit(solution)/shard_map/ppermute | solution.py:42
  56.5 5.4 %collective-permute-start.12 = (f32[2,128]{1,0:T(2,128)S(1)}, f32[2,128]{1,0:T(2,128)S(1)}, u32[]{:S(2)}, u32[]{:S(2)}) collective-permute-start(f32[2,128]{1,0:T(2,128)S(1)} %get-tuple-element.114), channel_id=1, source_target_pairs={{0,1},{1,2},{2,3},{3,0},{4,5},{5,6},{6,7},{7,4},{8,9},{9,10},{10,1... | collective-permute-start | bytes 3080 | tf_op jit(solution)/shard_map/ppermute | solution.py:42
  57.1 4.8 %collective-permute-start.13 = (f32[2,128]{1,0:T(2,128)S(1)}, f32[2,128]{1,0:T(2,128)S(1)}, u32[]{:S(2)}, u32[]{:S(2)}) collective-permute-start(f32[2,128]{1,0:T(2,128)S(1)} %get-tuple-element.115), channel_id=1, source_target_pairs={{0,3},{1,0},{2,1},{3,2},{4,7},{5,4},{6,5},{7,6},{8,11},{9,8},{10,9... | collective-permute-start | bytes 3080 | tf_op jit(solution)/shard_map/ppermute | solution.py:42
  61.8 17.3 %collective-permute-start.14 = (f32[64,8,128]{2,1,0:T(8,128)S(1)}, f32[64,8,128]{2,1,0:T(8,128)S(1)}, u32[]{:S(2)}, u32[]{:S(2)}) collective-permute-start(f32[64,8,128]{2,1,0:T(8,128)S(1)} %get-tuple-element.118), channel_id=1, source_target_pairs={{0,1},{1,2},{2,3},{4,5},{5,6},{6,7},{8,9},{9,10},{10,11},{12,13},{... | collective-permute-start | bytes 786440 | tf_op jit(solution)/shard_map/ppermute | solution.py:48
  64.2 14.9 %collective-permute-start.15 = (f32[64,8,128]{2,1,0:T(8,128)S(1)}, f32[64,8,128]{2,1,0:T(8,128)S(1)}, u32[]{:S(2)}, u32[]{:S(2)}) collective-permute-start(f32[64,8,128]{2,1,0:T(8,128)S(1)} %get-tuple-element.119), channel_id=1, source_target_pairs={{1,0},{2,1},{3,2},{5,4},{6,5},{7,6},{9,8},{10,9},{11,10},{13,12},{... | collective-permute-start | bytes 786440 | tf_op jit(solution)/shard_map/ppermute | solution.py:48
  66.5 4.3 %collective-permute-start.16 = (f32[2,32,128]{2,1,0:T(8,128)S(1)}, f32[2,32,128]{2,1,0:T(8,128)S(1)}, u32[]{:S(2)}, u32[]{:S(2)}) collective-permute-start(f32[2,32,128]{2,1,0:T(8,128)S(1)} %get-tuple-element.126), channel_id=1, source_target_pairs={{0,4},{4,8},{8,12},{12,16},{16,20},{20,24},{24,28},{28,0},{1,5},{5... | collective-permute-start | bytes 98312 | tf_op jit(solution)/shard_map/ppermute | solution.py:42
  66.5 4.2 %collective-permute-start.17 = (f32[2,32,128]{2,1,0:T(8,128)S(1)}, f32[2,32,128]{2,1,0:T(8,128)S(1)}, u32[]{:S(2)}, u32[]{:S(2)}) collective-permute-start(f32[2,32,128]{2,1,0:T(8,128)S(1)} %get-tuple-element.127), channel_id=1, source_target_pairs={{0,28},{4,0},{8,4},{12,8},{16,12},{20,16},{24,20},{28,24},{1,29},{... | collective-permute-start | bytes 98312 | tf_op jit(solution)/shard_map/ppermute | solution.py:42
  71.3 7.8 %collective-permute-start.18 = (f32[2,8,128]{2,1,0:T(8,128)S(1)}, f32[2,8,128]{2,1,0:T(8,128)S(1)}, u32[]{:S(2)}, u32[]{:S(2)}) collective-permute-start(f32[2,8,128]{2,1,0:T(8,128)S(1)} %get-tuple-element.129), channel_id=1, source_target_pairs={{0,1},{1,2},{2,3},{3,0},{4,5},{5,6},{6,7},{7,4},{8,9},{9,10},{10,1... | collective-permute-start | bytes 24584 | tf_op jit(solution)/shard_map/ppermute | solution.py:42
  74.0 5.1 %collective-permute-start.19 = (f32[2,8,128]{2,1,0:T(8,128)S(1)}, f32[2,8,128]{2,1,0:T(8,128)S(1)}, u32[]{:S(2)}, u32[]{:S(2)}) collective-permute-start(f32[2,8,128]{2,1,0:T(8,128)S(1)} %get-tuple-element.130), channel_id=1, source_target_pairs={{0,3},{1,0},{2,1},{3,2},{4,7},{5,4},{6,5},{7,6},{8,11},{9,8},{10,9... | collective-permute-start | bytes 24584 | tf_op jit(solution)/shard_map/ppermute | solution.py:42
  103.4 5.4 %collective-permute-start.20 = (f32[1,128]{1,0:T(1,128)S(1)}, f32[1,128]{1,0:T(1,128)S(1)}, u32[]{:S(2)}, u32[]{:S(2)}) collective-permute-start(f32[1,128]{1,0:T(1,128)S(1)} %get-tuple-element.133), channel_id=1, source_target_pairs={{0,28},{4,0},{8,4},{12,8},{16,12},{20,16},{24,20},{28,24},{1,29},{... | collective-permute-start | bytes 1544 | tf_op jit(solution)/shard_map/ppermute | solution.py:42
  105.2 3.9 %collective-permute-start.21 = (f32[1,128]{1,0:T(1,128)S(1)}, f32[1,128]{1,0:T(1,128)S(1)}, u32[]{:S(2)}, u32[]{:S(2)}) collective-permute-start(f32[1,128]{1,0:T(1,128)S(1)} %get-tuple-element.134), channel_id=1, source_target_pairs={{0,4},{4,8},{8,12},{12,16},{16,20},{20,24},{24,28},{28,0},{1,5},{5... | collective-permute-start | bytes 1544 | tf_op jit(solution)/shard_map/ppermute | solution.py:42
  105.3 4.9 %collective-permute-start.22 = (f32[1,128]{1,0:T(1,128)S(1)}, f32[1,128]{1,0:T(1,128)S(1)}, u32[]{:S(2)}, u32[]{:S(2)}) collective-permute-start(f32[1,128]{1,0:T(1,128)S(1)} %get-tuple-element.135), channel_id=1, source_target_pairs={{0,3},{1,0},{2,1},{3,2},{4,7},{5,4},{6,5},{7,6},{8,11},{9,8},{10,9... | collective-permute-start | bytes 1544 | tf_op jit(solution)/shard_map/ppermute | solution.py:42
  108.8 5.3 %collective-permute-start.23 = (f32[1,128]{1,0:T(1,128)S(1)}, f32[1,128]{1,0:T(1,128)S(1)}, u32[]{:S(2)}, u32[]{:S(2)}) collective-permute-start(f32[1,128]{1,0:T(1,128)S(1)} %get-tuple-element.136), channel_id=1, source_target_pairs={{0,1},{1,2},{2,3},{3,0},{4,5},{5,6},{6,7},{7,4},{8,9},{9,10},{10,1... | collective-permute-start | bytes 1544 | tf_op jit(solution)/shard_map/ppermute | solution.py:42
  (7 other events, 108.1 us)

commit v7 on v6

--- a/solution.py
+++ b/solution.py
@@ -15,7 +15,7 @@
 TILE = 8
 LANES = 128
 VMEM_ALL = 60 * 1024 * 1024
-VMEM_FLUID = 53 * 1024 * 1024
+VMEM_FLUID = 52 * 1024 * 1024
 VMEM_SOLID = 53 * 1024 * 1024
 BATCH = 8
 HIGHEST = lax.Precision.HIGHEST

time: 116 us -> 116 us (level)
  local copies, waits for them, and re-layouts: 0.28 us -> 1.77 us
  waiting for transfers between devices: 15.9 us -> 14.7 us
    unnamed x14, local copies, waits for them, and re-layouts: 0.28 us -> 1.77 us
    ppermute x18, waiting for transfers between devices: 12.6 us -> 11.4 us  [ring(): lax.ppermute(value, axis, [(i, (i + step) % count) for i in range(count)])]
  transfers between devices with their start and end apart: 24 -> 24, of which waited for: 9 -> 8; matrix products, arithmetic and copies ran while one was open for 0% -> 0% of each run, Pallas kernels for 19% -> 19%
where the time goes in v7:
time: 116 us
  Pallas kernels  52.5 us (45%)
  starting transfers between devices  45.1 us (39%)
  waiting for transfers between devices  14.7 us (13%)
  local copies, waits for them, and re-layouts  1.77 us (2%)
  between operations  1.51 us (1%)
    ppermute x18, starting transfers between devices, ring(): lax.ppermute(value, axis, [(i, (i + step) % count) for i in range(count)])  31.7 us
    pallas_call x1, Pallas kernels, solid_step(): pl.pallas_call(functools.partial(solid_kernel, cells_x, cells_y, depth, p...  24.3 us
    pallas_call x1, Pallas kernels, fluid_call(): pl.pallas_call(functools.partial(fluid_kernel, cells_x, cells_y, depth, n...  15.5 us
    ppermute x6, starting transfers between devices, chain(): return lax.ppermute(value, axis, pairs)  13.3 us
    ppermute x18, waiting for transfers between devices, ring(): lax.ppermute(value, axis, [(i, (i + step) % count) for i in range(count)])  11.4 us
    pallas_call x3, Pallas kernels, packing(): pl.pallas_call(kernel, out_shape=tuple((jax.ShapeDtypeStruct(shape, jnp.f...  4.69 us
    pallas_call x1, Pallas kernels, near_step(): pl.pallas_call(functools.partial(near_kernel, cells_x, cells_y, depth), o...  4.56 us
    pallas_call x4, Pallas kernels, small_call(): pl.pallas_call(kernel, out_shape=tuple((jax.ShapeDtypeStruct(shape, jnp.f...  3.42 us
  transfers between devices with their start and end apart: 24, of which 8 were waited for; matrix products, arithmetic and copies ran while one was open for 0% of the time, Pallas kernels for 19%

profile of v7, /device:TPU:0, one launch (start us, length us, event | category | flops | bytes accessed | tf_op | source)
XLA Modules:
  0.0 115.6 jit_solution(9649807755385303091)
XLA Ops:
  1.3 4.6 %shard_map.130 = (f32[24,32,128]{2,1,0:T(8,128)}, f32[24,32,128]{2,1,0:T(8,128)}, f32[24,32,128]{2,1,0:T(8,128)}, f32[24,32,128]{2,1,0:T(8,128)}, f32[32,128]{1,0:T(8,128)}) custom-call(s32[1]{0:T(128)S(6)} %copy.14.count_ref, f32[8,128]{1,0:T(8,128)} %bitcast.6, f32[32,32,512]{2,1,0:T(8,128)} %temp.4, f32[3,32,32,512]{3,2,1,0:T(8,128)} %velo.3, ...), custom_call_target="tpu_custom_call" | custom-call | bytes 14760000 | tf_op jit(solution)/shard_map/pallas_call | solution.py:193
  6.3 2.9 %collective-permute-start.1 = (f32[24,32,128]{2,1,0:T(8,128)}, f32[24,32,128]{2,1,0:T(8,128)S(1)}, u32[]{:S(2)}, u32[]{:S(2)}) collective-permute-start(f32[24,32,128]{2,1,0:T(8,128)} %get-tuple-element.72), channel_id=1, source_target_pairs={{0,28},{4,0},{8,4},{12,8},{16,12},{20,16},{24,20},{28,24},{1,29},{... | collective-permute-start | bytes 1179656 | tf_op jit(solution)/shard_map/ppermute | solution.py:42
  9.3 4.2 %collective-permute-start.2 = (f32[24,32,128]{2,1,0:T(8,128)}, f32[24,32,128]{2,1,0:T(8,128)S(1)}, u32[]{:S(2)}, u32[]{:S(2)}) collective-permute-start(f32[24,32,128]{2,1,0:T(8,128)} %get-tuple-element.86.own_hi), channel_id=1, source_target_pairs={{0,1},{1,2},{2,3},{4,5},{5,6},{6,7},{8,9},{9,10},{10,11},{12,13},{... | collective-permute-start | bytes 1179656 | tf_op jit(solution)/shard_map/ppermute | solution.py:48
  14.9 4.6 %shard_map.131 = (f32[64,32,128]{2,1,0:T(8,128)}, f32[64,32,128]{2,1,0:T(8,128)}, f32[256,8,128]{2,1,0:T(8,128)}, f32[256,8,128]{2,1,0:T(8,128)}) custom-call(f32[32,32,256]{2,1,0:T(8,128)} %cond.1, f32[32,32,256]{2,1,0:T(8,128)} %sink.1, f32[32,32,256]{2,1,0:T(8,128)} %heat.1, f32[32,32,256]{2,1,0:T(8,128)} %temp.5), custom_call_target="tpu_custom_call" | custom-call | bytes 11070000 | tf_op jit(solution)/shard_map/pallas_call | solution.py:260
  20.0 2.7 %collective-permute-start.4 = (f32[8,512]{1,0:T(8,128)S(1)}, f32[8,512]{1,0:T(8,128)S(1)}, u32[]{:S(2)}, u32[]{:S(2)}) collective-permute-start(f32[8,512]{1,0:T(8,128)S(1)} %get-tuple-element.88), channel_id=1, source_target_pairs={{0,1},{1,2},{2,3},{3,0},{4,5},{5,6},{6,7},{7,4},{8,9},{9,10},{10,1... | collective-permute-start | bytes 49160 | tf_op jit(solution)/shard_map/ppermute | solution.py:42
  22.7 2.1 %collective-permute-start.5 = (f32[8,512]{1,0:T(8,128)S(1)}, f32[8,512]{1,0:T(8,128)S(1)}, u32[]{:S(2)}, u32[]{:S(2)}) collective-permute-start(f32[8,512]{1,0:T(8,128)S(1)} %get-tuple-element.89), channel_id=1, source_target_pairs={{0,3},{1,0},{2,1},{3,2},{4,7},{5,4},{6,5},{7,6},{8,11},{9,8},{10,9... | collective-permute-start | bytes 49160 | tf_op jit(solution)/shard_map/ppermute | solution.py:42
  24.8 2.6 %collective-permute-start.7 = (f32[64,32,128]{2,1,0:T(8,128)}, f32[64,32,128]{2,1,0:T(8,128)S(1)}, u32[]{:S(2)}, u32[]{:S(2)}) collective-permute-start(f32[64,32,128]{2,1,0:T(8,128)} %get-tuple-element.103), channel_id=1, source_target_pairs={{0,28},{4,0},{8,4},{12,8},{16,12},{20,16},{24,20},{28,24},{1,29},{... | collective-permute-start | bytes 3145736 | tf_op jit(solution)/shard_map/ppermute | solution.py:42
  28.2 2.8 %collective-permute-start.8 = (f32[256,8,128]{2,1,0:T(8,128)}, f32[256,8,128]{2,1,0:T(8,128)}, u32[]{:S(2)}, u32[]{:S(2)}) collective-permute-start(f32[256,8,128]{2,1,0:T(8,128)} %get-tuple-element.108), channel_id=1, source_target_pairs={{0,1},{1,2},{2,3},{4,5},{5,6},{6,7},{8,9},{9,10},{10,11},{12,13},{... | collective-permute-start | bytes 3145736 | tf_op jit(solution)/shard_map/ppermute | solution.py:48
  33.5 15.5 %shard_map.134 = (f32[32,32,512]{2,1,0:T(8,128)}, f32[2,1024]{1,0:T(2,128)S(1)}, f32[2,128]{1,0:T(2,128)S(1)}, f32[2,128]{1,0:T(2,128)S(1)}, f32[2,128]{1,0:T(2,128)S(1)}, /*index=5*/f32[2,128]{1,0:T(2,128)S(1)}) custom-call(s32[5]{0:T(128)S(1)} %pad_add_fusion.flags, f32[32,128]{1,0:T(8,128)S(1)} %copy-done.5, f32[24,32,128]{2,1,0:T(8,128)S(1)} %collective-permute-done.xlo, ...), custom_call_target="tpu_custom_call" | custom-call | bytes 3690000 | tf_op jit(solution)/shard_map/pallas_call | solution.py:485
  49.0 1.4 %collective-permute-done.6.xlo = f32[64,32,128]{2,1,0:T(8,128)S(1)} collective-permute-done((f32[64,32,128]{2,1,0:T(8,128)}, f32[64,32,128]{2,1,0:T(8,128)S(1)}, u32[]{:S(2)}, u32[]{:S(2)}) %collective-permute-start.6) | collective-permute-done | bytes 1048608 | tf_op jit(solution)/shard_map/ppermute | solution.py:42
  51.5 1.6 %collective-permute-start.11 = (f32[2,128]{1,0:T(2,128)S(1)}, f32[2,128]{1,0:T(2,128)S(1)}, u32[]{:S(2)}, u32[]{:S(2)}) collective-permute-start(f32[2,128]{1,0:T(2,128)S(1)} %get-tuple-element.113), channel_id=1, source_target_pairs={{0,28},{4,0},{8,4},{12,8},{16,12},{20,16},{24,20},{28,24},{1,29},{... | collective-permute-start | bytes 3080 | tf_op jit(solution)/shard_map/ppermute | solution.py:42
  53.2 3.3 %collective-permute-done.9.yhi = f32[256,8,128]{2,1,0:T(8,128)} collective-permute-done((f32[256,8,128]{2,1,0:T(8,128)}, f32[256,8,128]{2,1,0:T(8,128)}, u32[]{:S(2)}, u32[]{:S(2)}) %collective-permute-start.9) | collective-permute-done | bytes 1048608 | tf_op jit(solution)/shard_map/ppermute | solution.py:48
  57.1 3.2 %collective-permute-start.13 = (f32[2,128]{1,0:T(2,128)S(1)}, f32[2,128]{1,0:T(2,128)S(1)}, u32[]{:S(2)}, u32[]{:S(2)}) collective-permute-start(f32[2,128]{1,0:T(2,128)S(1)} %get-tuple-element.115), channel_id=1, source_target_pairs={{0,3},{1,0},{2,1},{3,2},{4,7},{5,4},{6,5},{7,6},{8,11},{9,8},{10,9... | collective-permute-start | bytes 3080 | tf_op jit(solution)/shard_map/ppermute | solution.py:42
  61.8 2.3 %collective-permute-start.14 = (f32[64,8,128]{2,1,0:T(8,128)S(1)}, f32[64,8,128]{2,1,0:T(8,128)S(1)}, u32[]{:S(2)}, u32[]{:S(2)}) collective-permute-start(f32[64,8,128]{2,1,0:T(8,128)S(1)} %get-tuple-element.118), channel_id=1, source_target_pairs={{0,1},{1,2},{2,3},{4,5},{5,6},{6,7},{8,9},{9,10},{10,11},{12,13},{... | collective-permute-start | bytes 786440 | tf_op jit(solution)/shard_map/ppermute | solution.py:48
  66.5 2.6 %collective-permute-start.17 = (f32[2,32,128]{2,1,0:T(8,128)S(1)}, f32[2,32,128]{2,1,0:T(8,128)S(1)}, u32[]{:S(2)}, u32[]{:S(2)}) collective-permute-start(f32[2,32,128]{2,1,0:T(8,128)S(1)} %get-tuple-element.127), channel_id=1, source_target_pairs={{0,28},{4,0},{8,4},{12,8},{16,12},{20,16},{24,20},{28,24},{1,29},{... | collective-permute-start | bytes 98312 | tf_op jit(solution)/shard_map/ppermute | solution.py:42
  69.1 1.6 %collective-permute-done.16.low = f32[2,32,128]{2,1,0:T(8,128)S(1)} collective-permute-done((f32[2,32,128]{2,1,0:T(8,128)S(1)}, f32[2,32,128]{2,1,0:T(8,128)S(1)}, u32[]{:S(2)}, u32[]{:S(2)}) %collective-permute-start.16) | collective-permute-done | bytes 32800 | tf_op jit(solution)/shard_map/ppermute | solution.py:42
  71.3 2.7 %collective-permute-start.18 = (f32[2,8,128]{2,1,0:T(8,128)S(1)}, f32[2,8,128]{2,1,0:T(8,128)S(1)}, u32[]{:S(2)}, u32[]{:S(2)}) collective-permute-start(f32[2,8,128]{2,1,0:T(8,128)S(1)} %get-tuple-element.129), channel_id=1, source_target_pairs={{0,1},{1,2},{2,3},{3,0},{4,5},{5,6},{6,7},{7,4},{8,9},{9,10},{10,1... | collective-permute-start | bytes 24584 | tf_op jit(solution)/shard_map/ppermute | solution.py:42
  74.0 3.5 %collective-permute-start.19 = (f32[2,8,128]{2,1,0:T(8,128)S(1)}, f32[2,8,128]{2,1,0:T(8,128)S(1)}, u32[]{:S(2)}, u32[]{:S(2)}) collective-permute-start(f32[2,8,128]{2,1,0:T(8,128)S(1)} %get-tuple-element.130), channel_id=1, source_target_pairs={{0,3},{1,0},{2,1},{3,2},{4,7},{5,4},{6,5},{7,6},{8,11},{9,8},{10,9... | collective-permute-start | bytes 24584 | tf_op jit(solution)/shard_map/ppermute | solution.py:42
  77.5 1.6 %collective-permute-done.18.film_lo = f32[2,8,128]{2,1,0:T(8,128)S(1)} collective-permute-done((f32[2,8,128]{2,1,0:T(8,128)S(1)}, f32[2,8,128]{2,1,0:T(8,128)S(1)}, u32[]{:S(2)}, u32[]{:S(2)}) %collective-permute-start.18) | collective-permute-done | bytes 8224 | tf_op jit(solution)/shard_map/ppermute | solution.py:42
  79.1 24.3 %shard_map.138 = (f32[32,32,256]{2,1,0:T(8,128)}, f32[1,1024]{1,0:T(1,128)S(1)}, f32[1,128]{1,0:T(1,128)S(1)}, f32[1,128]{1,0:T(1,128)S(1)}, f32[1,128]{1,0:T(1,128)S(1)}, /*index=5*/f32[1,128]{1,0:T(1,128)S(1)}) custom-call(s32[5]{0:T(128)S(1)} %pad_add_fusion.flags, f32[32,32,256]{2,1,0:T(8,128)} %cond.1, f32[32,32,256]{2,1,0:T(8,128)} %sink.1, ...), custom_call_target="tpu_custom_call" | custom-call | bytes 110700000 | tf_op jit(solution)/shard_map/pallas_call | solution.py:657
  103.4 1.8 %collective-permute-start.20 = (f32[1,128]{1,0:T(1,128)S(1)}, f32[1,128]{1,0:T(1,128)S(1)}, u32[]{:S(2)}, u32[]{:S(2)}) collective-permute-start(f32[1,128]{1,0:T(1,128)S(1)} %get-tuple-element.133), channel_id=1, source_target_pairs={{0,28},{4,0},{8,4},{12,8},{16,12},{20,16},{24,20},{28,24},{1,29},{... | collective-permute-start | bytes 1544 | tf_op jit(solution)/shard_map/ppermute | solution.py:42
  105.3 3.6 %collective-permute-start.22 = (f32[1,128]{1,0:T(1,128)S(1)}, f32[1,128]{1,0:T(1,128)S(1)}, u32[]{:S(2)}, u32[]{:S(2)}) collective-permute-start(f32[1,128]{1,0:T(1,128)S(1)} %get-tuple-element.135), channel_id=1, source_target_pairs={{0,3},{1,0},{2,1},{3,2},{4,7},{5,4},{6,5},{7,6},{8,11},{9,8},{10,9... | collective-permute-start | bytes 1544 | tf_op jit(solution)/shard_map/ppermute | solution.py:42
  110.1 4.0 %collective-permute-done.23.from_3 = f32[1,128]{1,0:T(1,128)S(1)} collective-permute-done((f32[1,128]{1,0:T(1,128)S(1)}, f32[1,128]{1,0:T(1,128)S(1)}, u32[]{:S(2)}, u32[]{:S(2)}) %collective-permute-start.23) | collective-permute-done | bytes 544 | tf_op jit(solution)/shard_map/ppermute | solution.py:42
  114.2 1.4 %shard_map.139 = f32[1,1024]{1,0:T(1,128)} custom-call(s32[5]{0:T(128)S(1)} %pad_add_fusion.flags, f32[8,1024]{1,0:T(8,128)S(1)} %shard_map.132.route, f32[1,1024]{1,0:T(1,128)S(1)} %get-tuple-element.132.own, f32[1,128]{1,0:T(1,128)S(1)} %collective-permute-done.20.from_0, f32[1,128]{1,0:T(1,128)S(1)} %collective-permute-done.21.from_1, ...), custom_call_target="tpu_custom_call" | custom-call | bytes 3690000 | tf_op jit(solution)/shard_map/pallas_call | solution.py:774
  (50 shorter events, 13.0 us)
Async XLA Ops:
  5.8 13.7 %collective-permute-start = (f32[24,32,128]{2,1,0:T(8,128)}, f32[24,32,128]{2,1,0:T(8,128)S(1)}, u32[]{:S(2)}, u32[]{:S(2)}) collective-permute-start(f32[24,32,128]{2,1,0:T(8,128)} %get-tuple-element.71), channel_id=1, source_target_pairs={{0,4},{4,8},{8,12},{12,16},{16,20},{20,24},{24,28},{28,0},{1,5},{5... | collective-permute-start | bytes 1179656 | tf_op jit(solution)/shard_map/ppermute | solution.py:42
  6.3 13.2 %collective-permute-start.1 = (f32[24,32,128]{2,1,0:T(8,128)}, f32[24,32,128]{2,1,0:T(8,128)S(1)}, u32[]{:S(2)}, u32[]{:S(2)}) collective-permute-start(f32[24,32,128]{2,1,0:T(8,128)} %get-tuple-element.72), channel_id=1, source_target_pairs={{0,28},{4,0},{8,4},{12,8},{16,12},{20,16},{24,20},{28,24},{1,29},{... | collective-permute-start | bytes 1179656 | tf_op jit(solution)/shard_map/ppermute | solution.py:42
  9.3 15.5 %collective-permute-start.2 = (f32[24,32,128]{2,1,0:T(8,128)}, f32[24,32,128]{2,1,0:T(8,128)S(1)}, u32[]{:S(2)}, u32[]{:S(2)}) collective-permute-start(f32[24,32,128]{2,1,0:T(8,128)} %get-tuple-element.86.own_hi), channel_id=1, source_target_pairs={{0,1},{1,2},{2,3},{4,5},{5,6},{6,7},{8,9},{9,10},{10,11},{12,13},{... | collective-permute-start | bytes 1179656 | tf_op jit(solution)/shard_map/ppermute | solution.py:48
  13.5 14.0 %collective-permute-start.3 = (f32[24,32,128]{2,1,0:T(8,128)}, f32[24,32,128]{2,1,0:T(8,128)S(1)}, u32[]{:S(2)}, u32[]{:S(2)}) collective-permute-start(f32[24,32,128]{2,1,0:T(8,128)} %get-tuple-element.87.own_lo), channel_id=1, source_target_pairs={{1,0},{2,1},{3,2},{5,4},{6,5},{7,6},{9,8},{10,9},{11,10},{13,12},{... | collective-permute-start | bytes 1179656 | tf_op jit(solution)/shard_map/ppermute | solution.py:48
  20.0 8.2 %collective-permute-start.4 = (f32[8,512]{1,0:T(8,128)S(1)}, f32[8,512]{1,0:T(8,128)S(1)}, u32[]{:S(2)}, u32[]{:S(2)}) collective-permute-start(f32[8,512]{1,0:T(8,128)S(1)} %get-tuple-element.88), channel_id=1, source_target_pairs={{0,1},{1,2},{2,3},{3,0},{4,5},{5,6},{6,7},{7,4},{8,9},{9,10},{10,1... | collective-permute-start | bytes 49160 | tf_op jit(solution)/shard_map/ppermute | solution.py:42
  22.7 5.5 %collective-permute-start.5 = (f32[8,512]{1,0:T(8,128)S(1)}, f32[8,512]{1,0:T(8,128)S(1)}, u32[]{:S(2)}, u32[]{:S(2)}) collective-permute-start(f32[8,512]{1,0:T(8,128)S(1)} %get-tuple-element.89), channel_id=1, source_target_pairs={{0,3},{1,0},{2,1},{3,2},{4,7},{5,4},{6,5},{7,6},{8,11},{9,8},{10,9... | collective-permute-start | bytes 49160 | tf_op jit(solution)/shard_map/ppermute | solution.py:42
  24.8 25.6 %collective-permute-start.6 = (f32[64,32,128]{2,1,0:T(8,128)}, f32[64,32,128]{2,1,0:T(8,128)S(1)}, u32[]{:S(2)}, u32[]{:S(2)}) collective-permute-start(f32[64,32,128]{2,1,0:T(8,128)} %get-tuple-element.102), channel_id=1, source_target_pairs={{0,4},{4,8},{8,12},{12,16},{16,20},{20,24},{24,28},{28,0},{1,5},{5... | collective-permute-start | bytes 3145736 | tf_op jit(solution)/shard_map/ppermute | solution.py:42
  24.8 25.6 %collective-permute-start.7 = (f32[64,32,128]{2,1,0:T(8,128)}, f32[64,32,128]{2,1,0:T(8,128)S(1)}, u32[]{:S(2)}, u32[]{:S(2)}) collective-permute-start(f32[64,32,128]{2,1,0:T(8,128)} %get-tuple-element.103), channel_id=1, source_target_pairs={{0,28},{4,0},{8,4},{12,8},{16,12},{20,16},{24,20},{28,24},{1,29},{... | collective-permute-start | bytes 3145736 | tf_op jit(solution)/shard_map/ppermute | solution.py:42
  28.2 24.9 %collective-permute-start.8 = (f32[256,8,128]{2,1,0:T(8,128)}, f32[256,8,128]{2,1,0:T(8,128)}, u32[]{:S(2)}, u32[]{:S(2)}) collective-permute-start(f32[256,8,128]{2,1,0:T(8,128)} %get-tuple-element.108), channel_id=1, source_target_pairs={{0,1},{1,2},{2,3},{4,5},{5,6},{6,7},{8,9},{9,10},{10,11},{12,13},{... | collective-permute-start | bytes 3145736 | tf_op jit(solution)/shard_map/ppermute | solution.py:48
  31.1 25.4 %collective-permute-start.9 = (f32[256,8,128]{2,1,0:T(8,128)}, f32[256,8,128]{2,1,0:T(8,128)}, u32[]{:S(2)}, u32[]{:S(2)}) collective-permute-start(f32[256,8,128]{2,1,0:T(8,128)} %get-tuple-element.109), channel_id=1, source_target_pairs={{1,0},{2,1},{3,2},{5,4},{6,5},{7,6},{9,8},{10,9},{11,10},{13,12},{... | collective-permute-start | bytes 3145736 | tf_op jit(solution)/shard_map/ppermute | solution.py:48
  50.5 9.9 %collective-permute-start.10 = (f32[2,128]{1,0:T(2,128)S(1)}, f32[2,128]{1,0:T(2,128)S(1)}, u32[]{:S(2)}, u32[]{:S(2)}) collective-permute-start(f32[2,128]{1,0:T(2,128)S(1)} %get-tuple-element.112), channel_id=1, source_target_pairs={{0,4},{4,8},{8,12},{12,16},{16,20},{20,24},{24,28},{28,0},{1,5},{5... | collective-permute-start | bytes 3080 | tf_op jit(solution)/shard_map/ppermute | solution.py:42
  51.5 8.9 %collective-permute-start.11 = (f32[2,128]{1,0:T(2,128)S(1)}, f32[2,128]{1,0:T(2,128)S(1)}, u32[]{:S(2)}, u32[]{:S(2)}) collective-permute-start(f32[2,128]{1,0:T(2,128)S(1)} %get-tuple-element.113), channel_id=1, source_target_pairs={{0,28},{4,0},{8,4},{12,8},{16,12},{20,16},{24,20},{28,24},{1,29},{... | collective-permute-start | bytes 3080 | tf_op jit(solution)/shard_map/ppermute | solution.py:42
  56.5 5.4 %collective-permute-start.12 = (f32[2,128]{1,0:T(2,128)S(1)}, f32[2,128]{1,0:T(2,128)S(1)}, u32[]{:S(2)}, u32[]{:S(2)}) collective-permute-start(f32[2,128]{1,0:T(2,128)S(1)} %get-tuple-element.114), channel_id=1, source_target_pairs={{0,1},{1,2},{2,3},{3,0},{4,5},{5,6},{6,7},{7,4},{8,9},{9,10},{10,1... | collective-permute-start | bytes 3080 | tf_op jit(solution)/shard_map/ppermute | solution.py:42
  57.1 4.8 %collective-permute-start.13 = (f32[2,128]{1,0:T(2,128)S(1)}, f32[2,128]{1,0:T(2,128)S(1)}, u32[]{:S(2)}, u32[]{:S(2)}) collective-permute-start(f32[2,128]{1,0:T(2,128)S(1)} %get-tuple-element.115), channel_id=1, source_target_pairs={{0,3},{1,0},{2,1},{3,2},{4,7},{5,4},{6,5},{7,6},{8,11},{9,8},{10,9... | collective-permute-start | bytes 3080 | tf_op jit(solution)/shard_map/ppermute | solution.py:42
  61.8 17.3 %collective-permute-start.14 = (f32[64,8,128]{2,1,0:T(8,128)S(1)}, f32[64,8,128]{2,1,0:T(8,128)S(1)}, u32[]{:S(2)}, u32[]{:S(2)}) collective-permute-start(f32[64,8,128]{2,1,0:T(8,128)S(1)} %get-tuple-element.118), channel_id=1, source_target_pairs={{0,1},{1,2},{2,3},{4,5},{5,6},{6,7},{8,9},{9,10},{10,11},{12,13},{... | collective-permute-start | bytes 786440 | tf_op jit(solution)/shard_map/ppermute | solution.py:48
  64.2 15.0 %collective-permute-start.15 = (f32[64,8,128]{2,1,0:T(8,128)S(1)}, f32[64,8,128]{2,1,0:T(8,128)S(1)}, u32[]{:S(2)}, u32[]{:S(2)}) collective-permute-start(f32[64,8,128]{2,1,0:T(8,128)S(1)} %get-tuple-element.119), channel_id=1, source_target_pairs={{1,0},{2,1},{3,2},{5,4},{6,5},{7,6},{9,8},{10,9},{11,10},{13,12},{... | collective-permute-start | bytes 786440 | tf_op jit(solution)/shard_map/ppermute | solution.py:48
  66.4 4.3 %collective-permute-start.16 = (f32[2,32,128]{2,1,0:T(8,128)S(1)}, f32[2,32,128]{2,1,0:T(8,128)S(1)}, u32[]{:S(2)}, u32[]{:S(2)}) collective-permute-start(f32[2,32,128]{2,1,0:T(8,128)S(1)} %get-tuple-element.126), channel_id=1, source_target_pairs={{0,4},{4,8},{8,12},{12,16},{16,20},{20,24},{24,28},{28,0},{1,5},{5... | collective-permute-start | bytes 98312 | tf_op jit(solution)/shard_map/ppermute | solution.py:42
  66.5 4.2 %collective-permute-start.17 = (f32[2,32,128]{2,1,0:T(8,128)S(1)}, f32[2,32,128]{2,1,0:T(8,128)S(1)}, u32[]{:S(2)}, u32[]{:S(2)}) collective-permute-start(f32[2,32,128]{2,1,0:T(8,128)S(1)} %get-tuple-element.127), channel_id=1, source_target_pairs={{0,28},{4,0},{8,4},{12,8},{16,12},{20,16},{24,20},{28,24},{1,29},{... | collective-permute-start | bytes 98312 | tf_op jit(solution)/shard_map/ppermute | solution.py:42
  71.3 7.8 %collective-permute-start.18 = (f32[2,8,128]{2,1,0:T(8,128)S(1)}, f32[2,8,128]{2,1,0:T(8,128)S(1)}, u32[]{:S(2)}, u32[]{:S(2)}) collective-permute-start(f32[2,8,128]{2,1,0:T(8,128)S(1)} %get-tuple-element.129), channel_id=1, source_target_pairs={{0,1},{1,2},{2,3},{3,0},{4,5},{5,6},{6,7},{7,4},{8,9},{9,10},{10,1... | collective-permute-start | bytes 24584 | tf_op jit(solution)/shard_map/ppermute | solution.py:42
  74.0 5.1 %collective-permute-start.19 = (f32[2,8,128]{2,1,0:T(8,128)S(1)}, f32[2,8,128]{2,1,0:T(8,128)S(1)}, u32[]{:S(2)}, u32[]{:S(2)}) collective-permute-start(f32[2,8,128]{2,1,0:T(8,128)S(1)} %get-tuple-element.130), channel_id=1, source_target_pairs={{0,3},{1,0},{2,1},{3,2},{4,7},{5,4},{6,5},{7,6},{8,11},{9,8},{10,9... | collective-permute-start | bytes 24584 | tf_op jit(solution)/shard_map/ppermute | solution.py:42
  103.4 5.4 %collective-permute-start.20 = (f32[1,128]{1,0:T(1,128)S(1)}, f32[1,128]{1,0:T(1,128)S(1)}, u32[]{:S(2)}, u32[]{:S(2)}) collective-permute-start(f32[1,128]{1,0:T(1,128)S(1)} %get-tuple-element.133), channel_id=1, source_target_pairs={{0,28},{4,0},{8,4},{12,8},{16,12},{20,16},{24,20},{28,24},{1,29},{... | collective-permute-start | bytes 1544 | tf_op jit(solution)/shard_map/ppermute | solution.py:42
  105.3 3.9 %collective-permute-start.21 = (f32[1,128]{1,0:T(1,128)S(1)}, f32[1,128]{1,0:T(1,128)S(1)}, u32[]{:S(2)}, u32[]{:S(2)}) collective-permute-start(f32[1,128]{1,0:T(1,128)S(1)} %get-tuple-element.134), channel_id=1, source_target_pairs={{0,4},{4,8},{8,12},{12,16},{16,20},{20,24},{24,28},{28,0},{1,5},{5... | collective-permute-start | bytes 1544 | tf_op jit(solution)/shard_map/ppermute | solution.py:42
  105.3 4.9 %collective-permute-start.22 = (f32[1,128]{1,0:T(1,128)S(1)}, f32[1,128]{1,0:T(1,128)S(1)}, u32[]{:S(2)}, u32[]{:S(2)}) collective-permute-start(f32[1,128]{1,0:T(1,128)S(1)} %get-tuple-element.135), channel_id=1, source_target_pairs={{0,3},{1,0},{2,1},{3,2},{4,7},{5,4},{6,5},{7,6},{8,11},{9,8},{10,9... | collective-permute-start | bytes 1544 | tf_op jit(solution)/shard_map/ppermute | solution.py:42
  108.9 5.3 %collective-permute-start.23 = (f32[1,128]{1,0:T(1,128)S(1)}, f32[1,128]{1,0:T(1,128)S(1)}, u32[]{:S(2)}, u32[]{:S(2)}) collective-permute-start(f32[1,128]{1,0:T(1,128)S(1)} %get-tuple-element.136), channel_id=1, source_target_pairs={{0,1},{1,2},{2,3},{3,0},{4,5},{5,6},{6,7},{7,4},{8,9},{9,10},{10,1... | collective-permute-start | bytes 1544 | tf_op jit(solution)/shard_map/ppermute | solution.py:42
  (7 other events, 100.6 us)
